TPU v7x, 128 devices: a whole 4x4x4 slice. The times are simulated.
128 devices in a mesh: seq: 32 (over x, z, core), tp: 4 (over y).
Axes of the slice: x: 4, y: 4, z: 4, core: 2. Of those that a mesh axis runs over, the one named last changes fastest.
Arguments:
- tokens: bfloat16 [16384, 1024], P('seq'), may hold values from -6 to 6
- segment_start: int32 [8, 4], replicated, may hold values from 0 to 1, as said below
- norm_win: float32 [1024], replicated, may hold values from 0.5 to 1.5
- qkv_win: bfloat16 [1024, 3, 1024], P(None, None, 'tp'), may hold values from -0.1875 to 0.1875
- out_win: bfloat16 [1024, 1024], P('tp'), may hold values from -2 to 2
- norm_wffn: float32 [1024], replicated, may hold values from 0.5 to 1.5
- up_win: bfloat16 [1024, 4096], P(None, 'tp'), may hold values from -0.1875 to 0.1875
- down_win: bfloat16 [4096, 1024], P('tp'), may hold values from -0.09375 to 0.09375
- norm_tok: float32 [1024], replicated, may hold values from 0.5 to 1.5
- qkv_tok: bfloat16 [1024, 3, 1024], P(None, None, 'tp'), may hold values from -0.1875 to 0.1875
- out_tok: bfloat16 [2, 1024, 1024], P(None, 'tp'), may hold values from -2 to 2
- norm_ffn: float32 [1024], replicated, may hold values from 0.5 to 1.5
- up_tok: bfloat16 [1024, 4096], P(None, 'tp'), may hold values from -0.1875 to 0.1875
- down_tok: bfloat16 [4096, 1024], P('tp'), may hold values from -0.09375 to 0.09375
- norm_state: float32 [1024], replicated, may hold values from 0.5 to 1.5
- qkv_state: bfloat16 [1024, 3, 1024], P(None, None, 'tp'), may hold values from -0.1875 to 0.1875
- out_state: bfloat16 [2, 1024, 1024], P(None, 'tp'), may hold values from -2 to 2
- gate_bias: float32 [2, 1024], replicated, may hold values from 0 to 5
- norm_sffn: float32 [1024], replicated, may hold values from 0.5 to 1.5
- up_state: bfloat16 [1024, 4096], P(None, 'tp'), may hold values from -0.1875 to 0.1875
- down_state: bfloat16 [4096, 1024], P('tp'), may hold values from -0.09375 to 0.09375
- init_state: bfloat16 [512, 1024], replicated, may hold values from -6 to 6
- cotangent: bfloat16 [16384, 1024], P('seq'), may hold values from -6 to 6
Outputs:
- layer_output: bfloat16 [16384, 1024], P('seq')
- block_states: bfloat16 [16384, 1024], P('seq')
- grad_tokens: bfloat16 [16384, 1024], P('seq')
- grad_norm_win: float32 [1024], P('seq')
- grad_qkv_win: float32 [1024, 3, 1024], P('seq', None, 'tp')
- grad_out_win: float32 [1024, 1024], P('tp', 'seq')
- grad_norm_wffn: float32 [1024], P('seq')
- grad_up_win: float32 [1024, 4096], P('seq', 'tp')
- grad_down_win: float32 [4096, 1024], P('tp', 'seq')
- grad_norm_tok: float32 [1024], P('seq')
- grad_qkv_tok: float32 [1024, 3, 1024], P('seq', None, 'tp')
- grad_out_tok: float32 [2, 1024, 1024], P(None, 'tp', 'seq')
- grad_norm_ffn: float32 [1024], P('seq')
- grad_up_tok: float32 [1024, 4096], P('seq', 'tp')
- grad_down_tok: float32 [4096, 1024], P('tp', 'seq')
- grad_norm_state: float32 [1024], P('seq')
- grad_qkv_state: float32 [1024, 3, 1024], P('seq', None, 'tp')
- grad_out_state: float32 [2, 1024, 1024], P(None, 'tp', 'seq')
- grad_gate_bias: float32 [2, 1024], P(None, 'seq')
- grad_norm_sffn: float32 [1024], P('seq')
- grad_up_state: float32 [1024, 4096], P('seq', 'tp')
- grad_down_state: float32 [4096, 1024], P('tp', 'seq')
- grad_init_state: float32 [512, 1024], P(None, 'seq')
Inputs may be any that keep to these rules, and one draw needn't show every extreme that they name: segment_start[m, 0] = 1 for every m; segment_start[m, j] may be 1 only at j = 2 besides, so that segments span 4 or 2 blocks; at least one sequence is a single segment.
All inputs are finite; a program needn't handle non-finite values.
Results may differ from a plain program's by a relative error of at most 0.03.
Values may be sent and summed in bfloat16 or wider, within the bound.
No kernel may reach another device: no remote copies, remote signals or barrier semaphores. Data moves between devices by JAX's collectives and lax.ppermute only.
A program may use at most 256 MiB of HBM per device.

v0:
```python
import jax
import jax.numpy as jnp
from jax import lax
from jax.sharding import PartitionSpec as P

E = 128
CHAIN = 4


EPSILON = 1e-05
MASKED = -1e30


def passed_along(array, axis, by):
    devices = lax.axis_size(axis)
    pairs = [(i, i + by) for i in range(devices) if 0 <= i + by < devices]
    return lax.ppermute(array, axis, pairs)


def layer_norm(matrix, weights):
    average = jnp.mean(matrix, axis=-1, keepdims=True)
    centred = matrix - average
    spread = jnp.mean(centred * centred, axis=-1, keepdims=True)
    return centred * lax.rsqrt(spread + EPSILON) * weights


def gelu_exact(matrix):
    return jax.nn.gelu(matrix, approximate=False)


def plain_dot(former, latter):
    return jnp.dot(former, latter, preferred_element_type=jnp.float32)


def dot_first(former, latter):
    return lax.dot_general(
        former, latter, (((0,), (0,)), ((), ())), preferred_element_type=jnp.float32
    )


def dot_second(former, latter):
    return lax.dot_general(
        former, latter, (((1,), (1,)), ((), ())), preferred_element_type=jnp.float32
    )


def split_heads(matrix):
    return matrix.reshape(matrix.shape[0], -1, E)


def flatten(matrix):
    return matrix.reshape(matrix.shape[0], -1)


def zeros_low(row_count, col_count):
    return jnp.zeros((row_count, col_count), jnp.bfloat16)


def zeros_high(row_count, col_count):
    return jnp.zeros((row_count, col_count), jnp.float32)


def run_when(active, work):

    def resting():
        return jax.tree.map(jnp.zeros_like, work())

    return lax.cond(active, work, resting)


def pick(active, fresh, older):
    return jax.tree.map(
        lambda fresh_one, older_one: jnp.where(active, fresh_one, older_one), fresh, older
    )


def send_forward(paired):
    return passed_along(paired, "seq", 1)


def send_backward(paired):
    return passed_along(paired.astype(jnp.bfloat16), "seq", -1).astype(paired.dtype)


def heads_sum(heads, out_flat):
    return lax.psum(plain_dot(heads, out_flat).astype(jnp.bfloat16), "tp").astype(jnp.float32)


def mlp_sum(active, down):
    return lax.psum(plain_dot(active, down).astype(jnp.bfloat16), "tp").astype(jnp.float32)


def mlp_back_sum(grad_hidden, up):
    return lax.psum(dot_second(grad_hidden, up).astype(jnp.bfloat16), "tp").astype(jnp.float32)


def input_back_sum(grad_qkv, qkv_flat):
    return lax.psum(dot_second(grad_qkv, qkv_flat).astype(jnp.bfloat16), "tp").astype(jnp.float32)


def head_scores(queries, key_rows, allowed):
    raw_scores = jnp.einsum(
        "rhe,khe->hrk",
        split_heads(queries),
        split_heads(key_rows),
        preferred_element_type=jnp.float32,
    )
    return jnp.where(allowed, raw_scores * E ** (-0.5), MASKED)


def attend(queries, key_rows, value_rows, allowed):
    scores = head_scores(queries, key_rows, allowed)
    row_max = jnp.max(scores, axis=-1, keepdims=True)
    powers = jnp.exp(scores - row_max)
    totals = jnp.sum(powers, axis=-1, keepdims=True)
    chances = (powers / totals).astype(jnp.bfloat16)
    result = jnp.einsum(
        "hrk,khe->rhe", chances, split_heads(value_rows), preferred_element_type=jnp.float32
    )
    return (flatten(result).astype(jnp.bfloat16), row_max + jnp.log(totals))


def attend_back(queries, key_rows, value_rows, allowed, log_sums, grad_result):
    chances = jnp.exp(head_scores(queries, key_rows, allowed) - log_sums)
    grad_heads = split_heads(grad_result)
    grad_chances = jnp.einsum(
        "rhe,khe->hrk", grad_heads, split_heads(value_rows), preferred_element_type=jnp.float32
    )
    grad_values = jnp.einsum(
        "hrk,rhe->khe", chances.astype(jnp.bfloat16), grad_heads, preferred_element_type=jnp.float32
    )
    inner_sum = jnp.sum(chances * grad_chances, axis=-1, keepdims=True)
    grad_scores = (chances * (grad_chances - inner_sum) * E ** (-0.5)).astype(jnp.bfloat16)
    grad_queries = jnp.einsum(
        "hrk,khe->rhe", grad_scores, split_heads(key_rows), preferred_element_type=jnp.float32
    )
    grad_keys = jnp.einsum(
        "hrk,rhe->khe", grad_scores, split_heads(queries), preferred_element_type=jnp.float32
    )
    return (flatten(grad_queries), flatten(grad_keys), flatten(grad_values))


def sum_token_grads(gradients):
    return (
        lax.psum_scatter(
            gradients[0].astype(jnp.bfloat16), "seq", scatter_dimension=2, tiled=True
        ).astype(jnp.float32),
        lax.psum_scatter(
            gradients[1].astype(jnp.bfloat16), "seq", scatter_dimension=0, tiled=True
        ).astype(jnp.float32),
        lax.psum_scatter(
            gradients[2].astype(jnp.bfloat16), "seq", scatter_dimension=1, tiled=True
        ).astype(jnp.float32),
        lax.psum_scatter(
            gradients[3].astype(jnp.bfloat16), "seq", scatter_dimension=0, tiled=True
        ).astype(jnp.float32),
    )


def body(
    tokens,
    segment_start,
    norm_win,
    qkv_win,
    out_win,
    norm_wffn,
    up_win,
    down_win,
    norm_tok,
    qkv_tok,
    out_tok,
    norm_ffn,
    up_tok,
    down_tok,
    norm_state,
    qkv_state,
    out_state,
    gate_bias,
    norm_sffn,
    up_state,
    down_state,
    init_state,
    cotangent,
):
    seq_index = lax.axis_index("seq")
    position = seq_index % CHAIN
    micro_batch = seq_index // CHAIN
    row_table = lax.broadcasted_iota(jnp.int32, segment_start.shape, 0)
    col_table = lax.broadcasted_iota(jnp.int32, segment_start.shape, 1)
    picked = jnp.where((row_table == micro_batch) & (col_table == position), segment_start, 0)
    starts_here = jnp.sum(picked) == 1
    block_rows, model_width = tokens.shape
    state_rows = init_state.shape[0]
    local_width = qkv_tok.shape[2]
    heads_local = local_width // E
    hidden_local = up_tok.shape[1]
    qkv_win_flat = qkv_win.reshape(model_width, 3 * local_width)
    qkv_tok_flat = qkv_tok.reshape(model_width, 3 * local_width)
    out_tok_flat = out_tok.reshape(2 * local_width, model_width)
    qkv_state_flat = qkv_state.reshape(model_width, 3 * local_width)
    out_state_flat = out_state.reshape(2 * local_width, model_width)
    keep_gates = jax.nn.sigmoid(gate_bias)
    row_ids = lax.broadcasted_iota(jnp.int32, (block_rows, 2 * block_rows), 0)
    col_ids = lax.broadcasted_iota(jnp.int32, (block_rows, 2 * block_rows), 1)
    allowed = (col_ids >= block_rows) & (col_ids - block_rows <= row_ids) | (
        col_ids < block_rows
    ) & (col_ids > row_ids) & jnp.logical_not(starts_here)
    input_rows = tokens.astype(jnp.float32)
    win_normed_exact, win_norm_back = jax.vjp(layer_norm, input_rows, norm_win)
    win_normed = win_normed_exact.astype(jnp.bfloat16)
    win_queries, win_keys, win_values = jnp.split(
        plain_dot(win_normed, qkv_win_flat).astype(jnp.bfloat16), 3, axis=1
    )
    win_previous = send_forward(jnp.stack([win_keys, win_values]))
    win_all_keys = jnp.concatenate([win_previous[0], win_keys])
    win_all_values = jnp.concatenate([win_previous[1], win_values])
    win_heads, log_win = attend(win_queries, win_all_keys, win_all_values, allowed)
    win_mixed = input_rows + heads_sum(win_heads, out_win)
    win_ffn_exact, win_ffn_back = jax.vjp(layer_norm, win_mixed, norm_wffn)
    win_ffn_in = win_ffn_exact.astype(jnp.bfloat16)
    win_hidden = plain_dot(win_ffn_in, up_win)
    win_active_exact, win_gelu_back = jax.vjp(gelu_exact, win_hidden)
    win_active = win_active_exact.astype(jnp.bfloat16)
    token_rows = win_mixed + mlp_sum(win_active, down_win)
    normed_exact, norm_tok_back = jax.vjp(layer_norm, token_rows, norm_tok)
    normed = normed_exact.astype(jnp.bfloat16)
    queries, key_rows, value_rows = jnp.split(
        plain_dot(normed, qkv_tok_flat).astype(jnp.bfloat16), 3, axis=1
    )
    previous = send_forward(jnp.stack([key_rows, value_rows]))
    all_keys = jnp.concatenate([previous[0], key_rows])
    all_values = jnp.concatenate([previous[1], value_rows])
    zero_kept = (
        jnp.zeros_like(init_state),
        zeros_low(state_rows, local_width),
        zeros_low(state_rows, local_width),
        zeros_low(state_rows, local_width),
        jnp.zeros((heads_local, state_rows, 1), jnp.float32),
        jnp.zeros((heads_local, state_rows, 1), jnp.float32),
        zeros_low(state_rows, 2 * local_width),
        zeros_high(state_rows, model_width),
        zeros_high(state_rows, model_width),
        zeros_high(state_rows, hidden_local),
        zeros_low(state_rows, hidden_local),
        zeros_high(state_rows, model_width),
    )

    def forward_turn(turn_index, loop_carry):
        sent_state, kept_state = loop_carry
        arrived = passed_along(sent_state, "seq", 1)
        active_now = position == turn_index

        def heads_work():
            state_in = jnp.where(starts_here, init_state, arrived)
            state_normed = layer_norm(state_in.astype(jnp.float32), norm_state).astype(jnp.bfloat16)
            state_queries, state_keys, state_values = jnp.split(
                plain_dot(state_normed, qkv_state_flat).astype(jnp.bfloat16), 3, axis=1
            )
            state_own, log_own = attend(state_queries, state_keys, state_values, True)
            state_cross, log_cross = attend(state_queries, key_rows, value_rows, True)
            state_heads = jnp.concatenate([state_own, state_cross], axis=1)
            return (
                state_in,
                state_queries,
                state_keys,
                state_values,
                log_own,
                log_cross,
                state_heads,
                plain_dot(state_heads, out_state_flat),
            )

        heads_part = run_when(active_now, heads_work)
        update = lax.psum(heads_part[7].astype(jnp.bfloat16), "tp").astype(jnp.float32)
        state_exact = heads_part[0].astype(jnp.float32)

        def mlp_work():
            mid_state = keep_gates[0] * state_exact + (1.0 - keep_gates[0]) * update
            state_ffn_in = layer_norm(mid_state, norm_sffn).astype(jnp.bfloat16)
            state_hidden = plain_dot(state_ffn_in, up_state)
            state_active = gelu_exact(state_hidden).astype(jnp.bfloat16)
            return (mid_state, state_hidden, state_active, plain_dot(state_active, down_state))

        mlp_part = run_when(active_now, mlp_work)
        state_mlp = lax.psum(mlp_part[3].astype(jnp.bfloat16), "tp").astype(jnp.float32)
        state_next = (keep_gates[1] * mlp_part[0] + (1.0 - keep_gates[1]) * state_mlp).astype(
            jnp.bfloat16
        )
        fresh = heads_part[:7] + (update, mlp_part[0], mlp_part[1], mlp_part[2], state_mlp)
        return (jnp.where(active_now, state_next, sent_state), pick(active_now, fresh, kept_state))

    sent_state, kept_state = lax.fori_loop(
        0, CHAIN, forward_turn, (jnp.zeros_like(init_state), zero_kept)
    )
    (
        state_in,
        state_queries,
        state_keys,
        state_values,
        log_own,
        log_cross,
        state_heads,
        update,
        mid_state,
        state_hidden,
        state_active,
        state_mlp,
    ) = kept_state
    own_heads, log_token_own = attend(queries, all_keys, all_values, allowed)
    cross_heads, log_token_cross = attend(queries, state_keys, state_values, True)
    token_heads = jnp.concatenate([own_heads, cross_heads], axis=1)
    mixed_one = token_rows + heads_sum(token_heads, out_tok_flat)
    ffn_exact, ffn_back = jax.vjp(layer_norm, mixed_one, norm_ffn)
    ffn_in = ffn_exact.astype(jnp.bfloat16)
    hidden = plain_dot(ffn_in, up_tok)
    active_exact, gelu_back = jax.vjp(gelu_exact, hidden)
    active = active_exact.astype(jnp.bfloat16)
    layer_output = mixed_one + mlp_sum(active, down_tok)
    grad_output = cotangent.astype(jnp.float32)
    grad_down_tok = dot_first(active, cotangent)
    grad_hidden = gelu_back(dot_second(cotangent, down_tok))[0].astype(jnp.bfloat16)
    grad_up_tok = dot_first(ffn_in, grad_hidden)
    back_mixed, grad_norm_ffn = ffn_back(mlp_back_sum(grad_hidden, up_tok))
    grad_mixed = grad_output + back_mixed
    grad_proj = grad_mixed.astype(jnp.bfloat16)
    grad_out_tok = dot_first(token_heads, grad_proj).reshape(2, local_width, model_width)
    grad_heads = dot_second(grad_proj, out_tok_flat).astype(jnp.bfloat16)
    grad_own, grad_cross = jnp.split(grad_heads, 2, axis=1)
    query_grad_own, key_grad_all, value_grad_all = attend_back(
        queries, all_keys, all_values, allowed, log_token_own, grad_own
    )
    query_grad_cross, state_key_grad, state_value_grad = attend_back(
        queries, state_keys, state_values, True, log_token_cross, grad_cross
    )
    returned = send_backward(jnp.stack([key_grad_all[:block_rows], value_grad_all[:block_rows]]))
    token_grads = (grad_out_tok, grad_up_tok, grad_down_tok, grad_norm_ffn)
    state_exact = state_in.astype(jnp.float32)
    zero_results = (
        zeros_high(state_rows, model_width),
        jnp.zeros((model_width, 3, local_width), jnp.float32),
        jnp.zeros((2, local_width, model_width), jnp.float32),
        zeros_high(model_width, hidden_local),
        zeros_high(hidden_local, model_width),
        jnp.zeros((model_width,), jnp.float32),
        jnp.zeros((model_width,), jnp.float32),
        zeros_high(2, model_width),
        zeros_high(block_rows, local_width),
        zeros_high(block_rows, local_width),
    )

    def backward_turn(turn_back, loop_carry):
        sent_grad, results = loop_carry
        turn_index = CHAIN - 1 - turn_back
        arrived = passed_along(sent_grad.astype(jnp.bfloat16), "seq", -1).astype(sent_grad.dtype)
        active_now = position == turn_index

        def mlp_back_work():
            grad_mlp = ((1.0 - keep_gates[1]) * arrived).astype(jnp.bfloat16)
            bias_two = (
                jnp.sum(arrived * (mid_state - state_mlp), axis=0)
                * keep_gates[1]
                * (1.0 - keep_gates[1])
            )
            grad_down_state = dot_first(state_active, grad_mlp)
            state_gelu_back = jax.vjp(gelu_exact, state_hidden)[1]
            grad_state_hidden = state_gelu_back(dot_second(grad_mlp, down_state))[0].astype(
                jnp.bfloat16
            )
            sffn_exact = layer_norm(mid_state, norm_sffn)
            grad_up_state = dot_first(sffn_exact.astype(jnp.bfloat16), grad_state_hidden)
            return (
                bias_two,
                grad_down_state,
                grad_up_state,
                dot_second(grad_state_hidden, up_state),
            )

        mlp_part = run_when(active_now, mlp_back_work)
        grad_sffn_in = lax.psum(mlp_part[3].astype(jnp.bfloat16), "tp").astype(jnp.float32)

        def heads_back_work():
            sffn_back = jax.vjp(layer_norm, mid_state, norm_sffn)[1]
            back_mid, grad_norm_sffn = sffn_back(grad_sffn_in)
            grad_mid = keep_gates[1] * arrived + back_mid
            bias_one = (
                jnp.sum(grad_mid * (state_exact - update), axis=0)
                * keep_gates[0]
                * (1.0 - keep_gates[0])
            )
            grad_update = ((1.0 - keep_gates[0]) * grad_mid).astype(jnp.bfloat16)
            grad_out_state = dot_first(state_heads, grad_update).reshape(
                2, local_width, model_width
            )
            grad_state_heads = dot_second(grad_update, out_state_flat).astype(jnp.bfloat16)
            grad_state_own, grad_state_cross = jnp.split(grad_state_heads, 2, axis=1)
            query_grad_a, key_grad_a, value_grad_a = attend_back(
                state_queries, state_keys, state_values, True, log_own, grad_state_own
            )
            query_grad_b, token_key_grad, token_value_grad = attend_back(
                state_queries, key_rows, value_rows, True, log_cross, grad_state_cross
            )
            grad_state_qkv = jnp.concatenate(
                [
                    query_grad_a + query_grad_b,
                    key_grad_a + state_key_grad,
                    value_grad_a + state_value_grad,
                ],
                axis=1,
            ).astype(jnp.bfloat16)
            state_normed = layer_norm(state_exact, norm_state).astype(jnp.bfloat16)
            grad_qkv_state = dot_first(state_normed, grad_state_qkv).reshape(
                model_width, 3, local_width
            )
            return (
                grad_mid,
                bias_one,
                grad_norm_sffn,
                grad_out_state,
                grad_qkv_state,
                token_key_grad,
                token_value_grad,
                dot_second(grad_state_qkv, qkv_state_flat),
            )

        heads_part = run_when(active_now, heads_back_work)
        grad_state_normed = lax.psum(heads_part[7].astype(jnp.bfloat16), "tp").astype(jnp.float32)

        def norm_back_work():
            state_norm_back = jax.vjp(layer_norm, state_exact, norm_state)[1]
            back_state, grad_norm_state = state_norm_back(grad_state_normed)
            return (keep_gates[0] * heads_part[0] + back_state, grad_norm_state)

        norm_part = run_when(active_now, norm_back_work)
        grad_incoming = norm_part[0]
        gradients = (
            grad_incoming,
            heads_part[4],
            heads_part[3],
            mlp_part[2],
            mlp_part[1],
            norm_part[1],
            heads_part[2],
            jnp.stack([heads_part[1], mlp_part[0]]),
            heads_part[5],
            heads_part[6],
        )
        passed = jnp.where(active_now, jnp.where(starts_here, 0.0, grad_incoming), sent_grad)
        return (passed, pick(active_now, gradients, results))

    sent_grad, results = lax.fori_loop(
        0, CHAIN, backward_turn, (zeros_high(state_rows, model_width), zero_results)
    )
    (
        grad_incoming,
        grad_qkv_state,
        grad_out_state,
        grad_up_state,
        grad_down_state,
        grad_norm_state,
        grad_norm_sffn,
        grad_gate_bias,
        token_key_grad,
        token_value_grad,
    ) = results
    grad_init_state = jnp.where(starts_here, grad_incoming, 0.0)
    grad_queries = (query_grad_own + query_grad_cross).astype(jnp.bfloat16)
    grad_keys = (key_grad_all[block_rows:] + returned[0] + token_key_grad).astype(jnp.bfloat16)
    grad_values = (value_grad_all[block_rows:] + returned[1] + token_value_grad).astype(
        jnp.bfloat16
    )
    grad_qkv = jnp.concatenate([grad_queries, grad_keys, grad_values], axis=1)
    grad_qkv_tok = dot_first(normed, grad_qkv).reshape(model_width, 3, local_width)
    back_tokens, grad_norm_tok = norm_tok_back(input_back_sum(grad_qkv, qkv_tok_flat))
    grad_layer_one = grad_mixed + back_tokens
    grad_one_low = grad_layer_one.astype(jnp.bfloat16)
    grad_down_win = dot_first(win_active, grad_one_low)
    grad_win_hidden = win_gelu_back(dot_second(grad_one_low, down_win))[0].astype(jnp.bfloat16)
    grad_up_win = dot_first(win_ffn_in, grad_win_hidden)
    back_win_mixed, grad_norm_wffn = win_ffn_back(mlp_back_sum(grad_win_hidden, up_win))
    grad_win_mixed = grad_layer_one + back_win_mixed
    grad_win_proj = grad_win_mixed.astype(jnp.bfloat16)
    grad_out_win = dot_first(win_heads, grad_win_proj)
    grad_win_heads = dot_second(grad_win_proj, out_win).astype(jnp.bfloat16)
    win_query_grad, win_key_grad_all, win_value_grad_all = attend_back(
        win_queries, win_all_keys, win_all_values, allowed, log_win, grad_win_heads
    )
    win_returned = send_backward(
        jnp.stack([win_key_grad_all[:block_rows], win_value_grad_all[:block_rows]])
    )
    grad_win_qkv = jnp.concatenate(
        [
            win_query_grad,
            win_key_grad_all[block_rows:] + win_returned[0],
            win_value_grad_all[block_rows:] + win_returned[1],
        ],
        axis=1,
    ).astype(jnp.bfloat16)
    grad_qkv_win = dot_first(win_normed, grad_win_qkv).reshape(model_width, 3, local_width)
    back_win_tokens, grad_norm_win = win_norm_back(input_back_sum(grad_win_qkv, qkv_win_flat))
    grad_tokens = (grad_win_mixed + back_win_tokens).astype(jnp.bfloat16)
    final_sums = sum_token_grads(token_grads)
    sum_out_tok, sum_up_tok, sum_down_tok, sum_norm_ffn = final_sums
    (
        sum_norm_win,
        sum_qkv_win,
        sum_out_win,
        sum_norm_wffn,
        sum_up_win,
        sum_down_win,
        sum_norm_tok,
        sum_qkv_tok,
        sum_norm_state,
        sum_qkv_state,
        sum_out_state,
        sum_gate_bias,
        sum_norm_sffn,
        sum_up_state,
        sum_down_state,
        sum_init_state,
    ) = (
        lax.psum_scatter(
            grad_norm_win.astype(jnp.bfloat16), "seq", scatter_dimension=0, tiled=True
        ).astype(jnp.float32),
        lax.psum_scatter(
            grad_qkv_win.astype(jnp.bfloat16), "seq", scatter_dimension=0, tiled=True
        ).astype(jnp.float32),
        lax.psum_scatter(
            grad_out_win.astype(jnp.bfloat16), "seq", scatter_dimension=1, tiled=True
        ).astype(jnp.float32),
        lax.psum_scatter(
            grad_norm_wffn.astype(jnp.bfloat16), "seq", scatter_dimension=0, tiled=True
        ).astype(jnp.float32),
        lax.psum_scatter(
            grad_up_win.astype(jnp.bfloat16), "seq", scatter_dimension=0, tiled=True
        ).astype(jnp.float32),
        lax.psum_scatter(
            grad_down_win.astype(jnp.bfloat16), "seq", scatter_dimension=1, tiled=True
        ).astype(jnp.float32),
        lax.psum_scatter(
            grad_norm_tok.astype(jnp.bfloat16), "seq", scatter_dimension=0, tiled=True
        ).astype(jnp.float32),
        lax.psum_scatter(
            grad_qkv_tok.astype(jnp.bfloat16), "seq", scatter_dimension=0, tiled=True
        ).astype(jnp.float32),
        lax.psum_scatter(
            grad_norm_state.astype(jnp.bfloat16), "seq", scatter_dimension=0, tiled=True
        ).astype(jnp.float32),
        lax.psum_scatter(
            grad_qkv_state.astype(jnp.bfloat16), "seq", scatter_dimension=0, tiled=True
        ).astype(jnp.float32),
        lax.psum_scatter(
            grad_out_state.astype(jnp.bfloat16), "seq", scatter_dimension=2, tiled=True
        ).astype(jnp.float32),
        lax.psum_scatter(
            grad_gate_bias.astype(jnp.bfloat16), "seq", scatter_dimension=1, tiled=True
        ).astype(jnp.float32),
        lax.psum_scatter(
            grad_norm_sffn.astype(jnp.bfloat16), "seq", scatter_dimension=0, tiled=True
        ).astype(jnp.float32),
        lax.psum_scatter(
            grad_up_state.astype(jnp.bfloat16), "seq", scatter_dimension=0, tiled=True
        ).astype(jnp.float32),
        lax.psum_scatter(
            grad_down_state.astype(jnp.bfloat16), "seq", scatter_dimension=1, tiled=True
        ).astype(jnp.float32),
        lax.psum_scatter(
            grad_init_state.astype(jnp.bfloat16), "seq", scatter_dimension=1, tiled=True
        ).astype(jnp.float32),
    )
    return (
        layer_output.astype(jnp.bfloat16),
        sent_state,
        grad_tokens,
        sum_norm_win,
        sum_qkv_win,
        sum_out_win,
        sum_norm_wffn,
        sum_up_win,
        sum_down_win,
        sum_norm_tok,
        sum_qkv_tok,
        sum_out_tok,
        sum_norm_ffn,
        sum_up_tok,
        sum_down_tok,
        sum_norm_state,
        sum_qkv_state,
        sum_out_state,
        sum_gate_bias,
        sum_norm_sffn,
        sum_up_state,
        sum_down_state,
        sum_init_state,
    )


def solution(mesh):
    placed = (
        P("seq", None),
        P(),
        P(),
        P(None, None, "tp"),
        P("tp", None),
        P(),
        P(None, "tp"),
        P("tp", None),
        P(),
        P(None, None, "tp"),
        P(None, "tp", None),
        P(),
        P(None, "tp"),
        P("tp", None),
        P(),
        P(None, None, "tp"),
        P(None, "tp", None),
        P(),
        P(),
        P(None, "tp"),
        P("tp", None),
        P(),
        P("seq", None),
    )
    return jax.shard_map(
        body,
        mesh=mesh,
        in_specs=placed,
        out_specs=(
            P("seq", None),
            P("seq", None),
            P("seq", None),
            P("seq"),
            P("seq", None, "tp"),
            P("tp", "seq"),
            P("seq"),
            P("seq", "tp"),
            P("tp", "seq"),
            P("seq"),
            P("seq", None, "tp"),
            P(None, "tp", "seq"),
            P("seq"),
            P("seq", "tp"),
            P("tp", "seq"),
            P("seq"),
            P("seq", None, "tp"),
            P(None, "tp", "seq"),
            P(None, "seq"),
            P("seq"),
            P("seq", "tp"),
            P("tp", "seq"),
            P(None, "seq"),
        ),
        check_vma=False,
    )
```

profile of v0, /device:TPU:0, one launch (start us, length us, event | category | flops | bytes accessed | tf_op | source)
XLA Modules:
  0.0 3216.4 jit_solution(4919156687435520094)
XLA Ops:
  42.6 51.2 %all-reduce.20.cloned.1.call-done = bf16[512,1024]{1,0:T(8,128)(2,1)} async-done(((bf16[512,1024]{1,0:T(8,128)(2,1)}), bf16[512,1024]{1,0:T(8,128)(2,1)}) %all-reduce.20.cloned.1.call-update) | async-done | bytes 1048592 | tf_op jit(solution)/shard_map/psum | solution.py:86
  165.6 629.4 %while.72 = (s32[]{:T(128)}, bf16[512,1024]{1,0:T(8,128)(2,1)S(1)}, bf16[512,1024]{1,0:T(8,128)(2,1)}, bf16[512,256]{1,0:T(8,128)(2,1)}, bf16[512,256]{1,0:T(8,1...) while((s32[]{:T(128)}, bf16[512,1024]{1,0:T(8,128)(2,1)S(1)}, ...), condition=%wide.region_28.29_spmd.clone, body=%wide.region_13.28_spmd.clone.sunk | while | flops 4098233344 | bytes 185250832 | solution.py:292
  201.7 51.4 %all-reduce.34.cloned.1.call-done = bf16[512,1024]{1,0:T(8,128)(2,1)} async-done(((bf16[512,1024]{1,0:T(8,128)(2,1)}), bf16[512,1024]{1,0:T(8,128)(2,1)}) %all-reduce.34.cloned.1.call-update) | async-done | bytes 1048592 | tf_op jit(solution)/shard_map/while/body/eval_jaxpr/psum | solution.py:274
  346.3 64.2 %all-reduce.34.cloned.1.call-done = bf16[512,1024]{1,0:T(8,128)(2,1)} async-done(((bf16[512,1024]{1,0:T(8,128)(2,1)}), bf16[512,1024]{1,0:T(8,128)(2,1)}) %all-reduce.34.cloned.1.call-update) | async-done | bytes 1048592 | tf_op jit(solution)/shard_map/while/body/eval_jaxpr/psum | solution.py:274
  429.6 44.8 %all-reduce.36.cloned.1.call-done = bf16[512,1024]{1,0:T(8,128)(2,1)} async-done(((bf16[512,1024]{1,0:T(8,128)(2,1)}), bf16[512,1024]{1,0:T(8,128)(2,1)}) %all-reduce.36.cloned.1.call-update) | async-done | bytes 1048592 | tf_op jit(solution)/shard_map/while/body/eval_jaxpr/psum | solution.py:285
  502.1 65.5 %all-reduce.34.cloned.1.call-done = bf16[512,1024]{1,0:T(8,128)(2,1)} async-done(((bf16[512,1024]{1,0:T(8,128)(2,1)}), bf16[512,1024]{1,0:T(8,128)(2,1)}) %all-reduce.34.cloned.1.call-update) | async-done | bytes 1048592 | tf_op jit(solution)/shard_map/while/body/eval_jaxpr/psum | solution.py:274
  586.7 46.8 %all-reduce.36.cloned.1.call-done = bf16[512,1024]{1,0:T(8,128)(2,1)} async-done(((bf16[512,1024]{1,0:T(8,128)(2,1)}), bf16[512,1024]{1,0:T(8,128)(2,1)}) %all-reduce.36.cloned.1.call-update) | async-done | bytes 1048592 | tf_op jit(solution)/shard_map/while/body/eval_jaxpr/psum | solution.py:285
  661.2 63.6 %all-reduce.34.cloned.1.call-done = bf16[512,1024]{1,0:T(8,128)(2,1)} async-done(((bf16[512,1024]{1,0:T(8,128)(2,1)}), bf16[512,1024]{1,0:T(8,128)(2,1)}) %all-reduce.34.cloned.1.call-update) | async-done | bytes 1048592 | tf_op jit(solution)/shard_map/while/body/eval_jaxpr/psum | solution.py:274
  814.5 46.7 %all-reduce.24.cloned.1.call-done = bf16[512,1024]{1,0:T(8,128)(2,1)} async-done(((bf16[512,1024]{1,0:T(8,128)(2,1)}), bf16[512,1024]{1,0:T(8,128)(2,1)}) %all-reduce.24.cloned.1.call-update) | async-done | bytes 1048592 | tf_op jit(solution)/shard_map/psum | solution.py:86
  984.6 850.8 %while.73 = (s32[]{:T(128)}, bf16[512,1024]{1,0:T(8,128)(2,1)}, bf16[512,1024]{1,0:T(8,128)(2,1)}, bf16[1024,3,256]{0,2,1:T(8,128)(2,1)}, bf16[2,256,1024]{2,1,0...) while((s32[]{:T(128)}, bf16[512,1024]{1,0:T(8,128)(2,1)}, ...), condition=%wide.region_67.68_spmd.clone, body=%wide.region_40.67_spmd.clone.sunk | while | flops 8437925888 | bytes 271201984 | solution.py:450
  1001.6 78.5 %all-reduce.38.cloned.1.call-done = bf16[512,1024]{1,0:T(8,128)(2,1)} async-done(((bf16[512,1024]{1,0:T(8,128)(2,1)}), bf16[512,1024]{1,0:T(8,128)(2,1)}) %all-reduce.38.cloned.1.call-update) | async-done | bytes 1048592 | tf_op jit(solution)/shard_map/while/body/eval_jaxpr/psum | solution.py:379
  1094.3 93.1 %all-reduce.40.cloned.1.call-done = bf16[512,1024]{1,0:T(8,128)(2,1)} async-done(((bf16[512,1024]{1,0:T(8,128)(2,1)}), bf16[512,1024]{1,0:T(8,128)(2,1)}) %all-reduce.40.cloned.1.call-update) | async-done | bytes 1048592 | tf_op jit(solution)/shard_map/while/body/eval_jaxpr/psum | solution.py:426
  1211.6 72.2 %all-reduce.38.cloned.1.call-done = bf16[512,1024]{1,0:T(8,128)(2,1)} async-done(((bf16[512,1024]{1,0:T(8,128)(2,1)}), bf16[512,1024]{1,0:T(8,128)(2,1)}) %all-reduce.38.cloned.1.call-update) | async-done | bytes 1048592 | tf_op jit(solution)/shard_map/while/body/eval_jaxpr/psum | solution.py:379
  1300.9 92.5 %all-reduce.40.cloned.1.call-done = bf16[512,1024]{1,0:T(8,128)(2,1)} async-done(((bf16[512,1024]{1,0:T(8,128)(2,1)}), bf16[512,1024]{1,0:T(8,128)(2,1)}) %all-reduce.40.cloned.1.call-update) | async-done | bytes 1048592 | tf_op jit(solution)/shard_map/while/body/eval_jaxpr/psum | solution.py:426
  1418.3 81.2 %all-reduce.38.cloned.1.call-done = bf16[512,1024]{1,0:T(8,128)(2,1)} async-done(((bf16[512,1024]{1,0:T(8,128)(2,1)}), bf16[512,1024]{1,0:T(8,128)(2,1)}) %all-reduce.38.cloned.1.call-update) | async-done | bytes 1048592 | tf_op jit(solution)/shard_map/while/body/eval_jaxpr/psum | solution.py:379
  1516.6 90.5 %all-reduce.40.cloned.1.call-done = bf16[512,1024]{1,0:T(8,128)(2,1)} async-done(((bf16[512,1024]{1,0:T(8,128)(2,1)}), bf16[512,1024]{1,0:T(8,128)(2,1)}) %all-reduce.40.cloned.1.call-update) | async-done | bytes 1048592 | tf_op jit(solution)/shard_map/while/body/eval_jaxpr/psum | solution.py:426
  1704.4 60.1 %conditional.18 = (f32[512,1024]{1,0:T(8,128)}, bf16[1024]{0:T(1024)(128)(2,1)S(1)}, bf16[2,256,1024]{2,1,0:T(8,128)(2,1)}, bf16[1024,3,256]{0,2,1:T(8,128)(2,1)...) conditional(s32[]{:T(128)} %convert_element_type.978, ...), branch_computations={%region_47.47_spmd, %region_48.0_spmd} | conditional | flops 4069011456 | bytes 113179144 | solution.py:68
  1840.5 46.7 %all-reduce.28.cloned.1.call-done = bf16[512,1024]{1,0:T(8,128)(2,1)} async-done(((bf16[512,1024]{1,0:T(8,128)(2,1)}), bf16[512,1024]{1,0:T(8,128)(2,1)}) %all-reduce.28.cloned.1.call-update) | async-done | bytes 1048592 | tf_op jit(solution)/shard_map/psum | solution.py:98
  2029.9 78.9 %reduce-scatter.45.cloned.1.call-done = bf16[32,512]{1,0:T(8,128)(2,1)} async-done(((bf16[1024,512]{1,0:T(8,128)(2,1)}), bf16[32,512]{1,0:T(8,128)(2,1)}) %reduce-scatter.45.cloned.1.call-update) | async-done | bytes 32784
  2110.5 79.2 %reduce-scatter.29.cloned.1.call-done = bf16[2,256,32]{1,2,0:T(8,128)(2,1)} async-done(((bf16[2,256,1024]{1,2,0:T(8,128)(2,1)}), bf16[2,256,32]{1,2,0:T(8,128)(2,1)}) %reduce-scatter.29.cloned.1.call-update) | async-done | bytes 32784 | tf_op jit(solution)/shard_map/reduce_scatter | solution.py:145
  2191.1 78.9 %reduce-scatter.37.cloned.1.call-done = bf16[2,256,32]{1,2,0:T(8,128)(2,1)} async-done(((bf16[2,256,1024]{1,2,0:T(8,128)(2,1)}), bf16[2,256,32]{1,2,0:T(8,128)(2,1)}) %reduce-scatter.37.cloned.1.call-update) | async-done | bytes 32784 | tf_op jit(solution)/shard_map/reduce_scatter | solution.py:551
  2271.4 80.6 %reduce-scatter.31.cloned.1.call-done = bf16[32,1024]{1,0:T(8,128)(2,1)} async-done(((bf16[1024,1024]{1,0:T(8,128)(2,1)}), bf16[32,1024]{1,0:T(8,128)(2,1)}) %reduce-scatter.31.cloned.1.call-update) | async-done | bytes 65552 | tf_op jit(solution)/shard_map/reduce_scatter | solution.py:148
  2353.6 80.7 %reduce-scatter.33.cloned.1.call-done = bf16[1024,32]{0,1:T(8,128)(2,1)} async-done(((bf16[1024,1024]{0,1:T(8,128)(2,1)}), bf16[1024,32]{0,1:T(8,128)(2,1)}) %reduce-scatter.33.cloned.1.call-update) | async-done | bytes 65552 | tf_op jit(solution)/shard_map/reduce_scatter | solution.py:151
  2435.8 80.1 %reduce-scatter.35.cloned.1.call-done = bf16[32,3,256]{2,0,1:T(8,128)(2,1)} async-done(((bf16[1024,3,256]{2,0,1:T(8,128)(2,1)}), bf16[32,3,256]{2,0,1:T(8,128)(2,1)}) %reduce-scatter.35.cloned.1.call-update) | async-done | bytes 49168 | tf_op jit(solution)/shard_map/reduce_scatter | solution.py:548
  2517.3 80.0 %reduce-scatter.27.cloned.1.call-done = bf16[32,3,256]{2,0,1:T(8,128)(2,1)} async-done(((bf16[1024,3,256]{2,0,1:T(8,128)(2,1)}), bf16[32,3,256]{2,0,1:T(8,128)(2,1)}) %reduce-scatter.27.cloned.1.call-update) | async-done | bytes 49168 | tf_op jit(solution)/shard_map/reduce_scatter | solution.py:542
  2604.6 74.9 %reduce-scatter.41.cloned.1.call-done = bf16[1024,32]{0,1:T(8,128)(2,1)} async-done(((bf16[1024,1024]{0,1:T(8,128)(2,1)}), bf16[1024,32]{0,1:T(8,128)(2,1)}) %reduce-scatter.41.cloned.1.call-update) | async-done | bytes 65552 | tf_op jit(solution)/shard_map/reduce_scatter | solution.py:563
  2681.0 80.7 %reduce-scatter.39.cloned.1.call-done = bf16[32,1024]{1,0:T(8,128)(2,1)} async-done(((bf16[1024,1024]{1,0:T(8,128)(2,1)}), bf16[32,1024]{1,0:T(8,128)(2,1)}) %reduce-scatter.39.cloned.1.call-update) | async-done | bytes 65552 | tf_op jit(solution)/shard_map/reduce_scatter | solution.py:560
  2763.2 78.6 %reduce-scatter.21.cloned.1.call-done = bf16[256,32]{0,1:T(8,128)(2,1)} async-done(((bf16[256,1024]{0,1:T(8,128)(2,1)}), bf16[256,32]{0,1:T(8,128)(2,1)}) %reduce-scatter.21.cloned.1.call-update) | async-done | bytes 16400 | tf_op jit(solution)/shard_map/reduce_scatter | solution.py:527
  2843.1 80.8 %reduce-scatter.23.cloned.1.call-done = bf16[32,1024]{1,0:T(8,128)(2,1)} async-done(((bf16[1024,1024]{1,0:T(8,128)(2,1)}), bf16[32,1024]{1,0:T(8,128)(2,1)}) %reduce-scatter.23.cloned.1.call-update) | async-done | bytes 65552 | tf_op jit(solution)/shard_map/reduce_scatter | solution.py:533
  2925.5 80.7 %reduce-scatter.25.cloned.1.call-done = bf16[1024,32]{0,1:T(8,128)(2,1)} async-done(((bf16[1024,1024]{0,1:T(8,128)(2,1)}), bf16[1024,32]{0,1:T(8,128)(2,1)}) %reduce-scatter.25.cloned.1.call-update) | async-done | bytes 65552 | tf_op jit(solution)/shard_map/reduce_scatter | solution.py:536
  3007.7 59.7 %all-reduce.32.cloned.1.call-done = (bf16[512,1024]{1,0:T(8,128)(2,1)}, bf16[512,1024]{1,0:T(8,128)(2,1)}) async-done(((bf16[512,1024]{1,0:T(8,128)(2,1)}, bf16[512,1024]{1,0:T(8,128)(2,1)}), (bf16[512,1024]{1,0:T(8,128)(2,1)}, bf16[512,1024]{1,0:T(8,128)(2,1)})) %all-reduce.32.cloned.1.call-update) | async-done | bytes 2097168 | tf_op jit(solution)/shard_map/psum | solution.py:90
  3070.6 128.4 %all-reduce.6 = (bf16[1024]{0:T(1024)(128)(2,1)S(1)}, bf16[1024]{0:T(1024)(128)(2,1)S(1)}, bf16[1024]{0:T(1024)(128)(2,1)S(1)}, bf16[1024]{0:T(1024)(128)(2,1)S(...) all-reduce(bf16[1024]{0:T(1024)(128)(2,1)S(1)} %get-tuple-element.1, ...), channel_id=2, replica_groups=mesh['seq'=32,'tp'=4] {'seq'}, use_global_device_ids=true, to_apply=%region_79.80.clone | all-reduce | flops 6144 | bytes 24576
  (978 shorter events, 1194.0 us)
Async XLA Ops:
  42.3 111.3 %all-reduce.22.cloned.1.call-start = ((), (), s32[]{:S(2)}) async-start(), calls=%async_computation.15 | async-start | bytes 2097152 | tf_op jit(solution)/shard_map/psum | solution.py:90
  160.9 640.6 %collective-permute-start.3 = (bf16[2,512,256]{2,1,0:T(8,128)(2,1)}, bf16[2,512,256]{2,1,0:T(8,128)(2,1)}, u32[]{:S(2)}, u32[]{:S(2)}) collective-permute-start(bf16[2,512,256]{2,1,0:T(8,128)(2,1)} %pad_maximum_fusion.8), channel_id=1, source_target_pairs={{0,4},{4,8},{8,12},{12,16},{16,20},{20,24},{24,28},{28,32},{32,36}... | collective-permute-start | bytes 1572872 | tf_op jit(solution)/shard_map/ppermute | solution.py:17
  166.1 87.0 %all-reduce.34.cloned.1.call-start = ((), (), s32[]{:S(2)}) async-start(), calls=%async_computation.35 | async-start | bytes 2097152 | tf_op jit(solution)/shard_map/while/body/eval_jaxpr/psum | solution.py:274
  196.0 123.2 %all-reduce.36.cloned.1.call-start = ((), (), s32[]{:S(2)}) async-start(), calls=%async_computation.36 | async-start | bytes 2097152 | tf_op jit(solution)/shard_map/while/body/eval_jaxpr/psum | solution.py:285
  338.4 135.9 %all-reduce.36.cloned.1.call-start = ((), (), s32[]{:S(2)}) async-start(), calls=%async_computation.36 | async-start | bytes 2097152 | tf_op jit(solution)/shard_map/while/body/eval_jaxpr/psum | solution.py:285
  494.3 139.1 %all-reduce.36.cloned.1.call-start = ((), (), s32[]{:S(2)}) async-start(), calls=%async_computation.36 | async-start | bytes 2097152 | tf_op jit(solution)/shard_map/while/body/eval_jaxpr/psum | solution.py:285
  653.4 135.1 %all-reduce.36.cloned.1.call-start = ((), (), s32[]{:S(2)}) async-start(), calls=%async_computation.36 | async-start | bytes 2097152 | tf_op jit(solution)/shard_map/while/body/eval_jaxpr/psum | solution.py:285
  814.4 110.2 %all-reduce.26.cloned.1.call-start = ((), (), s32[]{:S(2)}) async-start(), calls=%async_computation.17 | async-start | bytes 2097152 | tf_op jit(solution)/shard_map/psum | solution.py:94
  984.8 95.3 %all-reduce.38.cloned.1.call-start = ((), (), s32[]{:S(2)}) async-start(), calls=%async_computation.37 | async-start | bytes 2097152 | tf_op jit(solution)/shard_map/while/body/eval_jaxpr/psum | solution.py:379
  997.4 190.0 %all-reduce.40.cloned.1.call-start = ((), (), s32[]{:S(2)}) async-start(), calls=%async_computation.38 | async-start | bytes 2097152 | tf_op jit(solution)/shard_map/while/body/eval_jaxpr/psum | solution.py:426
  1192.0 91.9 %all-reduce.38.cloned.1.call-start = ((), (), s32[]{:S(2)}) async-start(), calls=%async_computation.37 | async-start | bytes 2097152 | tf_op jit(solution)/shard_map/while/body/eval_jaxpr/psum | solution.py:379
  1205.2 188.3 %all-reduce.40.cloned.1.call-start = ((), (), s32[]{:S(2)}) async-start(), calls=%async_computation.38 | async-start | bytes 2097152 | tf_op jit(solution)/shard_map/while/body/eval_jaxpr/psum | solution.py:426
  1398.7 100.9 %all-reduce.38.cloned.1.call-start = ((), (), s32[]{:S(2)}) async-start(), calls=%async_computation.37 | async-start | bytes 2097152 | tf_op jit(solution)/shard_map/while/body/eval_jaxpr/psum | solution.py:379
  1411.9 195.2 %all-reduce.40.cloned.1.call-start = ((), (), s32[]{:S(2)}) async-start(), calls=%async_computation.38 | async-start | bytes 2097152 | tf_op jit(solution)/shard_map/while/body/eval_jaxpr/psum | solution.py:426
  1612.3 92.1 %all-reduce.38.cloned.1.call-start = ((), (), s32[]{:S(2)}) async-start(), calls=%async_computation.37 | async-start | bytes 2097152 | tf_op jit(solution)/shard_map/while/body/eval_jaxpr/psum | solution.py:379
  1653.4 160.7 %all-reduce.40.cloned.1.call-start = ((), (), s32[]{:S(2)}) async-start(), calls=%async_computation.38 | async-start | bytes 2097152 | tf_op jit(solution)/shard_map/while/body/eval_jaxpr/psum | solution.py:426
  1840.5 106.7 %all-reduce.30.cloned.1.call-start = ((), (), s32[]{:S(2)}) async-start(), calls=%async_computation.19 | async-start | bytes 2097152 | tf_op jit(solution)/shard_map/psum | solution.py:94
  1900.4 128.2 %reduce-scatter.43.cloned.1.call-start = ((), (), s32[]{:S(2)}) async-start(), calls=%async_computation.32 | async-start | bytes 270336
  1901.4 207.5 %reduce-scatter.45.cloned.1.call-start = ((), (), s32[]{:S(2)}) async-start(), calls=%async_computation.33 | async-start | bytes 1081344
  1905.3 284.4 %reduce-scatter.29.cloned.1.call-start = ((), (), s32[]{:S(2)}) async-start(), calls=%async_computation.25 | async-start | bytes 1081344 | tf_op jit(solution)/shard_map/reduce_scatter | solution.py:145
  1910.5 359.5 %reduce-scatter.37.cloned.1.call-start = ((), (), s32[]{:S(2)}) async-start(), calls=%async_computation.29 | async-start | bytes 1081344 | tf_op jit(solution)/shard_map/reduce_scatter | solution.py:551
  1911.9 440.2 %reduce-scatter.31.cloned.1.call-start = ((), (), s32[]{:S(2)}) async-start(), calls=%async_computation.26 | async-start | bytes 2162688 | tf_op jit(solution)/shard_map/reduce_scatter | solution.py:148
  1916.7 517.6 %reduce-scatter.33.cloned.1.call-start = ((), (), s32[]{:S(2)}) async-start(), calls=%async_computation.27 | async-start | bytes 2162688 | tf_op jit(solution)/shard_map/reduce_scatter | solution.py:151
  1923.2 592.6 %reduce-scatter.35.cloned.1.call-start = ((), (), s32[]{:S(2)}) async-start(), calls=%async_computation.28 | async-start | bytes 1622016 | tf_op jit(solution)/shard_map/reduce_scatter | solution.py:548
  1926.0 671.2 %reduce-scatter.27.cloned.1.call-start = ((), (), s32[]{:S(2)}) async-start(), calls=%async_computation.24 | async-start | bytes 1622016 | tf_op jit(solution)/shard_map/reduce_scatter | solution.py:542
  1932.8 746.7 %reduce-scatter.41.cloned.1.call-start = ((), (), s32[]{:S(2)}) async-start(), calls=%async_computation.31 | async-start | bytes 2162688 | tf_op jit(solution)/shard_map/reduce_scatter | solution.py:563
  1937.0 824.8 %reduce-scatter.39.cloned.1.call-start = ((), (), s32[]{:S(2)}) async-start(), calls=%async_computation.30 | async-start | bytes 2162688 | tf_op jit(solution)/shard_map/reduce_scatter | solution.py:560
  1937.7 904.1 %reduce-scatter.21.cloned.1.call-start = ((), (), s32[]{:S(2)}) async-start(), calls=%async_computation.21 | async-start | bytes 540672 | tf_op jit(solution)/shard_map/reduce_scatter | solution.py:527
  1955.1 968.9 %reduce-scatter.23.cloned.1.call-start = ((), (), s32[]{:S(2)}) async-start(), calls=%async_computation.22 | async-start | bytes 2162688 | tf_op jit(solution)/shard_map/reduce_scatter | solution.py:533
  1959.6 1046.7 %reduce-scatter.25.cloned.1.call-start = ((), (), s32[]{:S(2)}) async-start(), calls=%async_computation.23 | async-start | bytes 2162688 | tf_op jit(solution)/shard_map/reduce_scatter | solution.py:536
  1964.2 1103.2 %all-reduce.32.cloned.1.call-start = ((), (), s32[]{:S(2)}) async-start(), calls=%async_computation.34 | async-start | bytes 4194304 | tf_op jit(solution)/shard_map/psum | solution.py:90
  2013.0 1194.6 %reduce-scatter.19.cloned.1.call-start = ((), (), s32[]{:S(2)}) async-start(), calls=%async_computation.20 | async-start | bytes 1622016 | tf_op jit(solution)/shard_map/reduce_scatter | solution.py:524
  (220 other events, 4482.2 us)
Sparse Core Ops, SparseCore 0:
  42.4 51.3 all-reduce.19
  196.1 56.8 all-reduce.33
  272.4 46.6 all-reduce.35
  338.6 71.8 all-reduce.33
  418.2 56.0 all-reduce.35
  494.4 73.1 all-reduce.33
  575.3 58.0 all-reduce.35
  653.5 71.3 all-reduce.33
  732.6 55.8 all-reduce.35
  878.0 46.6 all-reduce.25
  997.5 82.5 all-reduce.37
  1090.5 96.8 all-reduce.39
  1205.3 78.5 all-reduce.37
  1294.3 99.1 all-reduce.39
  1412.0 87.5 all-reduce.37
  1510.0 97.0 all-reduce.39
  1653.6 50.7 all-reduce.37
  1950.7 77.8 reduce-scatter.42
  2031.9 76.8 reduce-scatter.44
  2112.7 76.8 reduce-scatter.28
  2193.0 76.9 reduce-scatter.36
  2273.8 78.1 reduce-scatter.30
  2356.0 78.2 reduce-scatter.32
  2438.2 77.5 reduce-scatter.34
  2519.7 77.5 reduce-scatter.26
  2601.2 78.2 reduce-scatter.40
  2683.5 78.2 reduce-scatter.38
  2765.4 76.3 reduce-scatter.20
  2845.8 78.1 reduce-scatter.22
  2927.9 78.2 reduce-scatter.24
  3009.2 58.1 all-reduce.31
  3070.8 78.0 reduce-scatter.18
  (5 shorter events, 232.8 us)
where the time goes:
time: 3230 us; the launch traced here: 3220 us
  waiting for transfers between devices  2300 us (71%)
  other arithmetic  334 us (10%)
  matrix products  241 us (7%)
  local copies, waits for them, and re-layouts  162 us (5%)
  blocking collectives  128 us (4%)
    psum x4, waiting for transfers between devices, backward_turn(): lax.psum(heads_part[7].astype(jnp.bfloat16), 'tp').astype(jnp.float32)  314 us
    psum x4, waiting for transfers between devices, backward_turn(): lax.psum(mlp_part[3].astype(jnp.bfloat16), 'tp').astype(jnp.float32)  275 us
    psum x4, waiting for transfers between devices, forward_turn(): lax.psum(heads_part[7].astype(jnp.bfloat16), 'tp').astype(jnp.float32)  245 us
    psum x4, waiting for transfers between devices, forward_turn(): lax.psum(mlp_part[3].astype(jnp.bfloat16), 'tp').astype(jnp.float32)  173 us
    select_n x68, other arithmetic, pick(): jnp.where(active, fresh_one, older_one)  155 us
    unnamed x1, blocking collectives  128 us
    psum x2, waiting for transfers between devices, mlp_sum(): lax.psum(plain_dot(active, down).astype(jnp.bfloat16), 'tp')  98.5 us
    psum x2, waiting for transfers between devices, heads_sum(): lax.psum(plain_dot(heads, out_flat).astype(jnp.bfloat16), 'tp')  97.9 us
  transfers between devices with their start and end apart: 49, of which 44 were waited for; matrix products, arithmetic and copies ran while one was open for 13% of the time, Pallas kernels for 0%

commit v1 on v0

v1 whole, which is shorter than its diff:
```python
import jax
import jax.numpy as jnp
from jax import lax
from jax.sharding import PartitionSpec as P

E = 128
CHAIN = 4
CORES = 2

EPSILON = 1e-05
MASKED = -1e30
LOW = jnp.bfloat16
HIGH = jnp.float32


def layer_norm(matrix, weights):
    average = jnp.mean(matrix, axis=-1, keepdims=True)
    centred = matrix - average
    spread = jnp.mean(centred * centred, axis=-1, keepdims=True)
    return centred * lax.rsqrt(spread + EPSILON) * weights


def gelu_exact(matrix):
    return jax.nn.gelu(matrix, approximate=False)


def gelu_slope(matrix, grad):
    return jax.vjp(gelu_exact, matrix)[1](grad)[0]


def plain_dot(former, latter):
    return jnp.dot(former, latter, preferred_element_type=HIGH)


def dot_first(former, latter):
    return lax.dot_general(
        former, latter, (((0,), (0,)), ((), ())), preferred_element_type=HIGH
    )


def dot_second(former, latter):
    return lax.dot_general(
        former, latter, (((1,), (1,)), ((), ())), preferred_element_type=HIGH
    )


def tp_from(array, k):
    n = lax.axis_size("tp")
    return lax.ppermute(array, "tp", [((i + k) % n, i) for i in range(n)])


def tp_to(array, k):
    n = lax.axis_size("tp")
    return lax.ppermute(array, "tp", [(i, (i + k) % n) for i in range(n)])


def far_first(n):
    return sorted(range(1, n), key=lambda k: -min(k, n - k))


def tp_gather(piece):
    n = lax.axis_size("tp")
    found = {k: tp_from(piece, k) for k in far_first(n)}
    return [piece] + [found[k] for k in range(1, n)]


def tp_scatter(parts):
    n = lax.axis_size("tp")
    total = parts[0]
    for k in far_first(n):
        total = total + tp_to(parts[k].astype(LOW), k).astype(HIGH)
    return total


def split_rows(matrix, n):
    size = matrix.shape[0] // n
    return [matrix[k * size : (k + 1) * size] for k in range(n)]


def group_pairs(k):
    n = lax.axis_size("seq")
    return [(s, s - s % CHAIN + (s + k) % CHAIN) for s in range(n)]


def pos_to(array, k):
    return lax.ppermute(array, "seq", group_pairs(k))


def pos_from(array, k):
    return lax.ppermute(array, "seq", group_pairs(-k))


def pos_gather(piece):
    return [piece] + [pos_from(piece, k) for k in range(1, CHAIN)]


def pos_scatter(parts):
    total = parts[0]
    for k in range(1, CHAIN):
        total = total + pos_to(parts[k].astype(LOW), k).astype(HIGH)
    return total


def choose(stacked, index):
    return lax.dynamic_index_in_dim(stacked, index, 0, keepdims=False)


def turned(array, start):
    twice = jnp.concatenate([array, array])
    return lax.dynamic_slice_in_dim(twice, start, array.shape[0], 0)


def seq_sum(grads):
    n = lax.axis_size("seq")
    z_size = 4 if n % 8 == 0 else n // CORES
    x_size = n // (z_size * CORES)
    here = lax.axis_index("seq")
    core, z_at, x_at = here % CORES, here // CORES % z_size, here // (CORES * z_size)

    def place(x, z, c):
        return (x % x_size * z_size + z % z_size) * CORES + c % CORES

    def pairs(dx, dz, dc):
        return [
            (place(x, z, c), place(x + dx, z + dz, c + dc))
            for x in range(x_size)
            for z in range(z_size)
            for c in range(CORES)
        ]

    def stage(array, dim, at, size, step):
        total = lax.dynamic_index_in_dim(array, at, dim, False).astype(HIGH)
        for k in far_first(size):
            sent = lax.dynamic_index_in_dim(array, (at + k) % size, dim, False)
            total = total + lax.ppermute(sent, "seq", pairs(*step(k))).astype(HIGH)
        return total.astype(LOW)

    width = grads.shape[1]
    array = grads.reshape(x_size * z_size, CORES, -1, width)
    array = stage(array, 1, core, CORES, lambda k: (0, 0, k))
    array = array.reshape(x_size, z_size, -1, width)
    half = width // 256 * 128
    one, two = array[..., :half], array[..., half:]

    def over_z(part, dim):
        return stage(part, dim, z_at, z_size, lambda k: (0, k, 0))

    def over_x(part, dim):
        return stage(part, dim, x_at, x_size, lambda k: (k, 0, 0))

    one, two = over_z(one, 1), over_x(two, 0)
    one, two = over_x(one, 0), over_z(two, 0)
    return jnp.concatenate([one, two], axis=1)


def heads_of(matrix):
    return [matrix[:, h * E : (h + 1) * E] for h in range(matrix.shape[1] // E)]


def full_attend(queries, key_rows, value_rows):
    results, logs = [], []
    for q, k, v in zip(heads_of(queries), heads_of(key_rows), heads_of(value_rows)):
        scores = dot_second(q, k) * E ** (-0.5)
        row_max = jnp.max(scores, axis=-1, keepdims=True)
        powers = jnp.exp(scores - row_max)
        totals = jnp.sum(powers, axis=-1, keepdims=True)
        results.append(plain_dot((powers / totals).astype(LOW), v).astype(LOW))
        logs.append(row_max + jnp.log(totals))
    return jnp.concatenate(results, axis=1), logs


def full_attend_back(queries, key_rows, value_rows, logs, grad_result):
    grads = ([], [], [])
    for q, k, v, log, g in zip(
        heads_of(queries), heads_of(key_rows), heads_of(value_rows), logs, heads_of(grad_result)
    ):
        chances = jnp.exp(dot_second(q, k) * E ** (-0.5) - log)
        grad_chances = dot_second(g, v)
        inner = jnp.sum(chances * grad_chances, axis=-1, keepdims=True)
        grad_scores = (chances * (grad_chances - inner) * E ** (-0.5)).astype(LOW)
        grads[0].append(plain_dot(grad_scores, k))
        grads[1].append(dot_first(grad_scores, q))
        grads[2].append(dot_first(chances.astype(LOW), g))
    return [jnp.concatenate(each, axis=1) for each in grads]


def band_scores(q, k, k_prev, below, starts_here):
    current = dot_second(q, k) * E ** (-0.5)
    before = jnp.where(starts_here, MASKED, dot_second(q, k_prev) * E ** (-0.5))
    return jnp.where(below, current, before)


def band_attend(queries, pair, pair_prev, below, starts_here):
    width = queries.shape[1]
    results, logs = [], []
    for q, k, v, kp, vp in zip(
        heads_of(queries),
        heads_of(pair[:, :width]),
        heads_of(pair[:, width:]),
        heads_of(pair_prev[:, :width]),
        heads_of(pair_prev[:, width:]),
    ):
        scores = band_scores(q, k, kp, below, starts_here)
        row_max = jnp.max(scores, axis=-1, keepdims=True)
        powers = jnp.exp(scores - row_max)
        totals = jnp.sum(powers, axis=-1, keepdims=True)
        chances = (powers / totals).astype(LOW)
        none = jnp.zeros_like(chances)
        result = plain_dot(jnp.where(below, chances, none), v) + plain_dot(
            jnp.where(below, none, chances), vp
        )
        results.append(result.astype(LOW))
        logs.append(row_max + jnp.log(totals))
    return jnp.concatenate(results, axis=1), logs


def band_attend_back(queries, pair, pair_prev, below, starts_here, logs, grad_result):
    width = queries.shape[1]
    grads = ([], [], [], [], [])
    for q, k, v, kp, vp, log, g in zip(
        heads_of(queries),
        heads_of(pair[:, :width]),
        heads_of(pair[:, width:]),
        heads_of(pair_prev[:, :width]),
        heads_of(pair_prev[:, width:]),
        logs,
        heads_of(grad_result),
    ):
        chances = jnp.exp(band_scores(q, k, kp, below, starts_here) - log)
        grad_chances = jnp.where(below, dot_second(g, v), dot_second(g, vp))
        inner = jnp.sum(chances * grad_chances, axis=-1, keepdims=True)
        grad_scores = (chances * (grad_chances - inner) * E ** (-0.5)).astype(LOW)
        low_chances = chances.astype(LOW)
        none = jnp.zeros_like(low_chances)
        scores_now = jnp.where(below, grad_scores, none)
        scores_prev = jnp.where(below, none, grad_scores)
        grads[0].append(plain_dot(scores_now, k) + plain_dot(scores_prev, kp))
        grads[1].append(dot_first(scores_now, q))
        grads[2].append(dot_first(jnp.where(below, low_chances, none), g))
        grads[3].append(dot_first(scores_prev, q))
        grads[4].append(dot_first(jnp.where(below, none, low_chances), g))
    query_grad = jnp.concatenate(grads[0], axis=1)
    pair_grad = jnp.concatenate(grads[1] + grads[2], axis=1)
    prev_grad = jnp.concatenate(grads[3] + grads[4], axis=1)
    return query_grad, pair_grad, prev_grad


def body(
    tokens,
    segment_start,
    norm_win,
    qkv_win,
    out_win,
    norm_wffn,
    up_win,
    down_win,
    norm_tok,
    qkv_tok,
    out_tok,
    norm_ffn,
    up_tok,
    down_tok,
    norm_state,
    qkv_state,
    out_state,
    gate_bias,
    norm_sffn,
    up_state,
    down_state,
    init_state,
    cotangent,
):
    seq_index = lax.axis_index("seq")
    tp_index = lax.axis_index("tp")
    n_tp = lax.axis_size("tp")
    position = seq_index % CHAIN
    flags = choose(segment_start, seq_index // CHAIN) == 1
    starts_here = choose(flags, position)
    block_rows, model_width = tokens.shape
    piece_rows = block_rows // n_tp
    state_rows = init_state.shape[0]
    slab_rows = state_rows // CHAIN
    thin_rows = slab_rows // n_tp
    width = qkv_tok.shape[2]
    qkv_win_flat = qkv_win.reshape(model_width, 3 * width)
    qkv_tok_flat = qkv_tok.reshape(model_width, 3 * width)
    out_tok_flat = out_tok.reshape(2 * width, model_width)
    qkv_state_flat = qkv_state.reshape(model_width, 3 * width)
    out_state_flat = out_state.reshape(2 * width, model_width)
    keep_one, keep_two = jax.nn.sigmoid(gate_bias)

    row_ids = (jnp.arange(block_rows) + tp_index * piece_rows) % block_rows
    below = row_ids[None, :] <= row_ids[:, None]
    token_rows = turned(tokens, tp_index * piece_rows)
    cotangent_rows = turned(cotangent, tp_index * piece_rows)

    def natural(pieces):
        whole = jnp.concatenate(pieces)
        return turned(whole, (n_tp - tp_index) % n_tp * piece_rows)

    input_rows = token_rows.astype(HIGH)
    win_normed = layer_norm(input_rows, norm_win).astype(LOW)
    win_qkv = plain_dot(win_normed, qkv_win_flat).astype(LOW)
    win_queries, win_pair = win_qkv[:, :width], win_qkv[:, width:]
    onward = [(s, s + 1) for s in range(lax.axis_size("seq")) if (s + 1) % CHAIN]
    win_prev = lax.ppermute(win_pair, "seq", onward)
    win_heads, win_logs = band_attend(win_queries, win_pair, win_prev, below, starts_here)
    own_input = input_rows[:piece_rows]
    win_mixed = own_input + tp_scatter(
        [plain_dot(part, out_win) for part in split_rows(win_heads, n_tp)]
    )
    win_ffn_in = tp_gather(layer_norm(win_mixed, norm_wffn).astype(LOW))
    win_hidden = [plain_dot(part, up_win) for part in win_ffn_in]
    win_active = [gelu_exact(part).astype(LOW) for part in win_hidden]
    layer_one = win_mixed + tp_scatter([plain_dot(part, down_win) for part in win_active])

    normed = jnp.concatenate(tp_gather(layer_norm(layer_one, norm_tok).astype(LOW)))
    token_qkv = plain_dot(normed, qkv_tok_flat).astype(LOW)
    queries, pair = token_qkv[:, :width], token_qkv[:, width:]
    pairs_all = pos_gather(pair)
    pair_prev = pairs_all[CHAIN - 1]
    pairs_stack = jnp.stack(pairs_all)

    init_thin = lax.dynamic_slice_in_dim(
        init_state, position * slab_rows + tp_index * thin_rows, thin_rows, 0
    )
    state_thin = init_thin
    turns = []
    states_out = []
    for turn in range(CHAIN):
        incoming = jnp.where(flags[turn], init_thin, state_thin).astype(HIGH)
        state_normed = jnp.concatenate(tp_gather(layer_norm(incoming, norm_state).astype(LOW)))
        state_qkv = plain_dot(state_normed, qkv_state_flat).astype(LOW)
        state_queries = state_qkv[:, :width]
        state_pair = jnp.concatenate(pos_gather(state_qkv[:, width:]))
        token_pair = choose(pairs_stack, (turn - position) % CHAIN)
        cross, cross_logs = full_attend(
            state_queries, token_pair[:, :width], token_pair[:, width:]
        )
        own, own_logs = full_attend(state_queries, state_pair[:, :width], state_pair[:, width:])
        state_heads = jnp.concatenate([own, cross], axis=1)
        update = tp_scatter(split_rows(plain_dot(state_heads, out_state_flat), n_tp))
        mid_state = keep_one * incoming + (1.0 - keep_one) * update
        state_ffn_in = jnp.concatenate(tp_gather(layer_norm(mid_state, norm_sffn).astype(LOW)))
        state_hidden = plain_dot(state_ffn_in, up_state)
        state_active = gelu_exact(state_hidden).astype(LOW)
        state_mlp = tp_scatter(split_rows(plain_dot(state_active, down_state), n_tp))
        state_thin = (keep_two * mid_state + (1.0 - keep_two) * state_mlp).astype(LOW)
        states_out.append(state_thin)
        turns.append(
            (
                incoming,
                state_normed,
                state_queries,
                state_pair,
                token_pair,
                cross_logs,
                own_logs,
                state_heads,
                update,
                mid_state,
                state_ffn_in,
                state_hidden,
                state_active,
                state_mlp,
            )
        )
    my_state_pair = turns[0][3]
    for turn in range(1, CHAIN):
        my_state_pair = jnp.where(position == turn, turns[turn][3], my_state_pair)

    own_heads, own_token_logs = band_attend(queries, pair, pair_prev, below, starts_here)
    cross_heads, cross_token_logs = full_attend(
        queries, my_state_pair[:, :width], my_state_pair[:, width:]
    )
    token_heads = jnp.concatenate([own_heads, cross_heads], axis=1)
    mixed_one = layer_one + tp_scatter(
        [plain_dot(part, out_tok_flat) for part in split_rows(token_heads, n_tp)]
    )
    ffn_in = tp_gather(layer_norm(mixed_one, norm_ffn).astype(LOW))
    hidden = [plain_dot(part, up_tok) for part in ffn_in]
    active = [gelu_exact(part).astype(LOW) for part in hidden]

    cotangents = split_rows(cotangent_rows, n_tp)
    grad_hidden = [
        gelu_slope(part, dot_second(grad, down_tok)).astype(LOW)
        for part, grad in zip(hidden, cotangents)
    ]
    grad_ffn_in = tp_scatter([dot_second(part, up_tok) for part in grad_hidden])
    back_mixed, grad_norm_ffn = jax.vjp(layer_norm, mixed_one, norm_ffn)[1](grad_ffn_in)
    grad_mixed = cotangents[0].astype(HIGH) + back_mixed
    grad_proj = jnp.concatenate(tp_gather(grad_mixed.astype(LOW)))
    grad_heads = dot_second(grad_proj, out_tok_flat).astype(LOW)
    cross_query_grad, cross_key_grad, cross_value_grad = full_attend_back(
        queries,
        my_state_pair[:, :width],
        my_state_pair[:, width:],
        cross_token_logs,
        grad_heads[:, width:],
    )
    cross_pair_grad = split_rows(
        jnp.concatenate([cross_key_grad, cross_value_grad], axis=1), CHAIN
    )
    cross_pieces = jnp.stack(
        [cross_pair_grad[0]]
        + [pos_to(cross_pair_grad[k].astype(LOW), k).astype(HIGH) for k in range(1, CHAIN)]
    )
    own_query_grad, own_pair_grad, prev_pair_grad = band_attend_back(
        queries, pair, pair_prev, below, starts_here, own_token_logs, grad_heads[:, :width]
    )
    homeward = [(s, s - 1) for s in range(lax.axis_size("seq")) if s % CHAIN]
    returned = lax.ppermute(prev_pair_grad.astype(LOW), "seq", homeward)

    layer_output = mixed_one + tp_scatter([plain_dot(part, down_tok) for part in active])
    output_rows = natural(tp_gather(layer_output.astype(LOW)))
    sum_token = seq_sum(
        jnp.concatenate(
            [
                dot_first(jnp.concatenate(ffn_in), jnp.concatenate(grad_hidden)).astype(LOW),
                dot_first(cotangent_rows, jnp.concatenate(active)).astype(LOW),
                dot_first(grad_proj, token_heads).astype(LOW),
            ],
            axis=1,
        )
    )

    states_stack = jnp.stack(states_out)
    state_pieces = [choose(states_stack, position)] + [
        pos_to(choose(states_stack, (position + k) % CHAIN), k) for k in range(1, CHAIN)
    ]
    by_slab = jnp.stack([state_pieces[(-k) % CHAIN] for k in range(CHAIN)])
    by_slab = turned(by_slab, (CHAIN - position) % CHAIN)
    by_tp = turned(jnp.stack(tp_gather(by_slab)), (n_tp - tp_index) % n_tp)
    state_rows_out = jnp.transpose(by_tp, (1, 0, 2, 3)).reshape(state_rows, model_width)

    grad_state = jnp.zeros((thin_rows, model_width), HIGH)
    init_grad = jnp.zeros((thin_rows, model_width), HIGH)
    bias_one = jnp.zeros((model_width,), HIGH)
    bias_two = jnp.zeros((model_width,), HIGH)
    grad_norm_sffn = jnp.zeros((model_width,), HIGH)
    grad_norm_state = jnp.zeros((model_width,), HIGH)
    kept = []
    token_pair_grads = [None] * CHAIN
    for turn in reversed(range(CHAIN)):
        (
            incoming,
            state_normed,
            state_queries,
            state_pair,
            token_pair,
            cross_logs,
            own_logs,
            state_heads,
            update,
            mid_state,
            state_ffn_in,
            state_hidden,
            state_active,
            state_mlp,
        ) = turns[turn]
        grad_mlp = jnp.concatenate(tp_gather(((1.0 - keep_two) * grad_state).astype(LOW)))
        bias_two = bias_two + jnp.sum(grad_state * (mid_state - state_mlp), axis=0)
        grad_state_hidden = gelu_slope(state_hidden, dot_second(grad_mlp, down_state)).astype(LOW)
        grad_sffn_in = tp_scatter(split_rows(dot_second(grad_state_hidden, up_state), n_tp))
        back_mid, norm_part = jax.vjp(layer_norm, mid_state, norm_sffn)[1](grad_sffn_in)
        grad_norm_sffn = grad_norm_sffn + norm_part
        grad_mid = keep_two * grad_state + back_mid
        bias_one = bias_one + jnp.sum(grad_mid * (incoming - update), axis=0)
        grad_update = jnp.concatenate(tp_gather(((1.0 - keep_one) * grad_mid).astype(LOW)))
        grad_state_heads = dot_second(grad_update, out_state_flat).astype(LOW)
        own_q, own_k, own_v = full_attend_back(
            state_queries,
            state_pair[:, :width],
            state_pair[:, width:],
            own_logs,
            grad_state_heads[:, :width],
        )
        pair_parts = split_rows(jnp.concatenate([own_k, own_v], axis=1), CHAIN)
        pair_total = pos_scatter(pair_parts) + choose(cross_pieces, (position - turn) % CHAIN)
        cross_q, cross_k, cross_v = full_attend_back(
            state_queries,
            token_pair[:, :width],
            token_pair[:, width:],
            cross_logs,
            grad_state_heads[:, width:],
        )
        token_pair_grads[turn] = jnp.concatenate([cross_k, cross_v], axis=1).astype(LOW)
        grad_state_qkv = jnp.concatenate([own_q + cross_q, pair_total], axis=1).astype(LOW)
        grad_state_normed = tp_scatter(
            split_rows(dot_second(grad_state_qkv, qkv_state_flat), n_tp)
        )
        back_state, norm_part = jax.vjp(layer_norm, incoming, norm_state)[1](grad_state_normed)
        grad_norm_state = grad_norm_state + norm_part
        grad_incoming = keep_one * grad_mid + back_state
        init_grad = init_grad + jnp.where(flags[turn], grad_incoming, 0.0)
        grad_state = jnp.where(flags[turn], 0.0, grad_incoming)
        kept.append(
            (
                state_normed,
                grad_state_qkv,
                state_heads,
                grad_update,
                state_ffn_in,
                grad_state_hidden,
                state_active,
                grad_mlp,
            )
        )
    bias_one = bias_one * keep_one * (1.0 - keep_one)
    bias_two = bias_two * keep_two * (1.0 - keep_two)
    (
        state_normed,
        grad_state_qkv,
        state_heads,
        grad_update,
        state_ffn_in,
        grad_state_hidden,
        state_active,
        grad_mlp,
    ) = [jnp.concatenate(each) for each in zip(*kept)]
    sum_state = seq_sum(
        jnp.concatenate(
            [
                dot_first(state_normed, grad_state_qkv).astype(LOW),
                dot_first(grad_update, state_heads).astype(LOW),
                dot_first(state_ffn_in, grad_state_hidden).astype(LOW),
                dot_first(grad_mlp, state_active).astype(LOW),
            ],
            axis=1,
        )
    )

    token_pair_stack = jnp.stack(token_pair_grads)
    pair_grad = own_pair_grad + returned.astype(HIGH)
    pair_grad = pair_grad + choose(token_pair_stack, position).astype(HIGH)
    for k in range(1, CHAIN):
        sent = choose(token_pair_stack, (position + k) % CHAIN)
        pair_grad = pair_grad + pos_to(sent, k).astype(HIGH)
    grad_qkv = jnp.concatenate([own_query_grad + cross_query_grad, pair_grad], axis=1).astype(LOW)
    grad_normed = tp_scatter(
        [dot_second(part, qkv_tok_flat) for part in split_rows(grad_qkv, n_tp)]
    )
    back_tokens, grad_norm_tok = jax.vjp(layer_norm, layer_one, norm_tok)[1](grad_normed)
    grad_layer_one = grad_mixed + back_tokens

    grad_win_out = tp_gather(grad_layer_one.astype(LOW))
    grad_win_hidden = [
        gelu_slope(part, dot_second(grad, down_win)).astype(LOW)
        for part, grad in zip(win_hidden, grad_win_out)
    ]
    grad_win_ffn_in = tp_scatter([dot_second(part, up_win) for part in grad_win_hidden])
    back_win, grad_norm_wffn = jax.vjp(layer_norm, win_mixed, norm_wffn)[1](grad_win_ffn_in)
    grad_win_mixed = grad_layer_one + back_win
    sum_middle = seq_sum(
        jnp.concatenate(
            [
                dot_first(normed, grad_qkv).astype(LOW),
                dot_first(jnp.concatenate(win_ffn_in), jnp.concatenate(grad_win_hidden)).astype(LOW),
                dot_first(jnp.concatenate(grad_win_out), jnp.concatenate(win_active)).astype(LOW),
            ],
            axis=1,
        )
    )
    grad_win_proj = jnp.concatenate(tp_gather(grad_win_mixed.astype(LOW)))
    grad_win_heads = dot_second(grad_win_proj, out_win).astype(LOW)
    win_query_grad, win_pair_grad, win_prev_grad = band_attend_back(
        win_queries, win_pair, win_prev, below, starts_here, win_logs, grad_win_heads
    )
    win_returned = lax.ppermute(win_prev_grad.astype(LOW), "seq", homeward)
    win_pair_grad = win_pair_grad + win_returned.astype(HIGH)
    grad_win_qkv = jnp.concatenate([win_query_grad, win_pair_grad], axis=1).astype(LOW)
    grad_win_normed = tp_scatter(
        [dot_second(part, qkv_win_flat) for part in split_rows(grad_win_qkv, n_tp)]
    )
    back_input, grad_norm_win = jax.vjp(layer_norm, own_input, norm_win)[1](grad_win_normed)
    grad_token_rows = natural(tp_gather((grad_win_mixed + back_input).astype(LOW)))

    init_columns = jnp.concatenate(
        [jnp.where(position == p, init_grad.T, 0.0) for p in range(CHAIN)], axis=1
    )
    vectors = [
        grad_norm_win,
        grad_norm_wffn,
        grad_norm_tok,
        grad_norm_ffn,
        grad_norm_state,
        grad_norm_sffn,
        bias_one,
        bias_two,
    ]
    small = jnp.concatenate([init_columns, jnp.stack(vectors, axis=1)], axis=1)
    small_width = small.shape[1]
    small = jnp.pad(small, ((0, 0), (0, -small_width % 256))).astype(LOW)
    sum_last = seq_sum(
        jnp.concatenate(
            [
                dot_first(win_normed, grad_win_qkv).astype(LOW),
                dot_first(grad_win_proj, win_heads).astype(LOW),
                small,
            ],
            axis=1,
        )
    )
    own_columns = model_width // lax.axis_size("seq")
    small_sums = tp_gather(sum_last[:, 4 * width : 4 * width + small_width])
    init_part = turned(
        jnp.stack([part[:, : CHAIN * thin_rows] for part in small_sums]),
        (n_tp - tp_index) % n_tp,
    ).reshape(n_tp, own_columns, CHAIN, thin_rows)
    sum_init = jnp.transpose(init_part, (2, 0, 3, 1)).reshape(state_rows, own_columns)
    vector_sums = sum(part[:, CHAIN * thin_rows :].astype(HIGH) for part in small_sums)

    def columns(sums, at, count):
        return sums[:, at : at + count].astype(HIGH)

    def qkv_of(sums, at):
        return columns(sums, at, 3 * width).reshape(own_columns, 3, width)

    def out_of(sums, at):
        return columns(sums, at, 2 * width).T.reshape(2, width, own_columns)

    inner_width = up_tok.shape[1]
    return (
        output_rows,
        state_rows_out,
        grad_token_rows,
        vector_sums[:, 0],
        qkv_of(sum_last, 0),
        columns(sum_last, 3 * width, width).T,
        vector_sums[:, 1],
        columns(sum_middle, 3 * width, inner_width),
        columns(sum_middle, 3 * width + inner_width, inner_width).T,
        vector_sums[:, 2],
        qkv_of(sum_middle, 0),
        out_of(sum_token, 2 * inner_width),
        vector_sums[:, 3],
        columns(sum_token, 0, inner_width),
        columns(sum_token, inner_width, inner_width).T,
        vector_sums[:, 4],
        qkv_of(sum_state, 0),
        out_of(sum_state, 3 * width),
        vector_sums[:, 6:8].T,
        vector_sums[:, 5],
        columns(sum_state, 5 * width, inner_width),
        columns(sum_state, 5 * width + inner_width, inner_width).T,
        sum_init.astype(HIGH),
    )

def solution(mesh):
    placed = (
        P("seq", None),
        P(),
        P(),
        P(None, None, "tp"),
        P("tp", None),
        P(),
        P(None, "tp"),
        P("tp", None),
        P(),
        P(None, None, "tp"),
        P(None, "tp", None),
        P(),
        P(None, "tp"),
        P("tp", None),
        P(),
        P(None, None, "tp"),
        P(None, "tp", None),
        P(),
        P(),
        P(None, "tp"),
        P("tp", None),
        P(),
        P("seq", None),
    )
    return jax.shard_map(
        body,
        mesh=mesh,
        in_specs=placed,
        out_specs=(
            P("seq", None),
            P("seq", None),
            P("seq", None),
            P("seq"),
            P("seq", None, "tp"),
            P("tp", "seq"),
            P("seq"),
            P("seq", "tp"),
            P("tp", "seq"),
            P("seq"),
            P("seq", None, "tp"),
            P(None, "tp", "seq"),
            P("seq"),
            P("seq", "tp"),
            P("tp", "seq"),
            P("seq"),
            P("seq", None, "tp"),
            P(None, "tp", "seq"),
            P(None, "seq"),
            P("seq"),
            P("seq", "tp"),
            P("tp", "seq"),
            P(None, "seq"),
        ),
        check_vma=False,
    )
```

time: 3230 us -> 1060 us (0.33)
  waiting for transfers between devices: 2300 us -> 293 us
  starting transfers between devices: 25.7 us -> 339 us
  other arithmetic: 334 us -> 143 us
  blocking collectives: 128 us -> 0 us
  matrix products: 241 us -> 164 us
  local copies, waits for them, and re-layouts: 162 us -> 104 us
    psum x23 -> x0, waiting for transfers between devices: 1300 us -> none  [the longest x4 314 us: backward_turn(): lax.psum(heads_part[7].astype(jnp.bfloat16), 'tp').astype(jnp.float32)]
    reduce_scatter x12 -> x0, waiting for transfers between devices: 875 us -> none  [the longest x1 80.8 us: body(): lax.psum_scatter(grad_up_win.astype(jnp.bfloat16), 'seq', scatter_dimensi...]
    ppermute x12 -> x241, starting transfers between devices: 23.2 us -> 339 us  [the longest x72 117 us: tp_to(): return lax.ppermute(array, 'tp', [(i, (i + k) % n) for i in range(n)])]
    ppermute x12 -> x241, waiting for transfers between devices: 26.6 us -> 293 us  [the longest x78 113 us: tp_from(): return lax.ppermute(array, 'tp', [((i + k) % n, i) for i in range(n)])]
    select_n x72 -> x4, other arithmetic: 164 us -> 5.16 us  [the longest x2 4.88 us: body(): jnp.where(position == p, init_grad.T, 0.0)]
    unnamed x1 -> x0, blocking collectives: 128 us -> none
    dot_general x44 -> x94, matrix products: 167 us -> 60.3 us  [plain_dot(): return jnp.dot(former, latter, preferred_element_type=HIGH)]
    unnamed x23 -> x0, waiting for transfers between devices: 93.7 us -> none
  transfers between devices with their start and end apart: 49 -> 241, of which waited for: 44 -> 136; matrix products, arithmetic and copies ran while one was open for 13% -> 33% of each run, Pallas kernels for 0% -> 0%
where the time goes in v1:
time: 1060 us; the launch traced here: 1050 us
  starting transfers between devices  339 us (32%)
  waiting for transfers between devices  293 us (28%)
  matrix products  164 us (15%)
  other arithmetic  143 us (13%)
  local copies, waits for them, and re-layouts  104 us (10%)
    ppermute x72, starting transfers between devices, tp_to(): return lax.ppermute(array, 'tp', [(i, (i + k) % n) for i in range(n)])  117 us
    ppermute x78, waiting for transfers between devices, tp_from(): return lax.ppermute(array, 'tp', [((i + k) % n, i) for i in range(n)])  113 us
    ppermute x78, starting transfers between devices, tp_from(): return lax.ppermute(array, 'tp', [((i + k) % n, i) for i in range(n)])  108 us
    ppermute x52, starting transfers between devices, stage(): total = total + lax.ppermute(sent, 'seq', pairs(*step(k))).astype(HIGH)  82.8 us
    ppermute x72, waiting for transfers between devices, tp_to(): return lax.ppermute(array, 'tp', [(i, (i + k) % n) for i in range(n)])  66.9 us
    dot_general x94, matrix products, dot_second(): lax.dot_general(former, latter, (((1,), (1,)), ((), ())), preferred_eleme...  60.6 us
    dot_general x94, matrix products, plain_dot(): return jnp.dot(former, latter, preferred_element_type=HIGH)  60.3 us
    dot_general x64, matrix products, dot_first(): lax.dot_general(former, latter, (((0,), (0,)), ((), ())), preferred_eleme...  42.8 us
  transfers between devices with their start and end apart: 241, of which 136 were waited for; matrix products, arithmetic and copies ran while one was open for 33% of the time, Pallas kernels for 0%

profile of v1, /device:TPU:0, one launch (start us, length us, event | category | flops | bytes accessed | tf_op | source)
XLA Modules:
  0.0 1051.5 jit_solution(16116883451820903244)
XLA Ops:
  40.8 4.2 collective-permute-start.18
  47.4 4.1 collective-permute-done.18
  64.1 4.3 collective-permute-done.1
  68.4 5.8 collective-permute-done.2
  81.1 6.0 collective-permute-done.4
  113.7 7.4 collective-permute-done.10
  129.0 11.0 %collective-permute-done.13 = bf16[512,512]{1,0:T(8,128)(2,1)S(1)} collective-permute-done((bf16[512,512]{1,0:T(8,128)(2,1)S(1)}, bf16[512,512]{1,0:T(8,128)(2,1)S(1)}, u32[]{:S(2)}, u32[]{:S(2)}) %collective-permute-start.13) | collective-permute-done | bytes 524320 | tf_op jit(solution)/shard_map/ppermute | solution.py:90
  140.2 11.3 %collective-permute-done.21 = bf16[512,512]{1,0:T(8,128)(2,1)S(1)} collective-permute-done((bf16[512,512]{1,0:T(8,128)(2,1)S(1)}, bf16[512,512]{1,0:T(8,128)(2,1)S(1)}, u32[]{:S(2)}, u32[]{:S(2)}) %collective-permute-start.21) | collective-permute-done | bytes 524320 | tf_op jit(solution)/shard_map/ppermute | solution.py:90
  258.2 5.1 collective-permute-done.50
  294.6 4.4 collective-permute-start.61
  443.2 5.4 collective-permute-done.98
  476.7 11.2 %pad_maximum_fusion.2 = bf16[1024,2560]{0,1:T(8,128)(2,1)} fusion(bf16[1024,512]{0,1:T(8,128)(2,1)S(1)} %convolution_convert_fusion.10, bf16[1024,1024]{0,1:T(8,128)(2,1)S(1)} %copy-done.87, bf16[1024,1024]{0,1:T(8,128)(2,1)S(1)} %copy-done.88), kind=kLoop, calls=%fused_computation.39 | loop fusion | flops 15728640 | bytes 10485760 | tf_op jit(solution)/shard_map/concatenate | solution.py:417
  496.5 7.9 copy.73
  522.1 4.9 collective-permute-done.114
  527.0 4.4 collective-permute-done.113
  717.4 9.7 copy.74
  727.3 4.2 dynamic-slice_bitcast_fusion
  739.2 4.2 fusion.927
  747.3 8.7 collective-permute-done.160
  764.5 5.3 collective-permute-done.161
  769.7 5.6 collective-permute-done.162
  782.5 6.4 collective-permute-done.164
  803.2 12.1 %pad_maximum_fusion.1 = bf16[1024,2816]{0,1:T(8,128)(2,1)} fusion(bf16[1024,1024]{0,1:T(8,128)(2,1)S(1)} %convolution_convert_fusion.4, bf16[1024,1024]{0,1:T(8,128)(2,1)S(1)} %convolution_convert_fusion.5, bf16[1024,768]{0,1:T(8,128)(2,1)S(1)} %convolution_convert_fusion.7), kind=kLoop, calls=%fused_computation.35 | loop fusion | flops 17301504 | bytes 11534336 | tf_op jit(solution)/shard_map/concatenate | solution.py:555
  815.3 8.5 copy.71
  823.8 3.8 dynamic-slice_bitcast_fusion.1
  866.7 5.1 collective-permute-done.222
  901.9 6.5 collective-permute-done.175
  918.4 4.4 copy.70
  927.9 3.9 fusion
  941.8 9.3 collective-permute-done.187
  982.7 4.4 collective-permute-done.195
  1014.9 7.7 collective-permute-start.238
  (1945 shorter events, 835.8 us)
Async XLA Ops:
  4.5 32.4 %collective-permute-start.14 = (bf16[32,1024]{1,0:T(8,128)(2,1)}, bf16[32,1024]{1,0:T(8,128)(2,1)S(1)}, u32[]{:S(2)}, u32[]{:S(2)}) collective-permute-start(bf16[32,1024]{1,0:T(8,128)(2,1)} %fusion.601), channel_id=1, source_target_pairs={{1,0},{2,1},{3,2},{0,3},{5,4},{6,5},{7,6},{4,7},{9,8},{10,9},{11,1... | collective-permute-start | bytes 196616 | tf_op jit(solution)/shard_map/ppermute | solution.py:49
  7.6 29.5 %collective-permute-start.15 = (bf16[32,1024]{1,0:T(8,128)(2,1)}, bf16[32,1024]{1,0:T(8,128)(2,1)S(1)}, u32[]{:S(2)}, u32[]{:S(2)}) collective-permute-start(bf16[32,1024]{1,0:T(8,128)(2,1)} %fusion.601), channel_id=1, source_target_pairs={{2,0},{3,1},{0,2},{1,3},{6,4},{7,5},{4,6},{5,7},{10,8},{11,9},{8,1... | collective-permute-start | bytes 196616 | tf_op jit(solution)/shard_map/ppermute | solution.py:49
  8.2 30.2 %collective-permute-start.16 = (bf16[32,1024]{1,0:T(8,128)(2,1)}, bf16[32,1024]{1,0:T(8,128)(2,1)}, u32[]{:S(2)}, u32[]{:S(2)}) collective-permute-start(bf16[32,1024]{1,0:T(8,128)(2,1)} %fusion.601), channel_id=1, source_target_pairs={{3,0},{0,1},{1,2},{2,3},{7,4},{4,5},{5,6},{6,7},{11,8},{8,9},{9,10... | collective-permute-start | bytes 196616 | tf_op jit(solution)/shard_map/ppermute | solution.py:49
  10.0 30.8 %collective-permute-start.101 = (bf16[32,1024]{1,0:T(8,128)(2,1)S(1)}, bf16[32,1024]{1,0:T(8,128)(2,1)S(1)}, u32[]{:S(2)}, u32[]{:S(2)}) collective-permute-start(bf16[32,1024]{1,0:T(8,128)(2,1)S(1)} %mul.1821), channel_id=1, source_target_pairs={{1,0},{2,1},{3,2},{0,3},{5,4},{6,5},{7,6},{4,7},{9,8},{10,9},{11,1... | collective-permute-start | bytes 196616 | tf_op jit(solution)/shard_map/ppermute | solution.py:49
  12.3 33.3 %collective-permute-start.102 = (bf16[32,1024]{1,0:T(8,128)(2,1)S(1)}, bf16[32,1024]{1,0:T(8,128)(2,1)S(1)}, u32[]{:S(2)}, u32[]{:S(2)}) collective-permute-start(bf16[32,1024]{1,0:T(8,128)(2,1)S(1)} %mul.1821), channel_id=1, source_target_pairs={{2,0},{3,1},{0,2},{1,3},{6,4},{7,5},{4,6},{5,7},{10,8},{11,9},{8,1... | collective-permute-start | bytes 196616 | tf_op jit(solution)/shard_map/ppermute | solution.py:49
  127.8 23.7 %collective-permute-start.21 = (bf16[512,512]{1,0:T(8,128)(2,1)S(1)}, bf16[512,512]{1,0:T(8,128)(2,1)S(1)}, u32[]{:S(2)}, u32[]{:S(2)}) collective-permute-start(bf16[512,512]{1,0:T(8,128)(2,1)S(1)} %get-tuple-element.259), channel_id=1, source_target_pairs={{0,8},{4,12},{8,0},{12,4},{16,24},{20,28},{24,16},{28,20},{32,40},... | collective-permute-start | bytes 1572872 | tf_op jit(solution)/shard_map/ppermute | solution.py:90
  367.7 24.0 %collective-permute-start.70 = (bf16[128,1024]{1,0:T(8,128)(2,1)S(1)}, bf16[128,1024]{1,0:T(8,128)(2,1)S(1)}, u32[]{:S(2)}, u32[]{:S(2)}) collective-permute-start(bf16[128,1024]{1,0:T(8,128)(2,1)S(1)} %multiply_convert_fusion.12), channel_id=1, source_target_pairs={{2,0},{3,1},{0,2},{1,3},{6,4},{7,5},{4,6},{5,7},{10,8},{11,9},{8,1... | collective-permute-start | bytes 786440 | tf_op jit(solution)/shard_map/ppermute | solution.py:49
  370.5 26.3 %collective-permute-start.72 = (bf16[128,1024]{1,0:T(8,128)(2,1)S(1)}, bf16[128,1024]{1,0:T(8,128)(2,1)S(1)}, u32[]{:S(2)}, u32[]{:S(2)}) collective-permute-start(bf16[128,1024]{1,0:T(8,128)(2,1)S(1)} %multiply_convert_fusion.12), channel_id=1, source_target_pairs={{1,0},{2,1},{3,2},{0,3},{5,4},{6,5},{7,6},{4,7},{9,8},{10,9},{11,1... | collective-permute-start | bytes 786440 | tf_op jit(solution)/shard_map/ppermute | solution.py:49
  382.4 28.0 %collective-permute-start.91 = (bf16[4,32,1024]{2,1,0:T(8,128)(2,1)S(1)}, bf16[4,32,1024]{2,1,0:T(8,128)(2,1)S(1)}, u32[]{:S(2)}, u32[]{:S(2)}) collective-permute-start(bf16[4,32,1024]{2,1,0:T(8,128)(2,1)S(1)} %get-tuple-element.192), channel_id=1, source_target_pairs={{1,0},{2,1},{3,2},{0,3},{5,4},{6,5},{7,6},{4,7},{9,8},{10,9},{11,1... | collective-permute-start | bytes 786440 | tf_op jit(solution)/shard_map/ppermute | solution.py:49
  385.7 26.9 %collective-permute-start.92 = (bf16[4,32,1024]{2,1,0:T(8,128)(2,1)S(1)}, bf16[4,32,1024]{2,1,0:T(8,128)(2,1)S(1)}, u32[]{:S(2)}, u32[]{:S(2)}) collective-permute-start(bf16[4,32,1024]{2,1,0:T(8,128)(2,1)S(1)} %get-tuple-element.192), channel_id=1, source_target_pairs={{2,0},{3,1},{0,2},{1,3},{6,4},{7,5},{4,6},{5,7},{10,8},{11,9},{8,1... | collective-permute-start | bytes 786440 | tf_op jit(solution)/shard_map/ppermute | solution.py:49
  391.7 21.7 %collective-permute-start.93 = (bf16[4,32,1024]{2,1,0:T(8,128)(2,1)S(1)}, bf16[4,32,1024]{2,1,0:T(8,128)(2,1)S(1)}, u32[]{:S(2)}, u32[]{:S(2)}) collective-permute-start(bf16[4,32,1024]{2,1,0:T(8,128)(2,1)S(1)} %get-tuple-element.192), channel_id=1, source_target_pairs={{3,0},{0,1},{1,2},{2,3},{7,4},{4,5},{5,6},{6,7},{11,8},{8,9},{9,10... | collective-permute-start | bytes 786440 | tf_op jit(solution)/shard_map/ppermute | solution.py:49
  396.8 134.7 %collective-permute-start.110 = (bf16[128,512]{0,1:T(8,128)(2,1)}, bf16[128,512]{0,1:T(8,128)(2,1)}, u32[]{:S(2)}, u32[]{:S(2)}) collective-permute-start(bf16[128,512]{0,1:T(8,128)(2,1)} %get-tuple-element.275), channel_id=1, source_target_pairs={{0,4},{4,8},{8,12},{12,0},{16,20},{20,24},{24,28},{28,16},{32,36},... | collective-permute-start | bytes 393224 | tf_op jit(solution)/shard_map/ppermute | solution.py:86
  401.2 130.3 %collective-permute-start.111 = (bf16[128,512]{0,1:T(8,128)(2,1)}, bf16[128,512]{0,1:T(8,128)(2,1)}, u32[]{:S(2)}, u32[]{:S(2)}) collective-permute-start(bf16[128,512]{0,1:T(8,128)(2,1)} %get-tuple-element.277), channel_id=1, source_target_pairs={{0,8},{4,12},{8,0},{12,4},{16,24},{20,28},{24,16},{28,20},{32,40},... | collective-permute-start | bytes 393224 | tf_op jit(solution)/shard_map/ppermute | solution.py:86
  442.8 88.7 %collective-permute-start.112 = (bf16[128,512]{0,1:T(8,128)(2,1)}, bf16[128,512]{0,1:T(8,128)(2,1)}, u32[]{:S(2)}, u32[]{:S(2)}) collective-permute-start(bf16[128,512]{0,1:T(8,128)(2,1)} %get-tuple-element.276), channel_id=1, source_target_pairs={{0,12},{4,0},{8,4},{12,8},{16,28},{20,16},{24,20},{28,24},{32,44},... | collective-permute-start | bytes 393224 | tf_op jit(solution)/shard_map/ppermute | solution.py:86
  448.6 41.3 %collective-permute-start.76 = (bf16[128,1024]{1,0:T(8,128)(2,1)}, bf16[128,1024]{1,0:T(8,128)(2,1)}, u32[]{:S(2)}, u32[]{:S(2)}) collective-permute-start(bf16[128,1024]{1,0:T(8,128)(2,1)} %get-tuple-element.196), channel_id=1, source_target_pairs={{1,0},{2,1},{3,2},{0,3},{5,4},{6,5},{7,6},{4,7},{9,8},{10,9},{11,1... | collective-permute-start | bytes 786440 | tf_op jit(solution)/shard_map/ppermute | solution.py:49
  453.2 40.1 %collective-permute-start.77 = (bf16[128,1024]{1,0:T(8,128)(2,1)}, bf16[128,1024]{1,0:T(8,128)(2,1)}, u32[]{:S(2)}, u32[]{:S(2)}) collective-permute-start(bf16[128,1024]{1,0:T(8,128)(2,1)} %get-tuple-element.196), channel_id=1, source_target_pairs={{2,0},{3,1},{0,2},{1,3},{6,4},{7,5},{4,6},{5,7},{10,8},{11,9},{8,1... | collective-permute-start | bytes 786440 | tf_op jit(solution)/shard_map/ppermute | solution.py:49
  493.4 250.7 %collective-permute-start.100 = (bf16[512,512]{0,1:T(8,128)(2,1)}, bf16[512,512]{0,1:T(8,128)(2,1)}, u32[]{:S(2)}, u32[]{:S(2)}) collective-permute-start(bf16[512,512]{0,1:T(8,128)(2,1)} %pad_maximum_fusion.21), channel_id=1, source_target_pairs={{4,0},{8,4},{12,8},{20,16},{24,20},{28,24},{36,32},{40,36},{44,40}... | collective-permute-start | bytes 1572872 | tf_op jit(solution)/shard_map/ppermute | solution.py:412
  531.3 301.7 %collective-permute-start.215 = (bf16[16,32,2560]{2,1,0:T(8,128)(2,1)}, bf16[16,32,2560]{2,1,0:T(8,128)(2,1)}, u32[]{:S(2)}, u32[]{:S(2)}) collective-permute-start(bf16[16,32,2560]{2,1,0:T(8,128)(2,1)} %dynamic-slice_bitcast_fusion.2), channel_id=1, source_target_pairs={{0,4},{4,0},{8,12},{12,8},{16,20},{20,16},{24,28},{28,24},{32,36},... | collective-permute-start | bytes 7864328 | tf_op jit(solution)/shard_map/ppermute | solution.py:135
  707.9 23.6 %collective-permute-start.183 = (bf16[32,1024]{1,0:T(8,128)(2,1)}, bf16[32,1024]{1,0:T(8,128)(2,1)}, u32[]{:S(2)}, u32[]{:S(2)}) collective-permute-start(bf16[32,1024]{1,0:T(8,128)(2,1)} %get-tuple-element.299), channel_id=1, source_target_pairs={{0,2},{1,3},{2,0},{3,1},{4,6},{5,7},{6,4},{7,5},{8,10},{9,11},{10,... | collective-permute-start | bytes 196616 | tf_op jit(solution)/shard_map/ppermute | solution.py:54
  709.5 22.9 %collective-permute-start.184 = (bf16[32,1024]{1,0:T(8,128)(2,1)}, bf16[32,1024]{1,0:T(8,128)(2,1)}, u32[]{:S(2)}, u32[]{:S(2)}) collective-permute-start(bf16[32,1024]{1,0:T(8,128)(2,1)} %get-tuple-element.301), channel_id=1, source_target_pairs={{0,1},{1,2},{2,3},{3,0},{4,5},{5,6},{6,7},{7,4},{8,9},{9,10},{10,1... | collective-permute-start | bytes 196616 | tf_op jit(solution)/shard_map/ppermute | solution.py:54
  709.6 23.7 %collective-permute-start.185 = (bf16[32,1024]{1,0:T(8,128)(2,1)}, bf16[32,1024]{1,0:T(8,128)(2,1)}, u32[]{:S(2)}, u32[]{:S(2)}) collective-permute-start(bf16[32,1024]{1,0:T(8,128)(2,1)} %get-tuple-element.300), channel_id=1, source_target_pairs={{0,3},{1,0},{2,1},{3,2},{4,7},{5,4},{6,5},{7,6},{8,11},{9,8},{10,9... | collective-permute-start | bytes 196616 | tf_op jit(solution)/shard_map/ppermute | solution.py:54
  733.3 22.7 %collective-permute-start.160 = (bf16[512,512]{0,1:T(8,128)(2,1)S(1)}, bf16[512,512]{0,1:T(8,128)(2,1)S(1)}, u32[]{:S(2)}, u32[]{:S(2)}) collective-permute-start(bf16[512,512]{0,1:T(8,128)(2,1)S(1)} %copy-done.121), channel_id=1, source_target_pairs={{0,12},{4,0},{8,4},{12,8},{16,28},{20,16},{24,20},{28,24},{32,44},... | collective-permute-start | bytes 1572872 | tf_op jit(solution)/shard_map/ppermute | solution.py:86
  744.0 183.8 %collective-permute-start.228 = (bf16[16,32,3328]{2,1,0:T(8,128)(2,1)}, bf16[16,32,3328]{2,1,0:T(8,128)(2,1)}, u32[]{:S(2)}, u32[]{:S(2)}) collective-permute-start(bf16[16,32,3328]{2,1,0:T(8,128)(2,1)} %dynamic-slice_bitcast_fusion), channel_id=1, source_target_pairs={{0,4},{4,0},{8,12},{12,8},{16,20},{20,16},{24,28},{28,24},{32,36},... | collective-permute-start | bytes 10223624 | tf_op jit(solution)/shard_map/ppermute | solution.py:135
  790.7 36.9 %collective-permute-start.165 = (bf16[128,1024]{1,0:T(8,128)(2,1)S(1)}, bf16[128,1024]{1,0:T(8,128)(2,1)}, u32[]{:S(2)}, u32[]{:S(2)}) collective-permute-start(bf16[128,1024]{1,0:T(8,128)(2,1)S(1)} %convolution_convert_fusion.21), channel_id=1, source_target_pairs={{0,2},{1,3},{2,0},{3,1},{4,6},{5,7},{6,4},{7,5},{8,10},{9,11},{10,... | collective-permute-start | bytes 786440 | tf_op jit(solution)/shard_map/ppermute | solution.py:54
  794.3 33.4 %collective-permute-start.167 = (bf16[128,1024]{1,0:T(8,128)(2,1)}, bf16[128,1024]{1,0:T(8,128)(2,1)}, u32[]{:S(2)}, u32[]{:S(2)}) collective-permute-start(bf16[128,1024]{1,0:T(8,128)(2,1)} %convolution_convert_fusion.20), channel_id=1, source_target_pairs={{0,1},{1,2},{2,3},{3,0},{4,5},{5,6},{6,7},{7,4},{8,9},{9,10},{10,1... | collective-permute-start | bytes 786440 | tf_op jit(solution)/shard_map/ppermute | solution.py:54
  798.4 29.3 %collective-permute-start.169 = (bf16[128,1024]{1,0:T(8,128)(2,1)}, bf16[128,1024]{1,0:T(8,128)(2,1)}, u32[]{:S(2)}, u32[]{:S(2)}) collective-permute-start(bf16[128,1024]{1,0:T(8,128)(2,1)} %convolution_convert_fusion.19), channel_id=1, source_target_pairs={{0,3},{1,0},{2,1},{3,2},{4,7},{5,4},{6,5},{7,6},{8,11},{9,8},{10,9... | collective-permute-start | bytes 786440 | tf_op jit(solution)/shard_map/ppermute | solution.py:54
  827.6 164.6 %collective-permute-start.202 = (bf16[16,32,2816]{2,1,0:T(8,128)(2,1)}, bf16[16,32,2816]{2,1,0:T(8,128)(2,1)}, u32[]{:S(2)}, u32[]{:S(2)}) collective-permute-start(bf16[16,32,2816]{2,1,0:T(8,128)(2,1)} %dynamic-slice_bitcast_fusion.1), channel_id=1, source_target_pairs={{0,4},{4,0},{8,12},{12,8},{16,20},{20,16},{24,28},{28,24},{32,36},... | collective-permute-start | bytes 8650760 | tf_op jit(solution)/shard_map/ppermute | solution.py:135
  933.2 74.2 %collective-permute-start.235 = (bf16[4,32,1664]{2,1,0:T(8,128)(2,1)}, bf16[4,32,1664]{2,1,0:T(8,128)(2,1)S(1)}, u32[]{:S(2)}, u32[]{:S(2)}) collective-permute-start(bf16[4,32,1664]{2,1,0:T(8,128)(2,1)} %get-tuple-element.237), channel_id=1, source_target_pairs={{0,64},{4,68},{8,72},{12,76},{16,80},{20,84},{24,88},{28,92},{32,9... | collective-permute-start | bytes 1277960 | tf_op jit(solution)/shard_map/ppermute | solution.py:135
  971.7 38.5 %collective-permute-start.236 = (bf16[4,32,1664]{2,1,0:T(8,128)(2,1)}, bf16[4,32,1664]{2,1,0:T(8,128)(2,1)}, u32[]{:S(2)}, u32[]{:S(2)}) collective-permute-start(bf16[4,32,1664]{2,1,0:T(8,128)(2,1)} %get-tuple-element.239), channel_id=1, source_target_pairs={{0,32},{4,36},{8,40},{12,44},{16,48},{20,52},{24,56},{28,60},{32,6... | collective-permute-start | bytes 1277960 | tf_op jit(solution)/shard_map/ppermute | solution.py:135
  973.1 24.8 %collective-permute-start.229 = (bf16[4,32,1664]{2,1,0:T(8,128)(2,1)}, bf16[4,32,1664]{2,1,0:T(8,128)(2,1)}, u32[]{:S(2)}, u32[]{:S(2)}) collective-permute-start(bf16[4,32,1664]{2,1,0:T(8,128)(2,1)} %get-tuple-element.240), channel_id=1, source_target_pairs={{0,16},{4,20},{8,24},{12,28},{16,0},{20,4},{24,8},{28,12},{32,48},... | collective-permute-start | bytes 1277960 | tf_op jit(solution)/shard_map/ppermute | solution.py:135
  1001.0 30.3 %collective-permute-start.203 = (bf16[4,32,1408]{2,1,0:T(8,128)(2,1)S(1)}, bf16[4,32,1408]{2,1,0:T(8,128)(2,1)S(1)}, u32[]{:S(2)}, u32[]{:S(2)}) collective-permute-start(bf16[4,32,1408]{2,1,0:T(8,128)(2,1)S(1)} %get-tuple-element.243), channel_id=1, source_target_pairs={{0,16},{4,20},{8,24},{12,28},{16,0},{20,4},{24,8},{28,12},{32,48},... | collective-permute-start | bytes 1081352 | tf_op jit(solution)/shard_map/ppermute | solution.py:135
  1004.4 30.1 %collective-permute-start.204 = (bf16[4,32,1408]{2,1,0:T(8,128)(2,1)S(1)}, bf16[4,32,1408]{2,1,0:T(8,128)(2,1)S(1)}, u32[]{:S(2)}, u32[]{:S(2)}) collective-permute-start(bf16[4,32,1408]{2,1,0:T(8,128)(2,1)S(1)} %get-tuple-element.244), channel_id=1, source_target_pairs={{0,8},{4,12},{8,16},{12,20},{16,24},{20,28},{24,0},{28,4},{32,40},... | collective-permute-start | bytes 1081352 | tf_op jit(solution)/shard_map/ppermute | solution.py:135
  (604 other events, 7182.5 us)

commit v2 on v1

--- a/solution.py
+++ b/solution.py
@@ -1,6 +1,8 @@
 import jax
 import jax.numpy as jnp
 from jax import lax
+from jax.experimental import pallas as pl
+from jax.experimental.pallas import tpu as pltpu
 from jax.sharding import PartitionSpec as P
 
 E = 128
@@ -42,6 +44,24 @@
     return lax.dot_general(
         former, latter, (((1,), (1,)), ((), ())), preferred_element_type=HIGH
     )
+
+
+def tied(value, *others):
+    return lax.optimization_barrier((value,) + others)[0]
+
+
+def norm_back(matrix, weights, grad):
+    average = jnp.mean(matrix, axis=-1, keepdims=True)
+    centred = matrix - average
+    spread = jnp.mean(centred * centred, axis=-1, keepdims=True)
+    scaled = centred * lax.rsqrt(spread + EPSILON)
+    inner = grad * weights
+    back = lax.rsqrt(spread + EPSILON) * (
+        inner
+        - jnp.mean(inner, axis=-1, keepdims=True)
+        - scaled * jnp.mean(inner * scaled, axis=-1, keepdims=True)
+    )
+    return back, jnp.sum(grad * scaled, axis=0)
 
 
 def tp_from(array, k):
@@ -72,33 +92,34 @@
     return total
 
 
+def tp_total(part):
+    low = part.astype(LOW)
+    total = part
+    for k in far_first(lax.axis_size("tp")):
+        total = total + tp_to(low, k).astype(HIGH)
+    return total
+
+
 def split_rows(matrix, n):
     size = matrix.shape[0] // n
     return [matrix[k * size : (k + 1) * size] for k in range(n)]
 
 
-def group_pairs(k):
+def swap(array, k):
     n = lax.axis_size("seq")
-    return [(s, s - s % CHAIN + (s + k) % CHAIN) for s in range(n)]
-
-
-def pos_to(array, k):
-    return lax.ppermute(array, "seq", group_pairs(k))
-
-
-def pos_from(array, k):
-    return lax.ppermute(array, "seq", group_pairs(-k))
+    return lax.ppermute(array, "seq", [(s, s ^ k) for s in range(n)])
 
 
 def pos_gather(piece):
-    return [piece] + [pos_from(piece, k) for k in range(1, CHAIN)]
+    beside, across = swap(piece, 1), swap(piece, 2)
+    return [piece, beside, across, swap(across, 1)]
 
 
 def pos_scatter(parts):
-    total = parts[0]
-    for k in range(1, CHAIN):
-        total = total + pos_to(parts[k].astype(LOW), k).astype(HIGH)
-    return total
+    low = jnp.concatenate([parts[1], parts[3]]).astype(LOW)
+    here, there = split_rows(swap(low, 1), 2)
+    across = swap((parts[2] + there.astype(HIGH)).astype(LOW), 2)
+    return parts[0] + here.astype(HIGH) + across.astype(HIGH)
 
 
 def choose(stacked, index):
@@ -110,47 +131,121 @@
     return lax.dynamic_slice_in_dim(twice, start, array.shape[0], 0)
 
 
-def seq_sum(grads):
-    n = lax.axis_size("seq")
-    z_size = 4 if n % 8 == 0 else n // CORES
-    x_size = n // (z_size * CORES)
-    here = lax.axis_index("seq")
-    core, z_at, x_at = here % CORES, here // CORES % z_size, here // (CORES * z_size)
-
-    def place(x, z, c):
-        return (x % x_size * z_size + z % z_size) * CORES + c % CORES
-
-    def pairs(dx, dz, dc):
+def weight_grads(pairs, extra=None):
+    n_seq = lax.axis_size("seq")
+    depth = pairs[0][0][0].shape[1]
+    unit = depth // n_seq
+    block = max(256, CORES * unit)
+    widths = [latter[0].shape[1] for _, latter in pairs]
+    total = sum(widths) + (0 if extra is None else extra.shape[1])
+    counts = [(len(former), len(latter)) for former, latter in pairs]
+    operands, specs = [], []
+    for former, latter in pairs:
+        for piece in former:
+            operands.append(piece)
+            specs.append(pl.BlockSpec((piece.shape[0], block), lambda i: (0, i)))
+        for piece in latter:
+            operands.append(piece)
+            specs.append(pl.BlockSpec(piece.shape, lambda i: (0, 0)))
+
+    if extra is not None:
+        operands.append(extra)
+        specs.append(pl.BlockSpec((block, extra.shape[1]), lambda i: (i, 0)))
+
+    def kernel(core_ref, *refs):
+        mine_ref, other_ref = refs[-2:]
+        first = core_ref[0] == 0
+
+        def keep(product, column):
+            columns = slice(column, column + product.shape[1])
+            for g in range(block // (CORES * unit)):
+                low = product[g * CORES * unit : g * CORES * unit + unit]
+                high = product[g * CORES * unit + unit : (g + 1) * CORES * unit]
+                rows = slice(g * unit, (g + 1) * unit)
+                mine_ref[rows, columns] = jnp.where(first, low, high)
+                other_ref[rows, columns] = jnp.where(first, high, low)
+
+        at, column = 0, 0
+        for (n_former, n_latter), width in zip(counts, widths):
+            former = [ref[...] for ref in refs[at : at + n_former]]
+            latter = [ref[...] for ref in refs[at + n_former : at + n_former + n_latter]]
+            at += n_former + n_latter
+            former = jnp.concatenate(former) if n_former > 1 else former[0]
+            latter = jnp.concatenate(latter) if n_latter > 1 else latter[0]
+            keep(dot_first(former, latter).astype(LOW), column)
+            column += width
+        if extra is not None:
+            keep(refs[at][...], column)
+
+    shape = jax.ShapeDtypeStruct((depth // CORES, total), LOW)
+    out_spec = pl.BlockSpec((block // CORES, total), lambda i: (i, 0))
+    rows = sum(piece.shape[0] for piece in pairs[0][0])
+    core = (lax.axis_index("seq") % CORES).astype(jnp.int32).reshape(1)
+    return pl.pallas_call(
+        kernel,
+        out_shape=(shape, shape),
+        grid=(depth // block,),
+        in_specs=[pl.BlockSpec(memory_space=pltpu.SMEM)] + specs,
+        out_specs=(out_spec, out_spec),
+        compiler_params=pltpu.CompilerParams(vmem_limit_bytes=32 * 1024 * 1024),
+        cost_estimate=pl.CostEstimate(
+            flops=2 * rows * depth * total,
+            bytes_accessed=2 * (rows * (depth + total) + depth * total),
+            transcendentals=0,
+        ),
+    )(core, *operands)
+
+
+class SeqSum:
+    def __init__(self, halves):
+        n = lax.axis_size("seq")
+        self.z_size = 4 if n % 8 == 0 else n // CORES
+        self.x_size = n // (self.z_size * CORES)
+        here = lax.axis_index("seq")
+        self.z_at = here // CORES % self.z_size
+        self.x_at = here // (CORES * self.z_size)
+        self.mine, self.other = halves
+
+    def pairs(self, dx, dz):
+        def place(x, z, c):
+            return (x % self.x_size * self.z_size + z % self.z_size) * CORES + c
+
         return [
-            (place(x, z, c), place(x + dx, z + dz, c + dc))
-            for x in range(x_size)
-            for z in range(z_size)
+            (place(x, z, c), place(x + dx, z + dz, c))
+            for x in range(self.x_size)
+            for z in range(self.z_size)
             for c in range(CORES)
         ]
 
-    def stage(array, dim, at, size, step):
+    def over_z(self, array, dim):
+        return self.stage(array, dim, self.z_at, self.z_size, lambda k: (0, k))
+
+    def over_x(self, array, dim):
+        return self.stage(array, dim, self.x_at, self.x_size, lambda k: (k, 0))
+
+    def stage(self, array, dim, at, size, step):
         total = lax.dynamic_index_in_dim(array, at, dim, False).astype(HIGH)
         for k in far_first(size):
             sent = lax.dynamic_index_in_dim(array, (at + k) % size, dim, False)
-            total = total + lax.ppermute(sent, "seq", pairs(*step(k))).astype(HIGH)
+            total = total + lax.ppermute(sent, "seq", self.pairs(*step(k))).astype(HIGH)
         return total.astype(LOW)
 
-    width = grads.shape[1]
-    array = grads.reshape(x_size * z_size, CORES, -1, width)
-    array = stage(array, 1, core, CORES, lambda k: (0, 0, k))
-    array = array.reshape(x_size, z_size, -1, width)
-    half = width // 256 * 128
-    one, two = array[..., :half], array[..., half:]
-
-    def over_z(part, dim):
-        return stage(part, dim, z_at, z_size, lambda k: (0, k, 0))
-
-    def over_x(part, dim):
-        return stage(part, dim, x_at, x_size, lambda k: (k, 0, 0))
-
-    one, two = over_z(one, 1), over_x(two, 0)
-    one, two = over_x(one, 0), over_z(two, 0)
-    return jnp.concatenate([one, two], axis=1)
+    def cores(self):
+        width = self.mine.shape[1]
+        array = (self.mine.astype(HIGH) + swap(self.other, 1).astype(HIGH)).astype(LOW)
+        array = array.reshape(self.x_size, self.z_size, -1, width)
+        half = width // 256 * 128
+        self.one, self.two = array[..., :half], array[..., half:]
+        return self.one, self.two
+
+    def first(self):
+        self.one, self.two = self.over_z(self.one, 1), self.over_x(self.two, 0)
+        return self.one, self.two
+
+    def second(self):
+        one, two = self.over_x(self.one, 0), self.over_z(self.two, 0)
+        self.total = jnp.concatenate([one, two], axis=1)
+        return self.total
 
 
 def heads_of(matrix):
@@ -312,41 +407,59 @@
     win_ffn_in = tp_gather(layer_norm(win_mixed, norm_wffn).astype(LOW))
     win_hidden = [plain_dot(part, up_win) for part in win_ffn_in]
     win_active = [gelu_exact(part).astype(LOW) for part in win_hidden]
+
+    init_slab = lax.dynamic_slice_in_dim(init_state, position * slab_rows, slab_rows, 0)
+
+    def own_rows(slab):
+        return lax.dynamic_slice_in_dim(slab, tp_index * thin_rows, thin_rows, 0)
+
+    def state_start(slab):
+        state_normed = layer_norm(slab.astype(HIGH), norm_state).astype(LOW)
+        state_qkv = plain_dot(state_normed, qkv_state_flat).astype(LOW)
+        state_queries = state_qkv[:, :width]
+        state_pair = jnp.concatenate(pos_gather(state_qkv[:, width:]))
+        own, own_logs = full_attend(state_queries, state_pair[:, :width], state_pair[:, width:])
+        return state_normed, state_queries, state_pair, own, own_logs
+
+    started = state_start(tied(init_slab, win_ffn_in[1]))
     layer_one = win_mixed + tp_scatter([plain_dot(part, down_win) for part in win_active])
-
-    normed = jnp.concatenate(tp_gather(layer_norm(layer_one, norm_tok).astype(LOW)))
+    layer_one = tied(layer_one, started[3])
+
+    normed_pieces = tp_gather(layer_norm(layer_one, norm_tok).astype(LOW))
+    normed = jnp.concatenate(normed_pieces)
     token_qkv = plain_dot(normed, qkv_tok_flat).astype(LOW)
     queries, pair = token_qkv[:, :width], token_qkv[:, width:]
     pairs_all = pos_gather(pair)
-    pair_prev = pairs_all[CHAIN - 1]
+    pair_prev = jnp.where(position % 2 == 1, pairs_all[1], pairs_all[3])
     pairs_stack = jnp.stack(pairs_all)
 
-    init_thin = lax.dynamic_slice_in_dim(
-        init_state, position * slab_rows + tp_index * thin_rows, thin_rows, 0
-    )
-    state_thin = init_thin
+    state_slab = init_slab
     turns = []
     states_out = []
     for turn in range(CHAIN):
-        incoming = jnp.where(flags[turn], init_thin, state_thin).astype(HIGH)
-        state_normed = jnp.concatenate(tp_gather(layer_norm(incoming, norm_state).astype(LOW)))
-        state_qkv = plain_dot(state_normed, qkv_state_flat).astype(LOW)
-        state_queries = state_qkv[:, :width]
-        state_pair = jnp.concatenate(pos_gather(state_qkv[:, width:]))
-        token_pair = choose(pairs_stack, (turn - position) % CHAIN)
+        state_slab = jnp.where(flags[turn], init_slab, state_slab)
+        incoming = state_slab.astype(HIGH)
+        if turn:
+            started = state_start(state_slab)
+        state_normed, state_queries, state_pair, own, own_logs = started
+        token_pair = choose(pairs_stack, position ^ turn)
         cross, cross_logs = full_attend(
             state_queries, token_pair[:, :width], token_pair[:, width:]
         )
-        own, own_logs = full_attend(state_queries, state_pair[:, :width], state_pair[:, width:])
         state_heads = jnp.concatenate([own, cross], axis=1)
-        update = tp_scatter(split_rows(plain_dot(state_heads, out_state_flat), n_tp))
+        update = tp_total(plain_dot(state_heads, out_state_flat))
+        if turn == 1:
+            own_heads, own_token_logs = band_attend(
+                tied(queries, state_heads), pair, pair_prev, below, starts_here
+            )
+            update = tied(update, own_heads)
         mid_state = keep_one * incoming + (1.0 - keep_one) * update
-        state_ffn_in = jnp.concatenate(tp_gather(layer_norm(mid_state, norm_sffn).astype(LOW)))
+        state_ffn_in = layer_norm(mid_state, norm_sffn).astype(LOW)
         state_hidden = plain_dot(state_ffn_in, up_state)
         state_active = gelu_exact(state_hidden).astype(LOW)
-        state_mlp = tp_scatter(split_rows(plain_dot(state_active, down_state), n_tp))
-        state_thin = (keep_two * mid_state + (1.0 - keep_two) * state_mlp).astype(LOW)
-        states_out.append(state_thin)
+        state_mlp = tp_total(plain_dot(state_active, down_state))
+        state_slab = (keep_two * mid_state + (1.0 - keep_two) * state_mlp).astype(LOW)
+        states_out.append(own_rows(state_slab))
         turns.append(
             (
                 incoming,
@@ -369,7 +482,6 @@
     for turn in range(1, CHAIN):
         my_state_pair = jnp.where(position == turn, turns[turn][3], my_state_pair)
 
-    own_heads, own_token_logs = band_attend(queries, pair, pair_prev, below, starts_here)
     cross_heads, cross_token_logs = full_attend(
         queries, my_state_pair[:, :width], my_state_pair[:, width:]
     )
@@ -379,7 +491,6 @@
     )
     ffn_in = tp_gather(layer_norm(mixed_one, norm_ffn).astype(LOW))
     hidden = [plain_dot(part, up_tok) for part in ffn_in]
-    active = [gelu_exact(part).astype(LOW) for part in hidden]
 
     cotangents = split_rows(cotangent_rows, n_tp)
     grad_hidden = [
@@ -387,9 +498,11 @@
         for part, grad in zip(hidden, cotangents)
     ]
     grad_ffn_in = tp_scatter([dot_second(part, up_tok) for part in grad_hidden])
-    back_mixed, grad_norm_ffn = jax.vjp(layer_norm, mixed_one, norm_ffn)[1](grad_ffn_in)
+    active = [gelu_exact(part).astype(LOW) for part in hidden]
+    back_mixed, grad_norm_ffn = norm_back(mixed_one, norm_ffn, grad_ffn_in)
     grad_mixed = cotangents[0].astype(HIGH) + back_mixed
-    grad_proj = jnp.concatenate(tp_gather(grad_mixed.astype(LOW)))
+    grad_proj_pieces = tp_gather(grad_mixed.astype(LOW))
+    grad_proj = jnp.concatenate(grad_proj_pieces)
     grad_heads = dot_second(grad_proj, out_tok_flat).astype(LOW)
     cross_query_grad, cross_key_grad, cross_value_grad = full_attend_back(
         queries,
@@ -403,44 +516,35 @@
     )
     cross_pieces = jnp.stack(
         [cross_pair_grad[0]]
-        + [pos_to(cross_pair_grad[k].astype(LOW), k).astype(HIGH) for k in range(1, CHAIN)]
-    )
-    own_query_grad, own_pair_grad, prev_pair_grad = band_attend_back(
-        queries, pair, pair_prev, below, starts_here, own_token_logs, grad_heads[:, :width]
+        + [swap(cross_pair_grad[k].astype(LOW), k).astype(HIGH) for k in range(1, CHAIN)]
     )
     homeward = [(s, s - 1) for s in range(lax.axis_size("seq")) if s % CHAIN]
-    returned = lax.ppermute(prev_pair_grad.astype(LOW), "seq", homeward)
-
-    layer_output = mixed_one + tp_scatter([plain_dot(part, down_tok) for part in active])
-    output_rows = natural(tp_gather(layer_output.astype(LOW)))
-    sum_token = seq_sum(
-        jnp.concatenate(
-            [
-                dot_first(jnp.concatenate(ffn_in), jnp.concatenate(grad_hidden)).astype(LOW),
-                dot_first(cotangent_rows, jnp.concatenate(active)).astype(LOW),
-                dot_first(grad_proj, token_heads).astype(LOW),
-            ],
-            axis=1,
+
+    def own_back():
+        query_grad, pair_grad, prev_grad = band_attend_back(
+            queries,
+            pair,
+            pair_prev,
+            below,
+            starts_here,
+            own_token_logs,
+            tied(grad_heads[:, :width], cross_pieces),
         )
-    )
-
-    states_stack = jnp.stack(states_out)
-    state_pieces = [choose(states_stack, position)] + [
-        pos_to(choose(states_stack, (position + k) % CHAIN), k) for k in range(1, CHAIN)
-    ]
-    by_slab = jnp.stack([state_pieces[(-k) % CHAIN] for k in range(CHAIN)])
-    by_slab = turned(by_slab, (CHAIN - position) % CHAIN)
-    by_tp = turned(jnp.stack(tp_gather(by_slab)), (n_tp - tp_index) % n_tp)
-    state_rows_out = jnp.transpose(by_tp, (1, 0, 2, 3)).reshape(state_rows, model_width)
-
-    grad_state = jnp.zeros((thin_rows, model_width), HIGH)
+        returned = lax.ppermute(prev_grad.astype(LOW), "seq", homeward)
+        return query_grad + cross_query_grad, pair_grad + returned.astype(HIGH)
+
+    def states_between():
+        states_stack = jnp.stack(states_out)
+        pieces = [choose(states_stack, position)]
+        pieces += [swap(choose(states_stack, position ^ k), k) for k in range(1, CHAIN)]
+        pieces = jnp.stack(pieces)
+        return jnp.stack([choose(pieces, position ^ q) for q in range(CHAIN)])
+
     init_grad = jnp.zeros((thin_rows, model_width), HIGH)
-    bias_one = jnp.zeros((model_width,), HIGH)
-    bias_two = jnp.zeros((model_width,), HIGH)
-    grad_norm_sffn = jnp.zeros((model_width,), HIGH)
-    grad_norm_state = jnp.zeros((model_width,), HIGH)
-    kept = []
+    bias_one = bias_two = grad_norm_sffn = grad_norm_state = jnp.zeros((model_width,), HIGH)
+    kept_qkv, kept_rest = [], []
     token_pair_grads = [None] * CHAIN
+    grad_state = None
     for turn in reversed(range(CHAIN)):
         (
             incoming,
@@ -458,89 +562,110 @@
             state_active,
             state_mlp,
         ) = turns[turn]
-        grad_mlp = jnp.concatenate(tp_gather(((1.0 - keep_two) * grad_state).astype(LOW)))
-        bias_two = bias_two + jnp.sum(grad_state * (mid_state - state_mlp), axis=0)
-        grad_state_hidden = gelu_slope(state_hidden, dot_second(grad_mlp, down_state)).astype(LOW)
-        grad_sffn_in = tp_scatter(split_rows(dot_second(grad_state_hidden, up_state), n_tp))
-        back_mid, norm_part = jax.vjp(layer_norm, mid_state, norm_sffn)[1](grad_sffn_in)
-        grad_norm_sffn = grad_norm_sffn + norm_part
-        grad_mid = keep_two * grad_state + back_mid
-        bias_one = bias_one + jnp.sum(grad_mid * (incoming - update), axis=0)
-        grad_update = jnp.concatenate(tp_gather(((1.0 - keep_one) * grad_mid).astype(LOW)))
-        grad_state_heads = dot_second(grad_update, out_state_flat).astype(LOW)
-        own_q, own_k, own_v = full_attend_back(
-            state_queries,
-            state_pair[:, :width],
-            state_pair[:, width:],
-            own_logs,
-            grad_state_heads[:, :width],
-        )
-        pair_parts = split_rows(jnp.concatenate([own_k, own_v], axis=1), CHAIN)
-        pair_total = pos_scatter(pair_parts) + choose(cross_pieces, (position - turn) % CHAIN)
-        cross_q, cross_k, cross_v = full_attend_back(
-            state_queries,
-            token_pair[:, :width],
-            token_pair[:, width:],
-            cross_logs,
-            grad_state_heads[:, width:],
-        )
-        token_pair_grads[turn] = jnp.concatenate([cross_k, cross_v], axis=1).astype(LOW)
-        grad_state_qkv = jnp.concatenate([own_q + cross_q, pair_total], axis=1).astype(LOW)
-        grad_state_normed = tp_scatter(
-            split_rows(dot_second(grad_state_qkv, qkv_state_flat), n_tp)
-        )
-        back_state, norm_part = jax.vjp(layer_norm, incoming, norm_state)[1](grad_state_normed)
+        pair_total = choose(cross_pieces, position ^ turn)
+        if turn == CHAIN - 1:
+            query_total = jnp.zeros((slab_rows, width), HIGH)
+        else:
+            grad_mlp = ((1.0 - keep_two) * grad_state).astype(LOW)
+            bias_two = bias_two + jnp.sum(grad_state * (mid_state - state_mlp), axis=0)
+            grad_state_hidden = gelu_slope(
+                state_hidden, dot_second(grad_mlp, down_state)
+            ).astype(LOW)
+            grad_sffn_in = tp_total(dot_second(grad_state_hidden, up_state))
+            if turn == CHAIN - 2:
+                token_grads = SeqSum(
+                    weight_grads(
+                        [
+                            (tied(tuple(ffn_in), grad_state_hidden), grad_hidden),
+                            ([cotangent_rows], active),
+                            (grad_proj_pieces, [token_heads]),
+                        ]
+                    )
+                )
+                grad_sffn_in = tied(grad_sffn_in, token_grads.other)
+            if turn == CHAIN - 3:
+                grad_sffn_in = tied(grad_sffn_in, *token_grads.first())
+            back_mid, norm_part = norm_back(mid_state, norm_sffn, grad_sffn_in)
+            grad_norm_sffn = grad_norm_sffn + norm_part
+            grad_mid = keep_two * grad_state + back_mid
+            bias_one = bias_one + jnp.sum(grad_mid * (incoming - update), axis=0)
+            grad_update = ((1.0 - keep_one) * grad_mid).astype(LOW)
+            grad_state_heads = dot_second(grad_update, out_state_flat).astype(LOW)
+            own_q, own_k, own_v = full_attend_back(
+                state_queries,
+                state_pair[:, :width],
+                state_pair[:, width:],
+                own_logs,
+                grad_state_heads[:, :width],
+            )
+            pair_total = pair_total + pos_scatter(
+                split_rows(jnp.concatenate([own_k, own_v], axis=1), CHAIN)
+            )
+            cross_q, cross_k, cross_v = full_attend_back(
+                state_queries,
+                token_pair[:, :width],
+                token_pair[:, width:],
+                cross_logs,
+                grad_state_heads[:, width:],
+            )
+            token_pair_grads[turn] = jnp.concatenate([cross_k, cross_v], axis=1)
+            query_total = own_q + cross_q
+            if turn == CHAIN - 3:
+                slabs = states_between()
+                pair_total = tied(pair_total, slabs)
+            if turn == CHAIN - 4:
+                by_tp = turned(jnp.stack(tp_gather(slabs)), (n_tp - tp_index) % n_tp)
+                state_rows_out = jnp.transpose(by_tp, (1, 0, 2, 3)).reshape(
+                    state_rows, model_width
+                )
+                pair_total = tied(pair_total, state_rows_out)
+            kept_rest.append(
+                (state_heads, grad_update, state_ffn_in, grad_state_hidden, state_active, grad_mlp)
+            )
+        grad_state_qkv = jnp.concatenate([query_total, pair_total], axis=1).astype(LOW)
+        kept_qkv.append((state_normed, grad_state_qkv))
+        grad_state_normed = tp_total(dot_second(grad_state_qkv, qkv_state_flat))
+        if turn == CHAIN - 1:
+            query_grad, pair_grad = own_back()
+            grad_state_normed = tied(grad_state_normed, query_grad)
+        if turn == CHAIN - 2:
+            grad_state_normed = tied(grad_state_normed, *token_grads.cores())
+        if turn == CHAIN - 3:
+            grad_state_normed = tied(grad_state_normed, token_grads.second())
+        back_state, norm_part = norm_back(incoming, norm_state, grad_state_normed)
         grad_norm_state = grad_norm_state + norm_part
-        grad_incoming = keep_one * grad_mid + back_state
-        init_grad = init_grad + jnp.where(flags[turn], grad_incoming, 0.0)
+        grad_incoming = back_state
+        if grad_state is not None:
+            grad_incoming = keep_one * grad_mid + back_state
+        init_grad = init_grad + jnp.where(flags[turn], own_rows(grad_incoming), 0.0)
         grad_state = jnp.where(flags[turn], 0.0, grad_incoming)
-        kept.append(
-            (
-                state_normed,
-                grad_state_qkv,
-                state_heads,
-                grad_update,
-                state_ffn_in,
-                grad_state_hidden,
-                state_active,
-                grad_mlp,
-            )
-        )
-    bias_one = bias_one * keep_one * (1.0 - keep_one)
-    bias_two = bias_two * keep_two * (1.0 - keep_two)
-    (
-        state_normed,
-        grad_state_qkv,
-        state_heads,
-        grad_update,
-        state_ffn_in,
-        grad_state_hidden,
-        state_active,
-        grad_mlp,
-    ) = [jnp.concatenate(each) for each in zip(*kept)]
-    sum_state = seq_sum(
-        jnp.concatenate(
-            [
-                dot_first(state_normed, grad_state_qkv).astype(LOW),
-                dot_first(grad_update, state_heads).astype(LOW),
-                dot_first(state_ffn_in, grad_state_hidden).astype(LOW),
-                dot_first(grad_mlp, state_active).astype(LOW),
-            ],
-            axis=1,
-        )
-    )
-
-    token_pair_stack = jnp.stack(token_pair_grads)
-    pair_grad = own_pair_grad + returned.astype(HIGH)
-    pair_grad = pair_grad + choose(token_pair_stack, position).astype(HIGH)
-    for k in range(1, CHAIN):
-        sent = choose(token_pair_stack, (position + k) % CHAIN)
-        pair_grad = pair_grad + pos_to(sent, k).astype(HIGH)
-    grad_qkv = jnp.concatenate([own_query_grad + cross_query_grad, pair_grad], axis=1).astype(LOW)
+    bias_one = bias_one * keep_one * (1.0 - keep_one) / n_tp
+    bias_two = bias_two * keep_two * (1.0 - keep_two) / n_tp
+    grad_norm_sffn = grad_norm_sffn / n_tp
+    grad_norm_state = grad_norm_state / n_tp
+    sum_token = token_grads.total
+
+    token_pair_grads[CHAIN - 1] = jnp.zeros_like(token_pair_grads[0])
+    pair_stack = jnp.stack(token_pair_grads)
+    pair_grad = pair_grad + pos_scatter([choose(pair_stack, position ^ k) for k in range(CHAIN)])
+    grad_qkv = jnp.concatenate([query_grad, pair_grad], axis=1).astype(LOW)
     grad_normed = tp_scatter(
         [dot_second(part, qkv_tok_flat) for part in split_rows(grad_qkv, n_tp)]
     )
-    back_tokens, grad_norm_tok = jax.vjp(layer_norm, layer_one, norm_tok)[1](grad_normed)
+    qkv_parts = list(zip(*kept_qkv))
+    rest_parts = list(zip(*kept_rest))
+    state_grads = SeqSum(
+        weight_grads(
+            [
+                (qkv_parts[0], qkv_parts[1]),
+                (rest_parts[1], rest_parts[0]),
+                (rest_parts[2], rest_parts[3]),
+                (rest_parts[5], rest_parts[4]),
+            ]
+        )
+    )
+    grad_normed = tied(grad_normed, state_grads.other)
+    back_tokens, grad_norm_tok = norm_back(layer_one, norm_tok, grad_normed)
     grad_layer_one = grad_mixed + back_tokens
 
     grad_win_out = tp_gather(grad_layer_one.astype(LOW))
@@ -549,31 +674,37 @@
         for part, grad in zip(win_hidden, grad_win_out)
     ]
     grad_win_ffn_in = tp_scatter([dot_second(part, up_win) for part in grad_win_hidden])
-    back_win, grad_norm_wffn = jax.vjp(layer_norm, win_mixed, norm_wffn)[1](grad_win_ffn_in)
+    grad_win_ffn_in = tied(grad_win_ffn_in, *state_grads.cores())
+    back_win, grad_norm_wffn = norm_back(win_mixed, norm_wffn, grad_win_ffn_in)
     grad_win_mixed = grad_layer_one + back_win
-    sum_middle = seq_sum(
-        jnp.concatenate(
+    grad_win_pieces = tp_gather(grad_win_mixed.astype(LOW))
+    middle_grads = SeqSum(
+        weight_grads(
             [
-                dot_first(normed, grad_qkv).astype(LOW),
-                dot_first(jnp.concatenate(win_ffn_in), jnp.concatenate(grad_win_hidden)).astype(LOW),
-                dot_first(jnp.concatenate(grad_win_out), jnp.concatenate(win_active)).astype(LOW),
-            ],
-            axis=1,
+                (normed_pieces, [grad_qkv]),
+                (win_ffn_in, grad_win_hidden),
+                (grad_win_out, win_active),
+            ]
         )
     )
-    grad_win_proj = jnp.concatenate(tp_gather(grad_win_mixed.astype(LOW)))
+    grad_win_proj = jnp.concatenate(tied(tuple(grad_win_pieces), middle_grads.other))
     grad_win_heads = dot_second(grad_win_proj, out_win).astype(LOW)
     win_query_grad, win_pair_grad, win_prev_grad = band_attend_back(
         win_queries, win_pair, win_prev, below, starts_here, win_logs, grad_win_heads
     )
     win_returned = lax.ppermute(win_prev_grad.astype(LOW), "seq", homeward)
-    win_pair_grad = win_pair_grad + win_returned.astype(HIGH)
+    win_pair_grad = win_pair_grad + tied(win_returned, *state_grads.first()).astype(HIGH)
     grad_win_qkv = jnp.concatenate([win_query_grad, win_pair_grad], axis=1).astype(LOW)
+    sum_state = state_grads.second()
+    middle_grads.cores()
     grad_win_normed = tp_scatter(
         [dot_second(part, qkv_win_flat) for part in split_rows(grad_win_qkv, n_tp)]
     )
-    back_input, grad_norm_win = jax.vjp(layer_norm, own_input, norm_win)[1](grad_win_normed)
+    back_input, grad_norm_win = norm_back(own_input, norm_win, grad_win_normed)
     grad_token_rows = natural(tp_gather((grad_win_mixed + back_input).astype(LOW)))
+
+    layer_output = mixed_one + tp_scatter([plain_dot(part, down_tok) for part in active])
+    output_rows = natural(tp_gather(layer_output.astype(LOW)))
 
     init_columns = jnp.concatenate(
         [jnp.where(position == p, init_grad.T, 0.0) for p in range(CHAIN)], axis=1
@@ -591,16 +722,16 @@
     small = jnp.concatenate([init_columns, jnp.stack(vectors, axis=1)], axis=1)
     small_width = small.shape[1]
     small = jnp.pad(small, ((0, 0), (0, -small_width % 256))).astype(LOW)
-    sum_last = seq_sum(
-        jnp.concatenate(
-            [
-                dot_first(win_normed, grad_win_qkv).astype(LOW),
-                dot_first(grad_win_proj, win_heads).astype(LOW),
-                small,
-            ],
-            axis=1,
+    last_grads = SeqSum(
+        weight_grads(
+            [([win_normed], [grad_win_qkv]), ([grad_win_proj], [win_heads])], small
         )
     )
+    middle_grads.first()
+    sum_middle = middle_grads.second()
+    last_grads.cores()
+    last_grads.first()
+    sum_last = last_grads.second()
     own_columns = model_width // lax.axis_size("seq")
     small_sums = tp_gather(sum_last[:, 4 * width : 4 * width + small_width])
     init_part = turned(

time: 1060 us -> 1070 us (level)
  starting transfers between devices: 339 us -> 256 us
  matrix products: 164 us -> 224 us
  local copies, waits for them, and re-layouts: 104 us -> 158 us
  waiting for transfers between devices: 293 us -> 244 us
  Pallas kernels: 0 us -> 20.4 us
    ppermute x78 -> x30, starting transfers between devices: 108 us -> 33.5 us  [tp_from(): return lax.ppermute(array, 'tp', [((i + k) % n, i) for i in range(n)])]
    ppermute x78 -> x30, waiting for transfers between devices: 113 us -> 57 us  [tp_from(): return lax.ppermute(array, 'tp', [((i + k) % n, i) for i in range(n)])]
    convert_element_type x0 -> x35, local copies, waits for them, and re-layouts: none -> 52.5 us  [the longest x4 7.18 us: body(): gelu_slope(part, dot_second(grad, down_tok)).astype(LOW)]
    ppermute x72 -> x69, waiting for transfers between devices: 66.9 us -> 116 us  [tp_to(): return lax.ppermute(array, 'tp', [(i, (i + k) % n) for i in range(n)])]
    dot_general x94 -> x89, matrix products: 60.3 us -> 108 us  [plain_dot(): return jnp.dot(former, latter, preferred_element_type=HIGH)]
    ppermute x89 -> x82, waiting for transfers between devices: 112 us -> 70.5 us  [the longest x48 38.6 us: stage(): total = total + lax.ppermute(sent, 'seq', self.pairs(*step(k))).astype(HIGH)]
    dot_general x94 -> x91, matrix products: 60.6 us -> 93.9 us  [dot_second(): lax.dot_general(former, latter, (((1,), (1,)), ((), ())), preferred_eleme...]
    concatenate x8 -> x2, local copies, waits for them, and re-layouts: 31.3 us -> 0.7 us  [the longest x1 0.69 us: body(): jnp.concatenate([query_total, pair_total], axis=1).astype(LOW)]
  transfers between devices with their start and end apart: 241 -> 183, of which waited for: 136 -> 72; matrix products, arithmetic and copies ran while one was open for 33% -> 37% of each run, Pallas kernels for 0% -> 2%
where the time goes in v2:
time: 1070 us; the launch traced here: 1060 us
  starting transfers between devices  256 us (24%)
  waiting for transfers between devices  244 us (23%)
  matrix products  224 us (21%)
  local copies, waits for them, and re-layouts  158 us (15%)
  other arithmetic  150 us (14%)
  Pallas kernels  20.4 us (2%)
    ppermute x69, starting transfers between devices, tp_to(): return lax.ppermute(array, 'tp', [(i, (i + k) % n) for i in range(n)])  120 us
    ppermute x69, waiting for transfers between devices, tp_to(): return lax.ppermute(array, 'tp', [(i, (i + k) % n) for i in range(n)])  116 us
    dot_general x89, matrix products, plain_dot(): return jnp.dot(former, latter, preferred_element_type=HIGH)  108 us
    dot_general x91, matrix products, dot_second(): lax.dot_general(former, latter, (((1,), (1,)), ((), ())), preferred_eleme...  93.9 us
    ppermute x48, starting transfers between devices, stage(): total = total + lax.ppermute(sent, 'seq', self.pairs(*step(k))).astype(HIGH)  83.6 us
    unnamed x887, local copies, waits for them, and re-layouts  57.2 us
    ppermute x30, waiting for transfers between devices, tp_from(): return lax.ppermute(array, 'tp', [((i + k) % n, i) for i in range(n)])  57 us
    ppermute x48, waiting for transfers between devices, stage(): total = total + lax.ppermute(sent, 'seq', self.pairs(*step(k))).astype(HIGH)  38.6 us
  transfers between devices with their start and end apart: 183, of which 72 were waited for; matrix products, arithmetic and copies ran while one was open for 37% of the time, Pallas kernels for 2%

profile of v2, /device:TPU:0, one launch (start us, length us, event | category | flops | bytes accessed | tf_op | source)
XLA Modules:
  0.0 1060.4 jit_solution(3310839108269074643)
XLA Ops:
  49.6 6.3 collective-permute-done.2
  66.6 6.0 collective-permute-done.6.refs_6_
  97.7 4.5 collective-permute-start.7
  102.2 12.2 %collective-permute-start.9 = (bf16[128,1024]{1,0:T(8,128)(2,1)}, bf16[128,1024]{1,0:T(8,128)(2,1)S(1)}, u32[]{:S(2)}, u32[]{:S(2)}) collective-permute-start(bf16[128,1024]{1,0:T(8,128)(2,1)} %convolution_convert_fusion.22), channel_id=1, source_target_pairs={{0,3},{1,0},{2,1},{3,2},{4,7},{5,4},{6,5},{7,6},{8,11},{9,8},{10,9... | collective-permute-start | bytes 786440 | tf_op jit(solution)/shard_map/ppermute | solution.py:74
  116.8 5.5 collective-permute-done.9
  129.3 7.6 collective-permute-done.10.refs_1_
  146.0 11.3 %collective-permute-done.17 = bf16[512,512]{1,0:T(8,128)(2,1)S(1)} collective-permute-done((bf16[512,512]{1,0:T(8,128)(2,1)S(1)}, bf16[512,512]{1,0:T(8,128)(2,1)S(1)}, u32[]{:S(2)}, u32[]{:S(2)}) %collective-permute-start.17) | collective-permute-done | bytes 524320 | tf_op jit(solution)/shard_map/ppermute | solution.py:110
  171.6 5.6 collective-permute-done.19
  177.2 5.2 collective-permute-done.20
  199.8 4.7 collective-permute-done.23
  264.0 4.6 collective-permute-done.32
  294.8 5.1 collective-permute-done.38
  318.7 4.6 collective-permute-done.41
  363.1 6.4 collective-permute-done.46
  369.5 4.9 collective-permute-done.47
  388.0 4.4 multiply_convert_fusion.18
  460.7 5.4 collective-permute-done.73.refs_14_
  512.6 5.4 collective-permute-done.60
  529.7 6.0 fusion.896
  554.0 5.7 shard_map.398
  604.8 4.4 collective-permute-done.69
  621.9 4.6 collective-permute-done.89
  666.7 7.3 collective-permute-done.96
  730.6 4.5 collective-permute-done.103
  797.7 6.2 shard_map.399
  806.5 4.3 fusion.267
  821.8 6.1 collective-permute-done.116
  835.6 6.5 collective-permute-done.117
  881.9 6.3 shard_map.400
  930.5 8.0 collective-permute-done.134
  985.1 7.8 collective-permute-start.166
  1012.1 5.1 collective-permute-done.172
  (1844 shorter events, 860.1 us)
Async XLA Ops:
  61.2 21.4 %collective-permute-start.4 = (bf16[128,1024]{1,0:T(8,128)(2,1)S(1)}, bf16[128,1024]{1,0:T(8,128)(2,1)S(1)}, u32[]{:S(2)}, u32[]{:S(2)}) collective-permute-start(bf16[128,1024]{1,0:T(8,128)(2,1)S(1)} %multiply_convert_fusion.32.refs_5_), channel_id=1, source_target_pairs={{2,0},{3,1},{0,2},{1,3},{6,4},{7,5},{4,6},{5,7},{10,8},{11,9},{8,1... | collective-permute-start | bytes 786440 | tf_op jit(solution)/shard_map/ppermute | solution.py:69
  61.8 24.9 %collective-permute-start.8 = (bf16[128,1024]{1,0:T(8,128)(2,1)S(1)}, bf16[128,1024]{1,0:T(8,128)(2,1)}, u32[]{:S(2)}, u32[]{:S(2)}) collective-permute-start(bf16[128,1024]{1,0:T(8,128)(2,1)S(1)} %multiply_convert_fusion.32.refs_5_), channel_id=1, source_target_pairs={{3,0},{0,1},{1,2},{2,3},{7,4},{4,5},{5,6},{6,7},{11,8},{8,9},{9,10... | collective-permute-start | bytes 786440 | tf_op jit(solution)/shard_map/ppermute | solution.py:69
  79.7 34.7 %collective-permute-start.13 = (bf16[128,512]{1,0:T(8,128)(2,1)S(1)}, bf16[128,512]{1,0:T(8,128)(2,1)}, u32[]{:S(2)}, u32[]{:S(2)}) collective-permute-start(bf16[128,512]{1,0:T(8,128)(2,1)S(1)} %slice.964), channel_id=1, source_target_pairs={{0,4},{4,0},{8,12},{12,8},{16,20},{20,16},{24,28},{28,24},{32,36},... | collective-permute-start | bytes 393224 | tf_op jit(solution)/shard_map/ppermute | solution.py:110
  91.6 22.8 %collective-permute-start.15 = (bf16[128,512]{1,0:T(8,128)(2,1)}, bf16[128,512]{1,0:T(8,128)(2,1)}, u32[]{:S(2)}, u32[]{:S(2)}) collective-permute-start(bf16[128,512]{1,0:T(8,128)(2,1)} %collective-permute-done.14), channel_id=1, source_target_pairs={{0,4},{4,0},{8,12},{12,8},{16,20},{20,16},{24,28},{28,24},{32,36},... | collective-permute-start | bytes 393224 | tf_op jit(solution)/shard_map/ppermute | solution.py:110
  102.2 20.0 %collective-permute-start.9 = (bf16[128,1024]{1,0:T(8,128)(2,1)}, bf16[128,1024]{1,0:T(8,128)(2,1)S(1)}, u32[]{:S(2)}, u32[]{:S(2)}) collective-permute-start(bf16[128,1024]{1,0:T(8,128)(2,1)} %convolution_convert_fusion.22), channel_id=1, source_target_pairs={{0,3},{1,0},{2,1},{3,2},{4,7},{5,4},{6,5},{7,6},{8,11},{9,8},{10,9... | collective-permute-start | bytes 786440 | tf_op jit(solution)/shard_map/ppermute | solution.py:74
  347.4 165.2 %collective-permute-start.58 = (bf16[128,1024]{0,1:T(8,128)(2,1)}, bf16[128,1024]{0,1:T(8,128)(2,1)}, u32[]{:S(2)}, u32[]{:S(2)}) collective-permute-start(bf16[128,1024]{0,1:T(8,128)(2,1)} %get-tuple-element.517), channel_id=1, source_target_pairs={{0,2},{1,3},{2,0},{3,1},{4,6},{5,7},{6,4},{7,5},{8,10},{9,11},{10,... | collective-permute-start | bytes 786440 | tf_op jit(solution)/shard_map/ppermute | solution.py:74
  348.1 164.5 %collective-permute-start.59 = (bf16[128,1024]{0,1:T(8,128)(2,1)}, bf16[128,1024]{0,1:T(8,128)(2,1)}, u32[]{:S(2)}, u32[]{:S(2)}) collective-permute-start(bf16[128,1024]{0,1:T(8,128)(2,1)} %get-tuple-element.517), channel_id=1, source_target_pairs={{0,1},{1,2},{2,3},{3,0},{4,5},{5,6},{6,7},{7,4},{8,9},{9,10},{10,1... | collective-permute-start | bytes 786440 | tf_op jit(solution)/shard_map/ppermute | solution.py:74
  376.2 24.7 %collective-permute-start.51 = (bf16[128,1024]{1,0:T(8,128)(2,1)S(1)}, bf16[128,1024]{1,0:T(8,128)(2,1)}, u32[]{:S(2)}, u32[]{:S(2)}) collective-permute-start(bf16[128,1024]{1,0:T(8,128)(2,1)S(1)} %multiply_convert_fusion.20.refs_0_), channel_id=1, source_target_pairs={{1,0},{2,1},{3,2},{0,3},{5,4},{6,5},{7,6},{4,7},{9,8},{10,9},{11,1... | collective-permute-start | bytes 786440 | tf_op jit(solution)/shard_map/ppermute | solution.py:69
  377.4 35.7 %collective-permute-start.53 = (bf16[128,1024]{1,0:T(8,128)(2,1)S(1)}, bf16[128,1024]{1,0:T(8,128)(2,1)}, u32[]{:S(2)}, u32[]{:S(2)}) collective-permute-start(bf16[128,1024]{1,0:T(8,128)(2,1)S(1)} %multiply_convert_fusion.20.refs_0_), channel_id=1, source_target_pairs={{3,0},{0,1},{1,2},{2,3},{7,4},{4,5},{5,6},{6,7},{11,8},{8,9},{9,10... | collective-permute-start | bytes 786440 | tf_op jit(solution)/shard_map/ppermute | solution.py:69
  491.3 19.2 %collective-permute-start.80 = (bf16[128,1024]{0,1:T(8,128)(2,1)S(1)}, bf16[128,1024]{0,1:T(8,128)(2,1)S(1)}, u32[]{:S(2)}, u32[]{:S(2)}) collective-permute-start(bf16[128,1024]{0,1:T(8,128)(2,1)S(1)} %get-tuple-element.503), channel_id=1, source_target_pairs={{0,2},{1,3},{2,0},{3,1},{4,6},{5,7},{6,4},{7,5},{8,10},{9,11},{10,... | collective-permute-start | bytes 786440 | tf_op jit(solution)/shard_map/ppermute | solution.py:74
  523.5 36.2 %collective-permute-start.83 = (bf16[128,1024]{0,1:T(8,128)(2,1)}, bf16[128,1024]{0,1:T(8,128)(2,1)}, u32[]{:S(2)}, u32[]{:S(2)}) collective-permute-start(bf16[128,1024]{0,1:T(8,128)(2,1)} %get-tuple-element.521), channel_id=1, source_target_pairs={{0,2},{1,3},{2,0},{3,1},{4,6},{5,7},{6,4},{7,5},{8,10},{9,11},{10,... | collective-permute-start | bytes 786440 | tf_op jit(solution)/shard_map/ppermute | solution.py:74
  525.3 36.3 %collective-permute-start.84 = (bf16[128,1024]{0,1:T(8,128)(2,1)}, bf16[128,1024]{0,1:T(8,128)(2,1)}, u32[]{:S(2)}, u32[]{:S(2)}) collective-permute-start(bf16[128,1024]{0,1:T(8,128)(2,1)} %get-tuple-element.521), channel_id=1, source_target_pairs={{0,1},{1,2},{2,3},{3,0},{4,5},{5,6},{6,7},{7,4},{8,9},{9,10},{10,1... | collective-permute-start | bytes 786440 | tf_op jit(solution)/shard_map/ppermute | solution.py:74
  526.6 35.1 %collective-permute-start.85 = (bf16[128,1024]{0,1:T(8,128)(2,1)}, bf16[128,1024]{0,1:T(8,128)(2,1)}, u32[]{:S(2)}, u32[]{:S(2)}) collective-permute-start(bf16[128,1024]{0,1:T(8,128)(2,1)} %get-tuple-element.521), channel_id=1, source_target_pairs={{0,3},{1,0},{2,1},{3,2},{4,7},{5,4},{6,5},{7,6},{8,11},{9,8},{10,9... | collective-permute-start | bytes 786440 | tf_op jit(solution)/shard_map/ppermute | solution.py:74
  535.8 44.2 %collective-permute-start.61 = (bf16[128,1024]{0,1:T(8,128)(2,1)}, bf16[128,1024]{0,1:T(8,128)(2,1)}, u32[]{:S(2)}, u32[]{:S(2)}) collective-permute-start(bf16[128,1024]{0,1:T(8,128)(2,1)} %get-tuple-element.519), channel_id=1, source_target_pairs={{0,2},{1,3},{2,0},{3,1},{4,6},{5,7},{6,4},{7,5},{8,10},{9,11},{10,... | collective-permute-start | bytes 786440 | tf_op jit(solution)/shard_map/ppermute | solution.py:74
  536.4 46.4 %collective-permute-start.62 = (bf16[128,1024]{0,1:T(8,128)(2,1)}, bf16[128,1024]{0,1:T(8,128)(2,1)}, u32[]{:S(2)}, u32[]{:S(2)}) collective-permute-start(bf16[128,1024]{0,1:T(8,128)(2,1)} %get-tuple-element.519), channel_id=1, source_target_pairs={{0,1},{1,2},{2,3},{3,0},{4,5},{5,6},{6,7},{7,4},{8,9},{9,10},{10,1... | collective-permute-start | bytes 786440 | tf_op jit(solution)/shard_map/ppermute | solution.py:74
  559.7 23.0 %collective-permute-start.63 = (bf16[128,1024]{0,1:T(8,128)(2,1)}, bf16[128,1024]{0,1:T(8,128)(2,1)}, u32[]{:S(2)}, u32[]{:S(2)}) collective-permute-start(bf16[128,1024]{0,1:T(8,128)(2,1)} %get-tuple-element.519), channel_id=1, source_target_pairs={{0,3},{1,0},{2,1},{3,2},{4,7},{5,4},{6,5},{7,6},{8,11},{9,8},{10,9... | collective-permute-start | bytes 786440 | tf_op jit(solution)/shard_map/ppermute | solution.py:74
  561.7 65.0 %collective-permute-start.91 = (bf16[512,2560]{1,0:T(8,128)(2,1)}, bf16[512,2560]{1,0:T(8,128)(2,1)}, u32[]{:S(2)}, u32[]{:S(2)}) collective-permute-start(bf16[512,2560]{1,0:T(8,128)(2,1)} %get-tuple-element.60), channel_id=1, source_target_pairs={{0,4},{4,0},{8,12},{12,8},{16,20},{20,16},{24,28},{28,24},{32,36},... | collective-permute-start | bytes 7864328 | tf_op jit(solution)/shard_map/ppermute | solution.py:110
  652.9 168.9 %collective-permute-start.79 = (bf16[512,512]{1,0:T(8,128)(2,1)}, bf16[512,512]{1,0:T(8,128)(2,1)}, u32[]{:S(2)}, u32[]{:S(2)}) collective-permute-start(bf16[512,512]{1,0:T(8,128)(2,1)} %pad_maximum_fusion.14), channel_id=1, source_target_pairs={{4,0},{8,4},{12,8},{20,16},{24,20},{28,24},{36,32},{40,36},{44,40}... | collective-permute-start | bytes 1572872 | tf_op jit(solution)/shard_map/ppermute | solution.py:533
  776.6 35.1 %collective-permute-start.115 = (bf16[1024,512]{1,0:T(8,128)(2,1)}, bf16[1024,512]{1,0:T(8,128)(2,1)}, u32[]{:S(2)}, u32[]{:S(2)}) collective-permute-start(bf16[1024,512]{1,0:T(8,128)(2,1)} %pad_maximum_fusion.6), channel_id=1, source_target_pairs={{0,4},{4,0},{8,12},{12,8},{16,20},{20,16},{24,28},{28,24},{32,36},... | collective-permute-start | bytes 3145736 | tf_op jit(solution)/shard_map/ppermute | solution.py:110
  803.8 87.1 %collective-permute-start.128 = (bf16[512,3328]{1,0:T(8,128)(2,1)}, bf16[512,3328]{1,0:T(8,128)(2,1)}, u32[]{:S(2)}, u32[]{:S(2)}) collective-permute-start(bf16[512,3328]{1,0:T(8,128)(2,1)} %get-tuple-element.68), channel_id=1, source_target_pairs={{0,4},{4,0},{8,12},{12,8},{16,20},{20,16},{24,28},{28,24},{32,36},... | collective-permute-start | bytes 10223624 | tf_op jit(solution)/shard_map/ppermute | solution.py:110
  848.7 19.4 %collective-permute-start.126 = (bf16[128,1024]{1,0:T(8,128)(2,1)}, bf16[128,1024]{1,0:T(8,128)(2,1)}, u32[]{:S(2)}, u32[]{:S(2)}) collective-permute-start(bf16[128,1024]{1,0:T(8,128)(2,1)} %get-tuple-element.271.refs_13_), channel_id=1, source_target_pairs={{3,0},{0,1},{1,2},{2,3},{7,4},{4,5},{5,6},{6,7},{11,8},{8,9},{9,10... | collective-permute-start | bytes 786440 | tf_op jit(solution)/shard_map/ppermute | solution.py:69
  889.8 89.3 %collective-permute-start.164 = (bf16[512,2816]{1,0:T(8,128)(2,1)}, bf16[512,2816]{1,0:T(8,128)(2,1)}, u32[]{:S(2)}, u32[]{:S(2)}) collective-permute-start(bf16[512,2816]{1,0:T(8,128)(2,1)} %get-tuple-element.72), channel_id=1, source_target_pairs={{0,4},{4,0},{8,12},{12,8},{16,20},{20,16},{24,28},{28,24},{32,36},... | collective-permute-start | bytes 8650760 | tf_op jit(solution)/shard_map/ppermute | solution.py:110
  899.7 24.9 %collective-permute-start.136 = (bf16[4,32,1664]{2,1,0:T(8,128)(2,1)S(1)}, bf16[4,32,1664]{2,1,0:T(8,128)(2,1)S(1)}, u32[]{:S(2)}, u32[]{:S(2)}) collective-permute-start(bf16[4,32,1664]{2,1,0:T(8,128)(2,1)S(1)} %get-tuple-element.336), channel_id=1, source_target_pairs={{0,64},{4,68},{8,72},{12,76},{16,80},{20,84},{24,88},{28,92},{32,9... | collective-permute-start | bytes 1277960 | tf_op jit(solution)/shard_map/ppermute | solution.py:230
  905.6 19.2 %collective-permute-start.137 = (bf16[4,32,1664]{2,1,0:T(8,128)(2,1)S(1)}, bf16[4,32,1664]{2,1,0:T(8,128)(2,1)S(1)}, u32[]{:S(2)}, u32[]{:S(2)}) collective-permute-start(bf16[4,32,1664]{2,1,0:T(8,128)(2,1)S(1)} %get-tuple-element.338), channel_id=1, source_target_pairs={{0,32},{4,36},{8,40},{12,44},{16,48},{20,52},{24,56},{28,60},{32,6... | collective-permute-start | bytes 1277960 | tf_op jit(solution)/shard_map/ppermute | solution.py:230
  907.4 20.8 %collective-permute-start.138 = (bf16[4,32,1664]{2,1,0:T(8,128)(2,1)S(1)}, bf16[4,32,1664]{2,1,0:T(8,128)(2,1)S(1)}, u32[]{:S(2)}, u32[]{:S(2)}) collective-permute-start(bf16[4,32,1664]{2,1,0:T(8,128)(2,1)S(1)} %get-tuple-element.337), channel_id=1, source_target_pairs={{0,96},{4,100},{8,104},{12,108},{16,112},{20,116},{24,120},{28,124... | collective-permute-start | bytes 1277960 | tf_op jit(solution)/shard_map/ppermute | solution.py:230
  928.1 23.3 %collective-permute-start.132 = (bf16[512,512]{1,0:T(8,128)(2,1)S(1)}, bf16[512,512]{1,0:T(8,128)(2,1)S(1)}, u32[]{:S(2)}, u32[]{:S(2)}) collective-permute-start(bf16[512,512]{1,0:T(8,128)(2,1)S(1)} %pad_maximum_fusion.15), channel_id=1, source_target_pairs={{4,0},{8,4},{12,8},{20,16},{24,20},{28,24},{36,32},{40,36},{44,40}... | collective-permute-start | bytes 1572872 | tf_op jit(solution)/shard_map/ppermute | solution.py:695
  964.6 20.5 %collective-permute-start.142 = (bf16[128,1024]{1,0:T(8,128)(2,1)}, bf16[128,1024]{1,0:T(8,128)(2,1)}, u32[]{:S(2)}, u32[]{:S(2)}) collective-permute-start(bf16[128,1024]{1,0:T(8,128)(2,1)} %get-tuple-element.268), channel_id=1, source_target_pairs={{1,0},{2,1},{3,2},{0,3},{5,4},{6,5},{7,6},{4,7},{9,8},{10,9},{11,1... | collective-permute-start | bytes 786440 | tf_op jit(solution)/shard_map/ppermute | solution.py:69
  967.3 26.6 %collective-permute-start.143 = (bf16[128,1024]{1,0:T(8,128)(2,1)}, bf16[128,1024]{1,0:T(8,128)(2,1)}, u32[]{:S(2)}, u32[]{:S(2)}) collective-permute-start(bf16[128,1024]{1,0:T(8,128)(2,1)} %get-tuple-element.268), channel_id=1, source_target_pairs={{2,0},{3,1},{0,2},{1,3},{6,4},{7,5},{4,6},{5,7},{10,8},{11,9},{8,1... | collective-permute-start | bytes 786440 | tf_op jit(solution)/shard_map/ppermute | solution.py:69
  967.8 27.9 %collective-permute-start.144 = (bf16[128,1024]{1,0:T(8,128)(2,1)}, bf16[128,1024]{1,0:T(8,128)(2,1)}, u32[]{:S(2)}, u32[]{:S(2)}) collective-permute-start(bf16[128,1024]{1,0:T(8,128)(2,1)} %get-tuple-element.268), channel_id=1, source_target_pairs={{3,0},{0,1},{1,2},{2,3},{7,4},{4,5},{5,6},{6,7},{11,8},{8,9},{9,10... | collective-permute-start | bytes 786440 | tf_op jit(solution)/shard_map/ppermute | solution.py:69
  979.0 46.5 %collective-permute-start.148 = (bf16[512,1280]{1,0:T(8,128)(2,1)S(1)}, bf16[512,1280]{1,0:T(8,128)(2,1)S(1)}, u32[]{:S(2)}, u32[]{:S(2)}) collective-permute-start(bf16[512,1280]{1,0:T(8,128)(2,1)S(1)} %get-tuple-element.79), channel_id=1, source_target_pairs={{0,4},{4,0},{8,12},{12,8},{16,20},{20,16},{24,28},{28,24},{32,36},... | collective-permute-start | bytes 3932168 | tf_op jit(solution)/shard_map/ppermute | solution.py:110
  982.0 20.8 %collective-permute-start.165 = (bf16[4,32,1408]{2,1,0:T(8,128)(2,1)S(1)}, bf16[4,32,1408]{2,1,0:T(8,128)(2,1)S(1)}, u32[]{:S(2)}, u32[]{:S(2)}) collective-permute-start(bf16[4,32,1408]{2,1,0:T(8,128)(2,1)S(1)} %get-tuple-element.342), channel_id=1, source_target_pairs={{0,16},{4,20},{8,24},{12,28},{16,0},{20,4},{24,8},{28,12},{32,48},... | collective-permute-start | bytes 1081352 | tf_op jit(solution)/shard_map/ppermute | solution.py:230
  985.1 20.3 %collective-permute-start.166 = (bf16[4,32,1408]{2,1,0:T(8,128)(2,1)S(1)}, bf16[4,32,1408]{2,1,0:T(8,128)(2,1)S(1)}, u32[]{:S(2)}, u32[]{:S(2)}) collective-permute-start(bf16[4,32,1408]{2,1,0:T(8,128)(2,1)S(1)} %get-tuple-element.343), channel_id=1, source_target_pairs={{0,8},{4,12},{8,16},{12,20},{16,24},{20,28},{24,0},{28,4},{32,40},... | collective-permute-start | bytes 1081352 | tf_op jit(solution)/shard_map/ppermute | solution.py:230
  (579 other events, 4420.1 us)

commit v3 on v2

--- a/solution.py
+++ b/solution.py
@@ -131,13 +131,13 @@
     return lax.dynamic_slice_in_dim(twice, start, array.shape[0], 0)
 
 
-def weight_grads(pairs, extra=None):
+def weight_grads(pairs):
     n_seq = lax.axis_size("seq")
     depth = pairs[0][0][0].shape[1]
     unit = depth // n_seq
     block = max(256, CORES * unit)
     widths = [latter[0].shape[1] for _, latter in pairs]
-    total = sum(widths) + (0 if extra is None else extra.shape[1])
+    total = sum(widths)
     counts = [(len(former), len(latter)) for former, latter in pairs]
     operands, specs = [], []
     for former, latter in pairs:
@@ -148,10 +148,6 @@
             operands.append(piece)
             specs.append(pl.BlockSpec(piece.shape, lambda i: (0, 0)))
 
-    if extra is not None:
-        operands.append(extra)
-        specs.append(pl.BlockSpec((block, extra.shape[1]), lambda i: (i, 0)))
-
     def kernel(core_ref, *refs):
         mine_ref, other_ref = refs[-2:]
         first = core_ref[0] == 0
@@ -174,8 +170,6 @@
             latter = jnp.concatenate(latter) if n_latter > 1 else latter[0]
             keep(dot_first(former, latter).astype(LOW), column)
             column += width
-        if extra is not None:
-            keep(refs[at][...], column)
 
     shape = jax.ShapeDtypeStruct((depth // CORES, total), LOW)
     out_spec = pl.BlockSpec((block // CORES, total), lambda i: (i, 0))
@@ -378,16 +372,12 @@
     thin_rows = slab_rows // n_tp
     width = qkv_tok.shape[2]
     qkv_win_flat = qkv_win.reshape(model_width, 3 * width)
-    qkv_tok_flat = qkv_tok.reshape(model_width, 3 * width)
     out_tok_flat = out_tok.reshape(2 * width, model_width)
-    qkv_state_flat = qkv_state.reshape(model_width, 3 * width)
     out_state_flat = out_state.reshape(2 * width, model_width)
-    keep_one, keep_two = jax.nn.sigmoid(gate_bias)
 
     row_ids = (jnp.arange(block_rows) + tp_index * piece_rows) % block_rows
     below = row_ids[None, :] <= row_ids[:, None]
     token_rows = turned(tokens, tp_index * piece_rows)
-    cotangent_rows = turned(cotangent, tp_index * piece_rows)
 
     def natural(pieces):
         whole = jnp.concatenate(pieces)
@@ -400,6 +390,13 @@
     onward = [(s, s + 1) for s in range(lax.axis_size("seq")) if (s + 1) % CHAIN]
     win_prev = lax.ppermute(win_pair, "seq", onward)
     win_heads, win_logs = band_attend(win_queries, win_pair, win_prev, below, starts_here)
+    cotangent, qkv_tok, qkv_state, gate_bias, init_state, _ = lax.optimization_barrier(
+        (cotangent, qkv_tok, qkv_state, gate_bias, init_state, win_heads)
+    )
+    qkv_tok_flat = qkv_tok.reshape(model_width, 3 * width)
+    qkv_state_flat = qkv_state.reshape(model_width, 3 * width)
+    keep_one, keep_two = jax.nn.sigmoid(gate_bias)
+    cotangent_rows = turned(cotangent, tp_index * piece_rows)
     own_input = input_rows[:piece_rows]
     win_mixed = own_input + tp_scatter(
         [plain_dot(part, out_win) for part in split_rows(win_heads, n_tp)]
@@ -486,16 +483,17 @@
         queries, my_state_pair[:, :width], my_state_pair[:, width:]
     )
     token_heads = jnp.concatenate([own_heads, cross_heads], axis=1)
-    mixed_one = layer_one + tp_scatter(
+    proj_total = tp_scatter(
         [plain_dot(part, out_tok_flat) for part in split_rows(token_heads, n_tp)]
     )
+    cotangents = split_rows(tied(cotangent_rows, token_heads), n_tp)
+    grad_active = [dot_second(part, down_tok) for part in cotangents]
+    mixed_one = layer_one + tied(proj_total, *grad_active)
     ffn_in = tp_gather(layer_norm(mixed_one, norm_ffn).astype(LOW))
     hidden = [plain_dot(part, up_tok) for part in ffn_in]
 
-    cotangents = split_rows(cotangent_rows, n_tp)
     grad_hidden = [
-        gelu_slope(part, dot_second(grad, down_tok)).astype(LOW)
-        for part, grad in zip(hidden, cotangents)
+        gelu_slope(part, grad).astype(LOW) for part, grad in zip(hidden, grad_active)
     ]
     grad_ffn_in = tp_scatter([dot_second(part, up_tok) for part in grad_hidden])
     active = [gelu_exact(part).astype(LOW) for part in hidden]
@@ -706,9 +704,6 @@
     layer_output = mixed_one + tp_scatter([plain_dot(part, down_tok) for part in active])
     output_rows = natural(tp_gather(layer_output.astype(LOW)))
 
-    init_columns = jnp.concatenate(
-        [jnp.where(position == p, init_grad.T, 0.0) for p in range(CHAIN)], axis=1
-    )
     vectors = [
         grad_norm_win,
         grad_norm_wffn,
@@ -719,12 +714,26 @@
         bias_one,
         bias_two,
     ]
-    small = jnp.concatenate([init_columns, jnp.stack(vectors, axis=1)], axis=1)
-    small_width = small.shape[1]
-    small = jnp.pad(small, ((0, 0), (0, -small_width % 256))).astype(LOW)
+    small_rows = jnp.concatenate(
+        [init_grad, jnp.stack(vectors), jnp.zeros((8, model_width), HIGH)]
+    ).astype(LOW)
+    small_width = CHAIN * thin_rows + len(vectors)
+    small_padded = small_width + -small_width % 256
+    row_of = lax.broadcasted_iota(jnp.int32, (small_rows.shape[0], small_padded), 0)
+    column_of = lax.broadcasted_iota(jnp.int32, (small_rows.shape[0], small_padded), 1)
+    column_for = jnp.where(
+        row_of < thin_rows,
+        position * thin_rows + row_of,
+        (CHAIN - 1) * thin_rows + row_of,
+    )
+    selector = (column_of == column_for).astype(LOW)
     last_grads = SeqSum(
         weight_grads(
-            [([win_normed], [grad_win_qkv]), ([grad_win_proj], [win_heads])], small
+            [
+                ([win_normed], [grad_win_qkv]),
+                ([grad_win_proj], [win_heads]),
+                ([small_rows], [selector]),
+            ]
         )
     )
     middle_grads.first()

time: 1070 us -> 853 us (0.80)
  local copies, waits for them, and re-layouts: 158 us -> 63.9 us
  matrix products: 224 us -> 134 us
  other arithmetic: 150 us -> 79.8 us
  waiting for transfers between devices: 244 us -> 299 us
  starting transfers between devices: 256 us -> 240 us
    convert_element_type x35 -> x0, local copies, waits for them, and re-layouts: 52.5 us -> none  [the longest x4 7.18 us: body(): gelu_slope(part, dot_second(grad, down_tok)).astype(LOW)]
    dot_general x89, matrix products: 108 us -> 65.4 us  [plain_dot(): return jnp.dot(former, latter, preferred_element_type=HIGH)]
    dot_general x91, matrix products: 93.9 us -> 53.4 us  [dot_second(): lax.dot_general(former, latter, (((1,), (1,)), ((), ())), preferred_eleme...]
    ppermute x69, waiting for transfers between devices: 116 us -> 145 us  [tp_to(): return lax.ppermute(array, 'tp', [(i, (i + k) % n) for i in range(n)])]
    ppermute x69, starting transfers between devices: 120 us -> 97.5 us  [tp_to(): return lax.ppermute(array, 'tp', [(i, (i + k) % n) for i in range(n)])]
    unnamed x887 -> x695, local copies, waits for them, and re-layouts: 57.2 us -> 37.4 us
    ppermute x30, waiting for transfers between devices: 57 us -> 70.8 us  [tp_from(): return lax.ppermute(array, 'tp', [((i + k) % n, i) for i in range(n)])]
    ppermute x33, waiting for transfers between devices: 31.9 us -> 42.7 us  [swap(): return lax.ppermute(array, 'seq', [(s, s ^ k) for s in range(n)])]
  transfers between devices with their start and end apart: 183 -> 183, of which waited for: 72 -> 84; matrix products, arithmetic and copies ran while one was open for 37% -> 22% of each run, Pallas kernels for 2% -> 2%
where the time goes in v3:
time: 853 us; the launch traced here: 842 us
  waiting for transfers between devices  299 us (35%)
  starting transfers between devices  240 us (28%)
  matrix products  134 us (16%)
  other arithmetic  79.8 us (9%)
  local copies, waits for them, and re-layouts  63.9 us (7%)
  Pallas kernels  17.3 us (2%)
    ppermute x69, waiting for transfers between devices, tp_to(): return lax.ppermute(array, 'tp', [(i, (i + k) % n) for i in range(n)])  145 us
    ppermute x69, starting transfers between devices, tp_to(): return lax.ppermute(array, 'tp', [(i, (i + k) % n) for i in range(n)])  97.5 us
    ppermute x48, starting transfers between devices, stage(): total = total + lax.ppermute(sent, 'seq', self.pairs(*step(k))).astype(HIGH)  86.9 us
    ppermute x30, waiting for transfers between devices, tp_from(): return lax.ppermute(array, 'tp', [((i + k) % n, i) for i in range(n)])  70.8 us
    dot_general x89, matrix products, plain_dot(): return jnp.dot(former, latter, preferred_element_type=HIGH)  65.4 us
    dot_general x91, matrix products, dot_second(): lax.dot_general(former, latter, (((1,), (1,)), ((), ())), preferred_eleme...  53.4 us
    ppermute x33, waiting for transfers between devices, swap(): return lax.ppermute(array, 'seq', [(s, s ^ k) for s in range(n)])  42.7 us
    ppermute x48, waiting for transfers between devices, stage(): total = total + lax.ppermute(sent, 'seq', self.pairs(*step(k))).astype(HIGH)  39.9 us
  transfers between devices with their start and end apart: 183, of which 84 were waited for; matrix products, arithmetic and copies ran while one was open for 22% of the time, Pallas kernels for 2%

profile of v3, /device:TPU:0, one launch (start us, length us, event | category | flops | bytes accessed | tf_op | source)
XLA Modules:
  0.0 842.2 jit_solution(959235525739742748)
XLA Ops:
  57.3 8.0 collective-permute-done.6.refs_6_
  115.8 11.3 %collective-permute-done.17 = bf16[512,512]{1,0:T(8,128)(2,1)S(1)} collective-permute-done((bf16[512,512]{1,0:T(8,128)(2,1)S(1)}, bf16[512,512]{1,0:T(8,128)(2,1)S(1)}, u32[]{:S(2)}, u32[]{:S(2)}) %collective-permute-start.17) | collective-permute-done | bytes 524320 | tf_op jit(solution)/shard_map/ppermute | solution.py:110
  137.7 6.1 collective-permute-done.19
  155.8 6.9 collective-permute-done.22
  189.1 5.0 collective-permute-done.29
  203.1 5.8 collective-permute-done.31
  208.9 4.6 collective-permute-done.32
  229.9 5.6 collective-permute-done.37
  235.5 4.8 collective-permute-done.38
  248.8 5.6 collective-permute-done.40
  254.4 4.6 collective-permute-done.41
  285.6 6.6 collective-permute-done.46
  292.2 5.1 collective-permute-done.47
  303.0 6.0 collective-permute-done.49.refs_2_
  340.6 4.7 collective-permute-done.73.refs_14_
  387.6 6.1 collective-permute-done.60
  453.1 6.0 collective-permute-done.67
  461.1 4.6 collective-permute-done.69
  471.5 5.6 collective-permute-done.88
  477.1 4.6 collective-permute-done.89
  516.7 7.3 collective-permute-done.96
  559.1 6.1 collective-permute-done.103
  576.0 6.2 collective-permute-done.112
  596.9 4.9 collective-permute-done.121
  606.7 5.2 shard_map.399
  622.9 8.8 %collective-permute-done.116 = bf16[512,512]{1,0:T(8,128)(2,1)S(1)} collective-permute-done((bf16[512,512]{1,0:T(8,128)(2,1)S(1)}, bf16[512,512]{1,0:T(8,128)(2,1)S(1)}, u32[]{:S(2)}, u32[]{:S(2)}) %collective-permute-start.116) | collective-permute-done | bytes 524320 | tf_op jit(solution)/shard_map/ppermute | solution.py:110
  637.6 6.6 collective-permute-done.117
  652.9 6.6 collective-permute-done.122.refs_15_
  670.0 5.5 shard_map.400
  688.0 4.8 collective-permute-done.130
  715.3 10.0 %collective-permute-done.134 = bf16[4,32,1664]{2,1,0:T(8,128)(2,1)S(1)} collective-permute-done((bf16[4,32,1664]{2,1,0:T(8,128)(2,1)S(1)}, bf16[4,32,1664]{2,1,0:T(8,128)(2,1)S(1)}, u32[]{:S(2)}, u32[]{:S(2)}) %collective-permute-start.134) | collective-permute-done | bytes 426016 | tf_op jit(solution)/shard_map/ppermute | solution.py:224
  765.3 5.4 collective-permute-start.166
  (1615 shorter events, 639.1 us)
Async XLA Ops:
  31.0 15.8 %collective-permute-start.1 = (bf16[128,1024]{1,0:T(8,128)(2,1)}, bf16[128,1024]{1,0:T(8,128)(2,1)}, u32[]{:S(2)}, u32[]{:S(2)}) collective-permute-start(bf16[128,1024]{1,0:T(8,128)(2,1)} %convolution_convert_fusion.27), channel_id=1, source_target_pairs={{0,2},{1,3},{2,0},{3,1},{4,6},{5,7},{6,4},{7,5},{8,10},{9,11},{10,... | collective-permute-start | bytes 786440 | tf_op jit(solution)/shard_map/ppermute | solution.py:74
  54.5 22.7 %collective-permute-start.8 = (bf16[128,1024]{1,0:T(8,128)(2,1)S(1)}, bf16[128,1024]{1,0:T(8,128)(2,1)S(1)}, u32[]{:S(2)}, u32[]{:S(2)}) collective-permute-start(bf16[128,1024]{1,0:T(8,128)(2,1)S(1)} %multiply_convert_fusion.30.refs_5_), channel_id=1, source_target_pairs={{3,0},{0,1},{1,2},{2,3},{7,4},{4,5},{5,6},{6,7},{11,8},{8,9},{9,10... | collective-permute-start | bytes 786440 | tf_op jit(solution)/shard_map/ppermute | solution.py:69
  270.1 117.4 %collective-permute-start.58 = (bf16[128,1024]{1,0:T(8,128)(2,1)S(1)}, bf16[128,1024]{1,0:T(8,128)(2,1)S(1)}, u32[]{:S(2)}, u32[]{:S(2)}) collective-permute-start(bf16[128,1024]{1,0:T(8,128)(2,1)S(1)} %get-tuple-element.483), channel_id=1, source_target_pairs={{0,2},{1,3},{2,0},{3,1},{4,6},{5,7},{6,4},{7,5},{8,10},{9,11},{10,... | collective-permute-start | bytes 786440 | tf_op jit(solution)/shard_map/ppermute | solution.py:74
  270.9 116.6 %collective-permute-start.59 = (bf16[128,1024]{1,0:T(8,128)(2,1)S(1)}, bf16[128,1024]{1,0:T(8,128)(2,1)S(1)}, u32[]{:S(2)}, u32[]{:S(2)}) collective-permute-start(bf16[128,1024]{1,0:T(8,128)(2,1)S(1)} %get-tuple-element.483), channel_id=1, source_target_pairs={{0,1},{1,2},{2,3},{3,0},{4,5},{5,6},{6,7},{7,4},{8,9},{9,10},{10,1... | collective-permute-start | bytes 786440 | tf_op jit(solution)/shard_map/ppermute | solution.py:74
  281.5 15.8 %collective-permute-start.47 = (bf16[128,1024]{1,0:T(8,128)(2,1)S(1)}, bf16[128,1024]{1,0:T(8,128)(2,1)S(1)}, u32[]{:S(2)}, u32[]{:S(2)}) collective-permute-start(bf16[128,1024]{1,0:T(8,128)(2,1)S(1)} %convolution_convert_fusion.20), channel_id=1, source_target_pairs={{0,1},{1,2},{2,3},{3,0},{4,5},{5,6},{6,7},{7,4},{8,9},{9,10},{10,1... | collective-permute-start | bytes 786440 | tf_op jit(solution)/shard_map/ppermute | solution.py:74
  300.3 16.0 %collective-permute-start.53 = (bf16[128,1024]{1,0:T(8,128)(2,1)S(1)}, bf16[128,1024]{1,0:T(8,128)(2,1)S(1)}, u32[]{:S(2)}, u32[]{:S(2)}) collective-permute-start(bf16[128,1024]{1,0:T(8,128)(2,1)S(1)} %multiply_convert_fusion.18.refs_0_), channel_id=1, source_target_pairs={{3,0},{0,1},{1,2},{2,3},{7,4},{4,5},{5,6},{6,7},{11,8},{8,9},{9,10... | collective-permute-start | bytes 786440 | tf_op jit(solution)/shard_map/ppermute | solution.py:69
  367.8 18.7 %collective-permute-start.80 = (bf16[128,1024]{1,0:T(8,128)(2,1)S(1)}, bf16[128,1024]{1,0:T(8,128)(2,1)S(1)}, u32[]{:S(2)}, u32[]{:S(2)}) collective-permute-start(bf16[128,1024]{1,0:T(8,128)(2,1)S(1)} %get-tuple-element.469), channel_id=1, source_target_pairs={{0,2},{1,3},{2,0},{3,1},{4,6},{5,7},{6,4},{7,5},{8,10},{9,11},{10,... | collective-permute-start | bytes 786440 | tf_op jit(solution)/shard_map/ppermute | solution.py:74
  369.9 16.7 %collective-permute-start.81 = (bf16[128,1024]{1,0:T(8,128)(2,1)S(1)}, bf16[128,1024]{1,0:T(8,128)(2,1)S(1)}, u32[]{:S(2)}, u32[]{:S(2)}) collective-permute-start(bf16[128,1024]{1,0:T(8,128)(2,1)S(1)} %get-tuple-element.469), channel_id=1, source_target_pairs={{0,1},{1,2},{2,3},{3,0},{4,5},{5,6},{6,7},{7,4},{8,9},{9,10},{10,1... | collective-permute-start | bytes 786440 | tf_op jit(solution)/shard_map/ppermute | solution.py:74
  370.9 15.7 %collective-permute-start.82 = (bf16[128,1024]{1,0:T(8,128)(2,1)S(1)}, bf16[128,1024]{1,0:T(8,128)(2,1)S(1)}, u32[]{:S(2)}, u32[]{:S(2)}) collective-permute-start(bf16[128,1024]{1,0:T(8,128)(2,1)S(1)} %get-tuple-element.469), channel_id=1, source_target_pairs={{0,3},{1,0},{2,1},{3,2},{4,7},{5,4},{6,5},{7,6},{8,11},{9,8},{10,9... | collective-permute-start | bytes 786440 | tf_op jit(solution)/shard_map/ppermute | solution.py:74
  398.9 31.1 %collective-permute-start.83 = (bf16[128,1024]{1,0:T(8,128)(2,1)}, bf16[128,1024]{1,0:T(8,128)(2,1)}, u32[]{:S(2)}, u32[]{:S(2)}) collective-permute-start(bf16[128,1024]{1,0:T(8,128)(2,1)} %get-tuple-element.487), channel_id=1, source_target_pairs={{0,2},{1,3},{2,0},{3,1},{4,6},{5,7},{6,4},{7,5},{8,10},{9,11},{10,... | collective-permute-start | bytes 786440 | tf_op jit(solution)/shard_map/ppermute | solution.py:74
  399.1 34.2 %collective-permute-start.84 = (bf16[128,1024]{1,0:T(8,128)(2,1)}, bf16[128,1024]{1,0:T(8,128)(2,1)}, u32[]{:S(2)}, u32[]{:S(2)}) collective-permute-start(bf16[128,1024]{1,0:T(8,128)(2,1)} %get-tuple-element.487), channel_id=1, source_target_pairs={{0,1},{1,2},{2,3},{3,0},{4,5},{5,6},{6,7},{7,4},{8,9},{9,10},{10,1... | collective-permute-start | bytes 786440 | tf_op jit(solution)/shard_map/ppermute | solution.py:74
  401.2 32.1 %collective-permute-start.85 = (bf16[128,1024]{1,0:T(8,128)(2,1)}, bf16[128,1024]{1,0:T(8,128)(2,1)}, u32[]{:S(2)}, u32[]{:S(2)}) collective-permute-start(bf16[128,1024]{1,0:T(8,128)(2,1)} %get-tuple-element.487), channel_id=1, source_target_pairs={{0,3},{1,0},{2,1},{3,2},{4,7},{5,4},{6,5},{7,6},{8,11},{9,8},{10,9... | collective-permute-start | bytes 786440 | tf_op jit(solution)/shard_map/ppermute | solution.py:74
  408.4 34.3 %collective-permute-start.61 = (bf16[128,1024]{1,0:T(8,128)(2,1)}, bf16[128,1024]{1,0:T(8,128)(2,1)S(1)}, u32[]{:S(2)}, u32[]{:S(2)}) collective-permute-start(bf16[128,1024]{1,0:T(8,128)(2,1)} %get-tuple-element.485), channel_id=1, source_target_pairs={{0,2},{1,3},{2,0},{3,1},{4,6},{5,7},{6,4},{7,5},{8,10},{9,11},{10,... | collective-permute-start | bytes 786440 | tf_op jit(solution)/shard_map/ppermute | solution.py:74
  410.5 32.6 %collective-permute-start.62 = (bf16[128,1024]{1,0:T(8,128)(2,1)}, bf16[128,1024]{1,0:T(8,128)(2,1)S(1)}, u32[]{:S(2)}, u32[]{:S(2)}) collective-permute-start(bf16[128,1024]{1,0:T(8,128)(2,1)} %get-tuple-element.485), channel_id=1, source_target_pairs={{0,1},{1,2},{2,3},{3,0},{4,5},{5,6},{6,7},{7,4},{8,9},{9,10},{10,1... | collective-permute-start | bytes 786440 | tf_op jit(solution)/shard_map/ppermute | solution.py:74
  433.3 48.6 %collective-permute-start.91 = (bf16[512,2560]{1,0:T(8,128)(2,1)S(1)}, bf16[512,2560]{1,0:T(8,128)(2,1)S(1)}, u32[]{:S(2)}, u32[]{:S(2)}) collective-permute-start(bf16[512,2560]{1,0:T(8,128)(2,1)S(1)} %get-tuple-element.74), channel_id=1, source_target_pairs={{0,4},{4,0},{8,12},{12,8},{16,20},{20,16},{24,28},{28,24},{32,36},... | collective-permute-start | bytes 7864328 | tf_op jit(solution)/shard_map/ppermute | solution.py:110
  491.5 17.0 %collective-permute-start.100 = (bf16[4,32,1280]{2,1,0:T(8,128)(2,1)S(1)}, bf16[4,32,1280]{2,1,0:T(8,128)(2,1)S(1)}, u32[]{:S(2)}, u32[]{:S(2)}) collective-permute-start(bf16[4,32,1280]{2,1,0:T(8,128)(2,1)S(1)} %get-tuple-element.329), channel_id=1, source_target_pairs={{0,96},{4,100},{8,104},{12,108},{16,112},{20,116},{24,120},{28,124... | collective-permute-start | bytes 983048 | tf_op jit(solution)/shard_map/ppermute | solution.py:224
  494.4 15.9 %collective-permute-start.98 = (bf16[4,32,1280]{2,1,0:T(8,128)(2,1)S(1)}, bf16[4,32,1280]{2,1,0:T(8,128)(2,1)S(1)}, u32[]{:S(2)}, u32[]{:S(2)}) collective-permute-start(bf16[4,32,1280]{2,1,0:T(8,128)(2,1)S(1)} %get-tuple-element.328), channel_id=1, source_target_pairs={{0,64},{4,68},{8,72},{12,76},{16,80},{20,84},{24,88},{28,92},{32,9... | collective-permute-start | bytes 983048 | tf_op jit(solution)/shard_map/ppermute | solution.py:224
  503.0 119.9 %collective-permute-start.79 = (bf16[512,512]{1,0:T(8,128)(2,1)S(1)}, bf16[512,512]{1,0:T(8,128)(2,1)S(1)}, u32[]{:S(2)}, u32[]{:S(2)}) collective-permute-start(bf16[512,512]{1,0:T(8,128)(2,1)S(1)} %copy-done.234), channel_id=1, source_target_pairs={{4,0},{8,4},{12,8},{20,16},{24,20},{28,24},{36,32},{40,36},{44,40}... | collective-permute-start | bytes 1572872 | tf_op jit(solution)/shard_map/ppermute | solution.py:531
  510.3 17.4 %collective-permute-start.97 = (bf16[4,32,1280]{2,1,0:T(8,128)(2,1)S(1)}, bf16[4,32,1280]{2,1,0:T(8,128)(2,1)S(1)}, u32[]{:S(2)}, u32[]{:S(2)}) collective-permute-start(bf16[4,32,1280]{2,1,0:T(8,128)(2,1)S(1)} %get-tuple-element.332), channel_id=1, source_target_pairs={{0,24},{4,28},{8,0},{12,4},{16,8},{20,12},{24,16},{28,20},{32,56},... | collective-permute-start | bytes 983048 | tf_op jit(solution)/shard_map/ppermute | solution.py:224
  595.6 22.0 %collective-permute-start.115 = (bf16[1024,512]{1,0:T(8,128)(2,1)S(1)}, bf16[1024,512]{1,0:T(8,128)(2,1)S(1)}, u32[]{:S(2)}, u32[]{:S(2)}) collective-permute-start(bf16[1024,512]{1,0:T(8,128)(2,1)S(1)} %pad_maximum_fusion.6), channel_id=1, source_target_pairs={{0,4},{4,0},{8,12},{12,8},{16,20},{20,16},{24,28},{28,24},{32,36},... | collective-permute-start | bytes 3145736 | tf_op jit(solution)/shard_map/ppermute | solution.py:110
  613.1 63.3 %collective-permute-start.128 = (bf16[512,3328]{1,0:T(8,128)(2,1)S(1)}, bf16[512,3328]{1,0:T(8,128)(2,1)S(1)}, u32[]{:S(2)}, u32[]{:S(2)}) collective-permute-start(bf16[512,3328]{1,0:T(8,128)(2,1)S(1)} %get-tuple-element.82), channel_id=1, source_target_pairs={{0,4},{4,0},{8,12},{12,8},{16,20},{20,16},{24,28},{28,24},{32,36},... | collective-permute-start | bytes 10223624 | tf_op jit(solution)/shard_map/ppermute | solution.py:110
  675.5 85.2 %collective-permute-start.164 = (bf16[512,2816]{1,0:T(8,128)(2,1)}, bf16[512,2816]{1,0:T(8,128)(2,1)}, u32[]{:S(2)}, u32[]{:S(2)}) collective-permute-start(bf16[512,2816]{1,0:T(8,128)(2,1)} %get-tuple-element.86), channel_id=1, source_target_pairs={{0,4},{4,0},{8,12},{12,8},{16,20},{20,16},{24,28},{28,24},{32,36},... | collective-permute-start | bytes 8650760 | tf_op jit(solution)/shard_map/ppermute | solution.py:110
  683.6 26.7 %collective-permute-start.136 = (bf16[4,32,1664]{2,1,0:T(8,128)(2,1)S(1)}, bf16[4,32,1664]{2,1,0:T(8,128)(2,1)S(1)}, u32[]{:S(2)}, u32[]{:S(2)}) collective-permute-start(bf16[4,32,1664]{2,1,0:T(8,128)(2,1)S(1)} %get-tuple-element.314), channel_id=1, source_target_pairs={{0,64},{4,68},{8,72},{12,76},{16,80},{20,84},{24,88},{28,92},{32,9... | collective-permute-start | bytes 1277960 | tf_op jit(solution)/shard_map/ppermute | solution.py:224
  688.0 22.4 %collective-permute-start.137 = (bf16[4,32,1664]{2,1,0:T(8,128)(2,1)S(1)}, bf16[4,32,1664]{2,1,0:T(8,128)(2,1)S(1)}, u32[]{:S(2)}, u32[]{:S(2)}) collective-permute-start(bf16[4,32,1664]{2,1,0:T(8,128)(2,1)S(1)} %get-tuple-element.316), channel_id=1, source_target_pairs={{0,32},{4,36},{8,40},{12,44},{16,48},{20,52},{24,56},{28,60},{32,6... | collective-permute-start | bytes 1277960 | tf_op jit(solution)/shard_map/ppermute | solution.py:224
  692.8 20.9 %collective-permute-start.138 = (bf16[4,32,1664]{2,1,0:T(8,128)(2,1)S(1)}, bf16[4,32,1664]{2,1,0:T(8,128)(2,1)S(1)}, u32[]{:S(2)}, u32[]{:S(2)}) collective-permute-start(bf16[4,32,1664]{2,1,0:T(8,128)(2,1)S(1)} %get-tuple-element.315), channel_id=1, source_target_pairs={{0,96},{4,100},{8,104},{12,108},{16,112},{20,116},{24,120},{28,124... | collective-permute-start | bytes 1277960 | tf_op jit(solution)/shard_map/ppermute | solution.py:224
  695.7 19.5 %collective-permute-start.133 = (bf16[4,32,1664]{2,1,0:T(8,128)(2,1)S(1)}, bf16[4,32,1664]{2,1,0:T(8,128)(2,1)S(1)}, u32[]{:S(2)}, u32[]{:S(2)}) collective-permute-start(bf16[4,32,1664]{2,1,0:T(8,128)(2,1)S(1)} %get-tuple-element.317), channel_id=1, source_target_pairs={{0,16},{4,20},{8,24},{12,28},{16,0},{20,4},{24,8},{28,12},{32,48},... | collective-permute-start | bytes 1277960 | tf_op jit(solution)/shard_map/ppermute | solution.py:224
  713.7 23.6 %collective-permute-start.132 = (bf16[512,512]{1,0:T(8,128)(2,1)S(1)}, bf16[512,512]{1,0:T(8,128)(2,1)S(1)}, u32[]{:S(2)}, u32[]{:S(2)}) collective-permute-start(bf16[512,512]{1,0:T(8,128)(2,1)S(1)} %pad_maximum_fusion.15), channel_id=1, source_target_pairs={{4,0},{8,4},{12,8},{20,16},{24,20},{28,24},{36,32},{40,36},{44,40}... | collective-permute-start | bytes 1572872 | tf_op jit(solution)/shard_map/ppermute | solution.py:693
  752.3 19.3 %collective-permute-start.143 = (bf16[128,1024]{1,0:T(8,128)(2,1)S(1)}, bf16[128,1024]{1,0:T(8,128)(2,1)}, u32[]{:S(2)}, u32[]{:S(2)}) collective-permute-start(bf16[128,1024]{1,0:T(8,128)(2,1)S(1)} %get-tuple-element.236), channel_id=1, source_target_pairs={{2,0},{3,1},{0,2},{1,3},{6,4},{7,5},{4,6},{5,7},{10,8},{11,9},{8,1... | collective-permute-start | bytes 786440 | tf_op jit(solution)/shard_map/ppermute | solution.py:69
  753.1 22.3 %collective-permute-start.144 = (bf16[128,1024]{1,0:T(8,128)(2,1)S(1)}, bf16[128,1024]{1,0:T(8,128)(2,1)}, u32[]{:S(2)}, u32[]{:S(2)}) collective-permute-start(bf16[128,1024]{1,0:T(8,128)(2,1)S(1)} %get-tuple-element.236), channel_id=1, source_target_pairs={{3,0},{0,1},{1,2},{2,3},{7,4},{4,5},{5,6},{6,7},{11,8},{8,9},{9,10... | collective-permute-start | bytes 786440 | tf_op jit(solution)/shard_map/ppermute | solution.py:69
  760.5 45.8 %collective-permute-start.148 = (bf16[512,1280]{1,0:T(8,128)(2,1)S(1)}, bf16[512,1280]{1,0:T(8,128)(2,1)S(1)}, u32[]{:S(2)}, u32[]{:S(2)}) collective-permute-start(bf16[512,1280]{1,0:T(8,128)(2,1)S(1)} %get-tuple-element.93), channel_id=1, source_target_pairs={{0,4},{4,0},{8,12},{12,8},{16,20},{20,16},{24,28},{28,24},{32,36},... | collective-permute-start | bytes 3932168 | tf_op jit(solution)/shard_map/ppermute | solution.py:110
  763.6 19.2 %collective-permute-start.165 = (bf16[4,32,1408]{2,1,0:T(8,128)(2,1)S(1)}, bf16[4,32,1408]{2,1,0:T(8,128)(2,1)S(1)}, u32[]{:S(2)}, u32[]{:S(2)}) collective-permute-start(bf16[4,32,1408]{2,1,0:T(8,128)(2,1)S(1)} %get-tuple-element.320), channel_id=1, source_target_pairs={{0,16},{4,20},{8,24},{12,28},{16,0},{20,4},{24,8},{28,12},{32,48},... | collective-permute-start | bytes 1081352 | tf_op jit(solution)/shard_map/ppermute | solution.py:224
  765.3 19.6 %collective-permute-start.166 = (bf16[4,32,1408]{2,1,0:T(8,128)(2,1)S(1)}, bf16[4,32,1408]{2,1,0:T(8,128)(2,1)S(1)}, u32[]{:S(2)}, u32[]{:S(2)}) collective-permute-start(bf16[4,32,1408]{2,1,0:T(8,128)(2,1)S(1)} %get-tuple-element.321), channel_id=1, source_target_pairs={{0,8},{4,12},{8,16},{12,20},{16,24},{20,28},{24,0},{28,4},{32,40},... | collective-permute-start | bytes 1081352 | tf_op jit(solution)/shard_map/ppermute | solution.py:224
  (484 other events, 4213.5 us)

commit v4 on v3

--- a/solution.py
+++ b/solution.py
@@ -56,12 +56,17 @@
     spread = jnp.mean(centred * centred, axis=-1, keepdims=True)
     scaled = centred * lax.rsqrt(spread + EPSILON)
     inner = grad * weights
-    back = lax.rsqrt(spread + EPSILON) * (
+    return lax.rsqrt(spread + EPSILON) * (
         inner
         - jnp.mean(inner, axis=-1, keepdims=True)
         - scaled * jnp.mean(inner * scaled, axis=-1, keepdims=True)
     )
-    return back, jnp.sum(grad * scaled, axis=0)
+
+
+def gain_grad(weights, grads, gain, first):
+    rows = lax.dynamic_slice_in_dim(weights, first, grads.shape[0], 0).astype(HIGH)
+    gains = lax.dynamic_slice_in_dim(gain, first, grads.shape[0], 0)
+    return jnp.sum(rows * grads, axis=1) / gains
 
 
 def tp_from(array, k):
@@ -146,7 +151,7 @@
             specs.append(pl.BlockSpec((piece.shape[0], block), lambda i: (0, i)))
         for piece in latter:
             operands.append(piece)
-            specs.append(pl.BlockSpec(piece.shape, lambda i: (0, 0)))
+            specs.append(pl.BlockSpec(piece.shape, lambda i: (0, 0), pipeline_mode=pl.Buffered(1)))
 
     def kernel(core_ref, *refs):
         mine_ref, other_ref = refs[-2:]
@@ -181,7 +186,7 @@
         grid=(depth // block,),
         in_specs=[pl.BlockSpec(memory_space=pltpu.SMEM)] + specs,
         out_specs=(out_spec, out_spec),
-        compiler_params=pltpu.CompilerParams(vmem_limit_bytes=32 * 1024 * 1024),
+        compiler_params=pltpu.CompilerParams(vmem_limit_bytes=20 * 1024 * 1024),
         cost_estimate=pl.CostEstimate(
             flops=2 * rows * depth * total,
             bytes_accessed=2 * (rows * (depth + total) + depth * total),
@@ -222,24 +227,40 @@
         for k in far_first(size):
             sent = lax.dynamic_index_in_dim(array, (at + k) % size, dim, False)
             total = total + lax.ppermute(sent, "seq", self.pairs(*step(k))).astype(HIGH)
-        return total.astype(LOW)
-
-    def cores(self):
+        return total
+
+    def cores(self, after):
         width = self.mine.shape[1]
-        array = (self.mine.astype(HIGH) + swap(self.other, 1).astype(HIGH)).astype(LOW)
+        sent = swap(tied(self.other, after), 1)
+        array = (self.mine.astype(HIGH) + sent.astype(HIGH)).astype(LOW)
         array = array.reshape(self.x_size, self.z_size, -1, width)
         half = width // 256 * 128
         self.one, self.two = array[..., :half], array[..., half:]
-        return self.one, self.two
-
-    def first(self):
-        self.one, self.two = self.over_z(self.one, 1), self.over_x(self.two, 0)
-        return self.one, self.two
-
-    def second(self):
-        one, two = self.over_x(self.one, 0), self.over_z(self.two, 0)
-        self.total = jnp.concatenate([one, two], axis=1)
-        return self.total
+        return array
+
+    def one_first(self, after):
+        self.one = self.over_z(tied(self.one, after), 1).astype(LOW)
+        return self.one
+
+    def two_first(self, after):
+        self.two = self.over_x(tied(self.two, after), 0).astype(LOW)
+        return self.two
+
+    def one_last(self, after):
+        self.one = self.over_x(tied(self.one, after), 0)
+        return self.one
+
+    def two_last(self, after):
+        self.two = self.over_z(tied(self.two, after), 0)
+        return self.two
+
+    def columns(self, at, count):
+        half = self.one.shape[1]
+        if at + count <= half:
+            return self.one[:, at : at + count]
+        if at >= half:
+            return self.two[:, at - half : at - half + count]
+        return jnp.concatenate([self.one[:, at:], self.two[:, : at + count - half]], axis=1)
 
 
 def heads_of(matrix):
@@ -430,6 +451,23 @@
     pair_prev = jnp.where(position % 2 == 1, pairs_all[1], pairs_all[3])
     pairs_stack = jnp.stack(pairs_all)
 
+    def state_rest(incoming, state_heads, meanwhile=lambda heads: ()):
+        update = tp_total(plain_dot(state_heads, out_state_flat))
+        update = tied(update, *meanwhile(state_heads))
+        mid_state = keep_one * incoming + (1.0 - keep_one) * update
+        state_ffn_in = layer_norm(mid_state, norm_sffn).astype(LOW)
+        state_hidden = plain_dot(state_ffn_in, up_state)
+        state_active = gelu_exact(state_hidden).astype(LOW)
+        state_mlp = tp_total(plain_dot(state_active, down_state))
+        slab = (keep_two * mid_state + (1.0 - keep_two) * state_mlp).astype(LOW)
+        return slab, (update, mid_state, state_ffn_in, state_hidden, state_active, state_mlp)
+
+    own_done = []
+
+    def own_attention(after):
+        own_done.extend(band_attend(tied(queries, after), pair, pair_prev, below, starts_here))
+        return own_done[:1]
+
     state_slab = init_slab
     turns = []
     states_out = []
@@ -439,42 +477,22 @@
         if turn:
             started = state_start(state_slab)
         state_normed, state_queries, state_pair, own, own_logs = started
+        if turn == CHAIN - 1:
+            turns.append((incoming, state_normed, state_queries, state_pair, own))
+            break
         token_pair = choose(pairs_stack, position ^ turn)
         cross, cross_logs = full_attend(
             state_queries, token_pair[:, :width], token_pair[:, width:]
         )
         state_heads = jnp.concatenate([own, cross], axis=1)
-        update = tp_total(plain_dot(state_heads, out_state_flat))
+        first = (incoming, state_normed, state_queries, state_pair)
         if turn == 1:
-            own_heads, own_token_logs = band_attend(
-                tied(queries, state_heads), pair, pair_prev, below, starts_here
-            )
-            update = tied(update, own_heads)
-        mid_state = keep_one * incoming + (1.0 - keep_one) * update
-        state_ffn_in = layer_norm(mid_state, norm_sffn).astype(LOW)
-        state_hidden = plain_dot(state_ffn_in, up_state)
-        state_active = gelu_exact(state_hidden).astype(LOW)
-        state_mlp = tp_total(plain_dot(state_active, down_state))
-        state_slab = (keep_two * mid_state + (1.0 - keep_two) * state_mlp).astype(LOW)
+            state_slab, rest = state_rest(incoming, state_heads, own_attention)
+        else:
+            state_slab, rest = state_rest(incoming, state_heads)
         states_out.append(own_rows(state_slab))
-        turns.append(
-            (
-                incoming,
-                state_normed,
-                state_queries,
-                state_pair,
-                token_pair,
-                cross_logs,
-                own_logs,
-                state_heads,
-                update,
-                mid_state,
-                state_ffn_in,
-                state_hidden,
-                state_active,
-                state_mlp,
-            )
-        )
+        turns.append(first + (token_pair, cross_logs, own_logs, state_heads) + rest)
+    own_heads, own_token_logs = own_done
     my_state_pair = turns[0][3]
     for turn in range(1, CHAIN):
         my_state_pair = jnp.where(position == turn, turns[turn][3], my_state_pair)
@@ -495,10 +513,9 @@
     grad_hidden = [
         gelu_slope(part, grad).astype(LOW) for part, grad in zip(hidden, grad_active)
     ]
+    active = [gelu_exact(part).astype(LOW) for part in hidden]
     grad_ffn_in = tp_scatter([dot_second(part, up_tok) for part in grad_hidden])
-    active = [gelu_exact(part).astype(LOW) for part in hidden]
-    back_mixed, grad_norm_ffn = norm_back(mixed_one, norm_ffn, grad_ffn_in)
-    grad_mixed = cotangents[0].astype(HIGH) + back_mixed
+    grad_mixed = cotangents[0].astype(HIGH) + norm_back(mixed_one, norm_ffn, grad_ffn_in)
     grad_proj_pieces = tp_gather(grad_mixed.astype(LOW))
     grad_proj = jnp.concatenate(grad_proj_pieces)
     grad_heads = dot_second(grad_proj, out_tok_flat).astype(LOW)
@@ -531,39 +548,29 @@
         returned = lax.ppermute(prev_grad.astype(LOW), "seq", homeward)
         return query_grad + cross_query_grad, pair_grad + returned.astype(HIGH)
 
-    def states_between():
-        states_stack = jnp.stack(states_out)
-        pieces = [choose(states_stack, position)]
-        pieces += [swap(choose(states_stack, position ^ k), k) for k in range(1, CHAIN)]
-        pieces = jnp.stack(pieces)
-        return jnp.stack([choose(pieces, position ^ q) for q in range(CHAIN)])
-
     init_grad = jnp.zeros((thin_rows, model_width), HIGH)
-    bias_one = bias_two = grad_norm_sffn = grad_norm_state = jnp.zeros((model_width,), HIGH)
+    bias_one = bias_two = jnp.zeros((model_width,), HIGH)
     kept_qkv, kept_rest = [], []
     token_pair_grads = [None] * CHAIN
     grad_state = None
     for turn in reversed(range(CHAIN)):
-        (
-            incoming,
-            state_normed,
-            state_queries,
-            state_pair,
-            token_pair,
-            cross_logs,
-            own_logs,
-            state_heads,
-            update,
-            mid_state,
-            state_ffn_in,
-            state_hidden,
-            state_active,
-            state_mlp,
-        ) = turns[turn]
+        incoming, state_normed, state_queries, state_pair = turns[turn][:4]
         pair_total = choose(cross_pieces, position ^ turn)
         if turn == CHAIN - 1:
             query_total = jnp.zeros((slab_rows, width), HIGH)
         else:
+            (
+                token_pair,
+                cross_logs,
+                own_logs,
+                state_heads,
+                update,
+                mid_state,
+                state_ffn_in,
+                state_hidden,
+                state_active,
+                state_mlp,
+            ) = turns[turn][4:]
             grad_mlp = ((1.0 - keep_two) * grad_state).astype(LOW)
             bias_two = bias_two + jnp.sum(grad_state * (mid_state - state_mlp), axis=0)
             grad_state_hidden = gelu_slope(
@@ -582,10 +589,11 @@
                 )
                 grad_sffn_in = tied(grad_sffn_in, token_grads.other)
             if turn == CHAIN - 3:
-                grad_sffn_in = tied(grad_sffn_in, *token_grads.first())
-            back_mid, norm_part = norm_back(mid_state, norm_sffn, grad_sffn_in)
-            grad_norm_sffn = grad_norm_sffn + norm_part
-            grad_mid = keep_two * grad_state + back_mid
+                step = token_grads.one_first(grad_state_hidden)
+            if turn == CHAIN - 4:
+                grad_sffn_in = tied(grad_sffn_in, step)
+                step = token_grads.one_last(grad_state_hidden)
+            grad_mid = keep_two * grad_state + norm_back(mid_state, norm_sffn, grad_sffn_in)
             bias_one = bias_one + jnp.sum(grad_mid * (incoming - update), axis=0)
             grad_update = ((1.0 - keep_one) * grad_mid).astype(LOW)
             grad_state_heads = dot_second(grad_update, out_state_flat).astype(LOW)
@@ -608,18 +616,11 @@
             )
             token_pair_grads[turn] = jnp.concatenate([cross_k, cross_v], axis=1)
             query_total = own_q + cross_q
-            if turn == CHAIN - 3:
-                slabs = states_between()
-                pair_total = tied(pair_total, slabs)
-            if turn == CHAIN - 4:
-                by_tp = turned(jnp.stack(tp_gather(slabs)), (n_tp - tp_index) % n_tp)
-                state_rows_out = jnp.transpose(by_tp, (1, 0, 2, 3)).reshape(
-                    state_rows, model_width
-                )
-                pair_total = tied(pair_total, state_rows_out)
             kept_rest.append(
                 (state_heads, grad_update, state_ffn_in, grad_state_hidden, state_active, grad_mlp)
             )
+        if turn == CHAIN - 3:
+            pair_total = tied(pair_total, step)
         grad_state_qkv = jnp.concatenate([query_total, pair_total], axis=1).astype(LOW)
         kept_qkv.append((state_normed, grad_state_qkv))
         grad_state_normed = tp_total(dot_second(grad_state_qkv, qkv_state_flat))
@@ -627,28 +628,22 @@
             query_grad, pair_grad = own_back()
             grad_state_normed = tied(grad_state_normed, query_grad)
         if turn == CHAIN - 2:
-            grad_state_normed = tied(grad_state_normed, *token_grads.cores())
+            grad_state_normed = tied(grad_state_normed, token_grads.cores(grad_state_qkv))
         if turn == CHAIN - 3:
-            grad_state_normed = tied(grad_state_normed, token_grads.second())
-        back_state, norm_part = norm_back(incoming, norm_state, grad_state_normed)
-        grad_norm_state = grad_norm_state + norm_part
-        grad_incoming = back_state
+            step = token_grads.two_first(grad_state_qkv)
+        grad_incoming = norm_back(incoming, norm_state, grad_state_normed)
         if grad_state is not None:
-            grad_incoming = keep_one * grad_mid + back_state
+            grad_incoming = keep_one * grad_mid + grad_incoming
         init_grad = init_grad + jnp.where(flags[turn], own_rows(grad_incoming), 0.0)
         grad_state = jnp.where(flags[turn], 0.0, grad_incoming)
     bias_one = bias_one * keep_one * (1.0 - keep_one) / n_tp
     bias_two = bias_two * keep_two * (1.0 - keep_two) / n_tp
-    grad_norm_sffn = grad_norm_sffn / n_tp
-    grad_norm_state = grad_norm_state / n_tp
-    sum_token = token_grads.total
 
     token_pair_grads[CHAIN - 1] = jnp.zeros_like(token_pair_grads[0])
     pair_stack = jnp.stack(token_pair_grads)
     pair_grad = pair_grad + pos_scatter([choose(pair_stack, position ^ k) for k in range(CHAIN)])
-    grad_qkv = jnp.concatenate([query_grad, pair_grad], axis=1).astype(LOW)
-    grad_normed = tp_scatter(
-        [dot_second(part, qkv_tok_flat) for part in split_rows(grad_qkv, n_tp)]
+    layer_output = mixed_one + tp_scatter(
+        [plain_dot(part, down_tok) for part in tied(tuple(active), pair_stack)]
     )
     qkv_parts = list(zip(*kept_qkv))
     rest_parts = list(zip(*kept_rest))
@@ -662,129 +657,149 @@
             ]
         )
     )
-    grad_normed = tied(grad_normed, state_grads.other)
-    back_tokens, grad_norm_tok = norm_back(layer_one, norm_tok, grad_normed)
-    grad_layer_one = grad_mixed + back_tokens
-
+    pair_grad = tied(pair_grad, step, layer_output, state_grads.other)
+    grad_qkv = jnp.concatenate([query_grad, pair_grad], axis=1).astype(LOW)
+    grad_normed = tp_scatter(
+        [dot_second(part, qkv_tok_flat) for part in split_rows(grad_qkv, n_tp)]
+    )
+    grad_normed = tied(grad_normed, state_grads.cores(grad_qkv))
+    grad_layer_one = grad_mixed + norm_back(layer_one, norm_tok, grad_normed)
+
+    step = token_grads.two_last(grad_layer_one)
     grad_win_out = tp_gather(grad_layer_one.astype(LOW))
     grad_win_hidden = [
         gelu_slope(part, dot_second(grad, down_win)).astype(LOW)
         for part, grad in zip(win_hidden, grad_win_out)
     ]
     grad_win_ffn_in = tp_scatter([dot_second(part, up_win) for part in grad_win_hidden])
-    grad_win_ffn_in = tied(grad_win_ffn_in, *state_grads.cores())
-    back_win, grad_norm_wffn = norm_back(win_mixed, norm_wffn, grad_win_ffn_in)
-    grad_win_mixed = grad_layer_one + back_win
-    grad_win_pieces = tp_gather(grad_win_mixed.astype(LOW))
+    step = state_grads.one_first(step), state_grads.two_first(step)
+
+    small_rows = jnp.concatenate(
+        [init_grad, jnp.stack([bias_one, bias_two]), jnp.zeros((14, model_width), HIGH)]
+    ).astype(LOW)
+    row_of = lax.broadcasted_iota(jnp.int32, (small_rows.shape[0], 256), 0)
+    column_of = lax.broadcasted_iota(jnp.int32, (small_rows.shape[0], 256), 1)
+    column_for = jnp.where(
+        row_of < thin_rows,
+        position * thin_rows + row_of,
+        (CHAIN - 1) * thin_rows + row_of,
+    )
+    selector = (column_of == column_for).astype(LOW)
     middle_grads = SeqSum(
         weight_grads(
             [
                 (normed_pieces, [grad_qkv]),
                 (win_ffn_in, grad_win_hidden),
                 (grad_win_out, win_active),
+                ([small_rows], [selector]),
             ]
         )
     )
-    grad_win_proj = jnp.concatenate(tied(tuple(grad_win_pieces), middle_grads.other))
+    grad_win_ffn_in = tied(grad_win_ffn_in, *step, middle_grads.other)
+    grad_win_mixed = grad_layer_one + norm_back(win_mixed, norm_wffn, grad_win_ffn_in)
+    grad_win_pieces = tp_gather(grad_win_mixed.astype(LOW))
+    step = middle_grads.cores(grad_win_mixed), state_grads.one_last(grad_win_mixed)
+    grad_win_proj = tied(jnp.concatenate(grad_win_pieces), *step)
     grad_win_heads = dot_second(grad_win_proj, out_win).astype(LOW)
     win_query_grad, win_pair_grad, win_prev_grad = band_attend_back(
         win_queries, win_pair, win_prev, below, starts_here, win_logs, grad_win_heads
     )
+    step = (
+        state_grads.two_last(grad_win_heads),
+        middle_grads.one_first(grad_win_heads),
+        middle_grads.two_first(grad_win_heads),
+    )
     win_returned = lax.ppermute(win_prev_grad.astype(LOW), "seq", homeward)
-    win_pair_grad = win_pair_grad + tied(win_returned, *state_grads.first()).astype(HIGH)
+    win_pair_grad = win_pair_grad + tied(win_returned, *step).astype(HIGH)
     grad_win_qkv = jnp.concatenate([win_query_grad, win_pair_grad], axis=1).astype(LOW)
-    sum_state = state_grads.second()
-    middle_grads.cores()
+    last_grads = SeqSum(
+        weight_grads([([win_normed], [grad_win_qkv]), ([grad_win_proj], [win_heads])])
+    )
     grad_win_normed = tp_scatter(
         [dot_second(part, qkv_win_flat) for part in split_rows(grad_win_qkv, n_tp)]
     )
-    back_input, grad_norm_win = norm_back(own_input, norm_win, grad_win_normed)
+    step = last_grads.cores(grad_win_qkv)
+    step = middle_grads.one_last(step), middle_grads.two_last(step)
+    last_grads.one_first(step[0])
+    last_grads.two_first(step[1])
+    last_grads.one_last(last_grads.two)
+    last_grads.two_last(last_grads.two)
+    back_input = norm_back(own_input, norm_win, grad_win_normed)
     grad_token_rows = natural(tp_gather((grad_win_mixed + back_input).astype(LOW)))
-
-    layer_output = mixed_one + tp_scatter([plain_dot(part, down_tok) for part in active])
-    output_rows = natural(tp_gather(layer_output.astype(LOW)))
-
+    output_rows = natural(tp_gather(tied(layer_output.astype(LOW), grad_win_heads)))
+
+    incoming, _, state_queries, _, own = turns[CHAIN - 1]
+    token_pair = choose(tied(pairs_stack, grad_win_heads), position ^ (CHAIN - 1))
+    cross, _ = full_attend(state_queries, token_pair[:, :width], token_pair[:, width:])
+    state_slab, _ = state_rest(incoming, jnp.concatenate([own, cross], axis=1))
+    states_out.append(own_rows(state_slab))
+    states_stack = jnp.stack(states_out)
+    pieces = [choose(states_stack, position)]
+    pieces += [swap(choose(states_stack, position ^ k), k) for k in range(1, CHAIN)]
+    pieces = jnp.stack(pieces)
+    slabs = jnp.stack([choose(pieces, position ^ q) for q in range(CHAIN)])
+    by_tp = turned(jnp.stack(tp_gather(slabs)), (n_tp - tp_index) % n_tp)
+    state_rows_out = jnp.transpose(by_tp, (1, 0, 2, 3)).reshape(state_rows, model_width)
+
+    own_columns = model_width // lax.axis_size("seq")
+    inner_width = up_tok.shape[1]
+    sum_qkv_win = last_grads.columns(0, 3 * width)
+    sum_qkv_tok = middle_grads.columns(0, 3 * width)
+    sum_qkv_state = state_grads.columns(0, 3 * width)
+    sum_up_win = middle_grads.columns(3 * width, inner_width)
+    sum_up_tok = token_grads.columns(0, inner_width)
+    sum_up_state = state_grads.columns(5 * width, inner_width)
+    small_sums = middle_grads.columns(3 * width + 2 * inner_width, CHAIN * thin_rows + 2)
+    first_row = seq_index * own_columns
     vectors = [
-        grad_norm_win,
-        grad_norm_wffn,
-        grad_norm_tok,
-        grad_norm_ffn,
-        grad_norm_state,
-        grad_norm_sffn,
-        bias_one,
-        bias_two,
+        gain_grad(qkv_win_flat, sum_qkv_win, norm_win, first_row),
+        gain_grad(up_win, sum_up_win, norm_wffn, first_row),
+        gain_grad(qkv_tok_flat, sum_qkv_tok, norm_tok, first_row),
+        gain_grad(up_tok, sum_up_tok, norm_ffn, first_row),
+        gain_grad(qkv_state_flat, sum_qkv_state, norm_state, first_row),
+        gain_grad(up_state, sum_up_state, norm_sffn, first_row),
     ]
-    small_rows = jnp.concatenate(
-        [init_grad, jnp.stack(vectors), jnp.zeros((8, model_width), HIGH)]
-    ).astype(LOW)
-    small_width = CHAIN * thin_rows + len(vectors)
-    small_padded = small_width + -small_width % 256
-    row_of = lax.broadcasted_iota(jnp.int32, (small_rows.shape[0], small_padded), 0)
-    column_of = lax.broadcasted_iota(jnp.int32, (small_rows.shape[0], small_padded), 1)
-    column_for = jnp.where(
-        row_of < thin_rows,
-        position * thin_rows + row_of,
-        (CHAIN - 1) * thin_rows + row_of,
-    )
-    selector = (column_of == column_for).astype(LOW)
-    last_grads = SeqSum(
-        weight_grads(
-            [
-                ([win_normed], [grad_win_qkv]),
-                ([grad_win_proj], [win_heads]),
-                ([small_rows], [selector]),
-            ]
-        )
-    )
-    middle_grads.first()
-    sum_middle = middle_grads.second()
-    last_grads.cores()
-    last_grads.first()
-    sum_last = last_grads.second()
-    own_columns = model_width // lax.axis_size("seq")
-    small_sums = tp_gather(sum_last[:, 4 * width : 4 * width + small_width])
+    small_sums = jnp.concatenate([small_sums, jnp.stack(vectors, axis=1)], axis=1)
+    small_sums = tp_gather(small_sums)
     init_part = turned(
         jnp.stack([part[:, : CHAIN * thin_rows] for part in small_sums]),
         (n_tp - tp_index) % n_tp,
     ).reshape(n_tp, own_columns, CHAIN, thin_rows)
     sum_init = jnp.transpose(init_part, (2, 0, 3, 1)).reshape(state_rows, own_columns)
-    vector_sums = sum(part[:, CHAIN * thin_rows :].astype(HIGH) for part in small_sums)
-
-    def columns(sums, at, count):
-        return sums[:, at : at + count].astype(HIGH)
-
-    def qkv_of(sums, at):
-        return columns(sums, at, 3 * width).reshape(own_columns, 3, width)
-
-    def out_of(sums, at):
-        return columns(sums, at, 2 * width).T.reshape(2, width, own_columns)
-
-    inner_width = up_tok.shape[1]
+    vector_sums = sum(part[:, CHAIN * thin_rows :] for part in small_sums)
+
+    def qkv_of(columns):
+        return columns.reshape(own_columns, 3, width)
+
+    def out_of(columns):
+        return columns.T.reshape(2, width, own_columns)
+
     return (
         output_rows,
         state_rows_out,
         grad_token_rows,
-        vector_sums[:, 0],
-        qkv_of(sum_last, 0),
-        columns(sum_last, 3 * width, width).T,
-        vector_sums[:, 1],
-        columns(sum_middle, 3 * width, inner_width),
-        columns(sum_middle, 3 * width + inner_width, inner_width).T,
         vector_sums[:, 2],
-        qkv_of(sum_middle, 0),
-        out_of(sum_token, 2 * inner_width),
+        qkv_of(sum_qkv_win),
+        last_grads.columns(3 * width, width).T,
         vector_sums[:, 3],
-        columns(sum_token, 0, inner_width),
-        columns(sum_token, inner_width, inner_width).T,
+        sum_up_win,
+        middle_grads.columns(3 * width + inner_width, inner_width).T,
         vector_sums[:, 4],
-        qkv_of(sum_state, 0),
-        out_of(sum_state, 3 * width),
-        vector_sums[:, 6:8].T,
+        qkv_of(sum_qkv_tok),
+        out_of(token_grads.columns(2 * inner_width, 2 * width)),
         vector_sums[:, 5],
-        columns(sum_state, 5 * width, inner_width),
-        columns(sum_state, 5 * width + inner_width, inner_width).T,
-        sum_init.astype(HIGH),
-    )
+        sum_up_tok,
+        token_grads.columns(inner_width, inner_width).T,
+        vector_sums[:, 6],
+        qkv_of(sum_qkv_state),
+        out_of(state_grads.columns(3 * width, 2 * width)),
+        vector_sums[:, 0:2].T,
+        vector_sums[:, 7],
+        sum_up_state,
+        state_grads.columns(5 * width + inner_width, inner_width).T,
+        sum_init,
+    )
+
 
 def solution(mesh):
     placed = (

time: 853 us -> 992 us (1.16)
  local copies, waits for them, and re-layouts: 63.9 us -> 117 us
  waiting for transfers between devices: 299 us -> 339 us
  other arithmetic: 79.8 us -> 111 us
  matrix products: 134 us -> 158 us
  starting transfers between devices: 240 us -> 230 us
    ppermute x69, waiting for transfers between devices: 145 us -> 195 us  [tp_to(): return lax.ppermute(array, 'tp', [(i, (i + k) % n) for i in range(n)])]
    dynamic_slice x0 -> x9, local copies, waits for them, and re-layouts: none -> 24.7 us  [the longest x8 23.6 us: stage(): sent = lax.dynamic_index_in_dim(array, (at + k) % size, dim, False)]
    convert_element_type x24 -> x15, other arithmetic: 6.41 us -> 22.3 us  [the longest x4 9.1 us: one_first(): self.one = self.over_z(tied(self.one, after), 1).astype(LOW)]
    unnamed x695 -> x455, local copies, waits for them, and re-layouts: 37.4 us -> 22.2 us
    ppermute x0 -> x6, local copies, waits for them, and re-layouts: none -> 14.6 us  [stage(): total = total + lax.ppermute(sent, 'seq', self.pairs(*step(k))).astype(HIGH)]
    ppermute x48, starting transfers between devices: 86.9 us -> 73.6 us  [stage(): total = total + lax.ppermute(sent, 'seq', self.pairs(*step(k))).astype(HIGH)]
    optimization_barrier x0 -> x2, local copies, waits for them, and re-layouts: none -> 13.1 us  [tied(): return lax.optimization_barrier((value,) + others)[0]]
    ppermute x30, waiting for transfers between devices: 70.8 us -> 59.4 us  [tp_from(): return lax.ppermute(array, 'tp', [((i + k) % n, i) for i in range(n)])]
  transfers between devices with their start and end apart: 183 -> 183, of which waited for: 84 -> 87; matrix products, arithmetic and copies ran while one was open for 22% -> 26% of each run, Pallas kernels for 2% -> 2%
where the time goes in v4:
time: 992 us; the launch traced here: 979 us
  waiting for transfers between devices  339 us (34%)
  starting transfers between devices  230 us (23%)
  matrix products  158 us (16%)
  local copies, waits for them, and re-layouts  117 us (12%)
  other arithmetic  111 us (11%)
  Pallas kernels  18 us (2%)
    ppermute x69, waiting for transfers between devices, tp_to(): return lax.ppermute(array, 'tp', [(i, (i + k) % n) for i in range(n)])  195 us
    ppermute x69, starting transfers between devices, tp_to(): return lax.ppermute(array, 'tp', [(i, (i + k) % n) for i in range(n)])  88.7 us
    dot_general x89, matrix products, plain_dot(): return jnp.dot(former, latter, preferred_element_type=HIGH)  73.7 us
    ppermute x48, starting transfers between devices, stage(): total = total + lax.ppermute(sent, 'seq', self.pairs(*step(k))).astype(HIGH)  73.6 us
    dot_general x91, matrix products, dot_second(): lax.dot_general(former, latter, (((1,), (1,)), ((), ())), preferred_eleme...  63.6 us
    ppermute x30, waiting for transfers between devices, tp_from(): return lax.ppermute(array, 'tp', [((i + k) % n, i) for i in range(n)])  59.4 us
    ppermute x33, waiting for transfers between devices, swap(): return lax.ppermute(array, 'seq', [(s, s ^ k) for s in range(n)])  42.9 us
    ppermute x30, starting transfers between devices, tp_from(): return lax.ppermute(array, 'tp', [((i + k) % n, i) for i in range(n)])  42.3 us
  transfers between devices with their start and end apart: 183, of which 87 were waited for; matrix products, arithmetic and copies ran while one was open for 26% of the time, Pallas kernels for 2%

profile of v4, /device:TPU:0, one launch (start us, length us, event | category | flops | bytes accessed | tf_op | source)
XLA Modules:
  0.0 979.4 jit_solution(17093395622301054175)
XLA Ops:
  62.3 8.9 collective-permute-done.6.refs_6_
  121.0 9.8 %collective-permute-done.17 = bf16[512,512]{1,0:T(8,128)(2,1)S(1)} collective-permute-done((bf16[512,512]{1,0:T(8,128)(2,1)S(1)}, bf16[512,512]{1,0:T(8,128)(2,1)S(1)}, u32[]{:S(2)}, u32[]{:S(2)}) %collective-permute-start.17) | collective-permute-done | bytes 524320 | tf_op jit(solution)/shard_map/ppermute | solution.py:115
  143.1 9.3 collective-permute-done.21
  163.0 6.6 collective-permute-done.24
  194.5 7.0 collective-permute-done.29
  209.5 5.5 collective-permute-done.33
  215.0 5.6 collective-permute-done.32
  235.5 5.5 collective-permute-done.39
  240.9 6.5 collective-permute-done.38
  254.8 7.7 collective-permute-done.42
  287.7 5.9 collective-permute-done.46
  304.4 10.6 %collective-permute-done.49.refs_1_ = bf16[128,1024]{1,0:T(8,128)(2,1)S(1)} collective-permute-done((bf16[128,1024]{1,0:T(8,128)(2,1)S(1)}, bf16[128,1024]{1,0:T(8,128)(2,1)S(1)}, u32[]{:S(2)}, u32[]{:S(2)}) %collective-permute-start.49) | collective-permute-done | bytes 262176 | tf_op jit(solution)/shard_map/ppermute | solution.py:74
  327.1 5.8 collective-permute-done.52
  346.3 6.8 collective-permute-done.56.refs_15_
  422.3 5.6 collective-permute-done.71
  427.9 6.7 collective-permute-done.70
  527.0 8.4 collective-permute-done.92
  541.9 5.2 shard_map.399
  547.1 5.9 collective-permute-done.95
  559.5 8.7 collective-permute-done.122
  579.6 5.6 collective-permute-done.103
  585.2 6.0 collective-permute-done.102
  606.9 6.8 copy.849
  650.2 6.4 shard_map.400
  700.4 8.9 collective-permute-done.127
  712.3 5.7 collective-permute-done.129
  765.3 6.3 copy.850
  827.7 7.6 collective-permute-done.149
  856.4 5.2 collective-permute-done.136
  879.8 5.5 collective-permute-done.156
  897.4 10.2 %collective-permute-done.158 = bf16[128,1024]{1,0:T(8,128)(2,1)S(1)} collective-permute-done((bf16[128,1024]{1,0:T(8,128)(2,1)S(1)}, bf16[128,1024]{1,0:T(8,128)(2,1)S(1)}, u32[]{:S(2)}, u32[]{:S(2)}) %collective-permute-start.158) | collective-permute-done | bytes 262176 | tf_op jit(solution)/shard_map/ppermute | solution.py:74
  928.4 7.3 collective-permute-done.167
  (1409 shorter events, 749.3 us)
Async XLA Ops:
  56.5 26.5 %collective-permute-start.8 = (bf16[128,1024]{1,0:T(8,128)(2,1)S(1)}, bf16[128,1024]{1,0:T(8,128)(2,1)S(1)}, u32[]{:S(2)}, u32[]{:S(2)}) collective-permute-start(bf16[128,1024]{1,0:T(8,128)(2,1)S(1)} %multiply_convert_fusion.30.refs_5_), channel_id=1, source_target_pairs={{3,0},{0,1},{1,2},{2,3},{7,4},{4,5},{5,6},{6,7},{11,8},{8,9},{9,10... | collective-permute-start | bytes 786440 | tf_op jit(solution)/shard_map/ppermute | solution.py:74
  299.2 25.0 %collective-permute-start.51 = (bf16[128,1024]{1,0:T(8,128)(2,1)S(1)}, bf16[128,1024]{1,0:T(8,128)(2,1)S(1)}, u32[]{:S(2)}, u32[]{:S(2)}) collective-permute-start(bf16[128,1024]{1,0:T(8,128)(2,1)S(1)} %multiply_convert_fusion.18.refs_0_), channel_id=1, source_target_pairs={{3,0},{0,1},{1,2},{2,3},{7,4},{4,5},{5,6},{6,7},{11,8},{8,9},{9,10... | collective-permute-start | bytes 786440 | tf_op jit(solution)/shard_map/ppermute | solution.py:74
  413.2 21.6 %collective-permute-start.72 = (bf16[512,2560]{1,0:T(8,128)(2,1)S(1)}, bf16[512,2560]{1,0:T(8,128)(2,1)S(1)}, u32[]{:S(2)}, u32[]{:S(2)}) collective-permute-start(bf16[512,2560]{1,0:T(8,128)(2,1)S(1)} %get-tuple-element.99), channel_id=1, source_target_pairs={{0,4},{4,0},{8,12},{12,8},{16,20},{20,16},{24,28},{28,24},{32,36},... | collective-permute-start | bytes 7864328 | tf_op jit(solution)/shard_map/ppermute | solution.py:115
  446.7 22.4 %collective-permute-start.78 = (bf16[4,32,1280]{2,1,0:T(8,128)(2,1)S(1)}, bf16[4,32,1280]{2,1,0:T(8,128)(2,1)S(1)}, u32[]{:S(2)}, u32[]{:S(2)}) collective-permute-start(bf16[4,32,1280]{2,1,0:T(8,128)(2,1)S(1)} %get-tuple-element.418), channel_id=1, source_target_pairs={{0,16},{4,20},{8,24},{12,28},{16,0},{20,4},{24,8},{28,12},{32,48},... | collective-permute-start | bytes 983048 | tf_op jit(solution)/shard_map/ppermute | solution.py:229
  520.1 20.0 %collective-permute-start.94 = (bf16[1024,512]{1,0:T(8,128)(2,1)S(1)}, bf16[1024,512]{1,0:T(8,128)(2,1)S(1)}, u32[]{:S(2)}, u32[]{:S(2)}) collective-permute-start(bf16[1024,512]{1,0:T(8,128)(2,1)S(1)} %pad_maximum_fusion.6), channel_id=1, source_target_pairs={{0,4},{4,0},{8,12},{12,8},{16,20},{20,16},{24,28},{28,24},{32,36},... | collective-permute-start | bytes 3145736 | tf_op jit(solution)/shard_map/ppermute | solution.py:115
  525.7 21.4 %collective-permute-start.93 = (bf16[512,512]{1,0:T(8,128)(2,1)S(1)}, bf16[512,512]{1,0:T(8,128)(2,1)S(1)}, u32[]{:S(2)}, u32[]{:S(2)}) collective-permute-start(bf16[512,512]{1,0:T(8,128)(2,1)S(1)} %copy-done.119), channel_id=1, source_target_pairs={{4,0},{8,4},{12,8},{20,16},{24,20},{28,24},{36,32},{40,36},{44,40}... | collective-permute-start | bytes 1572872 | tf_op jit(solution)/shard_map/ppermute | solution.py:548
  553.5 38.1 %collective-permute-start.104 = (bf16[512,3328]{1,0:T(8,128)(2,1)S(1)}, bf16[512,3328]{1,0:T(8,128)(2,1)S(1)}, u32[]{:S(2)}, u32[]{:S(2)}) collective-permute-start(bf16[512,3328]{1,0:T(8,128)(2,1)S(1)} %get-tuple-element.113), channel_id=1, source_target_pairs={{0,4},{4,0},{8,12},{12,8},{16,20},{20,16},{24,28},{28,24},{32,36},... | collective-permute-start | bytes 10223624 | tf_op jit(solution)/shard_map/ppermute | solution.py:115
  593.9 40.6 %collective-permute-start.109 = (bf16[128,1024]{1,0:T(8,128)(2,1)}, bf16[128,1024]{1,0:T(8,128)(2,1)}, u32[]{:S(2)}, u32[]{:S(2)}) collective-permute-start(bf16[128,1024]{1,0:T(8,128)(2,1)} %get-tuple-element.326.refs_13_), channel_id=1, source_target_pairs={{3,0},{0,1},{1,2},{2,3},{7,4},{4,5},{5,6},{6,7},{11,8},{8,9},{9,10... | collective-permute-start | bytes 786440 | tf_op jit(solution)/shard_map/ppermute | solution.py:74
  594.0 45.2 %collective-permute-start.107 = (bf16[128,1024]{1,0:T(8,128)(2,1)}, bf16[128,1024]{1,0:T(8,128)(2,1)}, u32[]{:S(2)}, u32[]{:S(2)}) collective-permute-start(bf16[128,1024]{1,0:T(8,128)(2,1)} %get-tuple-element.326.refs_13_), channel_id=1, source_target_pairs={{1,0},{2,1},{3,2},{0,3},{5,4},{6,5},{7,6},{4,7},{9,8},{10,9},{11,1... | collective-permute-start | bytes 786440 | tf_op jit(solution)/shard_map/ppermute | solution.py:74
  613.7 32.0 %collective-permute-start.105 = (bf16[128,1024]{1,0:T(8,128)(2,1)}, bf16[128,1024]{1,0:T(8,128)(2,1)}, u32[]{:S(2)}, u32[]{:S(2)}) collective-permute-start(bf16[128,1024]{1,0:T(8,128)(2,1)} %get-tuple-element.326.refs_13_), channel_id=1, source_target_pairs={{2,0},{3,1},{0,2},{1,3},{6,4},{7,5},{4,6},{5,7},{10,8},{11,9},{8,1... | collective-permute-start | bytes 786440 | tf_op jit(solution)/shard_map/ppermute | solution.py:74
  618.3 56.0 %collective-permute-start.117 = (bf16[4,32,1664]{2,1,0:T(8,128)(2,1)}, bf16[4,32,1664]{2,1,0:T(8,128)(2,1)}, u32[]{:S(2)}, u32[]{:S(2)}) collective-permute-start(bf16[4,32,1664]{2,1,0:T(8,128)(2,1)} %get-tuple-element.406), channel_id=1, source_target_pairs={{0,64},{4,68},{8,72},{12,76},{16,80},{20,84},{24,88},{28,92},{32,9... | collective-permute-start | bytes 1277960 | tf_op jit(solution)/shard_map/ppermute | solution.py:229
  621.0 56.4 %collective-permute-start.119 = (bf16[4,32,1664]{2,1,0:T(8,128)(2,1)}, bf16[4,32,1664]{2,1,0:T(8,128)(2,1)}, u32[]{:S(2)}, u32[]{:S(2)}) collective-permute-start(bf16[4,32,1664]{2,1,0:T(8,128)(2,1)} %get-tuple-element.407), channel_id=1, source_target_pairs={{0,96},{4,100},{8,104},{12,108},{16,112},{20,116},{24,120},{28,124... | collective-permute-start | bytes 1277960 | tf_op jit(solution)/shard_map/ppermute | solution.py:229
  634.5 31.2 %collective-permute-start.115 = (bf16[4,32,1664]{2,1,0:T(8,128)(2,1)}, bf16[4,32,1664]{2,1,0:T(8,128)(2,1)}, u32[]{:S(2)}, u32[]{:S(2)}) collective-permute-start(bf16[4,32,1664]{2,1,0:T(8,128)(2,1)} %bitcast.517), channel_id=1, source_target_pairs={{0,8},{4,12},{8,16},{12,20},{16,24},{20,28},{24,0},{28,4},{32,40},... | collective-permute-start | bytes 1277960 | tf_op jit(solution)/shard_map/ppermute | solution.py:229
  639.1 22.8 %collective-permute-start.116 = (bf16[4,32,1664]{2,1,0:T(8,128)(2,1)}, bf16[4,32,1664]{2,1,0:T(8,128)(2,1)}, u32[]{:S(2)}, u32[]{:S(2)}) collective-permute-start(bf16[4,32,1664]{2,1,0:T(8,128)(2,1)} %bitcast.57), channel_id=1, source_target_pairs={{0,24},{4,28},{8,0},{12,4},{16,8},{20,12},{24,16},{28,20},{32,56},... | collective-permute-start | bytes 1277960 | tf_op jit(solution)/shard_map/ppermute | solution.py:229
  685.6 41.9 %collective-permute-start.126 = (bf16[512,3072]{1,0:T(8,128)(2,1)}, bf16[512,3072]{1,0:T(8,128)(2,1)}, u32[]{:S(2)}, u32[]{:S(2)}) collective-permute-start(bf16[512,3072]{1,0:T(8,128)(2,1)} %get-tuple-element.121), channel_id=1, source_target_pairs={{0,4},{4,0},{8,12},{12,8},{16,20},{20,16},{24,28},{28,24},{32,36},... | collective-permute-start | bytes 9437192 | tf_op jit(solution)/shard_map/ppermute | solution.py:115
  696.1 22.0 %collective-permute-start.129 = (bf16[32,1664]{0,1:T(8,128)(2,1)S(1)}, bf16[32,1664]{0,1:T(8,128)(2,1)S(1)}, u32[]{:S(2)}, u32[]{:S(2)}) collective-permute-start(bf16[32,1664]{0,1:T(8,128)(2,1)S(1)} %get-tuple-element.404), channel_id=1, source_target_pairs={{0,96},{4,100},{8,104},{12,108},{16,112},{20,116},{24,120},{28,124... | collective-permute-start | bytes 319496 | tf_op jit(solution)/shard_map/ppermute | solution.py:229
  697.9 22.4 %collective-permute-start.128 = (bf16[32,1664]{0,1:T(8,128)(2,1)S(1)}, bf16[32,1664]{0,1:T(8,128)(2,1)S(1)}, u32[]{:S(2)}, u32[]{:S(2)}) collective-permute-start(bf16[32,1664]{0,1:T(8,128)(2,1)S(1)} %get-tuple-element.405), channel_id=1, source_target_pairs={{0,32},{4,36},{8,40},{12,44},{16,48},{20,52},{24,56},{28,60},{32,6... | collective-permute-start | bytes 319496 | tf_op jit(solution)/shard_map/ppermute | solution.py:229
  699.4 25.7 %collective-permute-start.125 = (bf16[128,1024]{1,0:T(8,128)(2,1)S(1)}, bf16[128,1024]{1,0:T(8,128)(2,1)}, u32[]{:S(2)}, u32[]{:S(2)}) collective-permute-start(bf16[128,1024]{1,0:T(8,128)(2,1)S(1)} %copy-done.110), channel_id=1, source_target_pairs={{3,0},{0,1},{1,2},{2,3},{7,4},{4,5},{5,6},{6,7},{11,8},{8,9},{9,10... | collective-permute-start | bytes 786440 | tf_op jit(solution)/shard_map/ppermute | solution.py:74
  739.4 77.7 %collective-permute-start.132 = (bf16[128,1024]{1,0:T(8,128)(2,1)}, bf16[128,1024]{1,0:T(8,128)(2,1)}, u32[]{:S(2)}, u32[]{:S(2)}) collective-permute-start(bf16[128,1024]{1,0:T(8,128)(2,1)} %add_add_fusion), channel_id=1, source_target_pairs={{3,0},{0,1},{1,2},{2,3},{7,4},{4,5},{5,6},{6,7},{11,8},{8,9},{9,10... | collective-permute-start | bytes 786440 | tf_op jit(solution)/shard_map/ppermute | solution.py:74
  740.8 72.5 %collective-permute-start.131 = (bf16[128,1024]{1,0:T(8,128)(2,1)}, bf16[128,1024]{1,0:T(8,128)(2,1)}, u32[]{:S(2)}, u32[]{:S(2)}) collective-permute-start(bf16[128,1024]{1,0:T(8,128)(2,1)} %add_add_fusion), channel_id=1, source_target_pairs={{2,0},{3,1},{0,2},{1,3},{6,4},{7,5},{4,6},{5,7},{10,8},{11,9},{8,1... | collective-permute-start | bytes 786440 | tf_op jit(solution)/shard_map/ppermute | solution.py:74
  759.5 34.2 %collective-permute-start.146 = (bf16[32,1664]{1,0:T(8,128)(2,1)}, bf16[32,1664]{1,0:T(8,128)(2,1)}, u32[]{:S(2)}, u32[]{:S(2)}) collective-permute-start(bf16[32,1664]{1,0:T(8,128)(2,1)} %get-tuple-element.445), channel_id=1, source_target_pairs={{0,16},{4,20},{8,24},{12,28},{16,0},{20,4},{24,8},{28,12},{32,48},... | collective-permute-start | bytes 319496 | tf_op jit(solution)/shard_map/ppermute | solution.py:229
  762.2 32.2 %collective-permute-start.148 = (bf16[32,1664]{1,0:T(8,128)(2,1)}, bf16[32,1664]{1,0:T(8,128)(2,1)}, u32[]{:S(2)}, u32[]{:S(2)}) collective-permute-start(bf16[32,1664]{1,0:T(8,128)(2,1)} %get-tuple-element.446), channel_id=1, source_target_pairs={{0,24},{4,28},{8,0},{12,4},{16,8},{20,12},{24,16},{28,20},{32,56},... | collective-permute-start | bytes 319496 | tf_op jit(solution)/shard_map/ppermute | solution.py:229
  763.5 32.2 %collective-permute-start.147 = (bf16[32,1664]{1,0:T(8,128)(2,1)}, bf16[32,1664]{1,0:T(8,128)(2,1)}, u32[]{:S(2)}, u32[]{:S(2)}) collective-permute-start(bf16[32,1664]{1,0:T(8,128)(2,1)} %get-tuple-element.447), channel_id=1, source_target_pairs={{0,8},{4,12},{8,16},{12,20},{16,24},{20,28},{24,0},{28,4},{32,40},... | collective-permute-start | bytes 319496 | tf_op jit(solution)/shard_map/ppermute | solution.py:229
  807.1 46.9 %collective-permute-start.145 = (bf16[512,512]{1,0:T(8,128)(2,1)}, bf16[512,512]{1,0:T(8,128)(2,1)}, u32[]{:S(2)}, u32[]{:S(2)}) collective-permute-start(bf16[512,512]{1,0:T(8,128)(2,1)} %pad_maximum_fusion.16), channel_id=1, source_target_pairs={{4,0},{8,4},{12,8},{20,16},{24,20},{28,24},{36,32},{40,36},{44,40}... | collective-permute-start | bytes 1572872 | tf_op jit(solution)/shard_map/ppermute | solution.py:712
  808.4 40.2 %collective-permute-start.152 = (bf16[4,32,1536]{2,1,0:T(8,128)(2,1)}, bf16[4,32,1536]{2,1,0:T(8,128)(2,1)}, u32[]{:S(2)}, u32[]{:S(2)}) collective-permute-start(bf16[4,32,1536]{2,1,0:T(8,128)(2,1)} %get-tuple-element.412), channel_id=1, source_target_pairs={{0,64},{4,68},{8,72},{12,76},{16,80},{20,84},{24,88},{28,92},{32,9... | collective-permute-start | bytes 1179656 | tf_op jit(solution)/shard_map/ppermute | solution.py:229
  812.0 30.4 %collective-permute-start.150 = (bf16[4,32,1536]{2,1,0:T(8,128)(2,1)}, bf16[4,32,1536]{2,1,0:T(8,128)(2,1)}, u32[]{:S(2)}, u32[]{:S(2)}) collective-permute-start(bf16[4,32,1536]{2,1,0:T(8,128)(2,1)} %bitcast.97), channel_id=1, source_target_pairs={{0,8},{4,12},{8,16},{12,20},{16,24},{20,28},{24,0},{28,4},{32,40},... | collective-permute-start | bytes 1179656 | tf_op jit(solution)/shard_map/ppermute | solution.py:229
  813.3 26.8 %collective-permute-start.151 = (bf16[4,32,1536]{2,1,0:T(8,128)(2,1)}, bf16[4,32,1536]{2,1,0:T(8,128)(2,1)}, u32[]{:S(2)}, u32[]{:S(2)}) collective-permute-start(bf16[4,32,1536]{2,1,0:T(8,128)(2,1)} %bitcast.98), channel_id=1, source_target_pairs={{0,24},{4,28},{8,0},{12,4},{16,8},{20,12},{24,16},{28,20},{32,56},... | collective-permute-start | bytes 1179656 | tf_op jit(solution)/shard_map/ppermute | solution.py:229
  874.8 34.0 %collective-permute-start.161 = (bf16[512,1024]{1,0:T(8,128)(2,1)S(1)}, bf16[512,1024]{1,0:T(8,128)(2,1)S(1)}, u32[]{:S(2)}, u32[]{:S(2)}) collective-permute-start(bf16[512,1024]{1,0:T(8,128)(2,1)S(1)} %get-tuple-element.132), channel_id=1, source_target_pairs={{0,4},{4,0},{8,12},{12,8},{16,20},{20,16},{24,28},{28,24},{32,36},... | collective-permute-start | bytes 3145736 | tf_op jit(solution)/shard_map/ppermute | solution.py:115
  915.2 20.6 %collective-permute-start.167 = (bf16[32,1536]{0,1:T(8,128)(2,1)S(1)}, bf16[32,1536]{0,1:T(8,128)(2,1)S(1)}, u32[]{:S(2)}, u32[]{:S(2)}) collective-permute-start(bf16[32,1536]{0,1:T(8,128)(2,1)S(1)} %get-tuple-element.410), channel_id=1, source_target_pairs={{0,96},{4,100},{8,104},{12,108},{16,112},{20,116},{24,120},{28,124... | collective-permute-start | bytes 294920 | tf_op jit(solution)/shard_map/ppermute | solution.py:229
  921.3 29.0 %collective-permute-start.171 = (bf16[4,32,512]{2,1,0:T(8,128)(2,1)}, bf16[4,32,512]{2,1,0:T(8,128)(2,1)}, u32[]{:S(2)}, u32[]{:S(2)}) collective-permute-start(bf16[4,32,512]{2,1,0:T(8,128)(2,1)} %get-tuple-element.433), channel_id=1, source_target_pairs={{0,64},{4,68},{8,72},{12,76},{16,80},{20,84},{24,88},{28,92},{32,9... | collective-permute-start | bytes 393224 | tf_op jit(solution)/shard_map/ppermute | solution.py:229
  923.0 28.1 %collective-permute-start.173 = (bf16[4,32,512]{2,1,0:T(8,128)(2,1)}, bf16[4,32,512]{2,1,0:T(8,128)(2,1)}, u32[]{:S(2)}, u32[]{:S(2)}) collective-permute-start(bf16[4,32,512]{2,1,0:T(8,128)(2,1)} %get-tuple-element.434), channel_id=1, source_target_pairs={{0,96},{4,100},{8,104},{12,108},{16,112},{20,116},{24,120},{28,124... | collective-permute-start | bytes 393224 | tf_op jit(solution)/shard_map/ppermute | solution.py:229
  927.1 24.0 %collective-permute-start.172 = (bf16[4,32,512]{2,1,0:T(8,128)(2,1)}, bf16[4,32,512]{2,1,0:T(8,128)(2,1)}, u32[]{:S(2)}, u32[]{:S(2)}) collective-permute-start(bf16[4,32,512]{2,1,0:T(8,128)(2,1)} %get-tuple-element.435), channel_id=1, source_target_pairs={{0,32},{4,36},{8,40},{12,44},{16,48},{20,52},{24,56},{28,60},{32,6... | collective-permute-start | bytes 393224 | tf_op jit(solution)/shard_map/ppermute | solution.py:229
  (366 other events, 3470.6 us)

commit v5 on v4

--- a/solution.py
+++ b/solution.py
@@ -2,6 +2,7 @@
 import jax.numpy as jnp
 from jax import lax
 from jax.experimental import pallas as pl
+from jax.experimental.layout import Layout, with_layout_constraint
 from jax.experimental.pallas import tpu as pltpu
 from jax.sharding import PartitionSpec as P
 
@@ -46,8 +47,12 @@
     )
 
 
+def row_major(array):
+    return with_layout_constraint(array, Layout(major_to_minor=tuple(range(array.ndim))))
+
+
 def tied(value, *others):
-    return lax.optimization_barrier((value,) + others)[0]
+    return lax.optimization_barrier((value, others))[0]
 
 
 def norm_back(matrix, weights, grad):
@@ -227,16 +232,19 @@
         for k in far_first(size):
             sent = lax.dynamic_index_in_dim(array, (at + k) % size, dim, False)
             total = total + lax.ppermute(sent, "seq", self.pairs(*step(k))).astype(HIGH)
-        return total
+        return row_major(total)
 
     def cores(self, after):
         width = self.mine.shape[1]
         sent = swap(tied(self.other, after), 1)
-        array = (self.mine.astype(HIGH) + sent.astype(HIGH)).astype(LOW)
-        array = array.reshape(self.x_size, self.z_size, -1, width)
         half = width // 256 * 128
-        self.one, self.two = array[..., :half], array[..., half:]
-        return array
+
+        def total(columns):
+            part = self.mine[:, columns].astype(HIGH) + sent[:, columns].astype(HIGH)
+            return part.astype(LOW).reshape(self.x_size, self.z_size, -1, part.shape[1])
+
+        self.one, self.two = total(slice(0, half)), total(slice(half, width))
+        return self.one, self.two
 
     def one_first(self, after):
         self.one = self.over_z(tied(self.one, after), 1).astype(LOW)
@@ -326,7 +334,7 @@
 
 def band_attend_back(queries, pair, pair_prev, below, starts_here, logs, grad_result):
     width = queries.shape[1]
-    grads = ([], [], [], [], [])
+    grads, kept = ([], [], [], [], []), []
     for q, k, v, kp, vp, log, g in zip(
         heads_of(queries),
         heads_of(pair[:, :width]),
@@ -342,16 +350,19 @@
         grad_scores = (chances * (grad_chances - inner) * E ** (-0.5)).astype(LOW)
         low_chances = chances.astype(LOW)
         none = jnp.zeros_like(low_chances)
+        scores_prev = jnp.where(below, none, grad_scores)
+        grads[3].append(dot_first(scores_prev, q))
+        grads[4].append(dot_first(jnp.where(below, none, low_chances), g))
+        kept.append((q, k, kp, g, scores_prev, grad_scores, low_chances))
+    prev_grad = jnp.concatenate(grads[3] + grads[4], axis=1).astype(LOW)
+    for q, k, kp, g, scores_prev, grad_scores, low_chances in tied(kept, prev_grad):
+        none = jnp.zeros_like(low_chances)
         scores_now = jnp.where(below, grad_scores, none)
-        scores_prev = jnp.where(below, none, grad_scores)
         grads[0].append(plain_dot(scores_now, k) + plain_dot(scores_prev, kp))
         grads[1].append(dot_first(scores_now, q))
         grads[2].append(dot_first(jnp.where(below, low_chances, none), g))
-        grads[3].append(dot_first(scores_prev, q))
-        grads[4].append(dot_first(jnp.where(below, none, low_chances), g))
     query_grad = jnp.concatenate(grads[0], axis=1)
     pair_grad = jnp.concatenate(grads[1] + grads[2], axis=1)
-    prev_grad = jnp.concatenate(grads[3] + grads[4], axis=1)
     return query_grad, pair_grad, prev_grad
 
 
@@ -453,7 +464,9 @@
 
     def state_rest(incoming, state_heads, meanwhile=lambda heads: ()):
         update = tp_total(plain_dot(state_heads, out_state_flat))
-        update = tied(update, *meanwhile(state_heads))
+        return state_end(incoming, tied(update, *meanwhile(state_heads)))
+
+    def state_end(incoming, update):
         mid_state = keep_one * incoming + (1.0 - keep_one) * update
         state_ffn_in = layer_norm(mid_state, norm_sffn).astype(LOW)
         state_hidden = plain_dot(state_ffn_in, up_state)
@@ -545,8 +558,30 @@
             own_token_logs,
             tied(grad_heads[:, :width], cross_pieces),
         )
-        returned = lax.ppermute(prev_grad.astype(LOW), "seq", homeward)
+        returned = lax.ppermute(prev_grad, "seq", homeward)
         return query_grad + cross_query_grad, pair_grad + returned.astype(HIGH)
+
+    incoming, _, state_queries, _, own = turns[CHAIN - 1]
+    token_pair = choose(pairs_stack, position ^ (CHAIN - 1))
+    cross, _ = full_attend(
+        tied(state_queries, grad_heads), token_pair[:, :width], token_pair[:, width:]
+    )
+    last_heads = jnp.concatenate([own, cross], axis=1)
+    last_update = tp_total(plain_dot(last_heads, out_state_flat))
+
+    def last_state(after):
+        state_slab, _ = state_end(incoming_last, tied(last_update, after))
+        states_stack = jnp.stack(states_out + [own_rows(state_slab)])
+        pieces = [choose(states_stack, position)]
+        pieces += [swap(choose(states_stack, position ^ k), k) for k in range(1, CHAIN)]
+        pieces = jnp.stack(pieces)
+        return jnp.stack([choose(pieces, position ^ q) for q in range(CHAIN)])
+
+    def states_whole(slabs):
+        by_tp = turned(jnp.stack(tp_gather(slabs)), (n_tp - tp_index) % n_tp)
+        return jnp.transpose(by_tp, (1, 0, 2, 3)).reshape(state_rows, model_width)
+
+    incoming_last = incoming
 
     init_grad = jnp.zeros((thin_rows, model_width), HIGH)
     bias_one = bias_two = jnp.zeros((model_width,), HIGH)
@@ -619,10 +654,18 @@
             kept_rest.append(
                 (state_heads, grad_update, state_ffn_in, grad_state_hidden, state_active, grad_mlp)
             )
+        if turn == CHAIN - 2:
+            slabs = last_state(grad_mid)
+            pair_total = tied(pair_total, slabs)
         if turn == CHAIN - 3:
             pair_total = tied(pair_total, step)
+        if turn == CHAIN - 4:
+            state_rows_out = states_whole(tied(slabs, grad_mid))
+            pair_total = tied(pair_total, state_rows_out)
         grad_state_qkv = jnp.concatenate([query_total, pair_total], axis=1).astype(LOW)
         kept_qkv.append((state_normed, grad_state_qkv))
+        if turn == 0:
+            break
         grad_state_normed = tp_total(dot_second(grad_state_qkv, qkv_state_flat))
         if turn == CHAIN - 1:
             query_grad, pair_grad = own_back()
@@ -636,6 +679,13 @@
             grad_incoming = keep_one * grad_mid + grad_incoming
         init_grad = init_grad + jnp.where(flags[turn], own_rows(grad_incoming), 0.0)
         grad_state = jnp.where(flags[turn], 0.0, grad_incoming)
+    grad_mid_first, grad_qkv_first = grad_mid, grad_state_qkv
+
+    def first_incoming_grad(after):
+        normed_grad = tp_total(dot_second(tied(grad_qkv_first, after), qkv_state_flat))
+        incoming = turns[0][0]
+        return keep_one * grad_mid_first + norm_back(incoming, norm_state, normed_grad)
+
     bias_one = bias_one * keep_one * (1.0 - keep_one) / n_tp
     bias_two = bias_two * keep_two * (1.0 - keep_two) / n_tp
 
@@ -671,8 +721,38 @@
         gelu_slope(part, dot_second(grad, down_win)).astype(LOW)
         for part, grad in zip(win_hidden, grad_win_out)
     ]
-    grad_win_ffn_in = tp_scatter([dot_second(part, up_win) for part in grad_win_hidden])
+    parts = [dot_second(part, up_win) for part in grad_win_hidden]
+    grad_win_ffn_in = tp_scatter(parts)
+    step = step, parts
     step = state_grads.one_first(step), state_grads.two_first(step)
+
+    middle_grads = SeqSum(
+        weight_grads(
+            [
+                (normed_pieces, [grad_qkv]),
+                (win_ffn_in, grad_win_hidden),
+                (grad_win_out, win_active),
+            ]
+        )
+    )
+    grad_win_ffn_in = tied(grad_win_ffn_in, *step, middle_grads.other)
+    grad_win_mixed = grad_layer_one + norm_back(win_mixed, norm_wffn, grad_win_ffn_in)
+    grad_win_pieces = tp_gather(grad_win_mixed.astype(LOW))
+    step = middle_grads.cores(grad_win_mixed), state_grads.one_last(grad_win_mixed)
+    grad_win_proj = tied(jnp.concatenate(grad_win_pieces), *step)
+    grad_win_heads = dot_second(grad_win_proj, out_win).astype(LOW)
+    win_query_grad, win_pair_grad, win_prev_grad = band_attend_back(
+        win_queries, win_pair, win_prev, below, starts_here, win_logs, grad_win_heads
+    )
+    win_returned = lax.ppermute(win_prev_grad, "seq", homeward)
+    after = win_query_grad, win_pair_grad
+    step = state_grads.two_last(after)
+    middle_grads.one_first(after)
+    middle_grads.two_first(after)
+    first_grad = own_rows(first_incoming_grad(after))
+    init_grad = init_grad + jnp.where(flags[0], first_grad, 0.0)
+    win_pair_grad = win_pair_grad + tied(win_returned, step).astype(HIGH)
+    grad_win_qkv = jnp.concatenate([win_query_grad, win_pair_grad], axis=1).astype(LOW)
 
     small_rows = jnp.concatenate(
         [init_grad, jnp.stack([bias_one, bias_two]), jnp.zeros((14, model_width), HIGH)]
@@ -685,61 +765,28 @@
         (CHAIN - 1) * thin_rows + row_of,
     )
     selector = (column_of == column_for).astype(LOW)
-    middle_grads = SeqSum(
+    last_grads = SeqSum(
         weight_grads(
             [
-                (normed_pieces, [grad_qkv]),
-                (win_ffn_in, grad_win_hidden),
-                (grad_win_out, win_active),
+                ([win_normed], [grad_win_qkv]),
+                ([grad_win_proj], [win_heads]),
                 ([small_rows], [selector]),
             ]
         )
     )
-    grad_win_ffn_in = tied(grad_win_ffn_in, *step, middle_grads.other)
-    grad_win_mixed = grad_layer_one + norm_back(win_mixed, norm_wffn, grad_win_ffn_in)
-    grad_win_pieces = tp_gather(grad_win_mixed.astype(LOW))
-    step = middle_grads.cores(grad_win_mixed), state_grads.one_last(grad_win_mixed)
-    grad_win_proj = tied(jnp.concatenate(grad_win_pieces), *step)
-    grad_win_heads = dot_second(grad_win_proj, out_win).astype(LOW)
-    win_query_grad, win_pair_grad, win_prev_grad = band_attend_back(
-        win_queries, win_pair, win_prev, below, starts_here, win_logs, grad_win_heads
-    )
-    step = (
-        state_grads.two_last(grad_win_heads),
-        middle_grads.one_first(grad_win_heads),
-        middle_grads.two_first(grad_win_heads),
-    )
-    win_returned = lax.ppermute(win_prev_grad.astype(LOW), "seq", homeward)
-    win_pair_grad = win_pair_grad + tied(win_returned, *step).astype(HIGH)
-    grad_win_qkv = jnp.concatenate([win_query_grad, win_pair_grad], axis=1).astype(LOW)
-    last_grads = SeqSum(
-        weight_grads([([win_normed], [grad_win_qkv]), ([grad_win_proj], [win_heads])])
-    )
     grad_win_normed = tp_scatter(
         [dot_second(part, qkv_win_flat) for part in split_rows(grad_win_qkv, n_tp)]
     )
-    step = last_grads.cores(grad_win_qkv)
+    step = last_grads.cores(last_grads.other)
     step = middle_grads.one_last(step), middle_grads.two_last(step)
-    last_grads.one_first(step[0])
-    last_grads.two_first(step[1])
-    last_grads.one_last(last_grads.two)
-    last_grads.two_last(last_grads.two)
+    last_grads.one_first(step)
+    last_grads.two_first(step)
+    step = last_grads.one, last_grads.two
+    last_grads.one_last(step)
+    last_grads.two_last(step)
     back_input = norm_back(own_input, norm_win, grad_win_normed)
     grad_token_rows = natural(tp_gather((grad_win_mixed + back_input).astype(LOW)))
-    output_rows = natural(tp_gather(tied(layer_output.astype(LOW), grad_win_heads)))
-
-    incoming, _, state_queries, _, own = turns[CHAIN - 1]
-    token_pair = choose(tied(pairs_stack, grad_win_heads), position ^ (CHAIN - 1))
-    cross, _ = full_attend(state_queries, token_pair[:, :width], token_pair[:, width:])
-    state_slab, _ = state_rest(incoming, jnp.concatenate([own, cross], axis=1))
-    states_out.append(own_rows(state_slab))
-    states_stack = jnp.stack(states_out)
-    pieces = [choose(states_stack, position)]
-    pieces += [swap(choose(states_stack, position ^ k), k) for k in range(1, CHAIN)]
-    pieces = jnp.stack(pieces)
-    slabs = jnp.stack([choose(pieces, position ^ q) for q in range(CHAIN)])
-    by_tp = turned(jnp.stack(tp_gather(slabs)), (n_tp - tp_index) % n_tp)
-    state_rows_out = jnp.transpose(by_tp, (1, 0, 2, 3)).reshape(state_rows, model_width)
+    output_rows = natural(tp_gather(tied(layer_output.astype(LOW), after)))
 
     own_columns = model_width // lax.axis_size("seq")
     inner_width = up_tok.shape[1]
@@ -749,7 +796,7 @@
     sum_up_win = middle_grads.columns(3 * width, inner_width)
     sum_up_tok = token_grads.columns(0, inner_width)
     sum_up_state = state_grads.columns(5 * width, inner_width)
-    small_sums = middle_grads.columns(3 * width + 2 * inner_width, CHAIN * thin_rows + 2)
+    small_sums = last_grads.columns(4 * width, CHAIN * thin_rows + 2)
     first_row = seq_index * own_columns
     vectors = [
         gain_grad(qkv_win_flat, sum_qkv_win, norm_win, first_row),

time: 992 us -> 886 us (0.89)
  local copies, waits for them, and re-layouts: 117 us -> 70.7 us
  waiting for transfers between devices: 339 us -> 312 us
  matrix products: 158 us -> 142 us
  other arithmetic: 111 us -> 101 us
    ppermute x69, waiting for transfers between devices: 195 us -> 156 us  [tp_to(): return lax.ppermute(array, 'tp', [(i, (i + k) % n) for i in range(n)])]
    dynamic_slice x8 -> x0, local copies, waits for them, and re-layouts: 23.6 us -> none  [stage(): sent = lax.dynamic_index_in_dim(array, (at + k) % size, dim, False)]
    ppermute x6 -> x0, local copies, waits for them, and re-layouts: 14.6 us -> none  [stage(): total = total + lax.ppermute(sent, 'seq', self.pairs(*step(k))).astype(HIGH)]
    optimization_barrier x2 -> x0, local copies, waits for them, and re-layouts: 13.1 us -> none  [tied(): return lax.optimization_barrier((value,) + others)[0]]
    unnamed x455 -> x698, local copies, waits for them, and re-layouts: 22.2 us -> 32.3 us
    ppermute x33, waiting for transfers between devices: 42.9 us -> 52.9 us  [swap(): return lax.ppermute(array, 'seq', [(s, s ^ k) for s in range(n)])]
  transfers between devices with their start and end apart: 183 -> 183, of which waited for: 87 -> 90; matrix products, arithmetic and copies ran while one was open for 26% -> 19% of each run, Pallas kernels for 2% -> 2%
where the time goes in v5:
time: 886 us; the launch traced here: 875 us
  waiting for transfers between devices  312 us (35%)
  starting transfers between devices  224 us (25%)
  matrix products  142 us (16%)
  other arithmetic  101 us (11%)
  local copies, waits for them, and re-layouts  70.7 us (8%)
  Pallas kernels  18.4 us (2%)
    ppermute x69, waiting for transfers between devices, tp_to(): return lax.ppermute(array, 'tp', [(i, (i + k) % n) for i in range(n)])  156 us
    ppermute x69, starting transfers between devices, tp_to(): return lax.ppermute(array, 'tp', [(i, (i + k) % n) for i in range(n)])  86.7 us
    ppermute x48, starting transfers between devices, stage(): total = total + lax.ppermute(sent, 'seq', self.pairs(*step(k))).astype(HIGH)  70.3 us
    dot_general x89, matrix products, plain_dot(): return jnp.dot(former, latter, preferred_element_type=HIGH)  66.5 us
    ppermute x30, waiting for transfers between devices, tp_from(): return lax.ppermute(array, 'tp', [((i + k) % n, i) for i in range(n)])  60.5 us
    dot_general x91, matrix products, dot_second(): lax.dot_general(former, latter, (((1,), (1,)), ((), ())), preferred_eleme...  55.3 us
    ppermute x33, waiting for transfers between devices, swap(): return lax.ppermute(array, 'seq', [(s, s ^ k) for s in range(n)])  52.9 us
    ppermute x48, waiting for transfers between devices, stage(): total = total + lax.ppermute(sent, 'seq', self.pairs(*step(k))).astype(HIGH)  42.2 us
  transfers between devices with their start and end apart: 183, of which 90 were waited for; matrix products, arithmetic and copies ran while one was open for 19% of the time, Pallas kernels for 2%

profile of v5, /device:TPU:0, one launch (start us, length us, event | category | flops | bytes accessed | tf_op | source)
XLA Modules:
  0.0 875.5 jit_solution(1833710580316365012)
XLA Ops:
  51.4 10.3 %collective-permute-start.14 = (bf16[128,512]{1,0:T(8,128)(2,1)S(1)}, bf16[128,512]{1,0:T(8,128)(2,1)S(1)}, u32[]{:S(2)}, u32[]{:S(2)}) collective-permute-start(bf16[128,512]{1,0:T(8,128)(2,1)S(1)} %slice.1016), channel_id=1, source_target_pairs={{0,8},{4,12},{8,0},{12,4},{16,24},{20,28},{24,16},{28,20},{32,40},... | collective-permute-start | bytes 393224 | tf_op jit(solution)/shard_map/ppermute | solution.py:120
  94.1 4.9 collective-permute-done.12.refs_3_
  108.2 11.5 %collective-permute-done.17 = bf16[512,512]{1,0:T(8,128)(2,1)S(1)} collective-permute-done((bf16[512,512]{1,0:T(8,128)(2,1)S(1)}, bf16[512,512]{1,0:T(8,128)(2,1)S(1)}, u32[]{:S(2)}, u32[]{:S(2)}) %collective-permute-start.17) | collective-permute-done | bytes 524320 | tf_op jit(solution)/shard_map/ppermute | solution.py:120
  132.1 9.9 %collective-permute-done.21 = bf16[128,1024]{1,0:T(8,128)(2,1)S(1)} collective-permute-done((bf16[128,1024]{1,0:T(8,128)(2,1)S(1)}, bf16[128,1024]{1,0:T(8,128)(2,1)S(1)}, u32[]{:S(2)}, u32[]{:S(2)}) %collective-permute-start.21) | collective-permute-done | bytes 262176 | tf_op jit(solution)/shard_map/ppermute | solution.py:84
  153.5 6.6 collective-permute-done.24
  160.1 5.1 collective-permute-done.23
  185.9 7.1 collective-permute-done.29
  200.9 4.9 collective-permute-done.33
  205.8 5.6 collective-permute-done.32
  226.1 5.3 collective-permute-done.39
  231.4 6.1 collective-permute-done.38
  245.5 7.5 collective-permute-done.42
  259.5 4.7 collective-permute-done.44
  279.3 6.0 collective-permute-done.46
  285.3 5.2 collective-permute-done.47
  296.5 10.6 %collective-permute-done.49.refs_1_ = bf16[128,1024]{1,0:T(8,128)(2,1)S(1)} collective-permute-done((bf16[128,1024]{1,0:T(8,128)(2,1)S(1)}, bf16[128,1024]{1,0:T(8,128)(2,1)S(1)}, u32[]{:S(2)}, u32[]{:S(2)}) %collective-permute-start.49) | collective-permute-done | bytes 262176 | tf_op jit(solution)/shard_map/ppermute | solution.py:79
  319.3 5.8 collective-permute-done.52
  333.9 4.6 collective-permute-done.57.refs_16_
  338.5 6.8 collective-permute-done.56.refs_15_
  411.7 4.6 fusion.851
  447.3 5.2 collective-permute-done.80
  452.5 6.7 collective-permute-done.79
  475.4 5.4 collective-permute-done.83
  566.4 10.4 %collective-permute-done.109 = bf16[128,512]{1,0:T(8,128)(2,1)S(1)} collective-permute-done((bf16[128,512]{1,0:T(8,128)(2,1)S(1)}, bf16[128,512]{1,0:T(8,128)(2,1)S(1)}, u32[]{:S(2)}, u32[]{:S(2)}) %collective-permute-start.109) | collective-permute-done | bytes 131104 | tf_op jit(solution)/shard_map/ppermute | solution.py:120
  577.0 6.1 shard_map.399
  603.9 7.7 collective-permute-done.114
  625.9 5.2 collective-permute-done.121.refs_16_
  642.2 5.1 collective-permute-done.120
  655.9 5.5 shard_map.400
  704.6 7.7 collective-permute-done.134
  787.5 6.2 collective-permute-done.157
  808.8 8.4 collective-permute-done.149
  (1641 shorter events, 654.7 us)
Async XLA Ops:
  41.2 30.8 %collective-permute-start.8 = (bf16[128,1024]{1,0:T(8,128)(2,1)S(1)}, bf16[128,1024]{1,0:T(8,128)(2,1)S(1)}, u32[]{:S(2)}, u32[]{:S(2)}) collective-permute-start(bf16[128,1024]{1,0:T(8,128)(2,1)S(1)} %multiply_convert_fusion.30.refs_5_), channel_id=1, source_target_pairs={{3,0},{0,1},{1,2},{2,3},{7,4},{4,5},{5,6},{6,7},{11,8},{8,9},{9,10... | collective-permute-start | bytes 786440 | tf_op jit(solution)/shard_map/ppermute | solution.py:79
  44.7 17.1 %collective-permute-start.4 = (bf16[128,1024]{1,0:T(8,128)(2,1)S(1)}, bf16[128,1024]{1,0:T(8,128)(2,1)S(1)}, u32[]{:S(2)}, u32[]{:S(2)}) collective-permute-start(bf16[128,1024]{1,0:T(8,128)(2,1)S(1)} %multiply_convert_fusion.30.refs_5_), channel_id=1, source_target_pairs={{2,0},{3,1},{0,2},{1,3},{6,4},{7,5},{4,6},{5,7},{10,8},{11,9},{8,1... | collective-permute-start | bytes 786440 | tf_op jit(solution)/shard_map/ppermute | solution.py:79
  51.4 23.0 %collective-permute-start.14 = (bf16[128,512]{1,0:T(8,128)(2,1)S(1)}, bf16[128,512]{1,0:T(8,128)(2,1)S(1)}, u32[]{:S(2)}, u32[]{:S(2)}) collective-permute-start(bf16[128,512]{1,0:T(8,128)(2,1)S(1)} %slice.1016), channel_id=1, source_target_pairs={{0,8},{4,12},{8,0},{12,4},{16,24},{20,28},{24,16},{28,20},{32,40},... | collective-permute-start | bytes 393224 | tf_op jit(solution)/shard_map/ppermute | solution.py:120
  291.3 25.1 %collective-permute-start.51 = (bf16[128,1024]{1,0:T(8,128)(2,1)S(1)}, bf16[128,1024]{1,0:T(8,128)(2,1)S(1)}, u32[]{:S(2)}, u32[]{:S(2)}) collective-permute-start(bf16[128,1024]{1,0:T(8,128)(2,1)S(1)} %multiply_convert_fusion.18.refs_0_), channel_id=1, source_target_pairs={{3,0},{0,1},{1,2},{2,3},{7,4},{4,5},{5,6},{6,7},{11,8},{8,9},{9,10... | collective-permute-start | bytes 786440 | tf_op jit(solution)/shard_map/ppermute | solution.py:79
  291.4 18.7 %collective-permute-start.50 = (bf16[128,1024]{1,0:T(8,128)(2,1)S(1)}, bf16[128,1024]{1,0:T(8,128)(2,1)S(1)}, u32[]{:S(2)}, u32[]{:S(2)}) collective-permute-start(bf16[128,1024]{1,0:T(8,128)(2,1)S(1)} %multiply_convert_fusion.18.refs_0_), channel_id=1, source_target_pairs={{2,0},{3,1},{0,2},{1,3},{6,4},{7,5},{4,6},{5,7},{10,8},{11,9},{8,1... | collective-permute-start | bytes 786440 | tf_op jit(solution)/shard_map/ppermute | solution.py:79
  348.0 38.7 %collective-permute-start.71 = (bf16[128,1024]{1,0:T(8,128)(2,1)S(1)}, bf16[128,1024]{1,0:T(8,128)(2,1)S(1)}, u32[]{:S(2)}, u32[]{:S(2)}) collective-permute-start(bf16[128,1024]{1,0:T(8,128)(2,1)S(1)} %get-tuple-element.604), channel_id=1, source_target_pairs={{0,3},{1,0},{2,1},{3,2},{4,7},{5,4},{6,5},{7,6},{8,11},{9,8},{10,9... | collective-permute-start | bytes 786440 | tf_op jit(solution)/shard_map/ppermute | solution.py:84
  350.1 38.5 %collective-permute-start.70 = (bf16[128,1024]{1,0:T(8,128)(2,1)S(1)}, bf16[128,1024]{1,0:T(8,128)(2,1)S(1)}, u32[]{:S(2)}, u32[]{:S(2)}) collective-permute-start(bf16[128,1024]{1,0:T(8,128)(2,1)S(1)} %get-tuple-element.604), channel_id=1, source_target_pairs={{0,1},{1,2},{2,3},{3,0},{4,5},{5,6},{6,7},{7,4},{8,9},{9,10},{10,1... | collective-permute-start | bytes 786440 | tf_op jit(solution)/shard_map/ppermute | solution.py:84
  439.7 19.6 %collective-permute-start.81 = (bf16[512,2560]{1,0:T(8,128)(2,1)S(1)}, bf16[512,2560]{1,0:T(8,128)(2,1)S(1)}, u32[]{:S(2)}, u32[]{:S(2)}) collective-permute-start(bf16[512,2560]{1,0:T(8,128)(2,1)S(1)} %copy-done.55), channel_id=1, source_target_pairs={{0,4},{4,0},{8,12},{12,8},{16,20},{20,16},{24,28},{28,24},{32,36},... | collective-permute-start | bytes 7864328 | tf_op jit(solution)/shard_map/ppermute | solution.py:120
  469.1 22.6 %collective-permute-start.87 = (bf16[4,32,1280]{2,1,0:T(8,128)(2,1)S(1)}, bf16[4,32,1280]{2,1,0:T(8,128)(2,1)S(1)}, u32[]{:S(2)}, u32[]{:S(2)}) collective-permute-start(bf16[4,32,1280]{2,1,0:T(8,128)(2,1)S(1)} %get-tuple-element.418), channel_id=1, source_target_pairs={{0,16},{4,20},{8,24},{12,28},{16,0},{20,4},{24,8},{28,12},{32,48},... | collective-permute-start | bytes 983048 | tf_op jit(solution)/shard_map/ppermute | solution.py:234
  472.7 18.9 %collective-permute-start.89 = (bf16[4,32,1280]{2,1,0:T(8,128)(2,1)S(1)}, bf16[4,32,1280]{2,1,0:T(8,128)(2,1)S(1)}, u32[]{:S(2)}, u32[]{:S(2)}) collective-permute-start(bf16[4,32,1280]{2,1,0:T(8,128)(2,1)S(1)} %get-tuple-element.419), channel_id=1, source_target_pairs={{0,24},{4,28},{8,0},{12,4},{16,8},{20,12},{24,16},{28,20},{32,56},... | collective-permute-start | bytes 983048 | tf_op jit(solution)/shard_map/ppermute | solution.py:234
  474.4 17.2 %collective-permute-start.88 = (bf16[4,32,1280]{2,1,0:T(8,128)(2,1)S(1)}, bf16[4,32,1280]{2,1,0:T(8,128)(2,1)S(1)}, u32[]{:S(2)}, u32[]{:S(2)}) collective-permute-start(bf16[4,32,1280]{2,1,0:T(8,128)(2,1)S(1)} %get-tuple-element.420), channel_id=1, source_target_pairs={{0,8},{4,12},{8,16},{12,20},{16,24},{20,28},{24,0},{28,4},{32,40},... | collective-permute-start | bytes 983048 | tf_op jit(solution)/shard_map/ppermute | solution.py:234
  499.9 17.5 %collective-permute-start.96 = (bf16[4,32,1280]{2,1,0:T(8,128)(2,1)S(1)}, bf16[4,32,1280]{2,1,0:T(8,128)(2,1)S(1)}, u32[]{:S(2)}, u32[]{:S(2)}) collective-permute-start(bf16[4,32,1280]{2,1,0:T(8,128)(2,1)S(1)} %get-tuple-element.415), channel_id=1, source_target_pairs={{0,64},{4,68},{8,72},{12,76},{16,80},{20,84},{24,88},{28,92},{32,9... | collective-permute-start | bytes 983048 | tf_op jit(solution)/shard_map/ppermute | solution.py:234
  503.0 17.5 %collective-permute-start.98 = (bf16[4,32,1280]{2,1,0:T(8,128)(2,1)S(1)}, bf16[4,32,1280]{2,1,0:T(8,128)(2,1)S(1)}, u32[]{:S(2)}, u32[]{:S(2)}) collective-permute-start(bf16[4,32,1280]{2,1,0:T(8,128)(2,1)S(1)} %get-tuple-element.416), channel_id=1, source_target_pairs={{0,96},{4,100},{8,104},{12,108},{16,112},{20,116},{24,120},{28,124... | collective-permute-start | bytes 983048 | tf_op jit(solution)/shard_map/ppermute | solution.py:234
  539.5 16.3 %collective-permute-start.112 = (bf16[4,32,1024]{2,1,0:T(8,128)(2,1)S(1)}, bf16[4,32,1024]{2,1,0:T(8,128)(2,1)S(1)}, u32[]{:S(2)}, u32[]{:S(2)}) collective-permute-start(bf16[4,32,1024]{2,1,0:T(8,128)(2,1)S(1)} %pad_maximum_fusion.23), channel_id=1, source_target_pairs={{3,0},{0,1},{1,2},{2,3},{7,4},{4,5},{5,6},{6,7},{11,8},{8,9},{9,10... | collective-permute-start | bytes 786440 | tf_op jit(solution)/shard_map/ppermute | solution.py:79
  557.6 25.6 %collective-permute-start.102 = (bf16[512,512]{1,0:T(8,128)(2,1)S(1)}, bf16[512,512]{1,0:T(8,128)(2,1)S(1)}, u32[]{:S(2)}, u32[]{:S(2)}) collective-permute-start(bf16[512,512]{1,0:T(8,128)(2,1)S(1)} %copy-done.211), channel_id=1, source_target_pairs={{4,0},{8,4},{12,8},{20,16},{24,20},{28,24},{36,32},{40,36},{44,40}... | collective-permute-start | bytes 1572872 | tf_op jit(solution)/shard_map/ppermute | solution.py:561
  558.9 17.8 %collective-permute-start.109 = (bf16[128,512]{1,0:T(8,128)(2,1)S(1)}, bf16[128,512]{1,0:T(8,128)(2,1)S(1)}, u32[]{:S(2)}, u32[]{:S(2)}) collective-permute-start(bf16[128,512]{1,0:T(8,128)(2,1)S(1)} %fusion.244), channel_id=1, source_target_pairs={{0,8},{4,12},{8,0},{12,4},{16,24},{20,28},{24,16},{28,20},{32,40},... | collective-permute-start | bytes 393224 | tf_op jit(solution)/shard_map/ppermute | solution.py:120
  565.4 17.8 %collective-permute-start.104 = (bf16[512,512]{1,0:T(8,128)(2,1)S(1)}, bf16[512,512]{1,0:T(8,128)(2,1)S(1)}, u32[]{:S(2)}, u32[]{:S(2)}) collective-permute-start(bf16[512,512]{1,0:T(8,128)(2,1)S(1)} %fusion.31), channel_id=1, source_target_pairs={{0,8},{4,12},{8,0},{12,4},{16,24},{20,28},{24,16},{28,20},{32,40},... | collective-permute-start | bytes 1572872 | tf_op jit(solution)/shard_map/ppermute | solution.py:120
  585.9 27.8 %collective-permute-start.116 = (bf16[512,3328]{1,0:T(8,128)(2,1)}, bf16[512,3328]{1,0:T(8,128)(2,1)}, u32[]{:S(2)}, u32[]{:S(2)}) collective-permute-start(bf16[512,3328]{1,0:T(8,128)(2,1)} %get-tuple-element.164), channel_id=1, source_target_pairs={{0,4},{4,0},{8,12},{12,8},{16,20},{20,16},{24,28},{28,24},{32,36},... | collective-permute-start | bytes 10223624 | tf_op jit(solution)/shard_map/ppermute | solution.py:120
  620.6 16.2 %collective-permute-start.117 = (bf16[128,1024]{1,0:T(8,128)(2,1)S(1)}, bf16[128,1024]{1,0:T(8,128)(2,1)S(1)}, u32[]{:S(2)}, u32[]{:S(2)}) collective-permute-start(bf16[128,1024]{1,0:T(8,128)(2,1)S(1)} %get-tuple-element.323.refs_13_), channel_id=1, source_target_pairs={{2,0},{3,1},{0,2},{1,3},{6,4},{7,5},{4,6},{5,7},{10,8},{11,9},{8,1... | collective-permute-start | bytes 786440 | tf_op jit(solution)/shard_map/ppermute | solution.py:79
  621.2 17.7 %collective-permute-start.123 = (bf16[32,1280]{1,0:T(8,128)(2,1)S(1)}, bf16[32,1280]{1,0:T(8,128)(2,1)S(1)}, u32[]{:S(2)}, u32[]{:S(2)}) collective-permute-start(bf16[32,1280]{1,0:T(8,128)(2,1)S(1)} %get-tuple-element.470), channel_id=1, source_target_pairs={{0,16},{4,20},{8,24},{12,28},{16,0},{20,4},{24,8},{28,12},{32,48},... | collective-permute-start | bytes 245768 | tf_op jit(solution)/shard_map/ppermute | solution.py:234
  648.4 18.0 %collective-permute-start.129 = (bf16[4,32,1664]{2,1,0:T(8,128)(2,1)S(1)}, bf16[4,32,1664]{2,1,0:T(8,128)(2,1)S(1)}, u32[]{:S(2)}, u32[]{:S(2)}) collective-permute-start(bf16[4,32,1664]{2,1,0:T(8,128)(2,1)S(1)} %get-tuple-element.403), channel_id=1, source_target_pairs={{0,64},{4,68},{8,72},{12,76},{16,80},{20,84},{24,88},{28,92},{32,9... | collective-permute-start | bytes 1277960 | tf_op jit(solution)/shard_map/ppermute | solution.py:234
  653.0 17.7 %collective-permute-start.131 = (bf16[4,32,1664]{2,1,0:T(8,128)(2,1)S(1)}, bf16[4,32,1664]{2,1,0:T(8,128)(2,1)S(1)}, u32[]{:S(2)}, u32[]{:S(2)}) collective-permute-start(bf16[4,32,1664]{2,1,0:T(8,128)(2,1)S(1)} %get-tuple-element.404), channel_id=1, source_target_pairs={{0,96},{4,100},{8,104},{12,108},{16,112},{20,116},{24,120},{28,124... | collective-permute-start | bytes 1277960 | tf_op jit(solution)/shard_map/ppermute | solution.py:234
  681.3 32.9 %collective-permute-start.135 = (bf16[512,2816]{1,0:T(8,128)(2,1)}, bf16[512,2816]{1,0:T(8,128)(2,1)}, u32[]{:S(2)}, u32[]{:S(2)}) collective-permute-start(bf16[512,2816]{1,0:T(8,128)(2,1)} %get-tuple-element.172), channel_id=1, source_target_pairs={{0,4},{4,0},{8,12},{12,8},{16,20},{20,16},{24,28},{28,24},{32,36},... | collective-permute-start | bytes 8650760 | tf_op jit(solution)/shard_map/ppermute | solution.py:120
  731.7 38.7 %collective-permute-start.141 = (bf16[128,1024]{1,0:T(8,128)(2,1)}, bf16[128,1024]{1,0:T(8,128)(2,1)}, u32[]{:S(2)}, u32[]{:S(2)}) collective-permute-start(bf16[128,1024]{1,0:T(8,128)(2,1)} %add_add_fusion), channel_id=1, source_target_pairs={{3,0},{0,1},{1,2},{2,3},{7,4},{4,5},{5,6},{6,7},{11,8},{8,9},{9,10... | collective-permute-start | bytes 786440 | tf_op jit(solution)/shard_map/ppermute | solution.py:79
  733.4 33.9 %collective-permute-start.140 = (bf16[128,1024]{1,0:T(8,128)(2,1)}, bf16[128,1024]{1,0:T(8,128)(2,1)}, u32[]{:S(2)}, u32[]{:S(2)}) collective-permute-start(bf16[128,1024]{1,0:T(8,128)(2,1)} %add_add_fusion), channel_id=1, source_target_pairs={{2,0},{3,1},{0,2},{1,3},{6,4},{7,5},{4,6},{5,7},{10,8},{11,9},{8,1... | collective-permute-start | bytes 786440 | tf_op jit(solution)/shard_map/ppermute | solution.py:79
  759.4 23.3 %collective-permute-start.142 = (bf16[512,512]{1,0:T(8,128)(2,1)}, bf16[512,512]{1,0:T(8,128)(2,1)S(1)}, u32[]{:S(2)}, u32[]{:S(2)}) collective-permute-start(bf16[512,512]{1,0:T(8,128)(2,1)} %pad_maximum_fusion.17), channel_id=1, source_target_pairs={{4,0},{8,4},{12,8},{20,16},{24,20},{28,24},{36,32},{40,36},{44,40}... | collective-permute-start | bytes 1572872 | tf_op jit(solution)/shard_map/ppermute | solution.py:747
  760.7 40.6 %collective-permute-start.162 = (bf16[4,32,1408]{2,1,0:T(8,128)(2,1)}, bf16[4,32,1408]{2,1,0:T(8,128)(2,1)S(1)}, u32[]{:S(2)}, u32[]{:S(2)}) collective-permute-start(bf16[4,32,1408]{2,1,0:T(8,128)(2,1)} %get-tuple-element.409), channel_id=1, source_target_pairs={{0,64},{4,68},{8,72},{12,76},{16,80},{20,84},{24,88},{28,92},{32,9... | collective-permute-start | bytes 1081352 | tf_op jit(solution)/shard_map/ppermute | solution.py:234
  765.1 39.3 %collective-permute-start.164 = (bf16[4,32,1408]{2,1,0:T(8,128)(2,1)}, bf16[4,32,1408]{2,1,0:T(8,128)(2,1)S(1)}, u32[]{:S(2)}, u32[]{:S(2)}) collective-permute-start(bf16[4,32,1408]{2,1,0:T(8,128)(2,1)} %get-tuple-element.410), channel_id=1, source_target_pairs={{0,96},{4,100},{8,104},{12,108},{16,112},{20,116},{24,120},{28,124... | collective-permute-start | bytes 1081352 | tf_op jit(solution)/shard_map/ppermute | solution.py:234
  767.2 18.0 %collective-permute-start.156 = (bf16[4,32,1408]{2,1,0:T(8,128)(2,1)S(1)}, bf16[4,32,1408]{2,1,0:T(8,128)(2,1)S(1)}, u32[]{:S(2)}, u32[]{:S(2)}) collective-permute-start(bf16[4,32,1408]{2,1,0:T(8,128)(2,1)S(1)} %copy-done.224), channel_id=1, source_target_pairs={{0,16},{4,20},{8,24},{12,28},{16,0},{20,4},{24,8},{28,12},{32,48},... | collective-permute-start | bytes 1081352 | tf_op jit(solution)/shard_map/ppermute | solution.py:234
  770.4 17.1 %collective-permute-start.158 = (bf16[4,32,1408]{2,1,0:T(8,128)(2,1)S(1)}, bf16[4,32,1408]{2,1,0:T(8,128)(2,1)S(1)}, u32[]{:S(2)}, u32[]{:S(2)}) collective-permute-start(bf16[4,32,1408]{2,1,0:T(8,128)(2,1)S(1)} %copy-done.223), channel_id=1, source_target_pairs={{0,24},{4,28},{8,0},{12,4},{16,8},{20,12},{24,16},{28,20},{32,56},... | collective-permute-start | bytes 1081352 | tf_op jit(solution)/shard_map/ppermute | solution.py:234
  800.0 18.4 %collective-permute-start.155 = (bf16[512,1280]{1,0:T(8,128)(2,1)S(1)}, bf16[512,1280]{1,0:T(8,128)(2,1)S(1)}, u32[]{:S(2)}, u32[]{:S(2)}) collective-permute-start(bf16[512,1280]{1,0:T(8,128)(2,1)S(1)} %get-tuple-element.194), channel_id=1, source_target_pairs={{0,4},{4,0},{8,12},{12,8},{16,20},{20,16},{24,28},{28,24},{32,36},... | collective-permute-start | bytes 3932168 | tf_op jit(solution)/shard_map/ppermute | solution.py:120
  801.3 16.0 %collective-permute-start.151 = (bf16[128,1024]{1,0:T(8,128)(2,1)S(1)}, bf16[128,1024]{1,0:T(8,128)(2,1)S(1)}, u32[]{:S(2)}, u32[]{:S(2)}) collective-permute-start(bf16[128,1024]{1,0:T(8,128)(2,1)S(1)} %get-tuple-element.316), channel_id=1, source_target_pairs={{3,0},{0,1},{1,2},{2,3},{7,4},{4,5},{5,6},{6,7},{11,8},{8,9},{9,10... | collective-permute-start | bytes 786440 | tf_op jit(solution)/shard_map/ppermute | solution.py:79
  (488 other events, 4901.1 us)

commit v6 on v5

--- a/solution.py
+++ b/solution.py
@@ -141,7 +141,7 @@
     return lax.dynamic_slice_in_dim(twice, start, array.shape[0], 0)
 
 
-def weight_grads(pairs):
+def weight_grads(pairs, split=True):
     n_seq = lax.axis_size("seq")
     depth = pairs[0][0][0].shape[1]
     unit = depth // n_seq
@@ -164,6 +164,9 @@
 
         def keep(product, column):
             columns = slice(column, column + product.shape[1])
+            if not split:
+                other_ref[:, columns] = product
+                return
             for g in range(block // (CORES * unit)):
                 low = product[g * CORES * unit : g * CORES * unit + unit]
                 high = product[g * CORES * unit + unit : (g + 1) * CORES * unit]
@@ -181,16 +184,19 @@
             keep(dot_first(former, latter).astype(LOW), column)
             column += width
 
-    shape = jax.ShapeDtypeStruct((depth // CORES, total), LOW)
-    out_spec = pl.BlockSpec((block // CORES, total), lambda i: (i, 0))
+    shapes = [jax.ShapeDtypeStruct((depth // CORES, total), LOW)] * 2
+    out_specs = [pl.BlockSpec((block // CORES, total), lambda i: (i, 0))] * 2
+    if not split:
+        shapes = [jax.ShapeDtypeStruct((depth, total), LOW)]
+        out_specs = [pl.BlockSpec((block, total), lambda i: (i, 0))]
     rows = sum(piece.shape[0] for piece in pairs[0][0])
     core = (lax.axis_index("seq") % CORES).astype(jnp.int32).reshape(1)
     return pl.pallas_call(
         kernel,
-        out_shape=(shape, shape),
+        out_shape=shapes,
         grid=(depth // block,),
         in_specs=[pl.BlockSpec(memory_space=pltpu.SMEM)] + specs,
-        out_specs=(out_spec, out_spec),
+        out_specs=out_specs,
         compiler_params=pltpu.CompilerParams(vmem_limit_bytes=20 * 1024 * 1024),
         cost_estimate=pl.CostEstimate(
             flops=2 * rows * depth * total,
@@ -198,6 +204,15 @@
             transcendentals=0,
         ),
     )(core, *operands)
+
+
+class ScatterSum:
+    def __init__(self, grads):
+        self.grads = grads[0]
+        self.total = lax.psum_scatter(self.grads, "seq", scatter_dimension=0, tiled=True)
+
+    def columns(self, at, count):
+        return self.total[:, at : at + count].astype(HIGH)
 
 
 class SeqSum:
@@ -271,99 +286,163 @@
         return jnp.concatenate([self.one[:, at:], self.two[:, : at + count - half]], axis=1)
 
 
-def heads_of(matrix):
-    return [matrix[:, h * E : (h + 1) * E] for h in range(matrix.shape[1] // E)]
-
-
-def full_attend(queries, key_rows, value_rows):
-    results, logs = [], []
-    for q, k, v in zip(heads_of(queries), heads_of(key_rows), heads_of(value_rows)):
-        scores = dot_second(q, k) * E ** (-0.5)
-        row_max = jnp.max(scores, axis=-1, keepdims=True)
-        powers = jnp.exp(scores - row_max)
-        totals = jnp.sum(powers, axis=-1, keepdims=True)
-        results.append(plain_dot((powers / totals).astype(LOW), v).astype(LOW))
-        logs.append(row_max + jnp.log(totals))
-    return jnp.concatenate(results, axis=1), logs
-
-
-def full_attend_back(queries, key_rows, value_rows, logs, grad_result):
-    grads = ([], [], [])
-    for q, k, v, log, g in zip(
-        heads_of(queries), heads_of(key_rows), heads_of(value_rows), logs, heads_of(grad_result)
-    ):
-        chances = jnp.exp(dot_second(q, k) * E ** (-0.5) - log)
-        grad_chances = dot_second(g, v)
-        inner = jnp.sum(chances * grad_chances, axis=-1, keepdims=True)
-        grad_scores = (chances * (grad_chances - inner) * E ** (-0.5)).astype(LOW)
-        grads[0].append(plain_dot(grad_scores, k))
-        grads[1].append(dot_first(grad_scores, q))
-        grads[2].append(dot_first(chances.astype(LOW), g))
-    return [jnp.concatenate(each, axis=1) for each in grads]
-
-
-def band_scores(q, k, k_prev, below, starts_here):
-    current = dot_second(q, k) * E ** (-0.5)
-    before = jnp.where(starts_here, MASKED, dot_second(q, k_prev) * E ** (-0.5))
-    return jnp.where(below, current, before)
-
-
-def band_attend(queries, pair, pair_prev, below, starts_here):
-    width = queries.shape[1]
-    results, logs = [], []
-    for q, k, v, kp, vp in zip(
-        heads_of(queries),
-        heads_of(pair[:, :width]),
-        heads_of(pair[:, width:]),
-        heads_of(pair_prev[:, :width]),
-        heads_of(pair_prev[:, width:]),
-    ):
-        scores = band_scores(q, k, kp, below, starts_here)
-        row_max = jnp.max(scores, axis=-1, keepdims=True)
-        powers = jnp.exp(scores - row_max)
-        totals = jnp.sum(powers, axis=-1, keepdims=True)
-        chances = (powers / totals).astype(LOW)
-        none = jnp.zeros_like(chances)
-        result = plain_dot(jnp.where(below, chances, none), v) + plain_dot(
-            jnp.where(below, none, chances), vp
-        )
-        results.append(result.astype(LOW))
-        logs.append(row_max + jnp.log(totals))
-    return jnp.concatenate(results, axis=1), logs
-
-
-def band_attend_back(queries, pair, pair_prev, below, starts_here, logs, grad_result):
-    width = queries.shape[1]
-    grads, kept = ([], [], [], [], []), []
-    for q, k, v, kp, vp, log, g in zip(
-        heads_of(queries),
-        heads_of(pair[:, :width]),
-        heads_of(pair[:, width:]),
-        heads_of(pair_prev[:, :width]),
-        heads_of(pair_prev[:, width:]),
-        logs,
-        heads_of(grad_result),
-    ):
-        chances = jnp.exp(band_scores(q, k, kp, below, starts_here) - log)
-        grad_chances = jnp.where(below, dot_second(g, v), dot_second(g, vp))
-        inner = jnp.sum(chances * grad_chances, axis=-1, keepdims=True)
-        grad_scores = (chances * (grad_chances - inner) * E ** (-0.5)).astype(LOW)
-        low_chances = chances.astype(LOW)
-        none = jnp.zeros_like(low_chances)
-        scores_prev = jnp.where(below, none, grad_scores)
-        grads[3].append(dot_first(scores_prev, q))
-        grads[4].append(dot_first(jnp.where(below, none, low_chances), g))
-        kept.append((q, k, kp, g, scores_prev, grad_scores, low_chances))
-    prev_grad = jnp.concatenate(grads[3] + grads[4], axis=1).astype(LOW)
-    for q, k, kp, g, scores_prev, grad_scores, low_chances in tied(kept, prev_grad):
-        none = jnp.zeros_like(low_chances)
-        scores_now = jnp.where(below, grad_scores, none)
-        grads[0].append(plain_dot(scores_now, k) + plain_dot(scores_prev, kp))
-        grads[1].append(dot_first(scores_now, q))
-        grads[2].append(dot_first(jnp.where(below, low_chances, none), g))
-    query_grad = jnp.concatenate(grads[0], axis=1)
-    pair_grad = jnp.concatenate(grads[1] + grads[2], axis=1)
-    return query_grad, pair_grad, prev_grad
+ATTEND_STEP = 256
+
+
+def attention_kernel(kernel, shapes, scratch, operands, scalars, work):
+    in_vmem = pl.BlockSpec(memory_space=pltpu.VMEM)
+    in_smem = pl.BlockSpec(memory_space=pltpu.SMEM)
+    products, exps = work
+    return pl.pallas_call(
+        kernel,
+        out_shape=shapes,
+        in_specs=[in_smem] * len(scalars) + [in_vmem] * len(operands),
+        out_specs=tuple([in_vmem] * len(shapes)),
+        scratch_shapes=scratch,
+        compiler_params=pltpu.CompilerParams(vmem_limit_bytes=16 * 1024 * 1024),
+        cost_estimate=pl.CostEstimate(
+            flops=2 * products * E,
+            bytes_accessed=sum(2 * operand.size for operand in operands),
+            transcendentals=exps,
+        ),
+    )(*scalars, *operands)
+
+
+def head_columns(head, width, part):
+    return slice(part * width + head * E, part * width + (head + 1) * E)
+
+
+def score_parts(query, key, before, spot):
+    if before is None:
+        return dot_second(key, query) * E ** (-0.5), None
+    key_before, shift, start, rows = before
+    count = key.shape[0]
+    key_ids = (lax.broadcasted_iota(jnp.int32, (count, rows), 0) + shift) % count
+    query_ids = (lax.broadcasted_iota(jnp.int32, (count, rows), 1) + shift + spot) % count
+    below = key_ids <= query_ids
+    scores = jnp.where(below, dot_second(key, query), dot_second(key_before, query))
+    return jnp.where(below | (start == 0), scores * E ** (-0.5), MASKED), below
+
+
+def attend(queries, pair, before=None):
+    count, width = queries.shape
+    heads = width // E
+    rows = min(count, ATTEND_STEP)
+    scalars = [] if before is None else [part.reshape(1) for part in before[1:]]
+    operands = [queries, pair] + ([] if before is None else [before[0]])
+
+    def kernel(*refs):
+        scalar_refs, refs = refs[: len(scalars)], refs[len(scalars) :]
+        query_ref, pair_ref = refs[:2]
+        result_ref, log_ref = refs[-2:]
+        for h in range(heads):
+            own = slice(h * E, (h + 1) * E)
+            key = pair_ref[:, head_columns(h, width, 0)]
+            value = pair_ref[:, head_columns(h, width, 1)]
+            if before is not None:
+                key_before = refs[2][:, head_columns(h, width, 0)]
+                value_before = refs[2][:, head_columns(h, width, 1)]
+            for spot in range(0, count, rows):
+                here = slice(spot, spot + rows)
+                mask = None
+                if before is not None:
+                    mask = key_before, scalar_refs[0][0], scalar_refs[1][0], rows
+                scores, below = score_parts(query_ref[here, own], key, mask, spot)
+                top = jnp.max(scores, axis=0, keepdims=True)
+                powers = jnp.exp(scores - top)
+                total = jnp.sum(powers, axis=0, keepdims=True)
+                chances = (powers * (1.0 / total)).astype(LOW)
+                if before is None:
+                    result = dot_first(value, chances)
+                else:
+                    none = jnp.zeros_like(chances)
+                    result = dot_first(value, jnp.where(below, chances, none)) + dot_first(
+                        value_before, jnp.where(below, none, chances)
+                    )
+                result_ref[here, own] = result.T.astype(LOW)
+                log_ref[h : h + 1, here] = top + jnp.log(total)
+
+    shapes = (
+        jax.ShapeDtypeStruct((count, width), LOW),
+        jax.ShapeDtypeStruct((heads, count), HIGH),
+    )
+    scores_count = heads * count * pair.shape[0]
+    return attention_kernel(
+        kernel, shapes, [], operands, scalars, (scores_count * len(operands), scores_count)
+    )
+
+
+def attend_back(queries, pair, logs, grad_result, before=None):
+    count, width = queries.shape
+    heads = width // E
+    rows = min(count, ATTEND_STEP)
+    keys = pair.shape[0]
+    scalars = [] if before is None else [part.reshape(1) for part in before[1:]]
+    operands = [queries, logs, grad_result, pair] + ([] if before is None else [before[0]])
+
+    def kernel(*refs):
+        scalar_refs, refs = refs[: len(scalars)], refs[len(scalars) :]
+        query_ref, log_ref, grad_ref, pair_ref = refs[:4]
+        outs = refs[len(operands) :]
+        query_out, pair_out = outs[:2]
+        for h in range(heads):
+            own = slice(h * E, (h + 1) * E)
+            key_at, value_at = head_columns(h, width, 0), head_columns(h, width, 1)
+            key, value = pair_ref[:, key_at], pair_ref[:, value_at]
+            if before is not None:
+                key_before, value_before = refs[4][:, key_at], refs[4][:, value_at]
+            sums = [jnp.zeros((keys, E), HIGH)] * 4
+            for spot in range(0, count, rows):
+                here = slice(spot, spot + rows)
+                query, grad = query_ref[here, own], grad_ref[here, own]
+                mask = None
+                if before is not None:
+                    mask = key_before, scalar_refs[0][0], scalar_refs[1][0], rows
+                scores, below = score_parts(query, key, mask, spot)
+                chances = jnp.exp(scores - log_ref[h : h + 1, here])
+                grad_chances = dot_second(value, grad)
+                if before is not None:
+                    grad_chances = jnp.where(below, grad_chances, dot_second(value_before, grad))
+                inner = jnp.sum(chances * grad_chances, axis=0, keepdims=True)
+                grad_scores = (chances * (grad_chances - inner) * E ** (-0.5)).astype(LOW)
+                chances = chances.astype(LOW)
+                if before is None:
+                    query_grad = dot_first(key, grad_scores)
+                    terms = [plain_dot(grad_scores, query), plain_dot(chances, grad)]
+                else:
+                    none = jnp.zeros_like(chances)
+                    scores_now = jnp.where(below, grad_scores, none)
+                    scores_before = jnp.where(below, none, grad_scores)
+                    query_grad = dot_first(key, scores_now) + dot_first(key_before, scores_before)
+                    terms = [
+                        plain_dot(scores_now, query),
+                        plain_dot(jnp.where(below, chances, none), grad),
+                        plain_dot(scores_before, query),
+                        plain_dot(jnp.where(below, none, chances), grad),
+                    ]
+                query_out[here, own] = query_grad.T
+                sums = [one + two for one, two in zip(sums, terms)]
+            pair_out[:, key_at] = sums[0]
+            pair_out[:, value_at] = sums[1]
+            if before is not None:
+                outs[2][:, key_at] = sums[2].astype(LOW)
+                outs[2][:, value_at] = sums[3].astype(LOW)
+
+    shapes = [
+        jax.ShapeDtypeStruct((count, width), HIGH),
+        jax.ShapeDtypeStruct((keys, 2 * width), HIGH),
+    ]
+    if before is not None:
+        shapes.append(jax.ShapeDtypeStruct((keys, 2 * width), LOW))
+    scores_count = heads * count * keys
+    return attention_kernel(
+        kernel,
+        tuple(shapes),
+        [],
+        operands,
+        scalars,
+        (scores_count * (5 if before is None else 10), scores_count),
+    )
 
 
 def body(
@@ -407,8 +486,8 @@
     out_tok_flat = out_tok.reshape(2 * width, model_width)
     out_state_flat = out_state.reshape(2 * width, model_width)
 
-    row_ids = (jnp.arange(block_rows) + tp_index * piece_rows) % block_rows
-    below = row_ids[None, :] <= row_ids[:, None]
+    shift = (tp_index * piece_rows).astype(jnp.int32)
+    start_flag = starts_here.astype(jnp.int32)
     token_rows = turned(tokens, tp_index * piece_rows)
 
     def natural(pieces):
@@ -421,7 +500,8 @@
     win_queries, win_pair = win_qkv[:, :width], win_qkv[:, width:]
     onward = [(s, s + 1) for s in range(lax.axis_size("seq")) if (s + 1) % CHAIN]
     win_prev = lax.ppermute(win_pair, "seq", onward)
-    win_heads, win_logs = band_attend(win_queries, win_pair, win_prev, below, starts_here)
+    win_before = win_prev, shift, start_flag
+    win_heads, win_logs = attend(win_queries, win_pair, win_before)
     cotangent, qkv_tok, qkv_state, gate_bias, init_state, _ = lax.optimization_barrier(
         (cotangent, qkv_tok, qkv_state, gate_bias, init_state, win_heads)
     )
@@ -447,7 +527,7 @@
         state_qkv = plain_dot(state_normed, qkv_state_flat).astype(LOW)
         state_queries = state_qkv[:, :width]
         state_pair = jnp.concatenate(pos_gather(state_qkv[:, width:]))
-        own, own_logs = full_attend(state_queries, state_pair[:, :width], state_pair[:, width:])
+        own, own_logs = attend(state_queries, state_pair)
         return state_normed, state_queries, state_pair, own, own_logs
 
     started = state_start(tied(init_slab, win_ffn_in[1]))
@@ -461,6 +541,7 @@
     pairs_all = pos_gather(pair)
     pair_prev = jnp.where(position % 2 == 1, pairs_all[1], pairs_all[3])
     pairs_stack = jnp.stack(pairs_all)
+    before = pair_prev, shift, start_flag
 
     def state_rest(incoming, state_heads, meanwhile=lambda heads: ()):
         update = tp_total(plain_dot(state_heads, out_state_flat))
@@ -478,7 +559,7 @@
     own_done = []
 
     def own_attention(after):
-        own_done.extend(band_attend(tied(queries, after), pair, pair_prev, below, starts_here))
+        own_done.extend(attend(tied(queries, after), pair, before))
         return own_done[:1]
 
     state_slab = init_slab
@@ -494,9 +575,7 @@
             turns.append((incoming, state_normed, state_queries, state_pair, own))
             break
         token_pair = choose(pairs_stack, position ^ turn)
-        cross, cross_logs = full_attend(
-            state_queries, token_pair[:, :width], token_pair[:, width:]
-        )
+        cross, cross_logs = attend(state_queries, token_pair)
         state_heads = jnp.concatenate([own, cross], axis=1)
         first = (incoming, state_normed, state_queries, state_pair)
         if turn == 1:
@@ -510,9 +589,7 @@
     for turn in range(1, CHAIN):
         my_state_pair = jnp.where(position == turn, turns[turn][3], my_state_pair)
 
-    cross_heads, cross_token_logs = full_attend(
-        queries, my_state_pair[:, :width], my_state_pair[:, width:]
-    )
+    cross_heads, cross_token_logs = attend(queries, my_state_pair)
     token_heads = jnp.concatenate([own_heads, cross_heads], axis=1)
     proj_total = tp_scatter(
         [plain_dot(part, out_tok_flat) for part in split_rows(token_heads, n_tp)]
@@ -532,16 +609,10 @@
     grad_proj_pieces = tp_gather(grad_mixed.astype(LOW))
     grad_proj = jnp.concatenate(grad_proj_pieces)
     grad_heads = dot_second(grad_proj, out_tok_flat).astype(LOW)
-    cross_query_grad, cross_key_grad, cross_value_grad = full_attend_back(
-        queries,
-        my_state_pair[:, :width],
-        my_state_pair[:, width:],
-        cross_token_logs,
-        grad_heads[:, width:],
-    )
-    cross_pair_grad = split_rows(
-        jnp.concatenate([cross_key_grad, cross_value_grad], axis=1), CHAIN
-    )
+    cross_query_grad, cross_pair_grad = attend_back(
+        queries, my_state_pair, cross_token_logs, grad_heads[:, width:]
+    )
+    cross_pair_grad = split_rows(cross_pair_grad, CHAIN)
     cross_pieces = jnp.stack(
         [cross_pair_grad[0]]
         + [swap(cross_pair_grad[k].astype(LOW), k).astype(HIGH) for k in range(1, CHAIN)]
@@ -549,28 +620,22 @@
     homeward = [(s, s - 1) for s in range(lax.axis_size("seq")) if s % CHAIN]
 
     def own_back():
-        query_grad, pair_grad, prev_grad = band_attend_back(
-            queries,
-            pair,
-            pair_prev,
-            below,
-            starts_here,
-            own_token_logs,
-            tied(grad_heads[:, :width], cross_pieces),
+        query_grad, pair_grad, prev_grad = attend_back(
+            queries, pair, own_token_logs, tied(grad_heads[:, :width], cross_pieces), before
         )
         returned = lax.ppermute(prev_grad, "seq", homeward)
         return query_grad + cross_query_grad, pair_grad + returned.astype(HIGH)
 
     incoming, _, state_queries, _, own = turns[CHAIN - 1]
     token_pair = choose(pairs_stack, position ^ (CHAIN - 1))
-    cross, _ = full_attend(
-        tied(state_queries, grad_heads), token_pair[:, :width], token_pair[:, width:]
-    )
+    cross, _ = attend(tied(state_queries, grad_heads), token_pair)
     last_heads = jnp.concatenate([own, cross], axis=1)
     last_update = tp_total(plain_dot(last_heads, out_state_flat))
 
     def last_state(after):
-        state_slab, _ = state_end(incoming_last, tied(last_update, after))
+        return state_end(incoming_last, tied(last_update, after))[0]
+
+    def states_between(state_slab):
         states_stack = jnp.stack(states_out + [own_rows(state_slab)])
         pieces = [choose(states_stack, position)]
         pieces += [swap(choose(states_stack, position ^ k), k) for k in range(1, CHAIN)]
@@ -613,52 +678,38 @@
             ).astype(LOW)
             grad_sffn_in = tp_total(dot_second(grad_state_hidden, up_state))
             if turn == CHAIN - 2:
-                token_grads = SeqSum(
+                token_grads = ScatterSum(
                     weight_grads(
                         [
                             (tied(tuple(ffn_in), grad_state_hidden), grad_hidden),
                             ([cotangent_rows], active),
                             (grad_proj_pieces, [token_heads]),
-                        ]
+                        ],
+                        False,
                     )
                 )
-                grad_sffn_in = tied(grad_sffn_in, token_grads.other)
-            if turn == CHAIN - 3:
-                step = token_grads.one_first(grad_state_hidden)
-            if turn == CHAIN - 4:
-                grad_sffn_in = tied(grad_sffn_in, step)
-                step = token_grads.one_last(grad_state_hidden)
+                grad_sffn_in = tied(grad_sffn_in, token_grads.grads)
             grad_mid = keep_two * grad_state + norm_back(mid_state, norm_sffn, grad_sffn_in)
             bias_one = bias_one + jnp.sum(grad_mid * (incoming - update), axis=0)
             grad_update = ((1.0 - keep_one) * grad_mid).astype(LOW)
             grad_state_heads = dot_second(grad_update, out_state_flat).astype(LOW)
-            own_q, own_k, own_v = full_attend_back(
-                state_queries,
-                state_pair[:, :width],
-                state_pair[:, width:],
-                own_logs,
-                grad_state_heads[:, :width],
+            own_q, own_pair = attend_back(
+                state_queries, state_pair, own_logs, grad_state_heads[:, :width]
             )
-            pair_total = pair_total + pos_scatter(
-                split_rows(jnp.concatenate([own_k, own_v], axis=1), CHAIN)
+            pair_total = pair_total + pos_scatter(split_rows(own_pair, CHAIN))
+            cross_q, token_pair_grads[turn] = attend_back(
+                state_queries, token_pair, cross_logs, grad_state_heads[:, width:]
             )
-            cross_q, cross_k, cross_v = full_attend_back(
-                state_queries,
-                token_pair[:, :width],
-                token_pair[:, width:],
-                cross_logs,
-                grad_state_heads[:, width:],
-            )
-            token_pair_grads[turn] = jnp.concatenate([cross_k, cross_v], axis=1)
             query_total = own_q + cross_q
             kept_rest.append(
                 (state_heads, grad_update, state_ffn_in, grad_state_hidden, state_active, grad_mlp)
             )
         if turn == CHAIN - 2:
-            slabs = last_state(grad_mid)
+            last_slab = last_state(grad_mid)
+            pair_total = tied(pair_total, last_slab)
+        if turn == CHAIN - 3:
+            slabs = states_between(tied(last_slab, grad_mid))
             pair_total = tied(pair_total, slabs)
-        if turn == CHAIN - 3:
-            pair_total = tied(pair_total, step)
         if turn == CHAIN - 4:
             state_rows_out = states_whole(tied(slabs, grad_mid))
             pair_total = tied(pair_total, state_rows_out)
@@ -670,10 +721,6 @@
         if turn == CHAIN - 1:
             query_grad, pair_grad = own_back()
             grad_state_normed = tied(grad_state_normed, query_grad)
-        if turn == CHAIN - 2:
-            grad_state_normed = tied(grad_state_normed, token_grads.cores(grad_state_qkv))
-        if turn == CHAIN - 3:
-            step = token_grads.two_first(grad_state_qkv)
         grad_incoming = norm_back(incoming, norm_state, grad_state_normed)
         if grad_state is not None:
             grad_incoming = keep_one * grad_mid + grad_incoming
@@ -697,34 +744,30 @@
     )
     qkv_parts = list(zip(*kept_qkv))
     rest_parts = list(zip(*kept_rest))
-    state_grads = SeqSum(
+    state_grads = ScatterSum(
         weight_grads(
             [
                 (qkv_parts[0], qkv_parts[1]),
                 (rest_parts[1], rest_parts[0]),
                 (rest_parts[2], rest_parts[3]),
                 (rest_parts[5], rest_parts[4]),
-            ]
+            ],
+            False,
         )
     )
-    pair_grad = tied(pair_grad, step, layer_output, state_grads.other)
+    pair_grad = tied(pair_grad, layer_output, state_grads.grads)
     grad_qkv = jnp.concatenate([query_grad, pair_grad], axis=1).astype(LOW)
     grad_normed = tp_scatter(
         [dot_second(part, qkv_tok_flat) for part in split_rows(grad_qkv, n_tp)]
     )
-    grad_normed = tied(grad_normed, state_grads.cores(grad_qkv))
     grad_layer_one = grad_mixed + norm_back(layer_one, norm_tok, grad_normed)
 
-    step = token_grads.two_last(grad_layer_one)
     grad_win_out = tp_gather(grad_layer_one.astype(LOW))
     grad_win_hidden = [
         gelu_slope(part, dot_second(grad, down_win)).astype(LOW)
         for part, grad in zip(win_hidden, grad_win_out)
     ]
-    parts = [dot_second(part, up_win) for part in grad_win_hidden]
-    grad_win_ffn_in = tp_scatter(parts)
-    step = step, parts
-    step = state_grads.one_first(step), state_grads.two_first(step)
+    grad_win_ffn_in = tp_scatter([dot_second(part, up_win) for part in grad_win_hidden])
 
     middle_grads = SeqSum(
         weight_grads(
@@ -735,20 +778,18 @@
             ]
         )
     )
-    grad_win_ffn_in = tied(grad_win_ffn_in, *step, middle_grads.other)
+    grad_win_ffn_in = tied(grad_win_ffn_in, middle_grads.other)
     grad_win_mixed = grad_layer_one + norm_back(win_mixed, norm_wffn, grad_win_ffn_in)
     grad_win_pieces = tp_gather(grad_win_mixed.astype(LOW))
-    step = middle_grads.cores(grad_win_mixed), state_grads.one_last(grad_win_mixed)
-    grad_win_proj = tied(jnp.concatenate(grad_win_pieces), *step)
+    step = middle_grads.cores(grad_win_mixed)
+    grad_win_proj = tied(jnp.concatenate(grad_win_pieces), step)
     grad_win_heads = dot_second(grad_win_proj, out_win).astype(LOW)
-    win_query_grad, win_pair_grad, win_prev_grad = band_attend_back(
-        win_queries, win_pair, win_prev, below, starts_here, win_logs, grad_win_heads
+    win_query_grad, win_pair_grad, win_prev_grad = attend_back(
+        win_queries, win_pair, win_logs, grad_win_heads, win_before
     )
     win_returned = lax.ppermute(win_prev_grad, "seq", homeward)
     after = win_query_grad, win_pair_grad
-    step = state_grads.two_last(after)
-    middle_grads.one_first(after)
-    middle_grads.two_first(after)
+    step = middle_grads.one_first(grad_win_heads), middle_grads.two_first(grad_win_heads)
     first_grad = own_rows(first_incoming_grad(after))
     init_grad = init_grad + jnp.where(flags[0], first_grad, 0.0)
     win_pair_grad = win_pair_grad + tied(win_returned, step).astype(HIGH)

time: 886 us -> 870 us (0.982)
  matrix products: 142 us -> 78.9 us
  Pallas kernels: 18.4 us -> 51.2 us
  starting transfers between devices: 224 us -> 192 us
  local copies, waits for them, and re-layouts: 70.7 us -> 85.7 us
  waiting for transfers between devices: 312 us -> 327 us
  between operations: 7.95 us -> 21.1 us
    ppermute x48 -> x24, starting transfers between devices: 70.3 us -> 34.8 us  [stage(): total = total + lax.ppermute(sent, 'seq', self.pairs(*step(k))).astype(HIGH)]
    pallas_call x4 -> x24, Pallas kernels: 18.4 us -> 51.2 us  [the longest x20 32.6 us: attention_kernel(): pl.pallas_call(kernel, out_shape=shapes, in_specs=[in_smem] * len(scalars...]
    ppermute x69, waiting for transfers between devices: 156 us -> 188 us  [tp_to(): return lax.ppermute(array, 'tp', [(i, (i + k) % n) for i in range(n)])]
    dot_general x91 -> x39, matrix products: 55.3 us -> 30.4 us  [dot_second(): lax.dot_general(former, latter, (((1,), (1,)), ((), ())), preferred_eleme...]
    dot_general x44 -> x0, matrix products: 19.8 us -> none  [dot_first(): lax.dot_general(former, latter, (((0,), (0,)), ((), ())), preferred_eleme...]
    dot_general x89 -> x41, matrix products: 66.5 us -> 48.4 us  [plain_dot(): return jnp.dot(former, latter, preferred_element_type=HIGH)]
    unnamed x698 -> x744, local copies, waits for them, and re-layouts: 32.3 us -> 45.6 us
    ppermute x33 -> x31, waiting for transfers between devices: 52.9 us -> 45.8 us  [swap(): return lax.ppermute(array, 'seq', [(s, s ^ k) for s in range(n)])]
  transfers between devices with their start and end apart: 183 -> 159, of which waited for: 90 -> 83; matrix products, arithmetic and copies ran while one was open for 19% -> 17% of each run, Pallas kernels for 2% -> 5%
where the time goes in v6:
time: 870 us; the launch traced here: 859 us
  waiting for transfers between devices  327 us (38%)
  starting transfers between devices  192 us (22%)
  other arithmetic  104 us (12%)
  local copies, waits for them, and re-layouts  85.7 us (10%)
  matrix products  78.9 us (9%)
  Pallas kernels  51.2 us (6%)
  between operations  21.1 us (2%)
    ppermute x69, waiting for transfers between devices, tp_to(): return lax.ppermute(array, 'tp', [(i, (i + k) % n) for i in range(n)])  188 us
    ppermute x69, starting transfers between devices, tp_to(): return lax.ppermute(array, 'tp', [(i, (i + k) % n) for i in range(n)])  89.3 us
    ppermute x30, waiting for transfers between devices, tp_from(): return lax.ppermute(array, 'tp', [((i + k) % n, i) for i in range(n)])  53.3 us
    dot_general x41, matrix products, plain_dot(): return jnp.dot(former, latter, preferred_element_type=HIGH)  48.4 us
    ppermute x31, waiting for transfers between devices, swap(): return lax.ppermute(array, 'seq', [(s, s ^ k) for s in range(n)])  45.8 us
    unnamed x744, local copies, waits for them, and re-layouts  45.6 us
    ppermute x30, starting transfers between devices, tp_from(): return lax.ppermute(array, 'tp', [((i + k) % n, i) for i in range(n)])  45.5 us
    ppermute x24, waiting for transfers between devices, stage(): total = total + lax.ppermute(sent, 'seq', self.pairs(*step(k))).astype(HIGH)  39.4 us
  transfers between devices with their start and end apart: 159, of which 83 were waited for; matrix products, arithmetic and copies ran while one was open for 17% of the time, Pallas kernels for 5%

profile of v6, /device:TPU:0, one launch (start us, length us, event | category | flops | bytes accessed | tf_op | source)
XLA Modules:
  0.0 859.4 jit_solution(12676671909159842795)
XLA Ops:
  32.2 6.3 collective-permute-done.2
  53.3 6.9 collective-permute-start.11
  97.2 6.9 collective-permute-done.14.refs_2_
  109.6 12.2 %collective-permute-done.17 = bf16[512,512]{1,0:T(8,128)(2,1)} collective-permute-done((bf16[512,512]{1,0:T(8,128)(2,1)S(1)}, bf16[512,512]{1,0:T(8,128)(2,1)}, u32[]{:S(2)}, u32[]{:S(2)}) %collective-permute-start.17) | collective-permute-done | bytes 524320 | tf_op jit(solution)/shard_map/ppermute | solution.py:120
  133.1 9.8 %collective-permute-done.21 = bf16[128,1024]{1,0:T(8,128)(2,1)S(1)} collective-permute-done((bf16[128,1024]{1,0:T(8,128)(2,1)S(1)}, bf16[128,1024]{1,0:T(8,128)(2,1)S(1)}, u32[]{:S(2)}, u32[]{:S(2)}) %collective-permute-start.21) | collective-permute-done | bytes 262176 | tf_op jit(solution)/shard_map/ppermute | solution.py:84
  153.8 6.6 collective-permute-done.24
  160.4 5.1 collective-permute-done.23
  188.8 7.2 collective-permute-done.29
  204.2 6.0 collective-permute-done.33
  210.2 5.8 collective-permute-done.32
  231.0 6.2 collective-permute-done.39
  237.2 6.2 collective-permute-done.38
  251.9 8.2 collective-permute-done.42
  296.1 5.1 collective-permute-done.47
  307.3 10.5 %collective-permute-done.49.refs_1_ = bf16[128,1024]{1,0:T(8,128)(2,1)S(1)} collective-permute-done((bf16[128,1024]{1,0:T(8,128)(2,1)S(1)}, bf16[128,1024]{1,0:T(8,128)(2,1)S(1)}, u32[]{:S(2)}, u32[]{:S(2)}) %collective-permute-start.49) | collective-permute-done | bytes 262176 | tf_op jit(solution)/shard_map/ppermute | solution.py:79
  330.1 5.8 collective-permute-done.52
  349.2 6.8 collective-permute-done.56.refs_15_
  433.0 6.2 collective-permute-done.73
  447.7 8.1 collective-permute-done.77
  501.6 5.6 collective-permute-done.88
  507.2 5.8 collective-permute-done.87
  559.5 5.7 collective-permute-done.92
  570.3 5.2 shard_map.418
  578.3 7.3 collective-permute-done.97
  619.3 6.3 collective-permute-start.107
  625.7 5.9 shard_map.419
  647.8 11.1 %collective-permute-done.114 = bf16[128,1024]{1,0:T(8,128)(2,1)S(1)} collective-permute-done((bf16[128,1024]{1,0:T(8,128)(2,1)S(1)}, bf16[128,1024]{1,0:T(8,128)(2,1)S(1)}, u32[]{:S(2)}, u32[]{:S(2)}) %collective-permute-start.114) | collective-permute-done | bytes 262176 | tf_op jit(solution)/shard_map/ppermute | solution.py:79
  676.8 9.9 %collective-permute-done.134 = bf16[128,1024]{1,0:T(8,128)(2,1)S(1)} collective-permute-done((bf16[128,1024]{1,0:T(8,128)(2,1)S(1)}, bf16[128,1024]{1,0:T(8,128)(2,1)S(1)}, u32[]{:S(2)}, u32[]{:S(2)}) %collective-permute-start.134) | collective-permute-done | bytes 262176 | tf_op jit(solution)/shard_map/ppermute | solution.py:84
  691.3 5.6 collective-permute-done.132
  711.3 6.0 collective-permute-done.120
  719.7 9.4 %collective-permute-done.122 = bf16[4,32,1408]{2,1,0:T(8,128)(2,1)S(1)} collective-permute-done((bf16[4,32,1408]{2,1,0:T(8,128)(2,1)S(1)}, bf16[4,32,1408]{2,1,0:T(8,128)(2,1)S(1)}, u32[]{:S(2)}, u32[]{:S(2)}) %collective-permute-start.122) | collective-permute-done | bytes 360480 | tf_op jit(solution)/shard_map/ppermute | solution.py:249
  731.0 9.1 %collective-permute-done.124 = bf16[4,32,1408]{2,1,0:T(8,128)(2,1)S(1)} collective-permute-done((bf16[4,32,1408]{2,1,0:T(8,128)(2,1)S(1)}, bf16[4,32,1408]{2,1,0:T(8,128)(2,1)S(1)}, u32[]{:S(2)}, u32[]{:S(2)}) %collective-permute-start.124) | collective-permute-done | bytes 360480 | tf_op jit(solution)/shard_map/ppermute | solution.py:249
  (1421 shorter events, 609.7 us)
Async XLA Ops:
  7.2 733.9 %reduce-scatter.3.cloned.1.call-start = ((), (), s32[]{:S(2)}) async-start(), calls=%async_computation.2 | async-start | bytes 5406720 | tf_op jit(solution)/shard_map/reduce_scatter | solution.py:212
  48.9 20.4 %collective-permute-start.8 = (bf16[128,1024]{1,0:T(8,128)(2,1)S(1)}, bf16[128,1024]{1,0:T(8,128)(2,1)S(1)}, u32[]{:S(2)}, u32[]{:S(2)}) collective-permute-start(bf16[128,1024]{1,0:T(8,128)(2,1)S(1)} %multiply_convert_fusion.24.refs_5_), channel_id=1, source_target_pairs={{3,0},{0,1},{1,2},{2,3},{7,4},{4,5},{5,6},{6,7},{11,8},{8,9},{9,10... | collective-permute-start | bytes 786440 | tf_op jit(solution)/shard_map/ppermute | solution.py:79
  53.3 22.1 %collective-permute-start.11 = (bf16[128,512]{1,0:T(8,128)(2,1)S(1)}, bf16[128,512]{1,0:T(8,128)(2,1)S(1)}, u32[]{:S(2)}, u32[]{:S(2)}) collective-permute-start(bf16[128,512]{1,0:T(8,128)(2,1)S(1)} %slice.449), channel_id=1, source_target_pairs={{0,8},{4,12},{8,0},{12,4},{16,24},{20,28},{24,16},{28,20},{32,40},... | collective-permute-start | bytes 393224 | tf_op jit(solution)/shard_map/ppermute | solution.py:120
  60.1 18.1 %collective-permute-start.10 = (bf16[128,512]{1,0:T(8,128)(2,1)S(1)}, bf16[128,512]{1,0:T(8,128)(2,1)S(1)}, u32[]{:S(2)}, u32[]{:S(2)}) collective-permute-start(bf16[128,512]{1,0:T(8,128)(2,1)S(1)} %slice.449), channel_id=1, source_target_pairs={{0,4},{4,0},{8,12},{12,8},{16,20},{20,16},{24,28},{28,24},{32,36},... | collective-permute-start | bytes 393224 | tf_op jit(solution)/shard_map/ppermute | solution.py:120
  64.5 16.1 %collective-permute-start.5 = (bf16[128,1024]{1,0:T(8,128)(2,1)S(1)}, bf16[128,1024]{1,0:T(8,128)(2,1)S(1)}, u32[]{:S(2)}, u32[]{:S(2)}) collective-permute-start(bf16[128,1024]{1,0:T(8,128)(2,1)S(1)} %convolution_convert_fusion.24), channel_id=1, source_target_pairs={{0,2},{1,3},{2,0},{3,1},{4,6},{5,7},{6,4},{7,5},{8,10},{9,11},{10,... | collective-permute-start | bytes 786440 | tf_op jit(solution)/shard_map/ppermute | solution.py:84
  87.9 16.2 %collective-permute-start.14 = (bf16[128,1024]{1,0:T(8,128)(2,1)S(1)}, bf16[128,1024]{1,0:T(8,128)(2,1)}, u32[]{:S(2)}, u32[]{:S(2)}) collective-permute-start(bf16[128,1024]{1,0:T(8,128)(2,1)S(1)} %multiply_convert_fusion.19.refs_0_), channel_id=1, source_target_pairs={{2,0},{3,1},{0,2},{1,3},{6,4},{7,5},{4,6},{5,7},{10,8},{11,9},{8,1... | collective-permute-start | bytes 786440 | tf_op jit(solution)/shard_map/ppermute | solution.py:79
  286.0 15.3 %collective-permute-start.47 = (bf16[128,1024]{1,0:T(8,128)(2,1)S(1)}, bf16[128,1024]{1,0:T(8,128)(2,1)S(1)}, u32[]{:S(2)}, u32[]{:S(2)}) collective-permute-start(bf16[128,1024]{1,0:T(8,128)(2,1)S(1)} %convolution_convert_fusion.20), channel_id=1, source_target_pairs={{0,1},{1,2},{2,3},{3,0},{4,5},{5,6},{6,7},{7,4},{8,9},{9,10},{10,1... | collective-permute-start | bytes 786440 | tf_op jit(solution)/shard_map/ppermute | solution.py:84
  302.1 25.0 %collective-permute-start.51 = (bf16[128,1024]{1,0:T(8,128)(2,1)S(1)}, bf16[128,1024]{1,0:T(8,128)(2,1)S(1)}, u32[]{:S(2)}, u32[]{:S(2)}) collective-permute-start(bf16[128,1024]{1,0:T(8,128)(2,1)S(1)} %multiply_convert_fusion.12.refs_0_), channel_id=1, source_target_pairs={{3,0},{0,1},{1,2},{2,3},{7,4},{4,5},{5,6},{6,7},{11,8},{8,9},{9,10... | collective-permute-start | bytes 786440 | tf_op jit(solution)/shard_map/ppermute | solution.py:79
  302.2 18.6 %collective-permute-start.50 = (bf16[128,1024]{1,0:T(8,128)(2,1)S(1)}, bf16[128,1024]{1,0:T(8,128)(2,1)S(1)}, u32[]{:S(2)}, u32[]{:S(2)}) collective-permute-start(bf16[128,1024]{1,0:T(8,128)(2,1)S(1)} %multiply_convert_fusion.12.refs_0_), channel_id=1, source_target_pairs={{2,0},{3,1},{0,2},{1,3},{6,4},{7,5},{4,6},{5,7},{10,8},{11,9},{8,1... | collective-permute-start | bytes 786440 | tf_op jit(solution)/shard_map/ppermute | solution.py:79
  370.8 16.1 %collective-permute-start.62 = (bf16[128,1024]{1,0:T(8,128)(2,1)S(1)}, bf16[128,1024]{1,0:T(8,128)(2,1)S(1)}, u32[]{:S(2)}, u32[]{:S(2)}) collective-permute-start(bf16[128,1024]{1,0:T(8,128)(2,1)S(1)} %get-tuple-element.480), channel_id=1, source_target_pairs={{0,1},{1,2},{2,3},{3,0},{4,5},{5,6},{6,7},{7,4},{8,9},{9,10},{10,1... | collective-permute-start | bytes 786440 | tf_op jit(solution)/shard_map/ppermute | solution.py:84
  370.8 16.1 %collective-permute-start.61 = (bf16[128,1024]{1,0:T(8,128)(2,1)S(1)}, bf16[128,1024]{1,0:T(8,128)(2,1)S(1)}, u32[]{:S(2)}, u32[]{:S(2)}) collective-permute-start(bf16[128,1024]{1,0:T(8,128)(2,1)S(1)} %get-tuple-element.480), channel_id=1, source_target_pairs={{0,2},{1,3},{2,0},{3,1},{4,6},{5,7},{6,4},{7,5},{8,10},{9,11},{10,... | collective-permute-start | bytes 786440 | tf_op jit(solution)/shard_map/ppermute | solution.py:84
  372.7 21.8 %collective-permute-start.71 = (bf16[128,1024]{1,0:T(8,128)(2,1)S(1)}, bf16[128,1024]{1,0:T(8,128)(2,1)S(1)}, u32[]{:S(2)}, u32[]{:S(2)}) collective-permute-start(bf16[128,1024]{1,0:T(8,128)(2,1)S(1)} %get-tuple-element.484), channel_id=1, source_target_pairs={{0,3},{1,0},{2,1},{3,2},{4,7},{5,4},{6,5},{7,6},{8,11},{9,8},{10,9... | collective-permute-start | bytes 786440 | tf_op jit(solution)/shard_map/ppermute | solution.py:84
  374.4 23.1 %collective-permute-start.70 = (bf16[128,1024]{1,0:T(8,128)(2,1)S(1)}, bf16[128,1024]{1,0:T(8,128)(2,1)S(1)}, u32[]{:S(2)}, u32[]{:S(2)}) collective-permute-start(bf16[128,1024]{1,0:T(8,128)(2,1)S(1)} %get-tuple-element.484), channel_id=1, source_target_pairs={{0,1},{1,2},{2,3},{3,0},{4,5},{5,6},{6,7},{7,4},{8,9},{9,10},{10,1... | collective-permute-start | bytes 786440 | tf_op jit(solution)/shard_map/ppermute | solution.py:84
  423.7 15.5 %collective-permute-start.73 = (bf16[128,1024]{1,0:T(8,128)(2,1)}, bf16[128,1024]{1,0:T(8,128)(2,1)S(1)}, u32[]{:S(2)}, u32[]{:S(2)}) collective-permute-start(bf16[128,1024]{1,0:T(8,128)(2,1)} %get-tuple-element.486), channel_id=1, source_target_pairs={{0,1},{1,2},{2,3},{3,0},{4,5},{5,6},{6,7},{7,4},{8,9},{9,10},{10,1... | collective-permute-start | bytes 786440 | tf_op jit(solution)/shard_map/ppermute | solution.py:84
  524.9 311.2 %reduce-scatter.5.cloned.1.call-start = ((), (), s32[]{:S(2)}) async-start(), calls=%async_computation.3 | async-start | bytes 7028736 | tf_op jit(solution)/shard_map/reduce_scatter | solution.py:212
  538.6 15.4 %collective-permute-start.102 = (bf16[4,32,1024]{2,1,0:T(8,128)(2,1)S(1)}, bf16[4,32,1024]{2,1,0:T(8,128)(2,1)S(1)}, u32[]{:S(2)}, u32[]{:S(2)}) collective-permute-start(bf16[4,32,1024]{2,1,0:T(8,128)(2,1)S(1)} %copy-done.201), channel_id=1, source_target_pairs={{3,0},{0,1},{1,2},{2,3},{7,4},{4,5},{5,6},{6,7},{11,8},{8,9},{9,10... | collective-permute-start | bytes 786440 | tf_op jit(solution)/shard_map/ppermute | solution.py:79
  555.3 23.0 %collective-permute-start.95 = (bf16[512,512]{1,0:T(8,128)(2,1)}, bf16[512,512]{1,0:T(8,128)(2,1)}, u32[]{:S(2)}, u32[]{:S(2)}) collective-permute-start(bf16[512,512]{1,0:T(8,128)(2,1)} %get-tuple-element.170), channel_id=1, source_target_pairs={{4,0},{8,4},{12,8},{20,16},{24,20},{28,24},{36,32},{40,36},{44,40}... | collective-permute-start | bytes 1572872 | tf_op jit(solution)/shard_map/ppermute | solution.py:626
  567.7 18.0 %collective-permute-start.97 = (bf16[512,512]{1,0:T(8,128)(2,1)}, bf16[512,512]{1,0:T(8,128)(2,1)}, u32[]{:S(2)}, u32[]{:S(2)}) collective-permute-start(bf16[512,512]{1,0:T(8,128)(2,1)} %fusion.19), channel_id=1, source_target_pairs={{0,8},{4,12},{8,0},{12,4},{16,24},{20,28},{24,16},{28,20},{32,40},... | collective-permute-start | bytes 1572872 | tf_op jit(solution)/shard_map/ppermute | solution.py:120
  612.8 18.8 %collective-permute-start.111 = (bf16[128,1024]{1,0:T(8,128)(2,1)S(1)}, bf16[128,1024]{1,0:T(8,128)(2,1)S(1)}, u32[]{:S(2)}, u32[]{:S(2)}) collective-permute-start(bf16[128,1024]{1,0:T(8,128)(2,1)S(1)} %convolution_convert_fusion.7), channel_id=1, source_target_pairs={{0,3},{1,0},{2,1},{3,2},{4,7},{5,4},{6,5},{7,6},{8,11},{9,8},{10,9... | collective-permute-start | bytes 786440 | tf_op jit(solution)/shard_map/ppermute | solution.py:84
  634.3 25.3 %collective-permute-start.115 = (bf16[512,2816]{1,0:T(8,128)(2,1)}, bf16[512,2816]{1,0:T(8,128)(2,1)}, u32[]{:S(2)}, u32[]{:S(2)}) collective-permute-start(bf16[512,2816]{1,0:T(8,128)(2,1)} %get-tuple-element.181), channel_id=1, source_target_pairs={{0,4},{4,0},{8,12},{12,8},{16,20},{20,16},{24,28},{28,24},{32,36},... | collective-permute-start | bytes 8650760 | tf_op jit(solution)/shard_map/ppermute | solution.py:120
  643.5 15.4 %collective-permute-start.114 = (bf16[128,1024]{1,0:T(8,128)(2,1)S(1)}, bf16[128,1024]{1,0:T(8,128)(2,1)S(1)}, u32[]{:S(2)}, u32[]{:S(2)}) collective-permute-start(bf16[128,1024]{1,0:T(8,128)(2,1)S(1)} %get-tuple-element.313), channel_id=1, source_target_pairs={{3,0},{0,1},{1,2},{2,3},{7,4},{4,5},{5,6},{6,7},{11,8},{8,9},{9,10... | collective-permute-start | bytes 786440 | tf_op jit(solution)/shard_map/ppermute | solution.py:79
  643.5 15.4 %collective-permute-start.113 = (bf16[128,1024]{1,0:T(8,128)(2,1)S(1)}, bf16[128,1024]{1,0:T(8,128)(2,1)S(1)}, u32[]{:S(2)}, u32[]{:S(2)}) collective-permute-start(bf16[128,1024]{1,0:T(8,128)(2,1)S(1)} %get-tuple-element.313), channel_id=1, source_target_pairs={{2,0},{3,1},{0,2},{1,3},{6,4},{7,5},{4,6},{5,7},{10,8},{11,9},{8,1... | collective-permute-start | bytes 786440 | tf_op jit(solution)/shard_map/ppermute | solution.py:79
  669.7 33.3 %collective-permute-start.118 = (bf16[128,1024]{1,0:T(8,128)(2,1)S(1)}, bf16[128,1024]{1,0:T(8,128)(2,1)S(1)}, u32[]{:S(2)}, u32[]{:S(2)}) collective-permute-start(bf16[128,1024]{1,0:T(8,128)(2,1)S(1)} %copy-done.202), channel_id=1, source_target_pairs={{3,0},{0,1},{1,2},{2,3},{7,4},{4,5},{5,6},{6,7},{11,8},{8,9},{9,10... | collective-permute-start | bytes 786440 | tf_op jit(solution)/shard_map/ppermute | solution.py:79
  670.5 30.4 %collective-permute-start.117 = (bf16[128,1024]{1,0:T(8,128)(2,1)S(1)}, bf16[128,1024]{1,0:T(8,128)(2,1)S(1)}, u32[]{:S(2)}, u32[]{:S(2)}) collective-permute-start(bf16[128,1024]{1,0:T(8,128)(2,1)S(1)} %copy-done.202), channel_id=1, source_target_pairs={{2,0},{3,1},{0,2},{1,3},{6,4},{7,5},{4,6},{5,7},{10,8},{11,9},{8,1... | collective-permute-start | bytes 786440 | tf_op jit(solution)/shard_map/ppermute | solution.py:79
  674.3 15.8 %collective-permute-start.133 = (bf16[128,1024]{1,0:T(8,128)(2,1)S(1)}, bf16[128,1024]{1,0:T(8,128)(2,1)S(1)}, u32[]{:S(2)}, u32[]{:S(2)}) collective-permute-start(bf16[128,1024]{1,0:T(8,128)(2,1)S(1)} %get-tuple-element.498), channel_id=1, source_target_pairs={{0,1},{1,2},{2,3},{3,0},{4,5},{5,6},{6,7},{7,4},{8,9},{9,10},{10,1... | collective-permute-start | bytes 786440 | tf_op jit(solution)/shard_map/ppermute | solution.py:84
  676.3 20.6 %collective-permute-start.132 = (bf16[128,1024]{1,0:T(8,128)(2,1)S(1)}, bf16[128,1024]{1,0:T(8,128)(2,1)S(1)}, u32[]{:S(2)}, u32[]{:S(2)}) collective-permute-start(bf16[128,1024]{1,0:T(8,128)(2,1)S(1)} %get-tuple-element.498), channel_id=1, source_target_pairs={{0,2},{1,3},{2,0},{3,1},{4,6},{5,7},{6,4},{7,5},{8,10},{9,11},{10,... | collective-permute-start | bytes 786440 | tf_op jit(solution)/shard_map/ppermute | solution.py:84
  690.1 52.7 %collective-permute-start.119 = (bf16[512,512]{1,0:T(8,128)(2,1)}, bf16[512,512]{1,0:T(8,128)(2,1)}, u32[]{:S(2)}, u32[]{:S(2)}) collective-permute-start(bf16[512,512]{1,0:T(8,128)(2,1)} %get-tuple-element.186), channel_id=1, source_target_pairs={{4,0},{8,4},{12,8},{20,16},{24,20},{28,24},{36,32},{40,36},{44,40}... | collective-permute-start | bytes 1572872 | tf_op jit(solution)/shard_map/ppermute | solution.py:790
  696.9 20.4 %collective-permute-start.120 = (bf16[4,32,1408]{2,1,0:T(8,128)(2,1)S(1)}, bf16[4,32,1408]{2,1,0:T(8,128)(2,1)S(1)}, u32[]{:S(2)}, u32[]{:S(2)}) collective-permute-start(bf16[4,32,1408]{2,1,0:T(8,128)(2,1)S(1)} %get-tuple-element.390), channel_id=1, source_target_pairs={{0,16},{4,20},{8,24},{12,28},{16,0},{20,4},{24,8},{28,12},{32,48},... | collective-permute-start | bytes 1081352 | tf_op jit(solution)/shard_map/ppermute | solution.py:249
  700.9 28.2 %collective-permute-start.122 = (bf16[4,32,1408]{2,1,0:T(8,128)(2,1)S(1)}, bf16[4,32,1408]{2,1,0:T(8,128)(2,1)S(1)}, u32[]{:S(2)}, u32[]{:S(2)}) collective-permute-start(bf16[4,32,1408]{2,1,0:T(8,128)(2,1)S(1)} %get-tuple-element.391), channel_id=1, source_target_pairs={{0,24},{4,28},{8,0},{12,4},{16,8},{20,12},{24,16},{28,20},{32,56},... | collective-permute-start | bytes 1081352 | tf_op jit(solution)/shard_map/ppermute | solution.py:249
  700.9 29.2 %collective-permute-start.121 = (bf16[4,32,1408]{2,1,0:T(8,128)(2,1)S(1)}, bf16[4,32,1408]{2,1,0:T(8,128)(2,1)S(1)}, u32[]{:S(2)}, u32[]{:S(2)}) collective-permute-start(bf16[4,32,1408]{2,1,0:T(8,128)(2,1)S(1)} %get-tuple-element.392), channel_id=1, source_target_pairs={{0,8},{4,12},{8,16},{12,20},{16,24},{20,28},{24,0},{28,4},{32,40},... | collective-permute-start | bytes 1081352 | tf_op jit(solution)/shard_map/ppermute | solution.py:249
  703.0 28.0 %collective-permute-start.123 = (bf16[4,32,1408]{2,1,0:T(8,128)(2,1)S(1)}, bf16[4,32,1408]{2,1,0:T(8,128)(2,1)S(1)}, u32[]{:S(2)}, u32[]{:S(2)}) collective-permute-start(bf16[4,32,1408]{2,1,0:T(8,128)(2,1)S(1)} %get-tuple-element.387), channel_id=1, source_target_pairs={{0,64},{4,68},{8,72},{12,76},{16,80},{20,84},{24,88},{28,92},{32,9... | collective-permute-start | bytes 1081352 | tf_op jit(solution)/shard_map/ppermute | solution.py:249
  754.5 31.4 %collective-permute-start.135 = (bf16[512,1280]{1,0:T(8,128)(2,1)}, bf16[512,1280]{1,0:T(8,128)(2,1)}, u32[]{:S(2)}, u32[]{:S(2)}) collective-permute-start(bf16[512,1280]{1,0:T(8,128)(2,1)} %get-tuple-element.192), channel_id=1, source_target_pairs={{0,4},{4,0},{8,12},{12,8},{16,20},{20,16},{24,28},{28,24},{32,36},... | collective-permute-start | bytes 3932168 | tf_op jit(solution)/shard_map/ppermute | solution.py:120
  (481 other events, 4353.0 us)
Sparse Core Ops, SparseCore 0:
  525.0 89.1 reduce-scatter.2
  648.0 102.5 reduce-scatter.4

commit v7 on v6

--- a/solution.py
+++ b/solution.py
@@ -289,46 +289,86 @@
 ATTEND_STEP = 256
 
 
-def attention_kernel(kernel, shapes, scratch, operands, scalars, work):
+def fused(kernel, outs, operands, products, scalars=(), exps=0):
     in_vmem = pl.BlockSpec(memory_space=pltpu.VMEM)
     in_smem = pl.BlockSpec(memory_space=pltpu.SMEM)
-    products, exps = work
+    scalars = [jnp.asarray(scalar, jnp.int32).reshape(1) for scalar in scalars]
     return pl.pallas_call(
         kernel,
-        out_shape=shapes,
+        out_shape=[jax.ShapeDtypeStruct(shape, kind) for shape, kind in outs],
         in_specs=[in_smem] * len(scalars) + [in_vmem] * len(operands),
-        out_specs=tuple([in_vmem] * len(shapes)),
-        scratch_shapes=scratch,
-        compiler_params=pltpu.CompilerParams(vmem_limit_bytes=16 * 1024 * 1024),
+        out_specs=[in_vmem] * len(outs),
+        compiler_params=pltpu.CompilerParams(vmem_limit_bytes=20 * 1024 * 1024),
         cost_estimate=pl.CostEstimate(
-            flops=2 * products * E,
+            flops=2 * products,
             bytes_accessed=sum(2 * operand.size for operand in operands),
             transcendentals=exps,
         ),
     )(*scalars, *operands)
 
 
-def head_columns(head, width, part):
-    return slice(part * width + head * E, part * width + (head + 1) * E)
-
-
 def score_parts(query, key, before, spot):
     if before is None:
         return dot_second(key, query) * E ** (-0.5), None
-    key_before, shift, start, rows = before
-    count = key.shape[0]
-    key_ids = (lax.broadcasted_iota(jnp.int32, (count, rows), 0) + shift) % count
-    query_ids = (lax.broadcasted_iota(jnp.int32, (count, rows), 1) + shift + spot) % count
+    key_before, _, shift, start = before
+    shape = key.shape[0], query.shape[0]
+    key_ids = (lax.broadcasted_iota(jnp.int32, shape, 0) + shift) % shape[0]
+    query_ids = (lax.broadcasted_iota(jnp.int32, shape, 1) + shift + spot) % shape[0]
     below = key_ids <= query_ids
     scores = jnp.where(below, dot_second(key, query), dot_second(key_before, query))
     return jnp.where(below | (start == 0), scores * E ** (-0.5), MASKED), below
+
+
+def head_attend(query, key, value, before=None, spot=0):
+    scores, below = score_parts(query, key, before, spot)
+    top = jnp.max(scores, axis=0, keepdims=True)
+    powers = jnp.exp(scores - top)
+    total = jnp.sum(powers, axis=0, keepdims=True)
+    chances = (powers * (1.0 / total)).astype(LOW)
+    if before is None:
+        result = dot_first(value, chances)
+    else:
+        none = jnp.zeros_like(chances)
+        result = dot_first(value, jnp.where(below, chances, none)) + dot_first(
+            before[1], jnp.where(below, none, chances)
+        )
+    return result.T.astype(LOW), top + jnp.log(total)
+
+
+def head_back(query, key, value, log, grad, before=None, spot=0):
+    scores, below = score_parts(query, key, before, spot)
+    chances = jnp.exp(scores - log)
+    grad_chances = dot_second(value, grad)
+    if before is not None:
+        grad_chances = jnp.where(below, grad_chances, dot_second(before[1], grad))
+    inner = jnp.sum(chances * grad_chances, axis=0, keepdims=True)
+    grad_scores = (chances * (grad_chances - inner) * E ** (-0.5)).astype(LOW)
+    chances = chances.astype(LOW)
+    if before is None:
+        terms = [plain_dot(grad_scores, query), plain_dot(chances, grad)]
+        return dot_first(key, grad_scores).T, terms
+    none = jnp.zeros_like(chances)
+    scores_now = jnp.where(below, grad_scores, none)
+    scores_before = jnp.where(below, none, grad_scores)
+    terms = [
+        plain_dot(scores_now, query),
+        plain_dot(jnp.where(below, chances, none), grad),
+        plain_dot(scores_before, query),
+        plain_dot(jnp.where(below, none, chances), grad),
+    ]
+    query_grad = dot_first(key, scores_now) + dot_first(before[0], scores_before)
+    return query_grad.T, terms
+
+
+def head_columns(head, width, part):
+    return slice(part * width + head * E, part * width + (head + 1) * E)
 
 
 def attend(queries, pair, before=None):
     count, width = queries.shape
     heads = width // E
     rows = min(count, ATTEND_STEP)
-    scalars = [] if before is None else [part.reshape(1) for part in before[1:]]
+    scalars = [] if before is None else before[1:]
     operands = [queries, pair] + ([] if before is None else [before[0]])
 
     def kernel(*refs):
@@ -337,39 +377,22 @@
         result_ref, log_ref = refs[-2:]
         for h in range(heads):
             own = slice(h * E, (h + 1) * E)
-            key = pair_ref[:, head_columns(h, width, 0)]
-            value = pair_ref[:, head_columns(h, width, 1)]
+            key_at, value_at = head_columns(h, width, 0), head_columns(h, width, 1)
+            mask = None
             if before is not None:
-                key_before = refs[2][:, head_columns(h, width, 0)]
-                value_before = refs[2][:, head_columns(h, width, 1)]
+                mask = (refs[2][:, key_at], refs[2][:, value_at]) + tuple(
+                    ref[0] for ref in scalar_refs
+                )
             for spot in range(0, count, rows):
                 here = slice(spot, spot + rows)
-                mask = None
-                if before is not None:
-                    mask = key_before, scalar_refs[0][0], scalar_refs[1][0], rows
-                scores, below = score_parts(query_ref[here, own], key, mask, spot)
-                top = jnp.max(scores, axis=0, keepdims=True)
-                powers = jnp.exp(scores - top)
-                total = jnp.sum(powers, axis=0, keepdims=True)
-                chances = (powers * (1.0 / total)).astype(LOW)
-                if before is None:
-                    result = dot_first(value, chances)
-                else:
-                    none = jnp.zeros_like(chances)
-                    result = dot_first(value, jnp.where(below, chances, none)) + dot_first(
-                        value_before, jnp.where(below, none, chances)
-                    )
-                result_ref[here, own] = result.T.astype(LOW)
-                log_ref[h : h + 1, here] = top + jnp.log(total)
-
-    shapes = (
-        jax.ShapeDtypeStruct((count, width), LOW),
-        jax.ShapeDtypeStruct((heads, count), HIGH),
-    )
+                result_ref[here, own], log_ref[h : h + 1, here] = head_attend(
+                    query_ref[here, own], pair_ref[:, key_at], pair_ref[:, value_at], mask, spot
+                )
+
     scores_count = heads * count * pair.shape[0]
-    return attention_kernel(
-        kernel, shapes, [], operands, scalars, (scores_count * len(operands), scores_count)
-    )
+    outs = [((count, width), LOW), ((heads, count), HIGH)]
+    products = scores_count * E * len(operands)
+    return fused(kernel, outs, operands, products, scalars, scores_count)
 
 
 def attend_back(queries, pair, logs, grad_result, before=None):
@@ -377,72 +400,263 @@
     heads = width // E
     rows = min(count, ATTEND_STEP)
     keys = pair.shape[0]
-    scalars = [] if before is None else [part.reshape(1) for part in before[1:]]
+    scalars = [] if before is None else before[1:]
     operands = [queries, logs, grad_result, pair] + ([] if before is None else [before[0]])
 
     def kernel(*refs):
         scalar_refs, refs = refs[: len(scalars)], refs[len(scalars) :]
         query_ref, log_ref, grad_ref, pair_ref = refs[:4]
         outs = refs[len(operands) :]
-        query_out, pair_out = outs[:2]
         for h in range(heads):
             own = slice(h * E, (h + 1) * E)
             key_at, value_at = head_columns(h, width, 0), head_columns(h, width, 1)
-            key, value = pair_ref[:, key_at], pair_ref[:, value_at]
+            mask = None
             if before is not None:
-                key_before, value_before = refs[4][:, key_at], refs[4][:, value_at]
-            sums = [jnp.zeros((keys, E), HIGH)] * 4
+                mask = (refs[4][:, key_at], refs[4][:, value_at]) + tuple(
+                    ref[0] for ref in scalar_refs
+                )
+            sums = None
             for spot in range(0, count, rows):
                 here = slice(spot, spot + rows)
-                query, grad = query_ref[here, own], grad_ref[here, own]
-                mask = None
-                if before is not None:
-                    mask = key_before, scalar_refs[0][0], scalar_refs[1][0], rows
-                scores, below = score_parts(query, key, mask, spot)
-                chances = jnp.exp(scores - log_ref[h : h + 1, here])
-                grad_chances = dot_second(value, grad)
-                if before is not None:
-                    grad_chances = jnp.where(below, grad_chances, dot_second(value_before, grad))
-                inner = jnp.sum(chances * grad_chances, axis=0, keepdims=True)
-                grad_scores = (chances * (grad_chances - inner) * E ** (-0.5)).astype(LOW)
-                chances = chances.astype(LOW)
-                if before is None:
-                    query_grad = dot_first(key, grad_scores)
-                    terms = [plain_dot(grad_scores, query), plain_dot(chances, grad)]
-                else:
-                    none = jnp.zeros_like(chances)
-                    scores_now = jnp.where(below, grad_scores, none)
-                    scores_before = jnp.where(below, none, grad_scores)
-                    query_grad = dot_first(key, scores_now) + dot_first(key_before, scores_before)
-                    terms = [
-                        plain_dot(scores_now, query),
-                        plain_dot(jnp.where(below, chances, none), grad),
-                        plain_dot(scores_before, query),
-                        plain_dot(jnp.where(below, none, chances), grad),
-                    ]
-                query_out[here, own] = query_grad.T
-                sums = [one + two for one, two in zip(sums, terms)]
-            pair_out[:, key_at] = sums[0]
-            pair_out[:, value_at] = sums[1]
+                outs[0][here, own], terms = head_back(
+                    query_ref[here, own],
+                    pair_ref[:, key_at],
+                    pair_ref[:, value_at],
+                    log_ref[h : h + 1, here],
+                    grad_ref[here, own],
+                    mask,
+                    spot,
+                )
+                sums = terms if sums is None else [one + two for one, two in zip(sums, terms)]
+            outs[1][:, key_at], outs[1][:, value_at] = sums[:2]
             if before is not None:
-                outs[2][:, key_at] = sums[2].astype(LOW)
-                outs[2][:, value_at] = sums[3].astype(LOW)
-
-    shapes = [
-        jax.ShapeDtypeStruct((count, width), HIGH),
-        jax.ShapeDtypeStruct((keys, 2 * width), HIGH),
-    ]
+                outs[2][:, key_at], outs[2][:, value_at] = sums[2].astype(LOW), sums[3].astype(LOW)
+
+    outs = [((count, width), HIGH), ((keys, 2 * width), HIGH)]
     if before is not None:
-        shapes.append(jax.ShapeDtypeStruct((keys, 2 * width), LOW))
+        outs.append(((keys, 2 * width), LOW))
     scores_count = heads * count * keys
-    return attention_kernel(
-        kernel,
-        tuple(shapes),
-        [],
-        operands,
-        scalars,
-        (scores_count * (5 if before is None else 10), scores_count),
-    )
+    products = scores_count * E * (5 if before is None else 10)
+    return fused(kernel, outs, operands, products, scalars, scores_count)
+
+
+def gelu_of(matrix):
+    return 0.5 * matrix * (1.0 + lax.erf(matrix * 0.5**0.5))
+
+
+def gelu_slope_of(matrix):
+    density = jnp.exp(-0.5 * matrix * matrix) * (2.0 * jnp.pi) ** (-0.5)
+    return 0.5 * (1.0 + lax.erf(matrix * 0.5**0.5)) + matrix * density
+
+
+def sent_around(low):
+    return [tp_to(low, k) for k in far_first(lax.axis_size("tp"))]
+
+
+def added(refs):
+    total = refs[0][...]
+    for ref in refs[1:]:
+        total = total + ref[...].astype(HIGH)
+    return total
+
+
+def chain_attend(queries, pieces, stack, index, out_flat):
+    count, width = queries.shape
+    n, keys = len(pieces), stack.shape[1]
+
+    def kernel(index_ref, query_ref, *refs):
+        pieces_refs, (stack_ref, out_ref) = refs[:n], refs[n : n + 2]
+        pair_ref, own_ref, cross_ref, heads_ref, part_ref, low_ref = refs[n + 2 :]
+        for k, ref in enumerate(pieces_refs):
+            pair_ref[k * (keys // n) : (k + 1) * (keys // n), :] = ref[...]
+        token = stack_ref[index_ref[0]]
+        for h in range(width // E):
+            own = slice(h * E, (h + 1) * E)
+            key_at, value_at = head_columns(h, width, 0), head_columns(h, width, 1)
+            row = slice(h, h + 1)
+            heads_ref[:, width + h * E : width + (h + 1) * E], cross_ref[row, :] = head_attend(
+                query_ref[:, own], token[:, key_at], token[:, value_at]
+            )
+            heads_ref[:, own], own_ref[row, :] = head_attend(
+                query_ref[:, own], pair_ref[:, key_at], pair_ref[:, value_at]
+            )
+        part = plain_dot(heads_ref[...], out_ref[...])
+        part_ref[...] = part
+        low_ref[...] = part.astype(LOW)
+
+    depth = out_flat.shape[1]
+    logs = ((width // E, count), HIGH)
+    outs = [((keys, 2 * width), LOW), logs, logs, ((count, 2 * width), LOW)]
+    outs += [((count, depth), HIGH), ((count, depth), LOW)]
+    products = count * width * (4 * keys + 2 * depth)
+    operands = [queries, *pieces, stack, out_flat]
+    return fused(kernel, outs, operands, products, [index], 2 * count * keys)
+
+
+def chain_mlp(parts, incoming, keeps, gain, up, down):
+    n = len(parts)
+
+    def kernel(*refs):
+        incoming_ref, keep_ref, gain_ref, up_ref, down_ref = refs[n : n + 5]
+        update_ref, mid_ref, normed_ref, hidden_ref, active_ref, part_ref, low_ref = refs[n + 5 :]
+        update = added(refs[:n])
+        keep = keep_ref[0:1, :]
+        mid = keep * incoming_ref[...] + (1.0 - keep) * update
+        normed = layer_norm(mid, gain_ref[...]).astype(LOW)
+        hidden = plain_dot(normed, up_ref[...])
+        active = gelu_of(hidden).astype(LOW)
+        part = plain_dot(active, down_ref[...])
+        update_ref[...], mid_ref[...], normed_ref[...] = update, mid, normed
+        hidden_ref[...], active_ref[...] = hidden, active
+        part_ref[...], low_ref[...] = part, part.astype(LOW)
+
+    count, depth = incoming.shape
+    inner = up.shape[1]
+    outs = [((count, depth), HIGH), ((count, depth), HIGH), ((count, depth), LOW)]
+    outs += [((count, inner), HIGH), ((count, inner), LOW)]
+    outs += [((count, depth), HIGH), ((count, depth), LOW)]
+    operands = [*parts, incoming, keeps, gain, up, down]
+    return fused(kernel, outs, operands, 2 * count * depth * inner, (), count * inner)
+
+
+def chain_start(parts, mid, keeps, init_slab, flag, gain, qkv_flat):
+    n = len(parts)
+    width = qkv_flat.shape[1] // 3
+
+    def kernel(flag_ref, *refs):
+        mid_ref, keep_ref, init_ref, gain_ref, qkv_ref = refs[n : n + 5]
+        mlp_ref, slab_ref, incoming_ref, normed_ref, query_ref, pair_ref = refs[n + 5 :]
+        mlp = added(refs[:n])
+        keep = keep_ref[1:2, :]
+        slab = (keep * mid_ref[...] + (1.0 - keep) * mlp).astype(LOW)
+        incoming = jnp.where(
+            flag_ref[0] == 1, init_ref[...].astype(HIGH), slab.astype(HIGH)
+        )
+        normed = layer_norm(incoming, gain_ref[...]).astype(LOW)
+        qkv = plain_dot(normed, qkv_ref[...]).astype(LOW)
+        mlp_ref[...], slab_ref[...], incoming_ref[...] = mlp, slab, incoming
+        normed_ref[...], query_ref[...], pair_ref[...] = normed, qkv[:, :width], qkv[:, width:]
+
+    count, depth = mid.shape
+    outs = [((count, depth), HIGH), ((count, depth), LOW), ((count, depth), HIGH)]
+    outs += [((count, depth), LOW), ((count, width), LOW), ((count, 2 * width), LOW)]
+    operands = [*parts, mid, keeps, init_slab, gain, qkv_flat]
+    return fused(kernel, outs, operands, 3 * count * depth * width, [flag])
+
+
+def chain_back_mlp(parts, incoming, grad_mid, flag, keeps, gain, mid, mlp, hidden, up, down):
+    n = len(parts)
+    operands = [*parts, incoming, keeps, gain, mid, mlp, hidden, up, down]
+    operands += [] if grad_mid is None else [grad_mid]
+
+    def kernel(flag_ref, *refs):
+        incoming_ref, keep_ref, gain_ref, mid_ref, mlp_ref, hidden_ref, up_ref, down_ref = refs[
+            n : n + 8
+        ]
+        grad_ref, state_ref, low_mlp_ref, low_hidden_ref, bias_ref, part_ref, low_ref = refs[-7:]
+        grad = norm_back(incoming_ref[...], gain_ref[...], added(refs[:n]))
+        if grad_mid is not None:
+            grad = keep_ref[0:1, :] * refs[n + 8][...] + grad
+        state = jnp.where(flag_ref[0] == 1, 0.0, grad)
+        low_mlp = ((1.0 - keep_ref[1:2, :]) * state).astype(LOW)
+        grad_active = dot_second(low_mlp, down_ref[...])
+        low_hidden = (gelu_slope_of(hidden_ref[...]) * grad_active).astype(LOW)
+        part = dot_second(low_hidden, up_ref[...])
+        grad_ref[...], state_ref[...] = grad, state
+        low_mlp_ref[...], low_hidden_ref[...] = low_mlp, low_hidden
+        bias_ref[...] = jnp.sum(state * (mid_ref[...] - mlp_ref[...]), axis=0, keepdims=True)
+        part_ref[...], low_ref[...] = part, part.astype(LOW)
+
+    count, depth = mid.shape
+    inner = up.shape[1]
+    outs = [((count, depth), HIGH), ((count, depth), HIGH), ((count, depth), LOW)]
+    outs += [((count, inner), LOW), ((1, depth), HIGH)]
+    outs += [((count, depth), HIGH), ((count, depth), LOW)]
+    return fused(kernel, outs, operands, 2 * count * depth * inner, [flag], count * inner)
+
+
+def chain_back_heads(
+    parts, mid, gain, keeps, grad_state, incoming, update, out_flat, queries, pair, logs, stack, index
+):
+    n = len(parts)
+    count, width = queries.shape
+    keys = pair.shape[0]
+    slab = keys // CHAIN
+
+    def kernel(index_ref, *refs):
+        mid_ref, gain_ref, keep_ref, state_ref, incoming_ref, update_ref, out_ref = refs[n : n + 7]
+        query_ref, pair_ref, own_log_ref, cross_log_ref, stack_ref = refs[n + 7 : n + 12]
+        outs = refs[n + 12 :]
+        mid_out, low_out, bias_out, query_out, here_out, across_out, sent_out, token_out = outs
+        grad_mid = keep_ref[1:2, :] * state_ref[...] + norm_back(
+            mid_ref[...], gain_ref[...], added(refs[:n])
+        )
+        mid_out[...] = grad_mid
+        low = ((1.0 - keep_ref[0:1, :]) * grad_mid).astype(LOW)
+        low_out[...] = low
+        bias_out[...] = jnp.sum(
+            grad_mid * (incoming_ref[...] - update_ref[...]), axis=0, keepdims=True
+        )
+        grad_heads = dot_second(low, out_ref[...]).astype(LOW)
+        token = stack_ref[index_ref[0]]
+        for h in range(width // E):
+            own = slice(h * E, (h + 1) * E)
+            row = slice(h, h + 1)
+            own_query, own_terms = head_back(
+                query_ref[:, own],
+                pair_ref[:, head_columns(h, width, 0)],
+                pair_ref[:, head_columns(h, width, 1)],
+                own_log_ref[row, :],
+                grad_heads[:, own],
+            )
+            cross_query, cross_terms = head_back(
+                query_ref[:, own],
+                token[:, head_columns(h, width, 0)],
+                token[:, head_columns(h, width, 1)],
+                cross_log_ref[row, :],
+                grad_heads[:, head_columns(h, width, 1)],
+            )
+            query_out[:, own] = own_query + cross_query
+            for part in range(2):
+                at = head_columns(h, width, part)
+                here_out[:, at] = own_terms[part][:slab]
+                across_out[:, at] = own_terms[part][2 * slab : 3 * slab]
+                sent_out[:slab, at] = own_terms[part][slab : 2 * slab].astype(LOW)
+                sent_out[slab:, at] = own_terms[part][3 * slab :].astype(LOW)
+                token_out[:, at] = cross_terms[part]
+
+    depth = mid.shape[1]
+    outs = [((count, depth), HIGH), ((count, depth), LOW), ((1, depth), HIGH)]
+    outs += [((count, width), HIGH), ((slab, 2 * width), HIGH), ((slab, 2 * width), HIGH)]
+    outs += [((2 * slab, 2 * width), LOW), ((keys, 2 * width), HIGH)]
+    operands = [*parts, mid, gain, keeps, grad_state, incoming, update, out_flat]
+    operands += [queries, pair, *logs, stack]
+    products = count * width * (10 * keys + 2 * depth)
+    return fused(kernel, outs, operands, products, [index], 2 * count * keys)
+
+
+def chain_back_inputs(query_grad, terms, stack, index, qkv_flat):
+    rows, depth = stack.shape[1], qkv_flat.shape[0]
+    width = qkv_flat.shape[1] // 3
+    first = [] if query_grad is None else [query_grad]
+
+    def kernel(index_ref, *refs):
+        stack_ref, qkv_ref = refs[len(first) + len(terms) : len(first) + len(terms) + 2]
+        grad_ref, part_ref, low_ref = refs[-3:]
+        pair = stack_ref[index_ref[0]]
+        for ref in refs[len(first) : len(first) + len(terms)]:
+            pair = pair + ref[...].astype(HIGH)
+        if first:
+            grad_ref[:, :width] = refs[0][...].astype(LOW)
+        else:
+            grad_ref[:, :width] = jnp.zeros((rows, width), LOW)
+        grad_ref[:, width:] = pair.astype(LOW)
+        part = dot_second(grad_ref[...], qkv_ref[...])
+        part_ref[...], low_ref[...] = part, part.astype(LOW)
+
+    outs = [((rows, 3 * width), LOW), ((rows, depth), HIGH), ((rows, depth), LOW)]
+    operands = [*first, *terms, stack, qkv_flat]
+    return fused(kernel, outs, operands, 3 * rows * depth * width, [index])
 
 
 def body(
@@ -491,8 +705,11 @@
     token_rows = turned(tokens, tp_index * piece_rows)
 
     def natural(pieces):
-        whole = jnp.concatenate(pieces)
-        return turned(whole, (n_tp - tp_index) % n_tp * piece_rows)
+        whole = jnp.zeros((block_rows, model_width), pieces[0].dtype)
+        for k, piece in enumerate(pieces):
+            at = (tp_index + k) % n_tp * piece_rows
+            whole = lax.dynamic_update_slice_in_dim(whole, piece, at, 0)
+        return whole
 
     input_rows = token_rows.astype(HIGH)
     win_normed = layer_norm(input_rows, norm_win).astype(LOW)
@@ -522,17 +739,14 @@
     def own_rows(slab):
         return lax.dynamic_slice_in_dim(slab, tp_index * thin_rows, thin_rows, 0)
 
-    def state_start(slab):
-        state_normed = layer_norm(slab.astype(HIGH), norm_state).astype(LOW)
-        state_qkv = plain_dot(state_normed, qkv_state_flat).astype(LOW)
-        state_queries = state_qkv[:, :width]
-        state_pair = jnp.concatenate(pos_gather(state_qkv[:, width:]))
-        own, own_logs = attend(state_queries, state_pair)
-        return state_normed, state_queries, state_pair, own, own_logs
-
-    started = state_start(tied(init_slab, win_ffn_in[1]))
+    init_late = tied(init_slab, win_ffn_in[1])
+    state_incoming = init_late.astype(HIGH)
+    state_normed = layer_norm(state_incoming, norm_state).astype(LOW)
+    state_qkv = plain_dot(state_normed, qkv_state_flat).astype(LOW)
+    state_queries = state_qkv[:, :width]
+    state_pieces = pos_gather(state_qkv[:, width:])
     layer_one = win_mixed + tp_scatter([plain_dot(part, down_win) for part in win_active])
-    layer_one = tied(layer_one, started[3])
+    layer_one = tied(layer_one, state_pieces)
 
     normed_pieces = tp_gather(layer_norm(layer_one, norm_tok).astype(LOW))
     normed = jnp.concatenate(normed_pieces)
@@ -543,50 +757,47 @@
     pairs_stack = jnp.stack(pairs_all)
     before = pair_prev, shift, start_flag
 
-    def state_rest(incoming, state_heads, meanwhile=lambda heads: ()):
-        update = tp_total(plain_dot(state_heads, out_state_flat))
-        return state_end(incoming, tied(update, *meanwhile(state_heads)))
-
-    def state_end(incoming, update):
-        mid_state = keep_one * incoming + (1.0 - keep_one) * update
-        state_ffn_in = layer_norm(mid_state, norm_sffn).astype(LOW)
-        state_hidden = plain_dot(state_ffn_in, up_state)
-        state_active = gelu_exact(state_hidden).astype(LOW)
-        state_mlp = tp_total(plain_dot(state_active, down_state))
-        slab = (keep_two * mid_state + (1.0 - keep_two) * state_mlp).astype(LOW)
-        return slab, (update, mid_state, state_ffn_in, state_hidden, state_active, state_mlp)
-
-    own_done = []
-
-    def own_attention(after):
-        own_done.extend(attend(tied(queries, after), pair, before))
-        return own_done[:1]
-
-    state_slab = init_slab
+    keeps = jnp.stack([keep_one, keep_two])
+    gain_state, gain_sffn = norm_state.reshape(1, -1), norm_sffn.reshape(1, -1)
     turns = []
-    states_out = []
-    for turn in range(CHAIN):
-        state_slab = jnp.where(flags[turn], init_slab, state_slab)
-        incoming = state_slab.astype(HIGH)
-        if turn:
-            started = state_start(state_slab)
-        state_normed, state_queries, state_pair, own, own_logs = started
-        if turn == CHAIN - 1:
-            turns.append((incoming, state_normed, state_queries, state_pair, own))
-            break
-        token_pair = choose(pairs_stack, position ^ turn)
-        cross, cross_logs = attend(state_queries, token_pair)
-        state_heads = jnp.concatenate([own, cross], axis=1)
-        first = (incoming, state_normed, state_queries, state_pair)
+    slabs_out = []
+    for turn in range(CHAIN - 1):
+        state_pair, own_logs, cross_logs, state_heads, part, low = chain_attend(
+            state_queries, state_pieces, pairs_stack, position ^ turn, out_state_flat
+        )
+        parts = [part] + sent_around(low)
         if turn == 1:
-            state_slab, rest = state_rest(incoming, state_heads, own_attention)
-        else:
-            state_slab, rest = state_rest(incoming, state_heads)
-        states_out.append(own_rows(state_slab))
-        turns.append(first + (token_pair, cross_logs, own_logs, state_heads) + rest)
-    own_heads, own_token_logs = own_done
-    my_state_pair = turns[0][3]
-    for turn in range(1, CHAIN):
+            own_heads, own_token_logs = attend(tied(queries, part), pair, before)
+            parts = tied(parts, own_heads)
+        update, mid_state, state_ffn_in, state_hidden, state_active, part, low = chain_mlp(
+            parts, state_incoming, keeps, gain_sffn, up_state, down_state
+        )
+        parts = [part] + sent_around(low)
+        state_mlp, slab, incoming_next, normed_next, queries_next, pair_next = chain_start(
+            parts, mid_state, keeps, init_slab, flags[turn + 1], gain_state, qkv_state_flat
+        )
+        slabs_out.append(slab)
+        turns.append(
+            (
+                state_incoming,
+                state_normed,
+                state_queries,
+                state_pair,
+                (own_logs, cross_logs),
+                state_heads,
+                update,
+                mid_state,
+                state_ffn_in,
+                state_hidden,
+                state_active,
+                state_mlp,
+            )
+        )
+        state_incoming, state_normed, state_queries = incoming_next, normed_next, queries_next
+        state_pieces = pos_gather(pair_next)
+    turns.append((state_incoming, state_normed))
+    my_state_pair = jnp.concatenate(state_pieces)
+    for turn in range(CHAIN - 1):
         my_state_pair = jnp.where(position == turn, turns[turn][3], my_state_pair)
 
     cross_heads, cross_token_logs = attend(queries, my_state_pair)
@@ -626,17 +837,25 @@
         returned = lax.ppermute(prev_grad, "seq", homeward)
         return query_grad + cross_query_grad, pair_grad + returned.astype(HIGH)
 
-    incoming, _, state_queries, _, own = turns[CHAIN - 1]
-    token_pair = choose(pairs_stack, position ^ (CHAIN - 1))
-    cross, _ = attend(tied(state_queries, grad_heads), token_pair)
-    last_heads = jnp.concatenate([own, cross], axis=1)
-    last_update = tp_total(plain_dot(last_heads, out_state_flat))
+    last_incoming = state_incoming
+    _, _, _, _, part, low = chain_attend(
+        tied(state_queries, grad_heads),
+        state_pieces,
+        pairs_stack,
+        position ^ (CHAIN - 1),
+        out_state_flat,
+    )
+    last_parts = [part] + sent_around(low)
 
     def last_state(after):
-        return state_end(incoming_last, tied(last_update, after))[0]
+        _, mid_state, _, _, _, part, _ = chain_mlp(
+            tied(last_parts, after), last_incoming, keeps, gain_sffn, up_state, down_state
+        )
+        state_mlp = tp_total(part)
+        return (keep_two * mid_state + (1.0 - keep_two) * state_mlp).astype(LOW)
 
     def states_between(state_slab):
-        states_stack = jnp.stack(states_out + [own_rows(state_slab)])
+        states_stack = jnp.stack([own_rows(slab) for slab in slabs_out + [state_slab]])
         pieces = [choose(states_stack, position)]
         pieces += [swap(choose(states_stack, position ^ k), k) for k in range(1, CHAIN)]
         pieces = jnp.stack(pieces)
@@ -646,95 +865,107 @@
         by_tp = turned(jnp.stack(tp_gather(slabs)), (n_tp - tp_index) % n_tp)
         return jnp.transpose(by_tp, (1, 0, 2, 3)).reshape(state_rows, model_width)
 
-    incoming_last = incoming
-
+    grad_state_qkv, part, low = chain_back_inputs(
+        None, [], cross_pieces, position ^ (CHAIN - 1), qkv_state_flat
+    )
+    parts = [part] + sent_around(low)
+    query_grad, pair_grad = own_back()
+    parts = tied(parts, query_grad)
+    kept_qkv, kept_rest = [(state_normed, grad_state_qkv)], []
+    token_pair_grads = [None] * CHAIN
     init_grad = jnp.zeros((thin_rows, model_width), HIGH)
-    bias_one = bias_two = jnp.zeros((model_width,), HIGH)
-    kept_qkv, kept_rest = [], []
-    token_pair_grads = [None] * CHAIN
-    grad_state = None
-    for turn in reversed(range(CHAIN)):
-        incoming, state_normed, state_queries, state_pair = turns[turn][:4]
-        pair_total = choose(cross_pieces, position ^ turn)
-        if turn == CHAIN - 1:
-            query_total = jnp.zeros((slab_rows, width), HIGH)
-        else:
-            (
-                token_pair,
-                cross_logs,
-                own_logs,
-                state_heads,
-                update,
-                mid_state,
-                state_ffn_in,
-                state_hidden,
-                state_active,
-                state_mlp,
-            ) = turns[turn][4:]
-            grad_mlp = ((1.0 - keep_two) * grad_state).astype(LOW)
-            bias_two = bias_two + jnp.sum(grad_state * (mid_state - state_mlp), axis=0)
-            grad_state_hidden = gelu_slope(
-                state_hidden, dot_second(grad_mlp, down_state)
-            ).astype(LOW)
-            grad_sffn_in = tp_total(dot_second(grad_state_hidden, up_state))
-            if turn == CHAIN - 2:
-                token_grads = ScatterSum(
-                    weight_grads(
-                        [
-                            (tied(tuple(ffn_in), grad_state_hidden), grad_hidden),
-                            ([cotangent_rows], active),
-                            (grad_proj_pieces, [token_heads]),
-                        ],
-                        False,
-                    )
+    bias_one = bias_two = jnp.zeros((1, model_width), HIGH)
+    grad_mid = None
+    for turn in reversed(range(CHAIN - 1)):
+        next_incoming = turns[turn + 1][0]
+        (
+            state_incoming,
+            state_normed,
+            state_queries,
+            state_pair,
+            logs,
+            state_heads,
+            update,
+            mid_state,
+            state_ffn_in,
+            state_hidden,
+            state_active,
+            state_mlp,
+        ) = turns[turn]
+        grad_next, grad_state, grad_mlp, grad_state_hidden, sums, part, low = chain_back_mlp(
+            parts,
+            next_incoming,
+            grad_mid,
+            flags[turn + 1],
+            keeps,
+            gain_state,
+            mid_state,
+            state_mlp,
+            state_hidden,
+            up_state,
+            down_state,
+        )
+        init_grad = init_grad + jnp.where(flags[turn + 1], own_rows(grad_next), 0.0)
+        bias_two = bias_two + sums
+        parts = [part] + sent_around(low)
+        if turn == CHAIN - 2:
+            token_grads = ScatterSum(
+                weight_grads(
+                    [
+                        (tied(tuple(ffn_in), part), grad_hidden),
+                        ([cotangent_rows], active),
+                        (grad_proj_pieces, [token_heads]),
+                    ],
+                    False,
                 )
-                grad_sffn_in = tied(grad_sffn_in, token_grads.grads)
-            grad_mid = keep_two * grad_state + norm_back(mid_state, norm_sffn, grad_sffn_in)
-            bias_one = bias_one + jnp.sum(grad_mid * (incoming - update), axis=0)
-            grad_update = ((1.0 - keep_one) * grad_mid).astype(LOW)
-            grad_state_heads = dot_second(grad_update, out_state_flat).astype(LOW)
-            own_q, own_pair = attend_back(
-                state_queries, state_pair, own_logs, grad_state_heads[:, :width]
             )
-            pair_total = pair_total + pos_scatter(split_rows(own_pair, CHAIN))
-            cross_q, token_pair_grads[turn] = attend_back(
-                state_queries, token_pair, cross_logs, grad_state_heads[:, width:]
-            )
-            query_total = own_q + cross_q
-            kept_rest.append(
-                (state_heads, grad_update, state_ffn_in, grad_state_hidden, state_active, grad_mlp)
-            )
+            parts = tied(parts, token_grads.grads)
+        if turn == 0:
+            parts = tied(parts, token_grads.total)
+        grad_mid, grad_update, sums, query_total, here, across, sent, token_grad = chain_back_heads(
+            parts,
+            mid_state,
+            gain_sffn,
+            keeps,
+            grad_state,
+            state_incoming,
+            update,
+            out_state_flat,
+            state_queries,
+            state_pair,
+            logs,
+            pairs_stack,
+            position ^ turn,
+        )
+        bias_one = bias_one + sums
+        token_pair_grads[turn] = token_grad
+        kept_rest.append(
+            (state_heads, grad_update, state_ffn_in, grad_state_hidden, state_active, grad_mlp)
+        )
+        beside, there = split_rows(swap(sent, 1), 2)
+        across = swap((across + there.astype(HIGH)).astype(LOW), 2)
         if turn == CHAIN - 2:
             last_slab = last_state(grad_mid)
-            pair_total = tied(pair_total, last_slab)
+            across = tied(across, last_slab)
         if turn == CHAIN - 3:
             slabs = states_between(tied(last_slab, grad_mid))
-            pair_total = tied(pair_total, slabs)
+            across = tied(across, slabs)
         if turn == CHAIN - 4:
             state_rows_out = states_whole(tied(slabs, grad_mid))
-            pair_total = tied(pair_total, state_rows_out)
-        grad_state_qkv = jnp.concatenate([query_total, pair_total], axis=1).astype(LOW)
+            across = tied(across, state_rows_out)
+        grad_state_qkv, part, low = chain_back_inputs(
+            query_total, [here, beside, across], cross_pieces, position ^ turn, qkv_state_flat
+        )
         kept_qkv.append((state_normed, grad_state_qkv))
-        if turn == 0:
-            break
-        grad_state_normed = tp_total(dot_second(grad_state_qkv, qkv_state_flat))
-        if turn == CHAIN - 1:
-            query_grad, pair_grad = own_back()
-            grad_state_normed = tied(grad_state_normed, query_grad)
-        grad_incoming = norm_back(incoming, norm_state, grad_state_normed)
-        if grad_state is not None:
-            grad_incoming = keep_one * grad_mid + grad_incoming
-        init_grad = init_grad + jnp.where(flags[turn], own_rows(grad_incoming), 0.0)
-        grad_state = jnp.where(flags[turn], 0.0, grad_incoming)
-    grad_mid_first, grad_qkv_first = grad_mid, grad_state_qkv
+        if turn:
+            parts = [part] + sent_around(low)
 
     def first_incoming_grad(after):
-        normed_grad = tp_total(dot_second(tied(grad_qkv_first, after), qkv_state_flat))
-        incoming = turns[0][0]
-        return keep_one * grad_mid_first + norm_back(incoming, norm_state, normed_grad)
-
-    bias_one = bias_one * keep_one * (1.0 - keep_one) / n_tp
-    bias_two = bias_two * keep_two * (1.0 - keep_two) / n_tp
+        normed_grad = tp_total(tied(part, after))
+        return keep_one * grad_mid + norm_back(turns[0][0], norm_state, normed_grad)
+
+    bias_one = bias_one[0] * keep_one * (1.0 - keep_one) / n_tp
+    bias_two = bias_two[0] * keep_two * (1.0 - keep_two) / n_tp
 
     token_pair_grads[CHAIN - 1] = jnp.zeros_like(token_pair_grads[0])
     pair_stack = jnp.stack(token_pair_grads)
@@ -789,10 +1020,11 @@
     )
     win_returned = lax.ppermute(win_prev_grad, "seq", homeward)
     after = win_query_grad, win_pair_grad
-    step = middle_grads.one_first(grad_win_heads), middle_grads.two_first(grad_win_heads)
+    middle_grads.one_first(grad_win_heads)
+    middle_grads.two_first(grad_win_heads)
     first_grad = own_rows(first_incoming_grad(after))
     init_grad = init_grad + jnp.where(flags[0], first_grad, 0.0)
-    win_pair_grad = win_pair_grad + tied(win_returned, step).astype(HIGH)
+    win_pair_grad = win_pair_grad + tied(win_returned, state_grads.total).astype(HIGH)
     grad_win_qkv = jnp.concatenate([win_query_grad, win_pair_grad], axis=1).astype(LOW)
 
     small_rows = jnp.concatenate(

time: 870 us -> 872 us (level)
  other arithmetic: 104 us -> 57.1 us
  local copies, waits for them, and re-layouts: 85.7 us -> 126 us
  Pallas kernels: 51.2 us -> 78 us
  matrix products: 78.9 us -> 58.7 us
  starting transfers between devices: 192 us -> 207 us
  waiting for transfers between devices: 327 us -> 313 us
    unnamed x744 -> x751, local copies, waits for them, and re-layouts: 45.6 us -> 86.7 us
    pallas_call x20 -> x27, Pallas kernels: 32.6 us -> 58.9 us  [fused(): pl.pallas_call(kernel, out_shape=[jax.ShapeDtypeStruct(shape, kind) for s...]
    ppermute x24, waiting for transfers between devices: 39.4 us -> 15.4 us  [stage(): total = total + lax.ppermute(sent, 'seq', self.pairs(*step(k))).astype(HIGH)]
    ppermute x30, waiting for transfers between devices: 53.3 us -> 71 us  [tp_from(): return lax.ppermute(array, 'tp', [((i + k) % n, i) for i in range(n)])]
    ppermute x30, starting transfers between devices: 45.5 us -> 28.8 us  [tp_from(): return lax.ppermute(array, 'tp', [((i + k) % n, i) for i in range(n)])]
    dot_general x41 -> x27, matrix products: 48.4 us -> 33.4 us  [plain_dot(): return jnp.dot(former, latter, preferred_element_type=HIGH)]
    ppermute x69, starting transfers between devices: 89.3 us -> 103 us  [tp_to(): return lax.ppermute(array, 'tp', [(i, (i + k) % n) for i in range(n)])]
    convert_element_type x14 -> x8, other arithmetic: 13.4 us -> 1.31 us  [the longest x1 0.89 us: last_state(): return (keep_two * mid_state + (1.0 - keep_two) * state_mlp).astype(LOW)]
  transfers between devices with their start and end apart: 159 -> 159, of which waited for: 83 -> 87; matrix products, arithmetic and copies ran while one was open for 17% -> 13% of each run, Pallas kernels for 5% -> 5%
where the time goes in v7:
time: 872 us; the launch traced here: 861 us
  waiting for transfers between devices  313 us (36%)
  starting transfers between devices  207 us (24%)
  local copies, waits for them, and re-layouts  126 us (14%)
  Pallas kernels  78 us (9%)
  matrix products  58.7 us (7%)
  other arithmetic  57.1 us (7%)
  between operations  21.4 us (2%)
    ppermute x69, waiting for transfers between devices, tp_to(): return lax.ppermute(array, 'tp', [(i, (i + k) % n) for i in range(n)])  182 us
    ppermute x69, starting transfers between devices, tp_to(): return lax.ppermute(array, 'tp', [(i, (i + k) % n) for i in range(n)])  103 us
    unnamed x751, local copies, waits for them, and re-layouts  86.7 us
    ppermute x30, waiting for transfers between devices, tp_from(): return lax.ppermute(array, 'tp', [((i + k) % n, i) for i in range(n)])  71 us
    pallas_call x27, Pallas kernels, fused(): pl.pallas_call(kernel, out_shape=[jax.ShapeDtypeStruct(shape, kind) for s...  58.9 us
    ppermute x31, waiting for transfers between devices, swap(): return lax.ppermute(array, 'seq', [(s, s ^ k) for s in range(n)])  43.8 us
    ppermute x24, starting transfers between devices, stage(): total = total + lax.ppermute(sent, 'seq', self.pairs(*step(k))).astype(HIGH)  41 us
    dot_general x27, matrix products, plain_dot(): return jnp.dot(former, latter, preferred_element_type=HIGH)  33.4 us
  transfers between devices with their start and end apart: 159, of which 87 were waited for; matrix products, arithmetic and copies ran while one was open for 13% of the time, Pallas kernels for 5%

profile of v7, /device:TPU:0, one launch (start us, length us, event | category | flops | bytes accessed | tf_op | source)
XLA Modules:
  0.0 861.1 jit_solution(4544279555182298498)
XLA Ops:
  33.9 6.3 collective-permute-done.2
  54.1 6.9 collective-permute-start.11
  105.9 10.9 %collective-permute-done.17 = bf16[512,512]{1,0:T(8,128)(2,1)S(1)} collective-permute-done((bf16[512,512]{1,0:T(8,128)(2,1)S(1)}, bf16[512,512]{1,0:T(8,128)(2,1)S(1)}, u32[]{:S(2)}, u32[]{:S(2)}) %collective-permute-start.17) | collective-permute-done | bytes 524320 | tf_op jit(solution)/shard_map/ppermute | solution.py:120
  127.7 5.8 collective-permute-done.19.refs_1_
  133.5 4.8 collective-permute-done.20.refs_2_
  155.8 4.6 collective-permute-done.23.refs_2_
  194.5 4.8 collective-permute-done.29.refs_2_
  206.0 5.3 collective-permute-done.31.refs_1_
  211.3 4.6 collective-permute-done.32.refs_2_
  239.8 5.9 collective-permute-done.37.refs_1_
  245.7 4.8 collective-permute-done.38.refs_2_
  258.8 5.3 collective-permute-done.40.refs_1_
  264.1 4.6 collective-permute-done.41.refs_2_
  303.8 5.2 collective-permute-done.47
  315.3 11.2 %collective-permute-done.51.refs_3_ = bf16[128,1024]{1,0:T(8,128)(2,1)} collective-permute-done((bf16[128,1024]{1,0:T(8,128)(2,1)}, bf16[128,1024]{1,0:T(8,128)(2,1)}, u32[]{:S(2)}, u32[]{:S(2)}) %collective-permute-start.51) | collective-permute-done | bytes 262176 | tf_op jit(solution)/shard_map/ppermute | solution.py:79
  343.5 4.9 collective-permute-done.53
  353.0 7.0 collective-permute-done.55.refs_14_
  400.8 4.7 shard_map.414
  447.6 5.1 collective-permute-done.73
  460.4 7.1 collective-permute-done.75.refs_1_
  467.5 4.7 collective-permute-done.76.refs_2_
  495.8 4.6 collective-permute-done.79.refs_2_
  522.9 6.4 collective-permute-done.86.refs_1_
  543.9 6.9 collective-permute-done.89.refs_1_
  550.8 4.6 collective-permute-done.90.refs_2_
  600.8 5.1 shard_map.425
  621.7 6.2 collective-permute-done.103
  637.1 7.3 collective-permute-done.106.refs_15_
  655.1 6.0 shard_map.426
  681.1 7.1 collective-permute-done.112
  712.1 5.7 collective-permute-done.127
  751.6 5.8 collective-permute-start.129
  (1315 shorter events, 649.3 us)
Async XLA Ops:
  7.2 548.2 %reduce-scatter.3.cloned.1.call-start = ((), (), s32[]{:S(2)}) async-start(), calls=%async_computation.2 | async-start | bytes 5406720 | tf_op jit(solution)/shard_map/reduce_scatter | solution.py:212
  50.5 20.3 %collective-permute-start.8 = (bf16[128,1024]{1,0:T(8,128)(2,1)S(1)}, bf16[128,1024]{1,0:T(8,128)(2,1)S(1)}, u32[]{:S(2)}, u32[]{:S(2)}) collective-permute-start(bf16[128,1024]{1,0:T(8,128)(2,1)S(1)} %multiply_convert_fusion.12.refs_5_), channel_id=1, source_target_pairs={{3,0},{0,1},{1,2},{2,3},{7,4},{4,5},{5,6},{6,7},{11,8},{8,9},{9,10... | collective-permute-start | bytes 786440 | tf_op jit(solution)/shard_map/ppermute | solution.py:79
  54.1 24.1 %collective-permute-start.11 = (bf16[128,512]{1,0:T(8,128)(2,1)S(1)}, bf16[128,512]{1,0:T(8,128)(2,1)S(1)}, u32[]{:S(2)}, u32[]{:S(2)}) collective-permute-start(bf16[128,512]{1,0:T(8,128)(2,1)S(1)} %slice.346.refs_0_), channel_id=1, source_target_pairs={{0,8},{4,12},{8,0},{12,4},{16,24},{20,28},{24,16},{28,20},{32,40},... | collective-permute-start | bytes 393224 | tf_op jit(solution)/shard_map/ppermute | solution.py:120
  63.8 15.0 %collective-permute-start.5 = (bf16[128,1024]{1,0:T(8,128)(2,1)S(1)}, bf16[128,1024]{1,0:T(8,128)(2,1)S(1)}, u32[]{:S(2)}, u32[]{:S(2)}) collective-permute-start(bf16[128,1024]{1,0:T(8,128)(2,1)S(1)} %convolution_convert_fusion.24), channel_id=1, source_target_pairs={{0,2},{1,3},{2,0},{3,1},{4,6},{5,7},{6,4},{7,5},{8,10},{9,11},{10,... | collective-permute-start | bytes 786440 | tf_op jit(solution)/shard_map/ppermute | solution.py:84
  311.1 15.4 %collective-permute-start.51 = (bf16[128,1024]{1,0:T(8,128)(2,1)}, bf16[128,1024]{1,0:T(8,128)(2,1)}, u32[]{:S(2)}, u32[]{:S(2)}) collective-permute-start(bf16[128,1024]{1,0:T(8,128)(2,1)} %multiply_convert_fusion.5.refs_0_), channel_id=1, source_target_pairs={{3,0},{0,1},{1,2},{2,3},{7,4},{4,5},{5,6},{6,7},{11,8},{8,9},{9,10... | collective-permute-start | bytes 786440 | tf_op jit(solution)/shard_map/ppermute | solution.py:79
  311.2 20.0 %collective-permute-start.50 = (bf16[128,1024]{1,0:T(8,128)(2,1)}, bf16[128,1024]{1,0:T(8,128)(2,1)S(1)}, u32[]{:S(2)}, u32[]{:S(2)}) collective-permute-start(bf16[128,1024]{1,0:T(8,128)(2,1)} %multiply_convert_fusion.5.refs_0_), channel_id=1, source_target_pairs={{2,0},{3,1},{0,2},{1,3},{6,4},{7,5},{4,6},{5,7},{10,8},{11,9},{8,1... | collective-permute-start | bytes 786440 | tf_op jit(solution)/shard_map/ppermute | solution.py:79
  313.2 20.8 %collective-permute-start.49 = (bf16[128,1024]{1,0:T(8,128)(2,1)}, bf16[128,1024]{1,0:T(8,128)(2,1)S(1)}, u32[]{:S(2)}, u32[]{:S(2)}) collective-permute-start(bf16[128,1024]{1,0:T(8,128)(2,1)} %multiply_convert_fusion.5.refs_0_), channel_id=1, source_target_pairs={{1,0},{2,1},{3,2},{0,3},{5,4},{6,5},{7,6},{4,7},{9,8},{10,9},{11,1... | collective-permute-start | bytes 786440 | tf_op jit(solution)/shard_map/ppermute | solution.py:79
  378.9 14.7 %collective-permute-start.62 = (bf16[128,1024]{1,0:T(8,128)(2,1)S(1)}, bf16[128,1024]{1,0:T(8,128)(2,1)S(1)}, u32[]{:S(2)}, u32[]{:S(2)}) collective-permute-start(bf16[128,1024]{1,0:T(8,128)(2,1)S(1)} %get-tuple-element.263), channel_id=1, source_target_pairs={{0,1},{1,2},{2,3},{3,0},{4,5},{5,6},{6,7},{7,4},{8,9},{9,10},{10,1... | collective-permute-start | bytes 786440 | tf_op jit(solution)/shard_map/ppermute | solution.py:84
  407.9 336.7 %reduce-scatter.5.cloned.1.call-start = ((), (), s32[]{:S(2)}) async-start(), calls=%async_computation.3 | async-start | bytes 7028736 | tf_op jit(solution)/shard_map/reduce_scatter | solution.py:212
  408.6 16.0 %collective-permute-start.65 = (bf16[128,1024]{1,0:T(8,128)(2,1)}, bf16[128,1024]{1,0:T(8,128)(2,1)S(1)}, u32[]{:S(2)}, u32[]{:S(2)}) collective-permute-start(bf16[128,1024]{1,0:T(8,128)(2,1)} %copy-done.262), channel_id=1, source_target_pairs={{0,1},{1,2},{2,3},{3,0},{4,5},{5,6},{6,7},{7,4},{8,9},{9,10},{10,1... | collective-permute-start | bytes 786440 | tf_op jit(solution)/shard_map/ppermute | solution.py:84
  437.6 15.1 %collective-permute-start.73 = (bf16[128,1024]{1,0:T(8,128)(2,1)S(1)}, bf16[128,1024]{1,0:T(8,128)(2,1)S(1)}, u32[]{:S(2)}, u32[]{:S(2)}) collective-permute-start(bf16[128,1024]{1,0:T(8,128)(2,1)S(1)} %convert_element_type.587), channel_id=1, source_target_pairs={{0,1},{1,2},{2,3},{3,0},{4,5},{5,6},{6,7},{7,4},{8,9},{9,10},{10,1... | collective-permute-start | bytes 786440 | tf_op jit(solution)/shard_map/ppermute | solution.py:84
  457.2 15.0 %collective-permute-start.76 = (bf16[128,1024]{1,0:T(8,128)(2,1)}, bf16[128,1024]{1,0:T(8,128)(2,1)}, u32[]{:S(2)}, u32[]{:S(2)}) collective-permute-start(bf16[128,1024]{1,0:T(8,128)(2,1)} %get-tuple-element.306), channel_id=1, source_target_pairs={{0,1},{1,2},{2,3},{3,0},{4,5},{5,6},{6,7},{7,4},{8,9},{9,10},{10,1... | collective-permute-start | bytes 786440 | tf_op jit(solution)/shard_map/ppermute | solution.py:84
  540.6 14.9 %collective-permute-start.90 = (bf16[128,1024]{1,0:T(8,128)(2,1)}, bf16[128,1024]{1,0:T(8,128)(2,1)}, u32[]{:S(2)}, u32[]{:S(2)}) collective-permute-start(bf16[128,1024]{1,0:T(8,128)(2,1)} %get-tuple-element.330), channel_id=1, source_target_pairs={{0,1},{1,2},{2,3},{3,0},{4,5},{5,6},{6,7},{7,4},{8,9},{9,10},{10,1... | collective-permute-start | bytes 786440 | tf_op jit(solution)/shard_map/ppermute | solution.py:84
  568.5 16.1 %collective-permute-start.102 = (bf16[4,32,1024]{2,1,0:T(8,128)(2,1)S(1)}, bf16[4,32,1024]{2,1,0:T(8,128)(2,1)S(1)}, u32[]{:S(2)}, u32[]{:S(2)}) collective-permute-start(bf16[4,32,1024]{2,1,0:T(8,128)(2,1)S(1)} %copy-done.299), channel_id=1, source_target_pairs={{3,0},{0,1},{1,2},{2,3},{7,4},{4,5},{5,6},{6,7},{11,8},{8,9},{9,10... | collective-permute-start | bytes 786440 | tf_op jit(solution)/shard_map/ppermute | solution.py:79
  570.1 15.1 %collective-permute-start.98 = (bf16[256,512]{1,0:T(8,128)(2,1)S(1)}, bf16[256,512]{1,0:T(8,128)(2,1)S(1)}, u32[]{:S(2)}, u32[]{:S(2)}) collective-permute-start(bf16[256,512]{1,0:T(8,128)(2,1)S(1)} %get-tuple-element.357), channel_id=1, source_target_pairs={{0,4},{4,0},{8,12},{12,8},{16,20},{20,16},{24,28},{28,24},{32,36},... | collective-permute-start | bytes 786440 | tf_op jit(solution)/shard_map/ppermute | solution.py:120
  570.3 25.4 %collective-permute-start.96 = (bf16[1024,512]{1,0:T(8,128)(2,1)S(1)}, bf16[1024,512]{1,0:T(8,128)(2,1)S(1)}, u32[]{:S(2)}, u32[]{:S(2)}) collective-permute-start(bf16[1024,512]{1,0:T(8,128)(2,1)S(1)} %pad_maximum_fusion.4), channel_id=1, source_target_pairs={{0,4},{4,0},{8,12},{12,8},{16,20},{20,16},{24,28},{28,24},{32,36},... | collective-permute-start | bytes 3145736 | tf_op jit(solution)/shard_map/ppermute | solution.py:120
  578.9 15.5 %collective-permute-start.93 = (bf16[128,1024]{1,0:T(8,128)(2,1)S(1)}, bf16[128,1024]{1,0:T(8,128)(2,1)S(1)}, u32[]{:S(2)}, u32[]{:S(2)}) collective-permute-start(bf16[128,1024]{1,0:T(8,128)(2,1)S(1)} %convolution_convert_fusion.14), channel_id=1, source_target_pairs={{0,1},{1,2},{2,3},{3,0},{4,5},{5,6},{6,7},{7,4},{8,9},{9,10},{10,1... | collective-permute-start | bytes 786440 | tf_op jit(solution)/shard_map/ppermute | solution.py:84
  585.2 23.7 %collective-permute-start.95 = (bf16[512,512]{1,0:T(8,128)(2,1)S(1)}, bf16[512,512]{1,0:T(8,128)(2,1)}, u32[]{:S(2)}, u32[]{:S(2)}) collective-permute-start(bf16[512,512]{1,0:T(8,128)(2,1)S(1)} %copy-done.250), channel_id=1, source_target_pairs={{4,0},{8,4},{12,8},{20,16},{24,20},{28,24},{36,32},{40,36},{44,40}... | collective-permute-start | bytes 1572872 | tf_op jit(solution)/shard_map/ppermute | solution.py:837
  635.4 15.0 %collective-permute-start.110 = (bf16[128,1024]{1,0:T(8,128)(2,1)S(1)}, bf16[128,1024]{1,0:T(8,128)(2,1)S(1)}, u32[]{:S(2)}, u32[]{:S(2)}) collective-permute-start(bf16[128,1024]{1,0:T(8,128)(2,1)S(1)} %get-tuple-element.509.refs_13_), channel_id=1, source_target_pairs={{3,0},{0,1},{1,2},{2,3},{7,4},{4,5},{5,6},{6,7},{11,8},{8,9},{9,10... | collective-permute-start | bytes 786440 | tf_op jit(solution)/shard_map/ppermute | solution.py:79
  646.3 14.8 %collective-permute-start.107 = (bf16[128,1024]{1,0:T(8,128)(2,1)S(1)}, bf16[128,1024]{1,0:T(8,128)(2,1)S(1)}, u32[]{:S(2)}, u32[]{:S(2)}) collective-permute-start(bf16[128,1024]{1,0:T(8,128)(2,1)S(1)} %convolution_convert_fusion.9), channel_id=1, source_target_pairs={{0,2},{1,3},{2,0},{3,1},{4,6},{5,7},{6,4},{7,5},{8,10},{9,11},{10,... | collective-permute-start | bytes 786440 | tf_op jit(solution)/shard_map/ppermute | solution.py:84
  663.9 28.8 %collective-permute-start.115 = (bf16[512,2816]{1,0:T(8,128)(2,1)}, bf16[512,2816]{1,0:T(8,128)(2,1)}, u32[]{:S(2)}, u32[]{:S(2)}) collective-permute-start(bf16[512,2816]{1,0:T(8,128)(2,1)} %get-tuple-element.385), channel_id=1, source_target_pairs={{0,4},{4,0},{8,12},{12,8},{16,20},{20,16},{24,28},{28,24},{32,36},... | collective-permute-start | bytes 8650760 | tf_op jit(solution)/shard_map/ppermute | solution.py:120
  676.3 15.3 %collective-permute-start.114 = (bf16[128,1024]{1,0:T(8,128)(2,1)S(1)}, bf16[128,1024]{1,0:T(8,128)(2,1)}, u32[]{:S(2)}, u32[]{:S(2)}) collective-permute-start(bf16[128,1024]{1,0:T(8,128)(2,1)S(1)} %copy-done.311), channel_id=1, source_target_pairs={{3,0},{0,1},{1,2},{2,3},{7,4},{4,5},{5,6},{6,7},{11,8},{8,9},{9,10... | collective-permute-start | bytes 786440 | tf_op jit(solution)/shard_map/ppermute | solution.py:79
  701.7 16.0 %collective-permute-start.127 = (bf16[128,1024]{1,0:T(8,128)(2,1)S(1)}, bf16[128,1024]{1,0:T(8,128)(2,1)S(1)}, u32[]{:S(2)}, u32[]{:S(2)}) collective-permute-start(bf16[128,1024]{1,0:T(8,128)(2,1)S(1)} %convert_element_type.641), channel_id=1, source_target_pairs={{0,1},{1,2},{2,3},{3,0},{4,5},{5,6},{6,7},{7,4},{8,9},{9,10},{10,1... | collective-permute-start | bytes 786440 | tf_op jit(solution)/shard_map/ppermute | solution.py:84
  702.9 18.5 %collective-permute-start.128 = (bf16[128,1024]{1,0:T(8,128)(2,1)S(1)}, bf16[128,1024]{1,0:T(8,128)(2,1)S(1)}, u32[]{:S(2)}, u32[]{:S(2)}) collective-permute-start(bf16[128,1024]{1,0:T(8,128)(2,1)S(1)} %convert_element_type.641), channel_id=1, source_target_pairs={{0,3},{1,0},{2,1},{3,2},{4,7},{5,4},{6,5},{7,6},{8,11},{9,8},{10,9... | collective-permute-start | bytes 786440 | tf_op jit(solution)/shard_map/ppermute | solution.py:84
  705.0 23.5 %collective-permute-start.116 = (bf16[128,1024]{1,0:T(8,128)(2,1)S(1)}, bf16[128,1024]{1,0:T(8,128)(2,1)S(1)}, u32[]{:S(2)}, u32[]{:S(2)}) collective-permute-start(bf16[128,1024]{1,0:T(8,128)(2,1)S(1)} %copy-done.312), channel_id=1, source_target_pairs={{1,0},{2,1},{3,2},{0,3},{5,4},{6,5},{7,6},{4,7},{9,8},{10,9},{11,1... | collective-permute-start | bytes 786440 | tf_op jit(solution)/shard_map/ppermute | solution.py:79
  705.5 24.0 %collective-permute-start.117 = (bf16[128,1024]{1,0:T(8,128)(2,1)S(1)}, bf16[128,1024]{1,0:T(8,128)(2,1)S(1)}, u32[]{:S(2)}, u32[]{:S(2)}) collective-permute-start(bf16[128,1024]{1,0:T(8,128)(2,1)S(1)} %copy-done.312), channel_id=1, source_target_pairs={{2,0},{3,1},{0,2},{1,3},{6,4},{7,5},{4,6},{5,7},{10,8},{11,9},{8,1... | collective-permute-start | bytes 786440 | tf_op jit(solution)/shard_map/ppermute | solution.py:79
  712.1 19.9 %collective-permute-start.118 = (bf16[128,1024]{1,0:T(8,128)(2,1)S(1)}, bf16[128,1024]{1,0:T(8,128)(2,1)S(1)}, u32[]{:S(2)}, u32[]{:S(2)}) collective-permute-start(bf16[128,1024]{1,0:T(8,128)(2,1)S(1)} %copy-done.312), channel_id=1, source_target_pairs={{3,0},{0,1},{1,2},{2,3},{7,4},{4,5},{5,6},{6,7},{11,8},{8,9},{9,10... | collective-permute-start | bytes 786440 | tf_op jit(solution)/shard_map/ppermute | solution.py:79
  717.8 25.2 %collective-permute-start.130 = (bf16[4,32,1408]{2,1,0:T(8,128)(2,1)S(1)}, bf16[4,32,1408]{2,1,0:T(8,128)(2,1)S(1)}, u32[]{:S(2)}, u32[]{:S(2)}) collective-permute-start(bf16[4,32,1408]{2,1,0:T(8,128)(2,1)S(1)} %get-tuple-element.543), channel_id=1, source_target_pairs={{0,16},{4,20},{8,24},{12,28},{16,0},{20,4},{24,8},{28,12},{32,48},... | collective-permute-start | bytes 1081352 | tf_op jit(solution)/shard_map/ppermute | solution.py:249
  751.6 40.8 %collective-permute-start.129 = (bf16[512,1280]{1,0:T(8,128)(2,1)}, bf16[512,1280]{1,0:T(8,128)(2,1)}, u32[]{:S(2)}, u32[]{:S(2)}) collective-permute-start(bf16[512,1280]{1,0:T(8,128)(2,1)} %get-tuple-element.404), channel_id=1, source_target_pairs={{0,4},{4,0},{8,12},{12,8},{16,20},{20,16},{24,28},{28,24},{32,36},... | collective-permute-start | bytes 3932168 | tf_op jit(solution)/shard_map/ppermute | solution.py:120
  757.8 14.8 %collective-permute-start.121 = (bf16[128,1024]{1,0:T(8,128)(2,1)S(1)}, bf16[128,1024]{1,0:T(8,128)(2,1)S(1)}, u32[]{:S(2)}, u32[]{:S(2)}) collective-permute-start(bf16[128,1024]{1,0:T(8,128)(2,1)S(1)} %convolution_convert_fusion.4), channel_id=1, source_target_pairs={{0,1},{1,2},{2,3},{3,0},{4,5},{5,6},{6,7},{7,4},{8,9},{9,10},{10,1... | collective-permute-start | bytes 786440 | tf_op jit(solution)/shard_map/ppermute | solution.py:84
  757.8 14.8 %collective-permute-start.122 = (bf16[128,1024]{1,0:T(8,128)(2,1)S(1)}, bf16[128,1024]{1,0:T(8,128)(2,1)S(1)}, u32[]{:S(2)}, u32[]{:S(2)}) collective-permute-start(bf16[128,1024]{1,0:T(8,128)(2,1)S(1)} %convolution_convert_fusion.3), channel_id=1, source_target_pairs={{0,3},{1,0},{2,1},{3,2},{4,7},{5,4},{6,5},{7,6},{8,11},{9,8},{10,9... | collective-permute-start | bytes 786440 | tf_op jit(solution)/shard_map/ppermute | solution.py:84
  775.8 14.9 %collective-permute-start.125 = (bf16[128,1024]{1,0:T(8,128)(2,1)}, bf16[128,1024]{1,0:T(8,128)(2,1)}, u32[]{:S(2)}, u32[]{:S(2)}) collective-permute-start(bf16[128,1024]{1,0:T(8,128)(2,1)} %get-tuple-element.506), channel_id=1, source_target_pairs={{3,0},{0,1},{1,2},{2,3},{7,4},{4,5},{5,6},{6,7},{11,8},{8,9},{9,10... | collective-permute-start | bytes 786440 | tf_op jit(solution)/shard_map/ppermute | solution.py:79
  (493 other events, 4570.6 us)
Sparse Core Ops, SparseCore 0:
  408.0 84.9 reduce-scatter.2
  620.5 87.3 reduce-scatter.4

commit v8 on v7

--- a/solution.py
+++ b/solution.py
@@ -70,8 +70,8 @@
 
 def gain_grad(weights, grads, gain, first):
     rows = lax.dynamic_slice_in_dim(weights, first, grads.shape[0], 0).astype(HIGH)
-    gains = lax.dynamic_slice_in_dim(gain, first, grads.shape[0], 0)
-    return jnp.sum(rows * grads, axis=1) / gains
+    gains = lax.dynamic_slice_in_dim(gain.reshape(-1, 1), first, grads.shape[0], 0)
+    return jnp.sum(rows * grads, axis=1, keepdims=True) / gains
 
 
 def tp_from(array, k):
@@ -258,32 +258,21 @@
             part = self.mine[:, columns].astype(HIGH) + sent[:, columns].astype(HIGH)
             return part.astype(LOW).reshape(self.x_size, self.z_size, -1, part.shape[1])
 
-        self.one, self.two = total(slice(0, half)), total(slice(half, width))
-        return self.one, self.two
-
-    def one_first(self, after):
-        self.one = self.over_z(tied(self.one, after), 1).astype(LOW)
-        return self.one
-
-    def two_first(self, after):
-        self.two = self.over_x(tied(self.two, after), 0).astype(LOW)
-        return self.two
-
-    def one_last(self, after):
-        self.one = self.over_x(tied(self.one, after), 0)
-        return self.one
-
-    def two_last(self, after):
-        self.two = self.over_z(tied(self.two, after), 0)
-        return self.two
-
-    def columns(self, at, count):
-        half = self.one.shape[1]
-        if at + count <= half:
-            return self.one[:, at : at + count]
-        if at >= half:
-            return self.two[:, at - half : at - half + count]
-        return jnp.concatenate([self.one[:, at:], self.two[:, : at + count - half]], axis=1)
+        return total(slice(0, half)), total(slice(half, width))
+
+    def across(self, one, two):
+        one, two = self.over_z(one, 1).astype(LOW), self.over_x(two, 0).astype(LOW)
+        return self.over_x(one, 0), self.over_z(two, 0)
+
+
+def columns_of(halves, at, count):
+    one, two = halves
+    half = one.shape[1]
+    if at + count <= half:
+        return one[:, at : at + count]
+    if at >= half:
+        return two[:, at - half : at - half + count]
+    return jnp.concatenate([one[:, at:], two[:, : at + count - half]], axis=1)
 
 
 ATTEND_STEP = 256
@@ -498,22 +487,21 @@
 
     def kernel(*refs):
         incoming_ref, keep_ref, gain_ref, up_ref, down_ref = refs[n : n + 5]
-        update_ref, mid_ref, normed_ref, hidden_ref, active_ref, part_ref, low_ref = refs[n + 5 :]
-        update = added(refs[:n])
+        mid_ref, normed_ref, slope_ref, active_ref, part_ref, low_ref = refs[n + 5 :]
         keep = keep_ref[0:1, :]
-        mid = keep * incoming_ref[...] + (1.0 - keep) * update
+        mid = keep * incoming_ref[...].astype(HIGH) + (1.0 - keep) * added(refs[:n])
         normed = layer_norm(mid, gain_ref[...]).astype(LOW)
         hidden = plain_dot(normed, up_ref[...])
         active = gelu_of(hidden).astype(LOW)
         part = plain_dot(active, down_ref[...])
-        update_ref[...], mid_ref[...], normed_ref[...] = update, mid, normed
-        hidden_ref[...], active_ref[...] = hidden, active
+        mid_ref[...], normed_ref[...] = mid, normed
+        slope_ref[...], active_ref[...] = gelu_slope_of(hidden).astype(LOW), active
         part_ref[...], low_ref[...] = part, part.astype(LOW)
 
     count, depth = incoming.shape
     inner = up.shape[1]
-    outs = [((count, depth), HIGH), ((count, depth), HIGH), ((count, depth), LOW)]
-    outs += [((count, inner), HIGH), ((count, inner), LOW)]
+    outs = [((count, depth), HIGH), ((count, depth), LOW)]
+    outs += [((count, inner), LOW), ((count, inner), LOW)]
     outs += [((count, depth), HIGH), ((count, depth), LOW)]
     operands = [*parts, incoming, keeps, gain, up, down]
     return fused(kernel, outs, operands, 2 * count * depth * inner, (), count * inner)
@@ -529,42 +517,40 @@
         mlp = added(refs[:n])
         keep = keep_ref[1:2, :]
         slab = (keep * mid_ref[...] + (1.0 - keep) * mlp).astype(LOW)
-        incoming = jnp.where(
-            flag_ref[0] == 1, init_ref[...].astype(HIGH), slab.astype(HIGH)
-        )
-        normed = layer_norm(incoming, gain_ref[...]).astype(LOW)
+        incoming = jnp.where(flag_ref[0] == 1, init_ref[...], slab)
+        normed = layer_norm(incoming.astype(HIGH), gain_ref[...]).astype(LOW)
         qkv = plain_dot(normed, qkv_ref[...]).astype(LOW)
-        mlp_ref[...], slab_ref[...], incoming_ref[...] = mlp, slab, incoming
+        mlp_ref[...], slab_ref[...], incoming_ref[...] = mlp.astype(LOW), slab, incoming
         normed_ref[...], query_ref[...], pair_ref[...] = normed, qkv[:, :width], qkv[:, width:]
 
     count, depth = mid.shape
-    outs = [((count, depth), HIGH), ((count, depth), LOW), ((count, depth), HIGH)]
-    outs += [((count, depth), LOW), ((count, width), LOW), ((count, 2 * width), LOW)]
+    outs = [((count, depth), LOW)] * 4 + [((count, width), LOW), ((count, 2 * width), LOW)]
     operands = [*parts, mid, keeps, init_slab, gain, qkv_flat]
     return fused(kernel, outs, operands, 3 * count * depth * width, [flag])
 
 
-def chain_back_mlp(parts, incoming, grad_mid, flag, keeps, gain, mid, mlp, hidden, up, down):
+def chain_back_mlp(parts, incoming, grad_mid, flag, keeps, gain, mid, mlp, slope, up, down):
     n = len(parts)
-    operands = [*parts, incoming, keeps, gain, mid, mlp, hidden, up, down]
+    operands = [*parts, incoming, keeps, gain, mid, mlp, slope, up, down]
     operands += [] if grad_mid is None else [grad_mid]
 
     def kernel(flag_ref, *refs):
-        incoming_ref, keep_ref, gain_ref, mid_ref, mlp_ref, hidden_ref, up_ref, down_ref = refs[
+        incoming_ref, keep_ref, gain_ref, mid_ref, mlp_ref, slope_ref, up_ref, down_ref = refs[
             n : n + 8
         ]
         grad_ref, state_ref, low_mlp_ref, low_hidden_ref, bias_ref, part_ref, low_ref = refs[-7:]
-        grad = norm_back(incoming_ref[...], gain_ref[...], added(refs[:n]))
+        grad = norm_back(incoming_ref[...].astype(HIGH), gain_ref[...], added(refs[:n]))
         if grad_mid is not None:
             grad = keep_ref[0:1, :] * refs[n + 8][...] + grad
         state = jnp.where(flag_ref[0] == 1, 0.0, grad)
         low_mlp = ((1.0 - keep_ref[1:2, :]) * state).astype(LOW)
         grad_active = dot_second(low_mlp, down_ref[...])
-        low_hidden = (gelu_slope_of(hidden_ref[...]) * grad_active).astype(LOW)
+        low_hidden = (slope_ref[...].astype(HIGH) * grad_active).astype(LOW)
         part = dot_second(low_hidden, up_ref[...])
         grad_ref[...], state_ref[...] = grad, state
         low_mlp_ref[...], low_hidden_ref[...] = low_mlp, low_hidden
-        bias_ref[...] = jnp.sum(state * (mid_ref[...] - mlp_ref[...]), axis=0, keepdims=True)
+        change = mid_ref[...] - mlp_ref[...].astype(HIGH)
+        bias_ref[...] = jnp.sum(state * change, axis=0, keepdims=True)
         part_ref[...], low_ref[...] = part, part.astype(LOW)
 
     count, depth = mid.shape
@@ -576,7 +562,7 @@
 
 
 def chain_back_heads(
-    parts, mid, gain, keeps, grad_state, incoming, update, out_flat, queries, pair, logs, stack, index
+    parts, mid, gain, keeps, grad_state, incoming, out_flat, queries, pair, logs, stack, index
 ):
     n = len(parts)
     count, width = queries.shape
@@ -584,9 +570,9 @@
     slab = keys // CHAIN
 
     def kernel(index_ref, *refs):
-        mid_ref, gain_ref, keep_ref, state_ref, incoming_ref, update_ref, out_ref = refs[n : n + 7]
-        query_ref, pair_ref, own_log_ref, cross_log_ref, stack_ref = refs[n + 7 : n + 12]
-        outs = refs[n + 12 :]
+        mid_ref, gain_ref, keep_ref, state_ref, incoming_ref, out_ref = refs[n : n + 6]
+        query_ref, pair_ref, own_log_ref, cross_log_ref, stack_ref = refs[n + 6 : n + 11]
+        outs = refs[n + 11 :]
         mid_out, low_out, bias_out, query_out, here_out, across_out, sent_out, token_out = outs
         grad_mid = keep_ref[1:2, :] * state_ref[...] + norm_back(
             mid_ref[...], gain_ref[...], added(refs[:n])
@@ -594,9 +580,8 @@
         mid_out[...] = grad_mid
         low = ((1.0 - keep_ref[0:1, :]) * grad_mid).astype(LOW)
         low_out[...] = low
-        bias_out[...] = jnp.sum(
-            grad_mid * (incoming_ref[...] - update_ref[...]), axis=0, keepdims=True
-        )
+        change = incoming_ref[...].astype(HIGH) - mid_ref[...]
+        bias_out[...] = jnp.sum(grad_mid * change, axis=0, keepdims=True)
         grad_heads = dot_second(low, out_ref[...]).astype(LOW)
         token = stack_ref[index_ref[0]]
         for h in range(width // E):
@@ -629,7 +614,7 @@
     outs = [((count, depth), HIGH), ((count, depth), LOW), ((1, depth), HIGH)]
     outs += [((count, width), HIGH), ((slab, 2 * width), HIGH), ((slab, 2 * width), HIGH)]
     outs += [((2 * slab, 2 * width), LOW), ((keys, 2 * width), HIGH)]
-    operands = [*parts, mid, gain, keeps, grad_state, incoming, update, out_flat]
+    operands = [*parts, mid, gain, keeps, grad_state, incoming, out_flat]
     operands += [queries, pair, *logs, stack]
     products = count * width * (10 * keys + 2 * depth)
     return fused(kernel, outs, operands, products, [index], 2 * count * keys)
@@ -740,8 +725,8 @@
         return lax.dynamic_slice_in_dim(slab, tp_index * thin_rows, thin_rows, 0)
 
     init_late = tied(init_slab, win_ffn_in[1])
-    state_incoming = init_late.astype(HIGH)
-    state_normed = layer_norm(state_incoming, norm_state).astype(LOW)
+    state_incoming = init_late
+    state_normed = layer_norm(state_incoming.astype(HIGH), norm_state).astype(LOW)
     state_qkv = plain_dot(state_normed, qkv_state_flat).astype(LOW)
     state_queries = state_qkv[:, :width]
     state_pieces = pos_gather(state_qkv[:, width:])
@@ -769,7 +754,7 @@
         if turn == 1:
             own_heads, own_token_logs = attend(tied(queries, part), pair, before)
             parts = tied(parts, own_heads)
-        update, mid_state, state_ffn_in, state_hidden, state_active, part, low = chain_mlp(
+        mid_state, state_ffn_in, state_slope, state_active, part, low = chain_mlp(
             parts, state_incoming, keeps, gain_sffn, up_state, down_state
         )
         parts = [part] + sent_around(low)
@@ -785,10 +770,9 @@
                 state_pair,
                 (own_logs, cross_logs),
                 state_heads,
-                update,
                 mid_state,
                 state_ffn_in,
-                state_hidden,
+                state_slope,
                 state_active,
                 state_mlp,
             )
@@ -848,7 +832,7 @@
     last_parts = [part] + sent_around(low)
 
     def last_state(after):
-        _, mid_state, _, _, _, part, _ = chain_mlp(
+        mid_state, _, _, _, part, _ = chain_mlp(
             tied(last_parts, after), last_incoming, keeps, gain_sffn, up_state, down_state
         )
         state_mlp = tp_total(part)
@@ -873,7 +857,7 @@
     parts = tied(parts, query_grad)
     kept_qkv, kept_rest = [(state_normed, grad_state_qkv)], []
     token_pair_grads = [None] * CHAIN
-    init_grad = jnp.zeros((thin_rows, model_width), HIGH)
+    init_grad = jnp.zeros((slab_rows, model_width), HIGH)
     bias_one = bias_two = jnp.zeros((1, model_width), HIGH)
     grad_mid = None
     for turn in reversed(range(CHAIN - 1)):
@@ -885,10 +869,9 @@
             state_pair,
             logs,
             state_heads,
-            update,
             mid_state,
             state_ffn_in,
-            state_hidden,
+            state_slope,
             state_active,
             state_mlp,
         ) = turns[turn]
@@ -901,11 +884,11 @@
             gain_state,
             mid_state,
             state_mlp,
-            state_hidden,
+            state_slope,
             up_state,
             down_state,
         )
-        init_grad = init_grad + jnp.where(flags[turn + 1], own_rows(grad_next), 0.0)
+        init_grad = init_grad + jnp.where(flags[turn + 1], grad_next, 0.0)
         bias_two = bias_two + sums
         parts = [part] + sent_around(low)
         if turn == CHAIN - 2:
@@ -929,7 +912,6 @@
             keeps,
             grad_state,
             state_incoming,
-            update,
             out_state_flat,
             state_queries,
             state_pair,
@@ -960,11 +942,10 @@
         if turn:
             parts = [part] + sent_around(low)
 
-    def first_incoming_grad(after):
-        normed_grad = tp_total(tied(part, after))
-        return keep_one * grad_mid + norm_back(turns[0][0], norm_state, normed_grad)
-
-    bias_one = bias_one[0] * keep_one * (1.0 - keep_one) / n_tp
+    init_grad = init_grad + jnp.where(flags[0], keep_one * grad_mid, 0.0)
+    first_part = norm_back(turns[0][0].astype(HIGH), norm_state, part)
+    init_grad = init_grad / n_tp + jnp.where(flags[0], first_part, 0.0)
+    bias_one = bias_one[0] * keep_one / n_tp
     bias_two = bias_two[0] * keep_two * (1.0 - keep_two) / n_tp
 
     token_pair_grads[CHAIN - 1] = jnp.zeros_like(token_pair_grads[0])
@@ -1012,30 +993,26 @@
     grad_win_ffn_in = tied(grad_win_ffn_in, middle_grads.other)
     grad_win_mixed = grad_layer_one + norm_back(win_mixed, norm_wffn, grad_win_ffn_in)
     grad_win_pieces = tp_gather(grad_win_mixed.astype(LOW))
-    step = middle_grads.cores(grad_win_mixed)
-    grad_win_proj = tied(jnp.concatenate(grad_win_pieces), step)
+    middle_halves = middle_grads.cores(grad_win_mixed)
+    grad_win_proj = jnp.concatenate(grad_win_pieces)
     grad_win_heads = dot_second(grad_win_proj, out_win).astype(LOW)
     win_query_grad, win_pair_grad, win_prev_grad = attend_back(
         win_queries, win_pair, win_logs, grad_win_heads, win_before
     )
     win_returned = lax.ppermute(win_prev_grad, "seq", homeward)
-    after = win_query_grad, win_pair_grad
-    middle_grads.one_first(grad_win_heads)
-    middle_grads.two_first(grad_win_heads)
-    first_grad = own_rows(first_incoming_grad(after))
-    init_grad = init_grad + jnp.where(flags[0], first_grad, 0.0)
     win_pair_grad = win_pair_grad + tied(win_returned, state_grads.total).astype(HIGH)
     grad_win_qkv = jnp.concatenate([win_query_grad, win_pair_grad], axis=1).astype(LOW)
 
     small_rows = jnp.concatenate(
         [init_grad, jnp.stack([bias_one, bias_two]), jnp.zeros((14, model_width), HIGH)]
     ).astype(LOW)
-    row_of = lax.broadcasted_iota(jnp.int32, (small_rows.shape[0], 256), 0)
-    column_of = lax.broadcasted_iota(jnp.int32, (small_rows.shape[0], 256), 1)
+    small_shape = small_rows.shape[0], state_rows + 128
+    row_of = lax.broadcasted_iota(jnp.int32, small_shape, 0)
+    column_of = lax.broadcasted_iota(jnp.int32, small_shape, 1)
     column_for = jnp.where(
-        row_of < thin_rows,
-        position * thin_rows + row_of,
-        (CHAIN - 1) * thin_rows + row_of,
+        row_of < slab_rows,
+        position * slab_rows + row_of,
+        (CHAIN - 1) * slab_rows + row_of,
     )
     selector = (column_of == column_for).astype(LOW)
     last_grads = SeqSum(
@@ -1050,26 +1027,29 @@
     grad_win_normed = tp_scatter(
         [dot_second(part, qkv_win_flat) for part in split_rows(grad_win_qkv, n_tp)]
     )
-    step = last_grads.cores(last_grads.other)
-    step = middle_grads.one_last(step), middle_grads.two_last(step)
-    last_grads.one_first(step)
-    last_grads.two_first(step)
-    step = last_grads.one, last_grads.two
-    last_grads.one_last(step)
-    last_grads.two_last(step)
+    last_halves = last_grads.cores(last_grads.other)
+    split_at = [half.shape[-1] for half in middle_halves]
+    one, two = last_grads.across(
+        *[jnp.concatenate(both, axis=-1) for both in zip(middle_halves, last_halves)]
+    )
+    middle_halves = one[:, : split_at[0]], two[:, : split_at[1]]
+    last_halves = one[:, split_at[0] :], two[:, split_at[1] :]
     back_input = norm_back(own_input, norm_win, grad_win_normed)
     grad_token_rows = natural(tp_gather((grad_win_mixed + back_input).astype(LOW)))
-    output_rows = natural(tp_gather(tied(layer_output.astype(LOW), after)))
+    output_rows = natural(tp_gather(tied(layer_output.astype(LOW), win_returned)))
 
     own_columns = model_width // lax.axis_size("seq")
     inner_width = up_tok.shape[1]
-    sum_qkv_win = last_grads.columns(0, 3 * width)
-    sum_qkv_tok = middle_grads.columns(0, 3 * width)
+    token_grads.total, state_grads.total = tied(
+        (token_grads.total, state_grads.total), last_grads.other
+    )
+    sum_qkv_win = columns_of(last_halves, 0, 3 * width)
+    sum_qkv_tok = columns_of(middle_halves, 0, 3 * width)
     sum_qkv_state = state_grads.columns(0, 3 * width)
-    sum_up_win = middle_grads.columns(3 * width, inner_width)
+    sum_up_win = columns_of(middle_halves, 3 * width, inner_width)
     sum_up_tok = token_grads.columns(0, inner_width)
     sum_up_state = state_grads.columns(5 * width, inner_width)
-    small_sums = last_grads.columns(4 * width, CHAIN * thin_rows + 2)
+    small_sums = columns_of(last_halves, 4 * width, state_rows + 2)
     first_row = seq_index * own_columns
     vectors = [
         gain_grad(qkv_win_flat, sum_qkv_win, norm_win, first_row),
@@ -1079,14 +1059,10 @@
         gain_grad(qkv_state_flat, sum_qkv_state, norm_state, first_row),
         gain_grad(up_state, sum_up_state, norm_sffn, first_row),
     ]
-    small_sums = jnp.concatenate([small_sums, jnp.stack(vectors, axis=1)], axis=1)
-    small_sums = tp_gather(small_sums)
-    init_part = turned(
-        jnp.stack([part[:, : CHAIN * thin_rows] for part in small_sums]),
-        (n_tp - tp_index) % n_tp,
-    ).reshape(n_tp, own_columns, CHAIN, thin_rows)
-    sum_init = jnp.transpose(init_part, (2, 0, 3, 1)).reshape(state_rows, own_columns)
-    vector_sums = sum(part[:, CHAIN * thin_rows :] for part in small_sums)
+    small_sums = sum(
+        tp_gather(jnp.concatenate([small_sums] + vectors, axis=1))
+    )
+    sum_init, vector_sums = small_sums[:, :state_rows].T, small_sums[:, state_rows:]
 
     def qkv_of(columns):
         return columns.reshape(own_columns, 3, width)
@@ -1100,10 +1076,10 @@
         grad_token_rows,
         vector_sums[:, 2],
         qkv_of(sum_qkv_win),
-        last_grads.columns(3 * width, width).T,
+        columns_of(last_halves, 3 * width, width).T,
         vector_sums[:, 3],
         sum_up_win,
-        middle_grads.columns(3 * width + inner_width, inner_width).T,
+        columns_of(middle_halves, 3 * width + inner_width, inner_width).T,
         vector_sums[:, 4],
         qkv_of(sum_qkv_tok),
         out_of(token_grads.columns(2 * inner_width, 2 * width)),

time: 872 us -> 865 us (level)
  starting transfers between devices: 207 us -> 186 us
    ppermute x69 -> x66, waiting for transfers between devices: 182 us -> 151 us  [tp_to(): return lax.ppermute(array, 'tp', [(i, (i + k) % n) for i in range(n)])]
    ppermute x24 -> x12, starting transfers between devices: 41 us -> 22.4 us  [stage(): total = total + lax.ppermute(sent, 'seq', self.pairs(*step(k))).astype(HIGH)]
    ppermute x30, waiting for transfers between devices: 71 us -> 85.9 us  [tp_from(): return lax.ppermute(array, 'tp', [((i + k) % n, i) for i in range(n)])]
    unnamed x751 -> x742, local copies, waits for them, and re-layouts: 86.7 us -> 96.6 us
    ppermute x31, waiting for transfers between devices: 43.8 us -> 53.4 us  [swap(): return lax.ppermute(array, 'seq', [(s, s ^ k) for s in range(n)])]
    ppermute x24 -> x12, waiting for transfers between devices: 15.4 us -> 20.2 us  [stage(): total = total + lax.ppermute(sent, 'seq', self.pairs(*step(k))).astype(HIGH)]
    ppermute x69 -> x66, starting transfers between devices: 103 us -> 102 us  [tp_to(): return lax.ppermute(array, 'tp', [(i, (i + k) % n) for i in range(n)])]
  transfers between devices with their start and end apart: 159 -> 144, of which waited for: 87 -> 82; matrix products, arithmetic and copies ran while one was open for 13% -> 13% of each run, Pallas kernels for 5% -> 6%
where the time goes in v8:
time: 865 us; the launch traced here: 854 us
  waiting for transfers between devices  311 us (36%)
  starting transfers between devices  186 us (22%)
  local copies, waits for them, and re-layouts  128 us (15%)
  Pallas kernels  82.7 us (10%)
  other arithmetic  62.5 us (7%)
  matrix products  62.5 us (7%)
  between operations  21.3 us (2%)
    ppermute x66, waiting for transfers between devices, tp_to(): return lax.ppermute(array, 'tp', [(i, (i + k) % n) for i in range(n)])  151 us
    ppermute x66, starting transfers between devices, tp_to(): return lax.ppermute(array, 'tp', [(i, (i + k) % n) for i in range(n)])  102 us
    unnamed x742, local copies, waits for them, and re-layouts  96.6 us
    ppermute x30, waiting for transfers between devices, tp_from(): return lax.ppermute(array, 'tp', [((i + k) % n, i) for i in range(n)])  85.9 us
    pallas_call x27, Pallas kernels, fused(): pl.pallas_call(kernel, out_shape=[jax.ShapeDtypeStruct(shape, kind) for s...  63.2 us
    ppermute x31, waiting for transfers between devices, swap(): return lax.ppermute(array, 'seq', [(s, s ^ k) for s in range(n)])  53.4 us
    dot_general x27, matrix products, plain_dot(): return jnp.dot(former, latter, preferred_element_type=HIGH)  39.6 us
    ppermute x30, starting transfers between devices, tp_from(): return lax.ppermute(array, 'tp', [((i + k) % n, i) for i in range(n)])  31.1 us
  transfers between devices with their start and end apart: 144, of which 82 were waited for; matrix products, arithmetic and copies ran while one was open for 13% of the time, Pallas kernels for 6%

profile of v8, /device:TPU:0, one launch (start us, length us, event | category | flops | bytes accessed | tf_op | source)
XLA Modules:
  0.0 853.7 jit_solution(8550198826508094740)
XLA Ops:
  39.5 6.2 collective-permute-done.2
  59.8 7.3 collective-permute-start.11
  115.1 11.1 %collective-permute-done.17 = bf16[512,512]{1,0:T(8,128)(2,1)S(1)} collective-permute-done((bf16[512,512]{1,0:T(8,128)(2,1)S(1)}, bf16[512,512]{1,0:T(8,128)(2,1)S(1)}, u32[]{:S(2)}, u32[]{:S(2)}) %collective-permute-start.17) | collective-permute-done | bytes 524320 | tf_op jit(solution)/shard_map/ppermute | solution.py:120
  139.8 5.8 collective-permute-done.19.refs_1_
  145.6 4.8 collective-permute-done.20.refs_2_
  205.6 4.8 collective-permute-done.29.refs_2_
  217.4 5.2 collective-permute-done.31.refs_1_
  250.9 5.8 collective-permute-done.37.refs_1_
  256.7 4.8 collective-permute-done.38.refs_2_
  270.0 5.2 collective-permute-done.40.refs_1_
  314.6 5.2 collective-permute-done.47
  326.2 11.2 %collective-permute-done.51.refs_3_ = bf16[128,1024]{1,0:T(8,128)(2,1)} collective-permute-done((bf16[128,1024]{1,0:T(8,128)(2,1)}, bf16[128,1024]{1,0:T(8,128)(2,1)}, u32[]{:S(2)}, u32[]{:S(2)}) %collective-permute-start.51) | collective-permute-done | bytes 262176 | tf_op jit(solution)/shard_map/ppermute | solution.py:79
  354.2 4.9 collective-permute-done.53
  363.6 7.0 collective-permute-done.55.refs_14_
  411.3 4.7 shard_map.414
  458.0 5.1 collective-permute-done.73
  470.9 7.1 collective-permute-done.75.refs_1_
  478.0 4.7 collective-permute-done.76.refs_2_
  600.3 4.8 collective-permute-done.102
  616.4 5.2 shard_map.425
  629.4 9.2 %collective-permute-done.97 = bf16[512,512]{1,0:T(8,128)(2,1)S(1)} collective-permute-done((bf16[512,512]{1,0:T(8,128)(2,1)S(1)}, bf16[512,512]{1,0:T(8,128)(2,1)S(1)}, u32[]{:S(2)}, u32[]{:S(2)}) %collective-permute-start.97) | collective-permute-done | bytes 524320 | tf_op jit(solution)/shard_map/ppermute | solution.py:120
  646.8 4.7 collective-permute-done.103
  658.5 7.5 collective-permute-done.106.refs_15_
  676.5 6.0 shard_map.426
  690.8 5.6 collective-permute-done.112
  699.3 4.9 collective-permute-done.114
  705.9 5.0 shard_map.427
  755.5 5.3 collective-permute-done.120
  771.0 7.2 collective-permute-done.122
  789.2 5.7 collective-permute-start.127
  795.5 5.8 collective-permute-done.133
  804.1 7.9 collective-permute-done.134
  (1258 shorter events, 637.2 us)
Async XLA Ops:
  7.2 571.1 %reduce-scatter.3.cloned.1.call-start = ((), (), s32[]{:S(2)}) async-start(), calls=%async_computation.2 | async-start | bytes 5406720 | tf_op jit(solution)/shard_map/reduce_scatter | solution.py:212
  55.4 21.4 %collective-permute-start.8 = (bf16[128,1024]{1,0:T(8,128)(2,1)S(1)}, bf16[128,1024]{1,0:T(8,128)(2,1)S(1)}, u32[]{:S(2)}, u32[]{:S(2)}) collective-permute-start(bf16[128,1024]{1,0:T(8,128)(2,1)S(1)} %multiply_convert_fusion.11.refs_5_), channel_id=1, source_target_pairs={{3,0},{0,1},{1,2},{2,3},{7,4},{4,5},{5,6},{6,7},{11,8},{8,9},{9,10... | collective-permute-start | bytes 786440 | tf_op jit(solution)/shard_map/ppermute | solution.py:79
  59.8 24.5 %collective-permute-start.11 = (bf16[128,512]{1,0:T(8,128)(2,1)S(1)}, bf16[128,512]{1,0:T(8,128)(2,1)S(1)}, u32[]{:S(2)}, u32[]{:S(2)}) collective-permute-start(bf16[128,512]{1,0:T(8,128)(2,1)S(1)} %slice.335.refs_0_), channel_id=1, source_target_pairs={{0,8},{4,12},{8,0},{12,4},{16,24},{20,28},{24,16},{28,20},{32,40},... | collective-permute-start | bytes 393224 | tf_op jit(solution)/shard_map/ppermute | solution.py:120
  69.8 14.9 %collective-permute-start.5 = (bf16[128,1024]{1,0:T(8,128)(2,1)S(1)}, bf16[128,1024]{1,0:T(8,128)(2,1)S(1)}, u32[]{:S(2)}, u32[]{:S(2)}) collective-permute-start(bf16[128,1024]{1,0:T(8,128)(2,1)S(1)} %convolution_convert_fusion.24), channel_id=1, source_target_pairs={{0,2},{1,3},{2,0},{3,1},{4,6},{5,7},{6,4},{7,5},{8,10},{9,11},{10,... | collective-permute-start | bytes 786440 | tf_op jit(solution)/shard_map/ppermute | solution.py:84
  321.9 15.4 %collective-permute-start.51 = (bf16[128,1024]{1,0:T(8,128)(2,1)}, bf16[128,1024]{1,0:T(8,128)(2,1)}, u32[]{:S(2)}, u32[]{:S(2)}) collective-permute-start(bf16[128,1024]{1,0:T(8,128)(2,1)} %multiply_convert_fusion.5.refs_0_), channel_id=1, source_target_pairs={{3,0},{0,1},{1,2},{2,3},{7,4},{4,5},{5,6},{6,7},{11,8},{8,9},{9,10... | collective-permute-start | bytes 786440 | tf_op jit(solution)/shard_map/ppermute | solution.py:79
  322.1 19.7 %collective-permute-start.50 = (bf16[128,1024]{1,0:T(8,128)(2,1)}, bf16[128,1024]{1,0:T(8,128)(2,1)S(1)}, u32[]{:S(2)}, u32[]{:S(2)}) collective-permute-start(bf16[128,1024]{1,0:T(8,128)(2,1)} %multiply_convert_fusion.5.refs_0_), channel_id=1, source_target_pairs={{2,0},{3,1},{0,2},{1,3},{6,4},{7,5},{4,6},{5,7},{10,8},{11,9},{8,1... | collective-permute-start | bytes 786440 | tf_op jit(solution)/shard_map/ppermute | solution.py:79
  324.0 20.6 %collective-permute-start.49 = (bf16[128,1024]{1,0:T(8,128)(2,1)}, bf16[128,1024]{1,0:T(8,128)(2,1)S(1)}, u32[]{:S(2)}, u32[]{:S(2)}) collective-permute-start(bf16[128,1024]{1,0:T(8,128)(2,1)} %multiply_convert_fusion.5.refs_0_), channel_id=1, source_target_pairs={{1,0},{2,1},{3,2},{0,3},{5,4},{6,5},{7,6},{4,7},{9,8},{10,9},{11,1... | collective-permute-start | bytes 786440 | tf_op jit(solution)/shard_map/ppermute | solution.py:79
  389.5 14.7 %collective-permute-start.62 = (bf16[128,1024]{1,0:T(8,128)(2,1)S(1)}, bf16[128,1024]{1,0:T(8,128)(2,1)S(1)}, u32[]{:S(2)}, u32[]{:S(2)}) collective-permute-start(bf16[128,1024]{1,0:T(8,128)(2,1)S(1)} %get-tuple-element.253), channel_id=1, source_target_pairs={{0,1},{1,2},{2,3},{3,0},{4,5},{5,6},{6,7},{7,4},{8,9},{9,10},{10,1... | collective-permute-start | bytes 786440 | tf_op jit(solution)/shard_map/ppermute | solution.py:84
  418.3 315.5 %reduce-scatter.5.cloned.1.call-start = ((), (), s32[]{:S(2)}) async-start(), calls=%async_computation.3 | async-start | bytes 7028736 | tf_op jit(solution)/shard_map/reduce_scatter | solution.py:212
  419.0 16.0 %collective-permute-start.65 = (bf16[128,1024]{1,0:T(8,128)(2,1)}, bf16[128,1024]{1,0:T(8,128)(2,1)S(1)}, u32[]{:S(2)}, u32[]{:S(2)}) collective-permute-start(bf16[128,1024]{1,0:T(8,128)(2,1)} %copy-done.267), channel_id=1, source_target_pairs={{0,1},{1,2},{2,3},{3,0},{4,5},{5,6},{6,7},{7,4},{8,9},{9,10},{10,1... | collective-permute-start | bytes 786440 | tf_op jit(solution)/shard_map/ppermute | solution.py:84
  448.1 15.1 %collective-permute-start.73 = (bf16[128,1024]{1,0:T(8,128)(2,1)S(1)}, bf16[128,1024]{1,0:T(8,128)(2,1)S(1)}, u32[]{:S(2)}, u32[]{:S(2)}) collective-permute-start(bf16[128,1024]{1,0:T(8,128)(2,1)S(1)} %convert_element_type.510), channel_id=1, source_target_pairs={{0,1},{1,2},{2,3},{3,0},{4,5},{5,6},{6,7},{7,4},{8,9},{9,10},{10,1... | collective-permute-start | bytes 786440 | tf_op jit(solution)/shard_map/ppermute | solution.py:84
  467.7 15.0 %collective-permute-start.76 = (bf16[128,1024]{1,0:T(8,128)(2,1)}, bf16[128,1024]{1,0:T(8,128)(2,1)}, u32[]{:S(2)}, u32[]{:S(2)}) collective-permute-start(bf16[128,1024]{1,0:T(8,128)(2,1)} %get-tuple-element.295), channel_id=1, source_target_pairs={{0,1},{1,2},{2,3},{3,0},{4,5},{5,6},{6,7},{7,4},{8,9},{9,10},{10,1... | collective-permute-start | bytes 786440 | tf_op jit(solution)/shard_map/ppermute | solution.py:84
  563.4 14.9 %collective-permute-start.90 = (bf16[128,1024]{1,0:T(8,128)(2,1)}, bf16[128,1024]{1,0:T(8,128)(2,1)}, u32[]{:S(2)}, u32[]{:S(2)}) collective-permute-start(bf16[128,1024]{1,0:T(8,128)(2,1)} %get-tuple-element.318), channel_id=1, source_target_pairs={{0,1},{1,2},{2,3},{3,0},{4,5},{5,6},{6,7},{7,4},{8,9},{9,10},{10,1... | collective-permute-start | bytes 786440 | tf_op jit(solution)/shard_map/ppermute | solution.py:84
  571.7 57.6 %collective-permute-start.95 = (bf16[512,512]{1,0:T(8,128)(2,1)}, bf16[512,512]{1,0:T(8,128)(2,1)}, u32[]{:S(2)}, u32[]{:S(2)}) collective-permute-start(bf16[512,512]{1,0:T(8,128)(2,1)} %copy-done.255), channel_id=1, source_target_pairs={{4,0},{8,4},{12,8},{20,16},{24,20},{28,24},{36,32},{40,36},{44,40}... | collective-permute-start | bytes 1572872 | tf_op jit(solution)/shard_map/ppermute | solution.py:821
  589.3 15.8 %collective-permute-start.102 = (bf16[4,32,1024]{2,1,0:T(8,128)(2,1)S(1)}, bf16[4,32,1024]{2,1,0:T(8,128)(2,1)S(1)}, u32[]{:S(2)}, u32[]{:S(2)}) collective-permute-start(bf16[4,32,1024]{2,1,0:T(8,128)(2,1)S(1)} %copy-done.300), channel_id=1, source_target_pairs={{3,0},{0,1},{1,2},{2,3},{7,4},{4,5},{5,6},{6,7},{11,8},{8,9},{9,10... | collective-permute-start | bytes 786440 | tf_op jit(solution)/shard_map/ppermute | solution.py:79
  590.1 15.4 %collective-permute-start.98 = (bf16[256,512]{1,0:T(8,128)(2,1)S(1)}, bf16[256,512]{1,0:T(8,128)(2,1)S(1)}, u32[]{:S(2)}, u32[]{:S(2)}) collective-permute-start(bf16[256,512]{1,0:T(8,128)(2,1)S(1)} %get-tuple-element.344), channel_id=1, source_target_pairs={{0,4},{4,0},{8,12},{12,8},{16,20},{20,16},{24,28},{28,24},{32,36},... | collective-permute-start | bytes 786440 | tf_op jit(solution)/shard_map/ppermute | solution.py:120
  597.1 27.4 %collective-permute-start.96 = (bf16[1024,512]{1,0:T(8,128)(2,1)}, bf16[1024,512]{1,0:T(8,128)(2,1)}, u32[]{:S(2)}, u32[]{:S(2)}) collective-permute-start(bf16[1024,512]{1,0:T(8,128)(2,1)} %pad_maximum_fusion.4), channel_id=1, source_target_pairs={{0,4},{4,0},{8,12},{12,8},{16,20},{20,16},{24,28},{28,24},{32,36},... | collective-permute-start | bytes 3145736 | tf_op jit(solution)/shard_map/ppermute | solution.py:120
  599.5 27.4 %collective-permute-start.92 = (bf16[128,1024]{1,0:T(8,128)(2,1)}, bf16[128,1024]{1,0:T(8,128)(2,1)}, u32[]{:S(2)}, u32[]{:S(2)}) collective-permute-start(bf16[128,1024]{1,0:T(8,128)(2,1)} %convolution_convert_fusion.15), channel_id=1, source_target_pairs={{0,2},{1,3},{2,0},{3,1},{4,6},{5,7},{6,4},{7,5},{8,10},{9,11},{10,... | collective-permute-start | bytes 786440 | tf_op jit(solution)/shard_map/ppermute | solution.py:84
  605.1 21.9 %collective-permute-start.93 = (bf16[128,1024]{1,0:T(8,128)(2,1)}, bf16[128,1024]{1,0:T(8,128)(2,1)}, u32[]{:S(2)}, u32[]{:S(2)}) collective-permute-start(bf16[128,1024]{1,0:T(8,128)(2,1)} %convolution_convert_fusion.14), channel_id=1, source_target_pairs={{0,1},{1,2},{2,3},{3,0},{4,5},{5,6},{6,7},{7,4},{8,9},{9,10},{10,1... | collective-permute-start | bytes 786440 | tf_op jit(solution)/shard_map/ppermute | solution.py:84
  610.7 16.3 %collective-permute-start.94 = (bf16[128,1024]{1,0:T(8,128)(2,1)}, bf16[128,1024]{1,0:T(8,128)(2,1)}, u32[]{:S(2)}, u32[]{:S(2)}) collective-permute-start(bf16[128,1024]{1,0:T(8,128)(2,1)} %convolution_convert_fusion.13), channel_id=1, source_target_pairs={{0,3},{1,0},{2,1},{3,2},{4,7},{5,4},{6,5},{7,6},{8,11},{9,8},{10,9... | collective-permute-start | bytes 786440 | tf_op jit(solution)/shard_map/ppermute | solution.py:84
  657.5 15.2 %collective-permute-start.110 = (bf16[128,1024]{1,0:T(8,128)(2,1)S(1)}, bf16[128,1024]{1,0:T(8,128)(2,1)S(1)}, u32[]{:S(2)}, u32[]{:S(2)}) collective-permute-start(bf16[128,1024]{1,0:T(8,128)(2,1)S(1)} %get-tuple-element.467.refs_13_), channel_id=1, source_target_pairs={{3,0},{0,1},{1,2},{2,3},{7,4},{4,5},{5,6},{6,7},{11,8},{8,9},{9,10... | collective-permute-start | bytes 786440 | tf_op jit(solution)/shard_map/ppermute | solution.py:79
  685.3 43.3 %collective-permute-start.125 = (bf16[512,2816]{1,0:T(8,128)(2,1)}, bf16[512,2816]{1,0:T(8,128)(2,1)}, u32[]{:S(2)}, u32[]{:S(2)}) collective-permute-start(bf16[512,2816]{1,0:T(8,128)(2,1)} %get-tuple-element.377), channel_id=1, source_target_pairs={{0,4},{4,0},{8,12},{12,8},{16,20},{20,16},{24,28},{28,24},{32,36},... | collective-permute-start | bytes 8650760 | tf_op jit(solution)/shard_map/ppermute | solution.py:120
  689.4 14.8 %collective-permute-start.114 = (bf16[128,1024]{1,0:T(8,128)(2,1)}, bf16[128,1024]{1,0:T(8,128)(2,1)S(1)}, u32[]{:S(2)}, u32[]{:S(2)}) collective-permute-start(bf16[128,1024]{1,0:T(8,128)(2,1)} %get-tuple-element.465), channel_id=1, source_target_pairs={{3,0},{0,1},{1,2},{2,3},{7,4},{4,5},{5,6},{6,7},{11,8},{8,9},{9,10... | collective-permute-start | bytes 786440 | tf_op jit(solution)/shard_map/ppermute | solution.py:79
  753.0 29.6 %collective-permute-start.126 = (bf16[512,1664]{1,0:T(8,128)(2,1)}, bf16[512,1664]{1,0:T(8,128)(2,1)}, u32[]{:S(2)}, u32[]{:S(2)}) collective-permute-start(bf16[512,1664]{1,0:T(8,128)(2,1)} %get-tuple-element.390), channel_id=1, source_target_pairs={{0,4},{4,0},{8,12},{12,8},{16,20},{20,16},{24,28},{28,24},{32,36},... | collective-permute-start | bytes 5111816 | tf_op jit(solution)/shard_map/ppermute | solution.py:120
  762.5 15.7 %collective-permute-start.122 = (bf16[128,1024]{1,0:T(8,128)(2,1)}, bf16[128,1024]{1,0:T(8,128)(2,1)S(1)}, u32[]{:S(2)}, u32[]{:S(2)}) collective-permute-start(bf16[128,1024]{1,0:T(8,128)(2,1)} %get-tuple-element.464), channel_id=1, source_target_pairs={{1,0},{2,1},{3,2},{0,3},{5,4},{6,5},{7,6},{4,7},{9,8},{10,9},{11,1... | collective-permute-start | bytes 786440 | tf_op jit(solution)/shard_map/ppermute | solution.py:79
  766.3 15.6 %collective-permute-start.124 = (bf16[128,1024]{1,0:T(8,128)(2,1)}, bf16[128,1024]{1,0:T(8,128)(2,1)S(1)}, u32[]{:S(2)}, u32[]{:S(2)}) collective-permute-start(bf16[128,1024]{1,0:T(8,128)(2,1)} %get-tuple-element.464), channel_id=1, source_target_pairs={{3,0},{0,1},{1,2},{2,3},{7,4},{4,5},{5,6},{6,7},{11,8},{8,9},{9,10... | collective-permute-start | bytes 786440 | tf_op jit(solution)/shard_map/ppermute | solution.py:79
  784.2 17.1 %collective-permute-start.133 = (bf16[4,32,2176]{2,1,0:T(8,128)(2,1)S(1)}, bf16[4,32,2176]{2,1,0:T(8,128)(2,1)S(1)}, u32[]{:S(2)}, u32[]{:S(2)}) collective-permute-start(bf16[4,32,2176]{2,1,0:T(8,128)(2,1)S(1)} %get-tuple-element.499), channel_id=1, source_target_pairs={{0,16},{4,20},{8,24},{12,28},{16,0},{20,4},{24,8},{28,12},{32,48},... | collective-permute-start | bytes 1671176 | tf_op jit(solution)/shard_map/ppermute | solution.py:249
  784.3 27.8 %collective-permute-start.134 = (bf16[4,32,2176]{2,1,0:T(8,128)(2,1)S(1)}, bf16[4,32,2176]{2,1,0:T(8,128)(2,1)S(1)}, u32[]{:S(2)}, u32[]{:S(2)}) collective-permute-start(bf16[4,32,2176]{2,1,0:T(8,128)(2,1)S(1)} %get-tuple-element.500), channel_id=1, source_target_pairs={{0,8},{4,12},{8,16},{12,20},{16,24},{20,28},{24,0},{28,4},{32,40},... | collective-permute-start | bytes 1671176 | tf_op jit(solution)/shard_map/ppermute | solution.py:249
  785.4 26.6 %collective-permute-start.135 = (bf16[4,32,2176]{2,1,0:T(8,128)(2,1)S(1)}, bf16[4,32,2176]{2,1,0:T(8,128)(2,1)S(1)}, u32[]{:S(2)}, u32[]{:S(2)}) collective-permute-start(bf16[4,32,2176]{2,1,0:T(8,128)(2,1)S(1)} %get-tuple-element.501), channel_id=1, source_target_pairs={{0,24},{4,28},{8,0},{12,4},{16,8},{20,12},{24,16},{28,20},{32,56},... | collective-permute-start | bytes 1671176 | tf_op jit(solution)/shard_map/ppermute | solution.py:249
  789.2 27.2 %collective-permute-start.127 = (bf16[4,32,2304]{2,1,0:T(8,128)(2,1)S(1)}, bf16[4,32,2304]{2,1,0:T(8,128)(2,1)S(1)}, u32[]{:S(2)}, u32[]{:S(2)}) collective-permute-start(bf16[4,32,2304]{2,1,0:T(8,128)(2,1)S(1)} %get-tuple-element.496), channel_id=1, source_target_pairs={{0,64},{4,68},{8,72},{12,76},{16,80},{20,84},{24,88},{28,92},{32,9... | collective-permute-start | bytes 1769480 | tf_op jit(solution)/shard_map/ppermute | solution.py:249
  794.9 27.0 %collective-permute-start.128 = (bf16[4,32,2304]{2,1,0:T(8,128)(2,1)S(1)}, bf16[4,32,2304]{2,1,0:T(8,128)(2,1)S(1)}, u32[]{:S(2)}, u32[]{:S(2)}) collective-permute-start(bf16[4,32,2304]{2,1,0:T(8,128)(2,1)S(1)} %get-tuple-element.497), channel_id=1, source_target_pairs={{0,32},{4,36},{8,40},{12,44},{16,48},{20,52},{24,56},{28,60},{32,6... | collective-permute-start | bytes 1769480 | tf_op jit(solution)/shard_map/ppermute | solution.py:249
  801.3 21.1 %collective-permute-start.129 = (bf16[4,32,2304]{2,1,0:T(8,128)(2,1)S(1)}, bf16[4,32,2304]{2,1,0:T(8,128)(2,1)S(1)}, u32[]{:S(2)}, u32[]{:S(2)}) collective-permute-start(bf16[4,32,2304]{2,1,0:T(8,128)(2,1)S(1)} %get-tuple-element.498), channel_id=1, source_target_pairs={{0,96},{4,100},{8,104},{12,108},{16,112},{20,116},{24,120},{28,124... | collective-permute-start | bytes 1769480 | tf_op jit(solution)/shard_map/ppermute | solution.py:249
  (477 other events, 4073.8 us)
Sparse Core Ops, SparseCore 0:
  418.4 85.8 reduce-scatter.2
  624.5 86.8 reduce-scatter.4

commit v9 on v8

--- a/solution.py
+++ b/solution.py
@@ -278,15 +278,80 @@
 ATTEND_STEP = 256
 
 
-def fused(kernel, outs, operands, products, scalars=(), exps=0):
+class Loaded:
+    def __init__(self, source, buffer, semaphore):
+        self.buffer, self.copy, self.waiting = buffer, None, True
+        self.copy = pltpu.make_async_copy(source, buffer, semaphore)
+        self.copy.start()
+
+    def __getitem__(self, index):
+        if self.waiting:
+            self.copy.wait()
+            self.waiting = False
+        return self.buffer[index]
+
+
+class Kept:
+    def __init__(self, target, buffer, semaphore):
+        self.buffer, self.started = buffer, False
+        self.copy = pltpu.make_async_copy(buffer, target, semaphore)
+
+    def __getitem__(self, index):
+        return self.buffer[index]
+
+    def __setitem__(self, index, value):
+        self.buffer[index] = value
+        if index is Ellipsis:
+            self.start()
+
+    def start(self):
+        self.copy.start()
+        self.started = True
+
+    def finish(self):
+        if not self.started:
+            self.start()
+        self.copy.wait()
+
+
+def fused(kernel, outs, operands, products, scalars=(), exps=0, loaded=(), chosen=None, kept=()):
     in_vmem = pl.BlockSpec(memory_space=pltpu.VMEM)
+    in_hbm = pl.BlockSpec(memory_space=pltpu.HBM)
     in_smem = pl.BlockSpec(memory_space=pltpu.SMEM)
     scalars = [jnp.asarray(scalar, jnp.int32).reshape(1) for scalar in scalars]
+    loaded = list(loaded) + ([] if chosen is None else [chosen])
+    n_scalars, n_in, n_out = len(scalars), len(operands), len(outs)
+    scratch = []
+    for k in loaded:
+        shape = operands[k].shape
+        scratch.append(pltpu.VMEM(shape[1:] if k == chosen else shape, operands[k].dtype))
+    for k in kept:
+        scratch.append(pltpu.VMEM(*outs[k]))
+    moved = len(scratch)
+    if moved:
+        scratch.append(pltpu.SemaphoreType.DMA((moved,)))
+
+    def whole(*refs):
+        views = list(refs[: n_scalars + n_in + n_out])
+        buffers = refs[n_scalars + n_in + n_out :]
+        for spot, k in enumerate(loaded):
+            source = views[n_scalars + k]
+            if k == chosen:
+                source = source.at[views[0][0]]
+            views[n_scalars + k] = Loaded(source, buffers[spot], buffers[-1].at[spot])
+        for spot, k in enumerate(kept, len(loaded)):
+            at = n_scalars + n_in + k
+            views[at] = Kept(views[at], buffers[spot], buffers[-1].at[spot])
+        kernel(*views)
+        for k in kept:
+            views[n_scalars + n_in + k].finish()
+
     return pl.pallas_call(
-        kernel,
+        whole,
         out_shape=[jax.ShapeDtypeStruct(shape, kind) for shape, kind in outs],
-        in_specs=[in_smem] * len(scalars) + [in_vmem] * len(operands),
-        out_specs=[in_vmem] * len(outs),
+        in_specs=[in_smem] * n_scalars + [in_hbm if k in loaded else in_vmem for k in range(n_in)],
+        out_specs=[in_hbm if k in kept else in_vmem for k in range(n_out)],
+        scratch_shapes=scratch,
         compiler_params=pltpu.CompilerParams(vmem_limit_bytes=20 * 1024 * 1024),
         cost_estimate=pl.CostEstimate(
             flops=2 * products,
@@ -458,17 +523,21 @@
         pair_ref, own_ref, cross_ref, heads_ref, part_ref, low_ref = refs[n + 2 :]
         for k, ref in enumerate(pieces_refs):
             pair_ref[k * (keys // n) : (k + 1) * (keys // n), :] = ref[...]
-        token = stack_ref[index_ref[0]]
         for h in range(width // E):
             own = slice(h * E, (h + 1) * E)
             key_at, value_at = head_columns(h, width, 0), head_columns(h, width, 1)
             row = slice(h, h + 1)
-            heads_ref[:, width + h * E : width + (h + 1) * E], cross_ref[row, :] = head_attend(
-                query_ref[:, own], token[:, key_at], token[:, value_at]
-            )
             heads_ref[:, own], own_ref[row, :] = head_attend(
                 query_ref[:, own], pair_ref[:, key_at], pair_ref[:, value_at]
             )
+        for h in range(width // E):
+            own = slice(h * E, (h + 1) * E)
+            key_at, value_at = head_columns(h, width, 0), head_columns(h, width, 1)
+            row = slice(h, h + 1)
+            heads_ref[:, value_at], cross_ref[row, :] = head_attend(
+                query_ref[:, own], stack_ref[:, key_at], stack_ref[:, value_at]
+            )
+        heads_ref.start()
         part = plain_dot(heads_ref[...], out_ref[...])
         part_ref[...] = part
         low_ref[...] = part.astype(LOW)
@@ -479,7 +548,8 @@
     outs += [((count, depth), HIGH), ((count, depth), LOW)]
     products = count * width * (4 * keys + 2 * depth)
     operands = [queries, *pieces, stack, out_flat]
-    return fused(kernel, outs, operands, products, [index], 2 * count * keys)
+    exps = 2 * count * keys
+    return fused(kernel, outs, operands, products, [index], exps, chosen=n + 1, kept=(3,))
 
 
 def chain_mlp(parts, incoming, keeps, gain, up, down):
@@ -487,24 +557,26 @@
 
     def kernel(*refs):
         incoming_ref, keep_ref, gain_ref, up_ref, down_ref = refs[n : n + 5]
-        mid_ref, normed_ref, slope_ref, active_ref, part_ref, low_ref = refs[n + 5 :]
+        mid_ref, normed_ref, slope_ref, active_ref, incoming_out, part_ref, low_ref = refs[n + 5 :]
+        incoming_out[...] = incoming_ref[...]
         keep = keep_ref[0:1, :]
         mid = keep * incoming_ref[...].astype(HIGH) + (1.0 - keep) * added(refs[:n])
         normed = layer_norm(mid, gain_ref[...]).astype(LOW)
+        mid_ref[...], normed_ref[...] = mid, normed
         hidden = plain_dot(normed, up_ref[...])
         active = gelu_of(hidden).astype(LOW)
+        slope_ref[...], active_ref[...] = gelu_slope_of(hidden).astype(LOW), active
         part = plain_dot(active, down_ref[...])
-        mid_ref[...], normed_ref[...] = mid, normed
-        slope_ref[...], active_ref[...] = gelu_slope_of(hidden).astype(LOW), active
         part_ref[...], low_ref[...] = part, part.astype(LOW)
 
     count, depth = incoming.shape
     inner = up.shape[1]
     outs = [((count, depth), HIGH), ((count, depth), LOW)]
-    outs += [((count, inner), LOW), ((count, inner), LOW)]
+    outs += [((count, inner), LOW), ((count, inner), LOW), ((count, depth), LOW)]
     outs += [((count, depth), HIGH), ((count, depth), LOW)]
     operands = [*parts, incoming, keeps, gain, up, down]
-    return fused(kernel, outs, operands, 2 * count * depth * inner, (), count * inner)
+    products = 2 * count * depth * inner
+    return fused(kernel, outs, operands, products, (), count * inner, kept=(1, 2, 3, 4))
 
 
 def chain_start(parts, mid, keeps, init_slab, flag, gain, qkv_flat):
@@ -513,20 +585,23 @@
 
     def kernel(flag_ref, *refs):
         mid_ref, keep_ref, init_ref, gain_ref, qkv_ref = refs[n : n + 5]
-        mlp_ref, slab_ref, incoming_ref, normed_ref, query_ref, pair_ref = refs[n + 5 :]
+        mlp_ref, slab_ref, incoming_ref, normed_ref, query_ref, pair_ref, mid_out = refs[n + 5 :]
+        mid_out[...] = mid_ref[...]
         mlp = added(refs[:n])
         keep = keep_ref[1:2, :]
         slab = (keep * mid_ref[...] + (1.0 - keep) * mlp).astype(LOW)
         incoming = jnp.where(flag_ref[0] == 1, init_ref[...], slab)
+        mlp_ref[...], slab_ref[...], incoming_ref[...] = mlp.astype(LOW), slab, incoming
         normed = layer_norm(incoming.astype(HIGH), gain_ref[...]).astype(LOW)
+        normed_ref[...] = normed
         qkv = plain_dot(normed, qkv_ref[...]).astype(LOW)
-        mlp_ref[...], slab_ref[...], incoming_ref[...] = mlp.astype(LOW), slab, incoming
-        normed_ref[...], query_ref[...], pair_ref[...] = normed, qkv[:, :width], qkv[:, width:]
+        query_ref[...], pair_ref[...] = qkv[:, :width], qkv[:, width:]
 
     count, depth = mid.shape
     outs = [((count, depth), LOW)] * 4 + [((count, width), LOW), ((count, 2 * width), LOW)]
+    outs += [((count, depth), HIGH)]
     operands = [*parts, mid, keeps, init_slab, gain, qkv_flat]
-    return fused(kernel, outs, operands, 3 * count * depth * width, [flag])
+    return fused(kernel, outs, operands, 3 * count * depth * width, [flag], kept=(0, 1, 3, 6))
 
 
 def chain_back_mlp(parts, incoming, grad_mid, flag, keeps, gain, mid, mlp, slope, up, down):
@@ -544,11 +619,11 @@
             grad = keep_ref[0:1, :] * refs[n + 8][...] + grad
         state = jnp.where(flag_ref[0] == 1, 0.0, grad)
         low_mlp = ((1.0 - keep_ref[1:2, :]) * state).astype(LOW)
+        grad_ref[...], state_ref[...], low_mlp_ref[...] = grad, state, low_mlp
         grad_active = dot_second(low_mlp, down_ref[...])
         low_hidden = (slope_ref[...].astype(HIGH) * grad_active).astype(LOW)
+        low_hidden_ref[...] = low_hidden
         part = dot_second(low_hidden, up_ref[...])
-        grad_ref[...], state_ref[...] = grad, state
-        low_mlp_ref[...], low_hidden_ref[...] = low_mlp, low_hidden
         change = mid_ref[...] - mlp_ref[...].astype(HIGH)
         bias_ref[...] = jnp.sum(state * change, axis=0, keepdims=True)
         part_ref[...], low_ref[...] = part, part.astype(LOW)
@@ -558,7 +633,9 @@
     outs = [((count, depth), HIGH), ((count, depth), HIGH), ((count, depth), LOW)]
     outs += [((count, inner), LOW), ((1, depth), HIGH)]
     outs += [((count, depth), HIGH), ((count, depth), LOW)]
-    return fused(kernel, outs, operands, 2 * count * depth * inner, [flag], count * inner)
+    loaded = (n, n + 3, n + 4, n + 5)
+    products = 2 * count * depth * inner
+    return fused(kernel, outs, operands, products, [flag], loaded=loaded, kept=(2, 3))
 
 
 def chain_back_heads(
@@ -583,7 +660,6 @@
         change = incoming_ref[...].astype(HIGH) - mid_ref[...]
         bias_out[...] = jnp.sum(grad_mid * change, axis=0, keepdims=True)
         grad_heads = dot_second(low, out_ref[...]).astype(LOW)
-        token = stack_ref[index_ref[0]]
         for h in range(width // E):
             own = slice(h * E, (h + 1) * E)
             row = slice(h, h + 1)
@@ -596,8 +672,8 @@
             )
             cross_query, cross_terms = head_back(
                 query_ref[:, own],
-                token[:, head_columns(h, width, 0)],
-                token[:, head_columns(h, width, 1)],
+                stack_ref[:, head_columns(h, width, 0)],
+                stack_ref[:, head_columns(h, width, 1)],
                 cross_log_ref[row, :],
                 grad_heads[:, head_columns(h, width, 1)],
             )
@@ -617,7 +693,9 @@
     operands = [*parts, mid, gain, keeps, grad_state, incoming, out_flat]
     operands += [queries, pair, *logs, stack]
     products = count * width * (10 * keys + 2 * depth)
-    return fused(kernel, outs, operands, products, [index], 2 * count * keys)
+    loaded = (n, n + 4, n + 6, n + 7)
+    exps = 2 * count * keys
+    return fused(kernel, outs, operands, products, [index], exps, loaded, n + 10, (1, 7))
 
 
 def chain_back_inputs(query_grad, terms, stack, index, qkv_flat):
@@ -628,7 +706,7 @@
     def kernel(index_ref, *refs):
         stack_ref, qkv_ref = refs[len(first) + len(terms) : len(first) + len(terms) + 2]
         grad_ref, part_ref, low_ref = refs[-3:]
-        pair = stack_ref[index_ref[0]]
+        pair = stack_ref[...]
         for ref in refs[len(first) : len(first) + len(terms)]:
             pair = pair + ref[...].astype(HIGH)
         if first:
@@ -636,12 +714,15 @@
         else:
             grad_ref[:, :width] = jnp.zeros((rows, width), LOW)
         grad_ref[:, width:] = pair.astype(LOW)
+        grad_ref.start()
         part = dot_second(grad_ref[...], qkv_ref[...])
         part_ref[...], low_ref[...] = part, part.astype(LOW)
 
     outs = [((rows, 3 * width), LOW), ((rows, depth), HIGH), ((rows, depth), LOW)]
     operands = [*first, *terms, stack, qkv_flat]
-    return fused(kernel, outs, operands, 3 * rows * depth * width, [index])
+    chosen = len(first) + len(terms)
+    products = 3 * rows * depth * width
+    return fused(kernel, outs, operands, products, [index], chosen=chosen, kept=(0,))
 
 
 def body(
@@ -754,17 +835,17 @@
         if turn == 1:
             own_heads, own_token_logs = attend(tied(queries, part), pair, before)
             parts = tied(parts, own_heads)
-        mid_state, state_ffn_in, state_slope, state_active, part, low = chain_mlp(
+        mid_state, state_ffn_in, state_slope, state_active, kept_incoming, part, low = chain_mlp(
             parts, state_incoming, keeps, gain_sffn, up_state, down_state
         )
         parts = [part] + sent_around(low)
-        state_mlp, slab, incoming_next, normed_next, queries_next, pair_next = chain_start(
+        state_mlp, slab, incoming_next, normed_next, queries_next, pair_next, mid_state = chain_start(
             parts, mid_state, keeps, init_slab, flags[turn + 1], gain_state, qkv_state_flat
         )
         slabs_out.append(slab)
         turns.append(
             (
-                state_incoming,
+                kept_incoming,
                 state_normed,
                 state_queries,
                 state_pair,
@@ -832,7 +913,7 @@
     last_parts = [part] + sent_around(low)
 
     def last_state(after):
-        mid_state, _, _, _, part, _ = chain_mlp(
+        mid_state, _, _, _, _, part, _ = chain_mlp(
             tied(last_parts, after), last_incoming, keeps, gain_sffn, up_state, down_state
         )
         state_mlp = tp_total(part)
@@ -854,7 +935,17 @@
     )
     parts = [part] + sent_around(low)
     query_grad, pair_grad = own_back()
-    parts = tied(parts, query_grad)
+    token_grads = ScatterSum(
+        weight_grads(
+            [
+                (tied(tuple(ffn_in), query_grad), grad_hidden),
+                ([cotangent_rows], active),
+                (grad_proj_pieces, [token_heads]),
+            ],
+            False,
+        )
+    )
+    parts = tied(parts, token_grads.grads)
     kept_qkv, kept_rest = [(state_normed, grad_state_qkv)], []
     token_pair_grads = [None] * CHAIN
     init_grad = jnp.zeros((slab_rows, model_width), HIGH)
@@ -891,18 +982,6 @@
         init_grad = init_grad + jnp.where(flags[turn + 1], grad_next, 0.0)
         bias_two = bias_two + sums
         parts = [part] + sent_around(low)
-        if turn == CHAIN - 2:
-            token_grads = ScatterSum(
-                weight_grads(
-                    [
-                        (tied(tuple(ffn_in), part), grad_hidden),
-                        ([cotangent_rows], active),
-                        (grad_proj_pieces, [token_heads]),
-                    ],
-                    False,
-                )
-            )
-            parts = tied(parts, token_grads.grads)
         if turn == 0:
             parts = tied(parts, token_grads.total)
         grad_mid, grad_update, sums, query_total, here, across, sent, token_grad = chain_back_heads(
@@ -1024,24 +1103,23 @@
             ]
         )
     )
-    grad_win_normed = tp_scatter(
-        [dot_second(part, qkv_win_flat) for part in split_rows(grad_win_qkv, n_tp)]
-    )
     last_halves = last_grads.cores(last_grads.other)
     split_at = [half.shape[-1] for half in middle_halves]
-    one, two = last_grads.across(
-        *[jnp.concatenate(both, axis=-1) for both in zip(middle_halves, last_halves)]
+    halves = [jnp.concatenate(both, axis=-1) for both in zip(middle_halves, last_halves)]
+    one, two = last_grads.across(*halves)
+    grad_win_normed = tp_scatter(
+        [dot_second(part, qkv_win_flat) for part in split_rows(tied(grad_win_qkv, halves), n_tp)]
     )
     middle_halves = one[:, : split_at[0]], two[:, : split_at[1]]
     last_halves = one[:, split_at[0] :], two[:, split_at[1] :]
     back_input = norm_back(own_input, norm_win, grad_win_normed)
     grad_token_rows = natural(tp_gather((grad_win_mixed + back_input).astype(LOW)))
-    output_rows = natural(tp_gather(tied(layer_output.astype(LOW), win_returned)))
+    output_rows = natural(tp_gather(tied(layer_output.astype(LOW), halves)))
 
     own_columns = model_width // lax.axis_size("seq")
     inner_width = up_tok.shape[1]
     token_grads.total, state_grads.total = tied(
-        (token_grads.total, state_grads.total), last_grads.other
+        (token_grads.total, state_grads.total), halves
     )
     sum_qkv_win = columns_of(last_halves, 0, 3 * width)
     sum_qkv_tok = columns_of(middle_halves, 0, 3 * width)

time: 865 us -> 867 us (level)
    ppermute x66, waiting for transfers between devices: 151 us -> 179 us  [tp_to(): return lax.ppermute(array, 'tp', [(i, (i + k) % n) for i in range(n)])]
    ppermute x30, waiting for transfers between devices: 85.9 us -> 74.3 us  [tp_from(): return lax.ppermute(array, 'tp', [((i + k) % n, i) for i in range(n)])]
    unnamed x742 -> x676, local copies, waits for them, and re-layouts: 96.6 us -> 87.8 us
  transfers between devices with their start and end apart: 144 -> 144, of which waited for: 82 -> 79; matrix products, arithmetic and copies ran while one was open for 13% -> 12% of each run, Pallas kernels for 6% -> 5%
where the time goes in v9:
time: 867 us; the launch traced here: 856 us
  waiting for transfers between devices  316 us (36%)
  starting transfers between devices  193 us (22%)
  local copies, waits for them, and re-layouts  121 us (14%)
  Pallas kernels  90.4 us (10%)
  other arithmetic  58.6 us (7%)
  matrix products  54.5 us (6%)
  between operations  21.6 us (2%)
    ppermute x66, waiting for transfers between devices, tp_to(): return lax.ppermute(array, 'tp', [(i, (i + k) % n) for i in range(n)])  179 us
    ppermute x66, starting transfers between devices, tp_to(): return lax.ppermute(array, 'tp', [(i, (i + k) % n) for i in range(n)])  103 us
    unnamed x676, local copies, waits for them, and re-layouts  87.8 us
    ppermute x30, waiting for transfers between devices, tp_from(): return lax.ppermute(array, 'tp', [((i + k) % n, i) for i in range(n)])  74.3 us
    pallas_call x27, Pallas kernels, fused(): pl.pallas_call(whole, out_shape=[jax.ShapeDtypeStruct(shape, kind) for sh...  71.6 us
    ppermute x31, waiting for transfers between devices, swap(): return lax.ppermute(array, 'seq', [(s, s ^ k) for s in range(n)])  47.1 us
    ppermute x30, starting transfers between devices, tp_from(): return lax.ppermute(array, 'tp', [((i + k) % n, i) for i in range(n)])  34.9 us
    dot_general x27, matrix products, plain_dot(): return jnp.dot(former, latter, preferred_element_type=HIGH)  32.1 us
  transfers between devices with their start and end apart: 144, of which 79 were waited for; matrix products, arithmetic and copies ran while one was open for 12% of the time, Pallas kernels for 5%

profile of v9, /device:TPU:0, one launch (start us, length us, event | category | flops | bytes accessed | tf_op | source)
XLA Modules:
  0.0 856.2 jit_solution(7323061337271236698)
XLA Ops:
  33.9 6.3 collective-permute-done.2
  54.7 6.8 collective-permute-start.11
  108.3 11.1 %collective-permute-done.17 = bf16[512,512]{1,0:T(8,128)(2,1)S(1)} collective-permute-done((bf16[512,512]{1,0:T(8,128)(2,1)S(1)}, bf16[512,512]{1,0:T(8,128)(2,1)S(1)}, u32[]{:S(2)}, u32[]{:S(2)}) %collective-permute-start.17) | collective-permute-done | bytes 524320 | tf_op jit(solution)/shard_map/ppermute | solution.py:120
  133.7 5.5 collective-permute-done.19.refs_1_
  139.2 4.8 collective-permute-done.20.refs_2_
  200.4 4.8 collective-permute-done.29.refs_2_
  212.5 5.2 collective-permute-done.31.refs_2_
  249.0 5.8 collective-permute-done.37.refs_1_
  254.9 4.8 collective-permute-done.38.refs_2_
  268.7 5.1 collective-permute-done.40.refs_2_
  306.0 5.0 collective-permute-done.46
  311.0 5.1 collective-permute-done.47
  323.3 8.8 %collective-permute-done.51.refs_3_ = bf16[128,1024]{1,0:T(8,128)(2,1)S(1)} collective-permute-done((bf16[128,1024]{1,0:T(8,128)(2,1)S(1)}, bf16[128,1024]{1,0:T(8,128)(2,1)S(1)}, u32[]{:S(2)}, u32[]{:S(2)}) %collective-permute-start.51) | collective-permute-done | bytes 262176 | tf_op jit(solution)/shard_map/ppermute | solution.py:79
  347.3 4.8 collective-permute-done.53
  356.4 7.0 collective-permute-done.55.refs_14_
  402.5 7.2 collective-permute-done.61.refs_2_
  454.5 5.9 collective-permute-done.72
  460.4 5.1 collective-permute-done.73
  473.7 6.9 collective-permute-done.75.refs_2_
  536.3 6.6 collective-permute-done.86.refs_2_
  559.6 6.0 collective-permute-done.89.refs_2_
  583.6 6.2 collective-permute-done.100
  604.0 5.2 shard_map.425
  628.4 5.7 collective-permute-done.93
  645.3 5.1 collective-permute-done.103
  659.7 6.6 collective-permute-done.107.refs_15_
  676.6 6.0 shard_map.426
  689.1 8.7 %collective-permute-done.113 = bf16[128,1024]{1,0:T(8,128)(2,1)S(1)} collective-permute-done((bf16[128,1024]{1,0:T(8,128)(2,1)S(1)}, bf16[128,1024]{1,0:T(8,128)(2,1)S(1)}, u32[]{:S(2)}, u32[]{:S(2)}) %collective-permute-start.113) | collective-permute-done | bytes 262176 | tf_op jit(solution)/shard_map/ppermute | solution.py:79
  768.6 4.9 collective-permute-start.133
  790.0 6.3 collective-permute-done.125
  805.7 7.9 collective-permute-done.127
  815.5 7.5 collective-permute-done.128
  (1196 shorter events, 635.9 us)
Async XLA Ops:
  7.2 563.0 %reduce-scatter.3.cloned.1.call-start = ((), (), s32[]{:S(2)}) async-start(), calls=%async_computation.2 | async-start | bytes 5406720 | tf_op jit(solution)/shard_map/reduce_scatter | solution.py:212
  50.4 20.9 %collective-permute-start.8 = (bf16[128,1024]{1,0:T(8,128)(2,1)S(1)}, bf16[128,1024]{1,0:T(8,128)(2,1)S(1)}, u32[]{:S(2)}, u32[]{:S(2)}) collective-permute-start(bf16[128,1024]{1,0:T(8,128)(2,1)S(1)} %multiply_convert_fusion.11.refs_5_), channel_id=1, source_target_pairs={{3,0},{0,1},{1,2},{2,3},{7,4},{4,5},{5,6},{6,7},{11,8},{8,9},{9,10... | collective-permute-start | bytes 786440 | tf_op jit(solution)/shard_map/ppermute | solution.py:79
  54.7 24.0 %collective-permute-start.11 = (bf16[128,512]{1,0:T(8,128)(2,1)S(1)}, bf16[128,512]{1,0:T(8,128)(2,1)S(1)}, u32[]{:S(2)}, u32[]{:S(2)}) collective-permute-start(bf16[128,512]{1,0:T(8,128)(2,1)S(1)} %slice.335.refs_2_), channel_id=1, source_target_pairs={{0,8},{4,12},{8,0},{12,4},{16,24},{20,28},{24,16},{28,20},{32,40},... | collective-permute-start | bytes 393224 | tf_op jit(solution)/shard_map/ppermute | solution.py:120
  64.3 14.9 %collective-permute-start.5 = (bf16[128,1024]{1,0:T(8,128)(2,1)S(1)}, bf16[128,1024]{1,0:T(8,128)(2,1)S(1)}, u32[]{:S(2)}, u32[]{:S(2)}) collective-permute-start(bf16[128,1024]{1,0:T(8,128)(2,1)S(1)} %convolution_convert_fusion.24), channel_id=1, source_target_pairs={{0,2},{1,3},{2,0},{3,1},{4,6},{5,7},{6,4},{7,5},{8,10},{9,11},{10,... | collective-permute-start | bytes 786440 | tf_op jit(solution)/shard_map/ppermute | solution.py:84
  317.0 15.1 %collective-permute-start.51 = (bf16[128,1024]{1,0:T(8,128)(2,1)S(1)}, bf16[128,1024]{1,0:T(8,128)(2,1)S(1)}, u32[]{:S(2)}, u32[]{:S(2)}) collective-permute-start(bf16[128,1024]{1,0:T(8,128)(2,1)S(1)} %multiply_convert_fusion.5.refs_0_), channel_id=1, source_target_pairs={{3,0},{0,1},{1,2},{2,3},{7,4},{4,5},{5,6},{6,7},{11,8},{8,9},{9,10... | collective-permute-start | bytes 786440 | tf_op jit(solution)/shard_map/ppermute | solution.py:79
  317.2 17.7 %collective-permute-start.50 = (bf16[128,1024]{1,0:T(8,128)(2,1)S(1)}, bf16[128,1024]{1,0:T(8,128)(2,1)S(1)}, u32[]{:S(2)}, u32[]{:S(2)}) collective-permute-start(bf16[128,1024]{1,0:T(8,128)(2,1)S(1)} %multiply_convert_fusion.5.refs_0_), channel_id=1, source_target_pairs={{2,0},{3,1},{0,2},{1,3},{6,4},{7,5},{4,6},{5,7},{10,8},{11,9},{8,1... | collective-permute-start | bytes 786440 | tf_op jit(solution)/shard_map/ppermute | solution.py:79
  319.1 18.5 %collective-permute-start.49 = (bf16[128,1024]{1,0:T(8,128)(2,1)S(1)}, bf16[128,1024]{1,0:T(8,128)(2,1)S(1)}, u32[]{:S(2)}, u32[]{:S(2)}) collective-permute-start(bf16[128,1024]{1,0:T(8,128)(2,1)S(1)} %multiply_convert_fusion.5.refs_0_), channel_id=1, source_target_pairs={{1,0},{2,1},{3,2},{0,3},{5,4},{6,5},{7,6},{4,7},{9,8},{10,9},{11,1... | collective-permute-start | bytes 786440 | tf_op jit(solution)/shard_map/ppermute | solution.py:79
  394.5 317.7 %reduce-scatter.5.cloned.1.call-start = ((), (), s32[]{:S(2)}) async-start(), calls=%async_computation.3 | async-start | bytes 7028736 | tf_op jit(solution)/shard_map/reduce_scatter | solution.py:212
  420.9 15.8 %collective-permute-start.65 = (bf16[128,1024]{1,0:T(8,128)(2,1)S(1)}, bf16[128,1024]{1,0:T(8,128)(2,1)S(1)}, u32[]{:S(2)}, u32[]{:S(2)}) collective-permute-start(bf16[128,1024]{1,0:T(8,128)(2,1)S(1)} %get-tuple-element.273), channel_id=1, source_target_pairs={{0,1},{1,2},{2,3},{3,0},{4,5},{5,6},{6,7},{7,4},{8,9},{9,10},{10,1... | collective-permute-start | bytes 786440 | tf_op jit(solution)/shard_map/ppermute | solution.py:84
  430.1 16.5 %collective-permute-start.70 = (bf16[128,1024]{1,0:T(8,128)(2,1)S(1)}, bf16[128,1024]{1,0:T(8,128)(2,1)S(1)}, u32[]{:S(2)}, u32[]{:S(2)}) collective-permute-start(bf16[128,1024]{1,0:T(8,128)(2,1)S(1)} %get-tuple-element.285), channel_id=1, source_target_pairs={{0,1},{1,2},{2,3},{3,0},{4,5},{5,6},{6,7},{7,4},{8,9},{9,10},{10,1... | collective-permute-start | bytes 786440 | tf_op jit(solution)/shard_map/ppermute | solution.py:84
  431.1 15.5 %collective-permute-start.71 = (bf16[128,1024]{1,0:T(8,128)(2,1)S(1)}, bf16[128,1024]{1,0:T(8,128)(2,1)S(1)}, u32[]{:S(2)}, u32[]{:S(2)}) collective-permute-start(bf16[128,1024]{1,0:T(8,128)(2,1)S(1)} %get-tuple-element.285), channel_id=1, source_target_pairs={{0,3},{1,0},{2,1},{3,2},{4,7},{5,4},{6,5},{7,6},{8,11},{9,8},{10,9... | collective-permute-start | bytes 786440 | tf_op jit(solution)/shard_map/ppermute | solution.py:84
  450.5 14.9 %collective-permute-start.73 = (bf16[128,1024]{1,0:T(8,128)(2,1)S(1)}, bf16[128,1024]{1,0:T(8,128)(2,1)S(1)}, u32[]{:S(2)}, u32[]{:S(2)}) collective-permute-start(bf16[128,1024]{1,0:T(8,128)(2,1)S(1)} %convert_element_type.512), channel_id=1, source_target_pairs={{0,1},{1,2},{2,3},{3,0},{4,5},{5,6},{6,7},{7,4},{8,9},{9,10},{10,1... | collective-permute-start | bytes 786440 | tf_op jit(solution)/shard_map/ppermute | solution.py:84
  470.5 14.8 %collective-permute-start.76 = (bf16[128,1024]{1,0:T(8,128)(2,1)}, bf16[128,1024]{1,0:T(8,128)(2,1)}, u32[]{:S(2)}, u32[]{:S(2)}) collective-permute-start(bf16[128,1024]{1,0:T(8,128)(2,1)} %get-tuple-element.295), channel_id=1, source_target_pairs={{0,1},{1,2},{2,3},{3,0},{4,5},{5,6},{6,7},{7,4},{8,9},{9,10},{10,1... | collective-permute-start | bytes 786440 | tf_op jit(solution)/shard_map/ppermute | solution.py:84
  615.8 19.6 %collective-permute-start.95 = (bf16[512,512]{1,0:T(8,128)(2,1)S(1)}, bf16[512,512]{1,0:T(8,128)(2,1)S(1)}, u32[]{:S(2)}, u32[]{:S(2)}) collective-permute-start(bf16[512,512]{1,0:T(8,128)(2,1)S(1)} %copy-done.239), channel_id=1, source_target_pairs={{4,0},{8,4},{12,8},{20,16},{24,20},{28,24},{36,32},{40,36},{44,40}... | collective-permute-start | bytes 1572872 | tf_op jit(solution)/shard_map/ppermute | solution.py:902
  619.3 14.8 %collective-permute-start.93 = (bf16[128,1024]{1,0:T(8,128)(2,1)S(1)}, bf16[128,1024]{1,0:T(8,128)(2,1)S(1)}, u32[]{:S(2)}, u32[]{:S(2)}) collective-permute-start(bf16[128,1024]{1,0:T(8,128)(2,1)S(1)} %convolution_convert_fusion.14), channel_id=1, source_target_pairs={{0,1},{1,2},{2,3},{3,0},{4,5},{5,6},{6,7},{7,4},{8,9},{9,10},{10,1... | collective-permute-start | bytes 786440 | tf_op jit(solution)/shard_map/ppermute | solution.py:84
  657.8 14.9 %collective-permute-start.108 = (bf16[128,1024]{1,0:T(8,128)(2,1)S(1)}, bf16[128,1024]{1,0:T(8,128)(2,1)S(1)}, u32[]{:S(2)}, u32[]{:S(2)}) collective-permute-start(bf16[128,1024]{1,0:T(8,128)(2,1)S(1)} %get-tuple-element.471.refs_13_), channel_id=1, source_target_pairs={{3,0},{0,1},{1,2},{2,3},{7,4},{4,5},{5,6},{6,7},{11,8},{8,9},{9,10... | collective-permute-start | bytes 786440 | tf_op jit(solution)/shard_map/ppermute | solution.py:79
  688.9 42.4 %collective-permute-start.112 = (bf16[512,2816]{1,0:T(8,128)(2,1)}, bf16[512,2816]{1,0:T(8,128)(2,1)}, u32[]{:S(2)}, u32[]{:S(2)}) collective-permute-start(bf16[512,2816]{1,0:T(8,128)(2,1)} %get-tuple-element.375), channel_id=1, source_target_pairs={{0,4},{4,0},{8,12},{12,8},{16,20},{20,16},{24,28},{28,24},{32,36},... | collective-permute-start | bytes 8650760 | tf_op jit(solution)/shard_map/ppermute | solution.py:120
  747.5 34.3 %collective-permute-start.118 = (bf16[128,1024]{1,0:T(8,128)(2,1)S(1)}, bf16[128,1024]{1,0:T(8,128)(2,1)}, u32[]{:S(2)}, u32[]{:S(2)}) collective-permute-start(bf16[128,1024]{1,0:T(8,128)(2,1)S(1)} %copy-done.289), channel_id=1, source_target_pairs={{1,0},{2,1},{3,2},{0,3},{5,4},{6,5},{7,6},{4,7},{9,8},{10,9},{11,1... | collective-permute-start | bytes 786440 | tf_op jit(solution)/shard_map/ppermute | solution.py:79
  747.5 35.3 %collective-permute-start.119 = (bf16[128,1024]{1,0:T(8,128)(2,1)S(1)}, bf16[128,1024]{1,0:T(8,128)(2,1)}, u32[]{:S(2)}, u32[]{:S(2)}) collective-permute-start(bf16[128,1024]{1,0:T(8,128)(2,1)S(1)} %copy-done.289), channel_id=1, source_target_pairs={{2,0},{3,1},{0,2},{1,3},{6,4},{7,5},{4,6},{5,7},{10,8},{11,9},{8,1... | collective-permute-start | bytes 786440 | tf_op jit(solution)/shard_map/ppermute | solution.py:79
  748.3 15.6 %collective-permute-start.121 = (bf16[128,1024]{1,0:T(8,128)(2,1)}, bf16[128,1024]{1,0:T(8,128)(2,1)}, u32[]{:S(2)}, u32[]{:S(2)}) collective-permute-start(bf16[128,1024]{1,0:T(8,128)(2,1)} %convolution_convert_fusion.5), channel_id=1, source_target_pairs={{0,2},{1,3},{2,0},{3,1},{4,6},{5,7},{6,4},{7,5},{8,10},{9,11},{10,... | collective-permute-start | bytes 786440 | tf_op jit(solution)/shard_map/ppermute | solution.py:84
  751.2 17.4 %collective-permute-start.122 = (bf16[128,1024]{1,0:T(8,128)(2,1)}, bf16[128,1024]{1,0:T(8,128)(2,1)}, u32[]{:S(2)}, u32[]{:S(2)}) collective-permute-start(bf16[128,1024]{1,0:T(8,128)(2,1)} %convolution_convert_fusion.4), channel_id=1, source_target_pairs={{0,1},{1,2},{2,3},{3,0},{4,5},{5,6},{6,7},{7,4},{8,9},{9,10},{10,1... | collective-permute-start | bytes 786440 | tf_op jit(solution)/shard_map/ppermute | solution.py:84
  753.2 20.2 %collective-permute-start.123 = (bf16[128,1024]{1,0:T(8,128)(2,1)}, bf16[128,1024]{1,0:T(8,128)(2,1)}, u32[]{:S(2)}, u32[]{:S(2)}) collective-permute-start(bf16[128,1024]{1,0:T(8,128)(2,1)} %convolution_convert_fusion.3), channel_id=1, source_target_pairs={{0,3},{1,0},{2,1},{3,2},{4,7},{5,4},{6,5},{7,6},{8,11},{9,8},{10,9... | collective-permute-start | bytes 786440 | tf_op jit(solution)/shard_map/ppermute | solution.py:84
  763.9 22.1 %collective-permute-start.120 = (bf16[128,1024]{1,0:T(8,128)(2,1)S(1)}, bf16[128,1024]{1,0:T(8,128)(2,1)S(1)}, u32[]{:S(2)}, u32[]{:S(2)}) collective-permute-start(bf16[128,1024]{1,0:T(8,128)(2,1)S(1)} %copy-done.289), channel_id=1, source_target_pairs={{3,0},{0,1},{1,2},{2,3},{7,4},{4,5},{5,6},{6,7},{11,8},{8,9},{9,10... | collective-permute-start | bytes 786440 | tf_op jit(solution)/shard_map/ppermute | solution.py:79
  768.6 31.7 %collective-permute-start.133 = (bf16[4,32,2176]{2,1,0:T(8,128)(2,1)}, bf16[4,32,2176]{2,1,0:T(8,128)(2,1)S(1)}, u32[]{:S(2)}, u32[]{:S(2)}) collective-permute-start(bf16[4,32,2176]{2,1,0:T(8,128)(2,1)} %get-tuple-element.503), channel_id=1, source_target_pairs={{0,16},{4,20},{8,24},{12,28},{16,0},{20,4},{24,8},{28,12},{32,48},... | collective-permute-start | bytes 1671176 | tf_op jit(solution)/shard_map/ppermute | solution.py:249
  781.8 21.6 %collective-permute-start.134 = (bf16[4,32,2176]{2,1,0:T(8,128)(2,1)S(1)}, bf16[4,32,2176]{2,1,0:T(8,128)(2,1)S(1)}, u32[]{:S(2)}, u32[]{:S(2)}) collective-permute-start(bf16[4,32,2176]{2,1,0:T(8,128)(2,1)S(1)} %copy-done.297), channel_id=1, source_target_pairs={{0,8},{4,12},{8,16},{12,20},{16,24},{20,28},{24,0},{28,4},{32,40},... | collective-permute-start | bytes 1671176 | tf_op jit(solution)/shard_map/ppermute | solution.py:249
  782.8 20.6 %collective-permute-start.135 = (bf16[4,32,2176]{2,1,0:T(8,128)(2,1)S(1)}, bf16[4,32,2176]{2,1,0:T(8,128)(2,1)S(1)}, u32[]{:S(2)}, u32[]{:S(2)}) collective-permute-start(bf16[4,32,2176]{2,1,0:T(8,128)(2,1)S(1)} %copy-done.296), channel_id=1, source_target_pairs={{0,24},{4,28},{8,0},{12,4},{16,8},{20,12},{24,16},{28,20},{32,56},... | collective-permute-start | bytes 1671176 | tf_op jit(solution)/shard_map/ppermute | solution.py:249
  796.3 17.4 %collective-permute-start.127 = (bf16[4,32,2304]{2,1,0:T(8,128)(2,1)S(1)}, bf16[4,32,2304]{2,1,0:T(8,128)(2,1)S(1)}, u32[]{:S(2)}, u32[]{:S(2)}) collective-permute-start(bf16[4,32,2304]{2,1,0:T(8,128)(2,1)S(1)} %copy-done.295), channel_id=1, source_target_pairs={{0,64},{4,68},{8,72},{12,76},{16,80},{20,84},{24,88},{28,92},{32,9... | collective-permute-start | bytes 1769480 | tf_op jit(solution)/shard_map/ppermute | solution.py:249
  799.1 23.9 %collective-permute-start.128 = (bf16[4,32,2304]{2,1,0:T(8,128)(2,1)S(1)}, bf16[4,32,2304]{2,1,0:T(8,128)(2,1)S(1)}, u32[]{:S(2)}, u32[]{:S(2)}) collective-permute-start(bf16[4,32,2304]{2,1,0:T(8,128)(2,1)S(1)} %copy-done.294), channel_id=1, source_target_pairs={{0,32},{4,36},{8,40},{12,44},{16,48},{20,52},{24,56},{28,60},{32,6... | collective-permute-start | bytes 1769480 | tf_op jit(solution)/shard_map/ppermute | solution.py:249
  801.2 21.8 %collective-permute-start.129 = (bf16[4,32,2304]{2,1,0:T(8,128)(2,1)S(1)}, bf16[4,32,2304]{2,1,0:T(8,128)(2,1)S(1)}, u32[]{:S(2)}, u32[]{:S(2)}) collective-permute-start(bf16[4,32,2304]{2,1,0:T(8,128)(2,1)S(1)} %copy-done.293), channel_id=1, source_target_pairs={{0,96},{4,100},{8,104},{12,108},{16,112},{20,116},{24,120},{28,124... | collective-permute-start | bytes 1769480 | tf_op jit(solution)/shard_map/ppermute | solution.py:249
  803.8 23.9 %collective-permute-start.136 = (bf16[32,2176]{1,0:T(8,128)(2,1)S(1)}, bf16[32,2176]{1,0:T(8,128)(2,1)S(1)}, u32[]{:S(2)}, u32[]{:S(2)}) collective-permute-start(bf16[32,2176]{1,0:T(8,128)(2,1)S(1)} %get-tuple-element.511), channel_id=1, source_target_pairs={{0,64},{4,68},{8,72},{12,76},{16,80},{20,84},{24,88},{28,92},{32,9... | collective-permute-start | bytes 417800 | tf_op jit(solution)/shard_map/ppermute | solution.py:249
  805.3 25.6 %collective-permute-start.137 = (bf16[32,2176]{1,0:T(8,128)(2,1)S(1)}, bf16[32,2176]{1,0:T(8,128)(2,1)S(1)}, u32[]{:S(2)}, u32[]{:S(2)}) collective-permute-start(bf16[32,2176]{1,0:T(8,128)(2,1)S(1)} %get-tuple-element.513), channel_id=1, source_target_pairs={{0,32},{4,36},{8,40},{12,44},{16,48},{20,52},{24,56},{28,60},{32,6... | collective-permute-start | bytes 417800 | tf_op jit(solution)/shard_map/ppermute | solution.py:249
  813.6 17.3 %collective-permute-start.138 = (bf16[32,2176]{1,0:T(8,128)(2,1)S(1)}, bf16[32,2176]{1,0:T(8,128)(2,1)S(1)}, u32[]{:S(2)}, u32[]{:S(2)}) collective-permute-start(bf16[32,2176]{1,0:T(8,128)(2,1)S(1)} %get-tuple-element.512), channel_id=1, source_target_pairs={{0,96},{4,100},{8,104},{12,108},{16,112},{20,116},{24,120},{28,124... | collective-permute-start | bytes 417800 | tf_op jit(solution)/shard_map/ppermute | solution.py:249
  (444 other events, 4390.4 us)
Sparse Core Ops, SparseCore 0:
  394.6 85.2 reduce-scatter.2
  612.2 87.7 reduce-scatter.4

commit v10 on v9

--- a/solution.py
+++ b/solution.py
@@ -261,7 +261,9 @@
         return total(slice(0, half)), total(slice(half, width))
 
     def across(self, one, two):
-        one, two = self.over_z(one, 1).astype(LOW), self.over_x(two, 0).astype(LOW)
+        return self.over_z(one, 1).astype(LOW), self.over_x(two, 0).astype(LOW)
+
+    def last(self, one, two):
         return self.over_x(one, 0), self.over_z(two, 0)
 
 
@@ -508,7 +510,7 @@
 
 
 def added(refs):
-    total = refs[0][...]
+    total = refs[0][...].astype(HIGH)
     for ref in refs[1:]:
         total = total + ref[...].astype(HIGH)
     return total
@@ -520,7 +522,7 @@
 
     def kernel(index_ref, query_ref, *refs):
         pieces_refs, (stack_ref, out_ref) = refs[:n], refs[n : n + 2]
-        pair_ref, own_ref, cross_ref, heads_ref, part_ref, low_ref = refs[n + 2 :]
+        pair_ref, own_ref, cross_ref, heads_ref, low_ref = refs[n + 2 :]
         for k, ref in enumerate(pieces_refs):
             pair_ref[k * (keys // n) : (k + 1) * (keys // n), :] = ref[...]
         for h in range(width // E):
@@ -538,14 +540,12 @@
                 query_ref[:, own], stack_ref[:, key_at], stack_ref[:, value_at]
             )
         heads_ref.start()
-        part = plain_dot(heads_ref[...], out_ref[...])
-        part_ref[...] = part
-        low_ref[...] = part.astype(LOW)
+        low_ref[...] = plain_dot(heads_ref[...], out_ref[...]).astype(LOW)
 
     depth = out_flat.shape[1]
     logs = ((width // E, count), HIGH)
     outs = [((keys, 2 * width), LOW), logs, logs, ((count, 2 * width), LOW)]
-    outs += [((count, depth), HIGH), ((count, depth), LOW)]
+    outs += [((count, depth), LOW)]
     products = count * width * (4 * keys + 2 * depth)
     operands = [queries, *pieces, stack, out_flat]
     exps = 2 * count * keys
@@ -557,8 +557,7 @@
 
     def kernel(*refs):
         incoming_ref, keep_ref, gain_ref, up_ref, down_ref = refs[n : n + 5]
-        mid_ref, normed_ref, slope_ref, active_ref, incoming_out, part_ref, low_ref = refs[n + 5 :]
-        incoming_out[...] = incoming_ref[...]
+        mid_ref, normed_ref, slope_ref, active_ref, low_ref = refs[n + 5 :]
         keep = keep_ref[0:1, :]
         mid = keep * incoming_ref[...].astype(HIGH) + (1.0 - keep) * added(refs[:n])
         normed = layer_norm(mid, gain_ref[...]).astype(LOW)
@@ -566,17 +565,16 @@
         hidden = plain_dot(normed, up_ref[...])
         active = gelu_of(hidden).astype(LOW)
         slope_ref[...], active_ref[...] = gelu_slope_of(hidden).astype(LOW), active
-        part = plain_dot(active, down_ref[...])
-        part_ref[...], low_ref[...] = part, part.astype(LOW)
+        low_ref[...] = plain_dot(active, down_ref[...]).astype(LOW)
 
     count, depth = incoming.shape
     inner = up.shape[1]
     outs = [((count, depth), HIGH), ((count, depth), LOW)]
     outs += [((count, inner), LOW), ((count, inner), LOW), ((count, depth), LOW)]
-    outs += [((count, depth), HIGH), ((count, depth), LOW)]
     operands = [*parts, incoming, keeps, gain, up, down]
     products = 2 * count * depth * inner
-    return fused(kernel, outs, operands, products, (), count * inner, kept=(1, 2, 3, 4))
+    exps = count * inner
+    return fused(kernel, outs, operands, products, (), exps, (n,), kept=(0, 1, 2, 3))
 
 
 def chain_start(parts, mid, keeps, init_slab, flag, gain, qkv_flat):
@@ -585,8 +583,7 @@
 
     def kernel(flag_ref, *refs):
         mid_ref, keep_ref, init_ref, gain_ref, qkv_ref = refs[n : n + 5]
-        mlp_ref, slab_ref, incoming_ref, normed_ref, query_ref, pair_ref, mid_out = refs[n + 5 :]
-        mid_out[...] = mid_ref[...]
+        mlp_ref, slab_ref, incoming_ref, normed_ref, query_ref, pair_ref = refs[n + 5 :]
         mlp = added(refs[:n])
         keep = keep_ref[1:2, :]
         slab = (keep * mid_ref[...] + (1.0 - keep) * mlp).astype(LOW)
@@ -599,21 +596,22 @@
 
     count, depth = mid.shape
     outs = [((count, depth), LOW)] * 4 + [((count, width), LOW), ((count, 2 * width), LOW)]
-    outs += [((count, depth), HIGH)]
     operands = [*parts, mid, keeps, init_slab, gain, qkv_flat]
-    return fused(kernel, outs, operands, 3 * count * depth * width, [flag], kept=(0, 1, 3, 6))
+    products = 3 * count * depth * width
+    return fused(kernel, outs, operands, products, [flag], 0, (n,), kept=(0, 1, 2, 3))
 
 
 def chain_back_mlp(parts, incoming, grad_mid, flag, keeps, gain, mid, mlp, slope, up, down):
     n = len(parts)
     operands = [*parts, incoming, keeps, gain, mid, mlp, slope, up, down]
     operands += [] if grad_mid is None else [grad_mid]
+    n_ins = len(operands)
 
     def kernel(flag_ref, *refs):
         incoming_ref, keep_ref, gain_ref, mid_ref, mlp_ref, slope_ref, up_ref, down_ref = refs[
             n : n + 8
         ]
-        grad_ref, state_ref, low_mlp_ref, low_hidden_ref, bias_ref, part_ref, low_ref = refs[-7:]
+        grad_ref, state_ref, low_mlp_ref, low_hidden_ref, bias_ref, low_ref = refs[n_ins:]
         grad = norm_back(incoming_ref[...].astype(HIGH), gain_ref[...], added(refs[:n]))
         if grad_mid is not None:
             grad = keep_ref[0:1, :] * refs[n + 8][...] + grad
@@ -623,19 +621,17 @@
         grad_active = dot_second(low_mlp, down_ref[...])
         low_hidden = (slope_ref[...].astype(HIGH) * grad_active).astype(LOW)
         low_hidden_ref[...] = low_hidden
-        part = dot_second(low_hidden, up_ref[...])
+        low_ref[...] = dot_second(low_hidden, up_ref[...]).astype(LOW)
         change = mid_ref[...] - mlp_ref[...].astype(HIGH)
         bias_ref[...] = jnp.sum(state * change, axis=0, keepdims=True)
-        part_ref[...], low_ref[...] = part, part.astype(LOW)
 
     count, depth = mid.shape
     inner = up.shape[1]
     outs = [((count, depth), HIGH), ((count, depth), HIGH), ((count, depth), LOW)]
-    outs += [((count, inner), LOW), ((1, depth), HIGH)]
-    outs += [((count, depth), HIGH), ((count, depth), LOW)]
-    loaded = (n, n + 3, n + 4, n + 5)
+    outs += [((count, inner), LOW), ((1, depth), HIGH), ((count, depth), LOW)]
+    loaded = (n, n + 3, n + 4, n + 5) + (() if grad_mid is None else (n + 8,))
     products = 2 * count * depth * inner
-    return fused(kernel, outs, operands, products, [flag], loaded=loaded, kept=(2, 3))
+    return fused(kernel, outs, operands, products, [flag], loaded=loaded, kept=(0, 1, 2, 3))
 
 
 def chain_back_heads(
@@ -693,9 +689,9 @@
     operands = [*parts, mid, gain, keeps, grad_state, incoming, out_flat]
     operands += [queries, pair, *logs, stack]
     products = count * width * (10 * keys + 2 * depth)
-    loaded = (n, n + 4, n + 6, n + 7)
+    loaded = (n, n + 3, n + 4, n + 6, n + 7)
     exps = 2 * count * keys
-    return fused(kernel, outs, operands, products, [index], exps, loaded, n + 10, (1, 7))
+    return fused(kernel, outs, operands, products, [index], exps, loaded, n + 10, (0, 1, 7))
 
 
 def chain_back_inputs(query_grad, terms, stack, index, qkv_flat):
@@ -705,7 +701,7 @@
 
     def kernel(index_ref, *refs):
         stack_ref, qkv_ref = refs[len(first) + len(terms) : len(first) + len(terms) + 2]
-        grad_ref, part_ref, low_ref = refs[-3:]
+        grad_ref, low_ref = refs[-2:]
         pair = stack_ref[...]
         for ref in refs[len(first) : len(first) + len(terms)]:
             pair = pair + ref[...].astype(HIGH)
@@ -715,10 +711,9 @@
             grad_ref[:, :width] = jnp.zeros((rows, width), LOW)
         grad_ref[:, width:] = pair.astype(LOW)
         grad_ref.start()
-        part = dot_second(grad_ref[...], qkv_ref[...])
-        part_ref[...], low_ref[...] = part, part.astype(LOW)
-
-    outs = [((rows, 3 * width), LOW), ((rows, depth), HIGH), ((rows, depth), LOW)]
+        low_ref[...] = dot_second(grad_ref[...], qkv_ref[...]).astype(LOW)
+
+    outs = [((rows, 3 * width), LOW), ((rows, depth), LOW)]
     operands = [*first, *terms, stack, qkv_flat]
     chosen = len(first) + len(terms)
     products = 3 * rows * depth * width
@@ -828,24 +823,24 @@
     turns = []
     slabs_out = []
     for turn in range(CHAIN - 1):
-        state_pair, own_logs, cross_logs, state_heads, part, low = chain_attend(
+        state_pair, own_logs, cross_logs, state_heads, low = chain_attend(
             state_queries, state_pieces, pairs_stack, position ^ turn, out_state_flat
         )
-        parts = [part] + sent_around(low)
+        parts = [low] + sent_around(low)
         if turn == 1:
-            own_heads, own_token_logs = attend(tied(queries, part), pair, before)
+            own_heads, own_token_logs = attend(tied(queries, low), pair, before)
             parts = tied(parts, own_heads)
-        mid_state, state_ffn_in, state_slope, state_active, kept_incoming, part, low = chain_mlp(
+        mid_state, state_ffn_in, state_slope, state_active, low = chain_mlp(
             parts, state_incoming, keeps, gain_sffn, up_state, down_state
         )
-        parts = [part] + sent_around(low)
-        state_mlp, slab, incoming_next, normed_next, queries_next, pair_next, mid_state = chain_start(
+        parts = [low] + sent_around(low)
+        state_mlp, slab, incoming_next, normed_next, queries_next, pair_next = chain_start(
             parts, mid_state, keeps, init_slab, flags[turn + 1], gain_state, qkv_state_flat
         )
         slabs_out.append(slab)
         turns.append(
             (
-                kept_incoming,
+                state_incoming,
                 state_normed,
                 state_queries,
                 state_pair,
@@ -903,20 +898,22 @@
         return query_grad + cross_query_grad, pair_grad + returned.astype(HIGH)
 
     last_incoming = state_incoming
-    _, _, _, _, part, low = chain_attend(
+    _, _, _, _, low = chain_attend(
         tied(state_queries, grad_heads),
         state_pieces,
         pairs_stack,
         position ^ (CHAIN - 1),
         out_state_flat,
     )
-    last_parts = [part] + sent_around(low)
+    last_parts = [low] + sent_around(low)
 
     def last_state(after):
-        mid_state, _, _, _, _, part, _ = chain_mlp(
+        mid_state, _, _, _, low = chain_mlp(
             tied(last_parts, after), last_incoming, keeps, gain_sffn, up_state, down_state
         )
-        state_mlp = tp_total(part)
+        state_mlp = low.astype(HIGH)
+        for received in sent_around(low):
+            state_mlp = state_mlp + received.astype(HIGH)
         return (keep_two * mid_state + (1.0 - keep_two) * state_mlp).astype(LOW)
 
     def states_between(state_slab):
@@ -930,10 +927,10 @@
         by_tp = turned(jnp.stack(tp_gather(slabs)), (n_tp - tp_index) % n_tp)
         return jnp.transpose(by_tp, (1, 0, 2, 3)).reshape(state_rows, model_width)
 
-    grad_state_qkv, part, low = chain_back_inputs(
+    grad_state_qkv, low = chain_back_inputs(
         None, [], cross_pieces, position ^ (CHAIN - 1), qkv_state_flat
     )
-    parts = [part] + sent_around(low)
+    parts = [low] + sent_around(low)
     query_grad, pair_grad = own_back()
     token_grads = ScatterSum(
         weight_grads(
@@ -966,7 +963,7 @@
             state_active,
             state_mlp,
         ) = turns[turn]
-        grad_next, grad_state, grad_mlp, grad_state_hidden, sums, part, low = chain_back_mlp(
+        grad_next, grad_state, grad_mlp, grad_state_hidden, sums, low = chain_back_mlp(
             parts,
             next_incoming,
             grad_mid,
@@ -981,7 +978,7 @@
         )
         init_grad = init_grad + jnp.where(flags[turn + 1], grad_next, 0.0)
         bias_two = bias_two + sums
-        parts = [part] + sent_around(low)
+        parts = [low] + sent_around(low)
         if turn == 0:
             parts = tied(parts, token_grads.total)
         grad_mid, grad_update, sums, query_total, here, across, sent, token_grad = chain_back_heads(
@@ -1014,15 +1011,15 @@
         if turn == CHAIN - 4:
             state_rows_out = states_whole(tied(slabs, grad_mid))
             across = tied(across, state_rows_out)
-        grad_state_qkv, part, low = chain_back_inputs(
+        grad_state_qkv, low = chain_back_inputs(
             query_total, [here, beside, across], cross_pieces, position ^ turn, qkv_state_flat
         )
         kept_qkv.append((state_normed, grad_state_qkv))
         if turn:
-            parts = [part] + sent_around(low)
+            parts = [low] + sent_around(low)
 
     init_grad = init_grad + jnp.where(flags[0], keep_one * grad_mid, 0.0)
-    first_part = norm_back(turns[0][0].astype(HIGH), norm_state, part)
+    first_part = norm_back(turns[0][0].astype(HIGH), norm_state, low.astype(HIGH))
     init_grad = init_grad / n_tp + jnp.where(flags[0], first_part, 0.0)
     bias_one = bias_one[0] * keep_one / n_tp
     bias_two = bias_two[0] * keep_two * (1.0 - keep_two) / n_tp
@@ -1106,20 +1103,20 @@
     last_halves = last_grads.cores(last_grads.other)
     split_at = [half.shape[-1] for half in middle_halves]
     halves = [jnp.concatenate(both, axis=-1) for both in zip(middle_halves, last_halves)]
-    one, two = last_grads.across(*halves)
-    grad_win_normed = tp_scatter(
-        [dot_second(part, qkv_win_flat) for part in split_rows(tied(grad_win_qkv, halves), n_tp)]
-    )
+    parts = [dot_second(part, qkv_win_flat) for part in split_rows(grad_win_qkv, n_tp)]
+    grad_win_normed = tp_scatter(parts)
+    firsts = last_grads.across(*tied(halves, parts))
+    one, two = last_grads.last(*firsts)
     middle_halves = one[:, : split_at[0]], two[:, : split_at[1]]
     last_halves = one[:, split_at[0] :], two[:, split_at[1] :]
-    back_input = norm_back(own_input, norm_win, grad_win_normed)
+    back_input = norm_back(own_input, norm_win, tied(grad_win_normed, firsts))
     grad_token_rows = natural(tp_gather((grad_win_mixed + back_input).astype(LOW)))
-    output_rows = natural(tp_gather(tied(layer_output.astype(LOW), halves)))
+    output_rows = natural(tp_gather(tied(layer_output.astype(LOW), grad_win_heads)))
 
     own_columns = model_width // lax.axis_size("seq")
     inner_width = up_tok.shape[1]
     token_grads.total, state_grads.total = tied(
-        (token_grads.total, state_grads.total), halves
+        (token_grads.total, state_grads.total), firsts
     )
     sum_qkv_win = columns_of(last_halves, 0, 3 * width)
     sum_qkv_tok = columns_of(middle_halves, 0, 3 * width)

time: 867 us -> 837 us (0.965)
  waiting for transfers between devices: 316 us -> 297 us
    ppermute x66, waiting for transfers between devices: 179 us -> 168 us  [tp_to(): return lax.ppermute(array, 'tp', [(i, (i + k) % n) for i in range(n)])]
    ppermute x30, waiting for transfers between devices: 74.3 us -> 64.3 us  [tp_from(): return lax.ppermute(array, 'tp', [((i + k) % n, i) for i in range(n)])]
    unnamed x676 -> x638, local copies, waits for them, and re-layouts: 87.8 us -> 80.6 us
  transfers between devices with their start and end apart: 144 -> 144, of which waited for: 79 -> 77; matrix products, arithmetic and copies ran while one was open for 12% -> 15% of each run, Pallas kernels for 5% -> 6%
where the time goes in v10:
time: 837 us; the launch traced here: 827 us
  waiting for transfers between devices  297 us (35%)
  starting transfers between devices  192 us (23%)
  local copies, waits for them, and re-layouts  118 us (14%)
  Pallas kernels  90.1 us (11%)
  other arithmetic  55.3 us (7%)
  matrix products  53.2 us (6%)
  between operations  21.5 us (3%)
    ppermute x66, waiting for transfers between devices, tp_to(): return lax.ppermute(array, 'tp', [(i, (i + k) % n) for i in range(n)])  168 us
    ppermute x66, starting transfers between devices, tp_to(): return lax.ppermute(array, 'tp', [(i, (i + k) % n) for i in range(n)])  103 us
    unnamed x638, local copies, waits for them, and re-layouts  80.6 us
    pallas_call x27, Pallas kernels, fused(): pl.pallas_call(whole, out_shape=[jax.ShapeDtypeStruct(shape, kind) for sh...  72.2 us
    ppermute x30, waiting for transfers between devices, tp_from(): return lax.ppermute(array, 'tp', [((i + k) % n, i) for i in range(n)])  64.3 us
    ppermute x31, waiting for transfers between devices, swap(): return lax.ppermute(array, 'seq', [(s, s ^ k) for s in range(n)])  47.5 us
    ppermute x30, starting transfers between devices, tp_from(): return lax.ppermute(array, 'tp', [((i + k) % n, i) for i in range(n)])  34.1 us
    dot_general x27, matrix products, plain_dot(): return jnp.dot(former, latter, preferred_element_type=HIGH)  31.2 us
  transfers between devices with their start and end apart: 144, of which 77 were waited for; matrix products, arithmetic and copies ran while one was open for 15% of the time, Pallas kernels for 6%

profile of v10, /device:TPU:0, one launch (start us, length us, event | category | flops | bytes accessed | tf_op | source)
XLA Modules:
  0.0 827.3 jit_solution(13139652794353862663)
XLA Ops:
  33.9 6.3 collective-permute-done.2
  54.4 7.2 collective-permute-start.11
  104.9 11.1 %collective-permute-done.17 = bf16[512,512]{1,0:T(8,128)(2,1)S(1)} collective-permute-done((bf16[512,512]{1,0:T(8,128)(2,1)S(1)}, bf16[512,512]{1,0:T(8,128)(2,1)S(1)}, u32[]{:S(2)}, u32[]{:S(2)}) %collective-permute-start.17) | collective-permute-done | bytes 524320 | tf_op jit(solution)/shard_map/ppermute | solution.py:120
  130.2 6.0 collective-permute-done.19.refs_1_
  136.2 4.8 collective-permute-done.20.refs_2_
  196.1 4.8 collective-permute-done.29.refs_2_
  208.0 5.4 collective-permute-done.31.refs_2_
  213.4 4.6 collective-permute-done.32.refs_3_
  243.4 6.0 collective-permute-done.37.refs_1_
  249.4 4.8 collective-permute-done.38.refs_2_
  263.0 5.2 collective-permute-done.40.refs_2_
  300.4 5.1 collective-permute-done.46
  305.6 5.2 collective-permute-done.47
  317.8 9.0 %collective-permute-done.51.refs_3_ = bf16[128,1024]{1,0:T(8,128)(2,1)S(1)} collective-permute-done((bf16[128,1024]{1,0:T(8,128)(2,1)S(1)}, bf16[128,1024]{1,0:T(8,128)(2,1)S(1)}, u32[]{:S(2)}, u32[]{:S(2)}) %collective-permute-start.51) | collective-permute-done | bytes 262176 | tf_op jit(solution)/shard_map/ppermute | solution.py:79
  342.0 4.8 collective-permute-done.53
  351.1 7.0 collective-permute-done.55.refs_14_
  397.2 7.2 collective-permute-done.61.refs_2_
  456.1 5.2 collective-permute-done.73
  470.0 5.7 collective-permute-done.75.refs_2_
  475.7 4.6 collective-permute-done.76.refs_3_
  504.2 4.6 collective-permute-done.79.refs_3_
  532.6 6.6 collective-permute-done.86.refs_2_
  554.7 6.0 collective-permute-done.89.refs_2_
  560.7 4.6 collective-permute-done.90.refs_3_
  570.0 4.8 shard_map.423
  599.2 5.2 shard_map.425
  621.2 5.7 collective-permute-done.93
  656.1 5.8 collective-permute-done.106.refs_15_
  672.9 6.0 shard_map.426
  689.7 6.8 collective-permute-done.112
  745.7 7.2 collective-permute-done.124
  755.5 7.4 collective-permute-done.125
  (1158 shorter events, 614.9 us)
Async XLA Ops:
  7.2 558.1 %reduce-scatter.3.cloned.1.call-start = ((), (), s32[]{:S(2)}) async-start(), calls=%async_computation.2 | async-start | bytes 5406720 | tf_op jit(solution)/shard_map/reduce_scatter | solution.py:212
  50.1 21.4 %collective-permute-start.8 = (bf16[128,1024]{1,0:T(8,128)(2,1)S(1)}, bf16[128,1024]{1,0:T(8,128)(2,1)S(1)}, u32[]{:S(2)}, u32[]{:S(2)}) collective-permute-start(bf16[128,1024]{1,0:T(8,128)(2,1)S(1)} %multiply_convert_fusion.11.refs_5_), channel_id=1, source_target_pairs={{3,0},{0,1},{1,2},{2,3},{7,4},{4,5},{5,6},{6,7},{11,8},{8,9},{9,10... | collective-permute-start | bytes 786440 | tf_op jit(solution)/shard_map/ppermute | solution.py:79
  54.4 24.4 %collective-permute-start.11 = (bf16[128,512]{1,0:T(8,128)(2,1)S(1)}, bf16[128,512]{1,0:T(8,128)(2,1)S(1)}, u32[]{:S(2)}, u32[]{:S(2)}) collective-permute-start(bf16[128,512]{1,0:T(8,128)(2,1)S(1)} %slice.335.refs_2_), channel_id=1, source_target_pairs={{0,8},{4,12},{8,0},{12,4},{16,24},{20,28},{24,16},{28,20},{32,40},... | collective-permute-start | bytes 393224 | tf_op jit(solution)/shard_map/ppermute | solution.py:120
  64.5 14.8 %collective-permute-start.5 = (bf16[128,1024]{1,0:T(8,128)(2,1)S(1)}, bf16[128,1024]{1,0:T(8,128)(2,1)S(1)}, u32[]{:S(2)}, u32[]{:S(2)}) collective-permute-start(bf16[128,1024]{1,0:T(8,128)(2,1)S(1)} %convolution_convert_fusion.21), channel_id=1, source_target_pairs={{0,2},{1,3},{2,0},{3,1},{4,6},{5,7},{6,4},{7,5},{8,10},{9,11},{10,... | collective-permute-start | bytes 786440 | tf_op jit(solution)/shard_map/ppermute | solution.py:84
  311.7 15.2 %collective-permute-start.51 = (bf16[128,1024]{1,0:T(8,128)(2,1)S(1)}, bf16[128,1024]{1,0:T(8,128)(2,1)S(1)}, u32[]{:S(2)}, u32[]{:S(2)}) collective-permute-start(bf16[128,1024]{1,0:T(8,128)(2,1)S(1)} %multiply_convert_fusion.5.refs_0_), channel_id=1, source_target_pairs={{3,0},{0,1},{1,2},{2,3},{7,4},{4,5},{5,6},{6,7},{11,8},{8,9},{9,10... | collective-permute-start | bytes 786440 | tf_op jit(solution)/shard_map/ppermute | solution.py:79
  311.7 17.8 %collective-permute-start.50 = (bf16[128,1024]{1,0:T(8,128)(2,1)S(1)}, bf16[128,1024]{1,0:T(8,128)(2,1)S(1)}, u32[]{:S(2)}, u32[]{:S(2)}) collective-permute-start(bf16[128,1024]{1,0:T(8,128)(2,1)S(1)} %multiply_convert_fusion.5.refs_0_), channel_id=1, source_target_pairs={{2,0},{3,1},{0,2},{1,3},{6,4},{7,5},{4,6},{5,7},{10,8},{11,9},{8,1... | collective-permute-start | bytes 786440 | tf_op jit(solution)/shard_map/ppermute | solution.py:79
  313.8 18.6 %collective-permute-start.49 = (bf16[128,1024]{1,0:T(8,128)(2,1)S(1)}, bf16[128,1024]{1,0:T(8,128)(2,1)S(1)}, u32[]{:S(2)}, u32[]{:S(2)}) collective-permute-start(bf16[128,1024]{1,0:T(8,128)(2,1)S(1)} %multiply_convert_fusion.5.refs_0_), channel_id=1, source_target_pairs={{1,0},{2,1},{3,2},{0,3},{5,4},{6,5},{7,6},{4,7},{9,8},{10,9},{11,1... | collective-permute-start | bytes 786440 | tf_op jit(solution)/shard_map/ppermute | solution.py:79
  389.2 327.3 %reduce-scatter.5.cloned.1.call-start = ((), (), s32[]{:S(2)}) async-start(), calls=%async_computation.3 | async-start | bytes 7028736 | tf_op jit(solution)/shard_map/reduce_scatter | solution.py:212
  417.4 15.9 %collective-permute-start.65 = (bf16[128,1024]{1,0:T(8,128)(2,1)S(1)}, bf16[128,1024]{1,0:T(8,128)(2,1)S(1)}, u32[]{:S(2)}, u32[]{:S(2)}) collective-permute-start(bf16[128,1024]{1,0:T(8,128)(2,1)S(1)} %get-tuple-element.247.refs_1_), channel_id=1, source_target_pairs={{0,1},{1,2},{2,3},{3,0},{4,5},{5,6},{6,7},{7,4},{8,9},{9,10},{10,1... | collective-permute-start | bytes 786440 | tf_op jit(solution)/shard_map/ppermute | solution.py:84
  426.7 16.4 %collective-permute-start.70 = (bf16[128,1024]{1,0:T(8,128)(2,1)S(1)}, bf16[128,1024]{1,0:T(8,128)(2,1)S(1)}, u32[]{:S(2)}, u32[]{:S(2)}) collective-permute-start(bf16[128,1024]{1,0:T(8,128)(2,1)S(1)} %get-tuple-element.259.refs_0_), channel_id=1, source_target_pairs={{0,1},{1,2},{2,3},{3,0},{4,5},{5,6},{6,7},{7,4},{8,9},{9,10},{10,1... | collective-permute-start | bytes 786440 | tf_op jit(solution)/shard_map/ppermute | solution.py:84
  427.6 15.5 %collective-permute-start.71 = (bf16[128,1024]{1,0:T(8,128)(2,1)S(1)}, bf16[128,1024]{1,0:T(8,128)(2,1)S(1)}, u32[]{:S(2)}, u32[]{:S(2)}) collective-permute-start(bf16[128,1024]{1,0:T(8,128)(2,1)S(1)} %get-tuple-element.259.refs_0_), channel_id=1, source_target_pairs={{0,3},{1,0},{2,1},{3,2},{4,7},{5,4},{6,5},{7,6},{8,11},{9,8},{10,9... | collective-permute-start | bytes 786440 | tf_op jit(solution)/shard_map/ppermute | solution.py:84
  446.5 14.8 %collective-permute-start.73 = (bf16[128,1024]{1,0:T(8,128)(2,1)S(1)}, bf16[128,1024]{1,0:T(8,128)(2,1)S(1)}, u32[]{:S(2)}, u32[]{:S(2)}) collective-permute-start(bf16[128,1024]{1,0:T(8,128)(2,1)S(1)} %get-tuple-element.264), channel_id=1, source_target_pairs={{0,1},{1,2},{2,3},{3,0},{4,5},{5,6},{6,7},{7,4},{8,9},{9,10},{10,1... | collective-permute-start | bytes 786440 | tf_op jit(solution)/shard_map/ppermute | solution.py:84
  465.6 14.7 %collective-permute-start.76 = (bf16[128,1024]{1,0:T(8,128)(2,1)}, bf16[128,1024]{1,0:T(8,128)(2,1)}, u32[]{:S(2)}, u32[]{:S(2)}) collective-permute-start(bf16[128,1024]{1,0:T(8,128)(2,1)} %get-tuple-element.266.refs_1_), channel_id=1, source_target_pairs={{0,1},{1,2},{2,3},{3,0},{4,5},{5,6},{6,7},{7,4},{8,9},{9,10},{10,1... | collective-permute-start | bytes 786440 | tf_op jit(solution)/shard_map/ppermute | solution.py:84
  550.6 14.7 %collective-permute-start.90 = (bf16[128,1024]{1,0:T(8,128)(2,1)}, bf16[128,1024]{1,0:T(8,128)(2,1)}, u32[]{:S(2)}, u32[]{:S(2)}) collective-permute-start(bf16[128,1024]{1,0:T(8,128)(2,1)} %get-tuple-element.287.refs_1_), channel_id=1, source_target_pairs={{0,1},{1,2},{2,3},{3,0},{4,5},{5,6},{6,7},{7,4},{8,9},{9,10},{10,1... | collective-permute-start | bytes 786440 | tf_op jit(solution)/shard_map/ppermute | solution.py:84
  581.5 33.9 %collective-permute-start.96 = (bf16[1024,512]{1,0:T(8,128)(2,1)}, bf16[1024,512]{1,0:T(8,128)(2,1)}, u32[]{:S(2)}, u32[]{:S(2)}) collective-permute-start(bf16[1024,512]{1,0:T(8,128)(2,1)} %pad_maximum_fusion.6), channel_id=1, source_target_pairs={{0,4},{4,0},{8,12},{12,8},{16,20},{20,16},{24,28},{28,24},{32,36},... | collective-permute-start | bytes 3145736 | tf_op jit(solution)/shard_map/ppermute | solution.py:120
  608.6 19.6 %collective-permute-start.95 = (bf16[512,512]{1,0:T(8,128)(2,1)}, bf16[512,512]{1,0:T(8,128)(2,1)S(1)}, u32[]{:S(2)}, u32[]{:S(2)}) collective-permute-start(bf16[512,512]{1,0:T(8,128)(2,1)} %copy-done.227), channel_id=1, source_target_pairs={{4,0},{8,4},{12,8},{20,16},{24,20},{28,24},{36,32},{40,36},{44,40}... | collective-permute-start | bytes 1572872 | tf_op jit(solution)/shard_map/ppermute | solution.py:897
  611.6 15.3 %collective-permute-start.93 = (bf16[128,1024]{1,0:T(8,128)(2,1)S(1)}, bf16[128,1024]{1,0:T(8,128)(2,1)S(1)}, u32[]{:S(2)}, u32[]{:S(2)}) collective-permute-start(bf16[128,1024]{1,0:T(8,128)(2,1)S(1)} %convolution_convert_fusion.11), channel_id=1, source_target_pairs={{0,1},{1,2},{2,3},{3,0},{4,5},{5,6},{6,7},{7,4},{8,9},{9,10},{10,1... | collective-permute-start | bytes 786440 | tf_op jit(solution)/shard_map/ppermute | solution.py:84
  654.2 14.8 %collective-permute-start.110 = (bf16[128,1024]{1,0:T(8,128)(2,1)S(1)}, bf16[128,1024]{1,0:T(8,128)(2,1)S(1)}, u32[]{:S(2)}, u32[]{:S(2)}) collective-permute-start(bf16[128,1024]{1,0:T(8,128)(2,1)S(1)} %get-tuple-element.437.refs_13_), channel_id=1, source_target_pairs={{3,0},{0,1},{1,2},{2,3},{7,4},{4,5},{5,6},{6,7},{11,8},{8,9},{9,10... | collective-permute-start | bytes 786440 | tf_op jit(solution)/shard_map/ppermute | solution.py:79
  663.7 15.1 %collective-permute-start.107 = (bf16[128,1024]{1,0:T(8,128)(2,1)S(1)}, bf16[128,1024]{1,0:T(8,128)(2,1)S(1)}, u32[]{:S(2)}, u32[]{:S(2)}) collective-permute-start(bf16[128,1024]{1,0:T(8,128)(2,1)S(1)} %convolution_convert_fusion.6), channel_id=1, source_target_pairs={{0,2},{1,3},{2,0},{3,1},{4,6},{5,7},{6,4},{7,5},{8,10},{9,11},{10,... | collective-permute-start | bytes 786440 | tf_op jit(solution)/shard_map/ppermute | solution.py:84
  681.6 41.4 %collective-permute-start.122 = (bf16[512,2816]{1,0:T(8,128)(2,1)}, bf16[512,2816]{1,0:T(8,128)(2,1)}, u32[]{:S(2)}, u32[]{:S(2)}) collective-permute-start(bf16[512,2816]{1,0:T(8,128)(2,1)} %get-tuple-element.345), channel_id=1, source_target_pairs={{0,4},{4,0},{8,12},{12,8},{16,20},{20,16},{24,28},{28,24},{32,36},... | collective-permute-start | bytes 8650760 | tf_op jit(solution)/shard_map/ppermute | solution.py:120
  684.7 15.3 %collective-permute-start.114 = (bf16[128,1024]{1,0:T(8,128)(2,1)S(1)}, bf16[128,1024]{1,0:T(8,128)(2,1)S(1)}, u32[]{:S(2)}, u32[]{:S(2)}) collective-permute-start(bf16[128,1024]{1,0:T(8,128)(2,1)S(1)} %get-tuple-element.435), channel_id=1, source_target_pairs={{3,0},{0,1},{1,2},{2,3},{7,4},{4,5},{5,6},{6,7},{11,8},{8,9},{9,10... | collective-permute-start | bytes 786440 | tf_op jit(solution)/shard_map/ppermute | solution.py:79
  735.7 17.2 %collective-permute-start.124 = (bf16[4,32,2176]{2,1,0:T(8,128)(2,1)S(1)}, bf16[4,32,2176]{2,1,0:T(8,128)(2,1)S(1)}, u32[]{:S(2)}, u32[]{:S(2)}) collective-permute-start(bf16[4,32,2176]{2,1,0:T(8,128)(2,1)S(1)} %get-tuple-element.469), channel_id=1, source_target_pairs={{0,16},{4,20},{8,24},{12,28},{16,0},{20,4},{24,8},{28,12},{32,48},... | collective-permute-start | bytes 1671176 | tf_op jit(solution)/shard_map/ppermute | solution.py:249
  738.3 24.7 %collective-permute-start.125 = (bf16[4,32,2176]{2,1,0:T(8,128)(2,1)S(1)}, bf16[4,32,2176]{2,1,0:T(8,128)(2,1)S(1)}, u32[]{:S(2)}, u32[]{:S(2)}) collective-permute-start(bf16[4,32,2176]{2,1,0:T(8,128)(2,1)S(1)} %get-tuple-element.471), channel_id=1, source_target_pairs={{0,8},{4,12},{8,16},{12,20},{16,24},{20,28},{24,0},{28,4},{32,40},... | collective-permute-start | bytes 1671176 | tf_op jit(solution)/shard_map/ppermute | solution.py:249
  738.3 24.7 %collective-permute-start.126 = (bf16[4,32,2176]{2,1,0:T(8,128)(2,1)S(1)}, bf16[4,32,2176]{2,1,0:T(8,128)(2,1)S(1)}, u32[]{:S(2)}, u32[]{:S(2)}) collective-permute-start(bf16[4,32,2176]{2,1,0:T(8,128)(2,1)S(1)} %get-tuple-element.470), channel_id=1, source_target_pairs={{0,24},{4,28},{8,0},{12,4},{16,8},{20,12},{24,16},{28,20},{32,56},... | collective-permute-start | bytes 1671176 | tf_op jit(solution)/shard_map/ppermute | solution.py:249
  742.3 25.0 %collective-permute-start.127 = (bf16[4,32,2304]{2,1,0:T(8,128)(2,1)S(1)}, bf16[4,32,2304]{2,1,0:T(8,128)(2,1)S(1)}, u32[]{:S(2)}, u32[]{:S(2)}) collective-permute-start(bf16[4,32,2304]{2,1,0:T(8,128)(2,1)S(1)} %get-tuple-element.466), channel_id=1, source_target_pairs={{0,64},{4,68},{8,72},{12,76},{16,80},{20,84},{24,88},{28,92},{32,9... | collective-permute-start | bytes 1769480 | tf_op jit(solution)/shard_map/ppermute | solution.py:249
  745.3 27.5 %collective-permute-start.128 = (bf16[4,32,2304]{2,1,0:T(8,128)(2,1)S(1)}, bf16[4,32,2304]{2,1,0:T(8,128)(2,1)S(1)}, u32[]{:S(2)}, u32[]{:S(2)}) collective-permute-start(bf16[4,32,2304]{2,1,0:T(8,128)(2,1)S(1)} %get-tuple-element.468), channel_id=1, source_target_pairs={{0,32},{4,36},{8,40},{12,44},{16,48},{20,52},{24,56},{28,60},{32,6... | collective-permute-start | bytes 1769480 | tf_op jit(solution)/shard_map/ppermute | solution.py:249
  752.9 20.0 %collective-permute-start.129 = (bf16[4,32,2304]{2,1,0:T(8,128)(2,1)S(1)}, bf16[4,32,2304]{2,1,0:T(8,128)(2,1)S(1)}, u32[]{:S(2)}, u32[]{:S(2)}) collective-permute-start(bf16[4,32,2304]{2,1,0:T(8,128)(2,1)S(1)} %get-tuple-element.467), channel_id=1, source_target_pairs={{0,96},{4,100},{8,104},{12,108},{16,112},{20,116},{24,120},{28,124... | collective-permute-start | bytes 1769480 | tf_op jit(solution)/shard_map/ppermute | solution.py:249
  764.1 26.1 %collective-permute-start.136 = (bf16[32,2176]{1,0:T(8,128)(2,1)}, bf16[32,2176]{1,0:T(8,128)(2,1)}, u32[]{:S(2)}, u32[]{:S(2)}) collective-permute-start(bf16[32,2176]{1,0:T(8,128)(2,1)} %get-tuple-element.477), channel_id=1, source_target_pairs={{0,64},{4,68},{8,72},{12,76},{16,80},{20,84},{24,88},{28,92},{32,9... | collective-permute-start | bytes 417800 | tf_op jit(solution)/shard_map/ppermute | solution.py:249
  767.0 26.0 %collective-permute-start.137 = (bf16[32,2176]{1,0:T(8,128)(2,1)}, bf16[32,2176]{1,0:T(8,128)(2,1)}, u32[]{:S(2)}, u32[]{:S(2)}) collective-permute-start(bf16[32,2176]{1,0:T(8,128)(2,1)} %get-tuple-element.479), channel_id=1, source_target_pairs={{0,32},{4,36},{8,40},{12,44},{16,48},{20,52},{24,56},{28,60},{32,6... | collective-permute-start | bytes 417800 | tf_op jit(solution)/shard_map/ppermute | solution.py:249
  767.3 25.7 %collective-permute-start.138 = (bf16[32,2176]{1,0:T(8,128)(2,1)}, bf16[32,2176]{1,0:T(8,128)(2,1)}, u32[]{:S(2)}, u32[]{:S(2)}) collective-permute-start(bf16[32,2176]{1,0:T(8,128)(2,1)} %get-tuple-element.478), channel_id=1, source_target_pairs={{0,96},{4,100},{8,104},{12,108},{16,112},{20,116},{24,120},{28,124... | collective-permute-start | bytes 417800 | tf_op jit(solution)/shard_map/ppermute | solution.py:249
  781.3 34.7 %collective-permute-start.130 = (bf16[128,1024]{1,0:T(8,128)(2,1)}, bf16[128,1024]{1,0:T(8,128)(2,1)}, u32[]{:S(2)}, u32[]{:S(2)}) collective-permute-start(bf16[128,1024]{1,0:T(8,128)(2,1)} %get-tuple-element.434), channel_id=1, source_target_pairs={{1,0},{2,1},{3,2},{0,3},{5,4},{6,5},{7,6},{4,7},{9,8},{10,9},{11,1... | collective-permute-start | bytes 786440 | tf_op jit(solution)/shard_map/ppermute | solution.py:79
  783.3 34.3 %collective-permute-start.131 = (bf16[128,1024]{1,0:T(8,128)(2,1)}, bf16[128,1024]{1,0:T(8,128)(2,1)}, u32[]{:S(2)}, u32[]{:S(2)}) collective-permute-start(bf16[128,1024]{1,0:T(8,128)(2,1)} %get-tuple-element.434), channel_id=1, source_target_pairs={{2,0},{3,1},{0,2},{1,3},{6,4},{7,5},{4,6},{5,7},{10,8},{11,9},{8,1... | collective-permute-start | bytes 786440 | tf_op jit(solution)/shard_map/ppermute | solution.py:79
  (425 other events, 3959.3 us)
Sparse Core Ops, SparseCore 0:
  389.3 83.7 reduce-scatter.2
  607.4 85.7 reduce-scatter.4

commit v11 on v10

--- a/solution.py
+++ b/solution.py
@@ -807,7 +807,7 @@
     state_queries = state_qkv[:, :width]
     state_pieces = pos_gather(state_qkv[:, width:])
     layer_one = win_mixed + tp_scatter([plain_dot(part, down_win) for part in win_active])
-    layer_one = tied(layer_one, state_pieces)
+    layer_one = tied(layer_one, state_pieces, cotangent_rows)
 
     normed_pieces = tp_gather(layer_norm(layer_one, norm_tok).astype(LOW))
     normed = jnp.concatenate(normed_pieces)
@@ -890,9 +890,9 @@
     )
     homeward = [(s, s - 1) for s in range(lax.axis_size("seq")) if s % CHAIN]
 
-    def own_back():
+    def own_back(after):
         query_grad, pair_grad, prev_grad = attend_back(
-            queries, pair, own_token_logs, tied(grad_heads[:, :width], cross_pieces), before
+            queries, pair, own_token_logs, tied(grad_heads[:, :width], after), before
         )
         returned = lax.ppermute(prev_grad, "seq", homeward)
         return query_grad + cross_query_grad, pair_grad + returned.astype(HIGH)
@@ -931,7 +931,7 @@
         None, [], cross_pieces, position ^ (CHAIN - 1), qkv_state_flat
     )
     parts = [low] + sent_around(low)
-    query_grad, pair_grad = own_back()
+    query_grad, pair_grad = own_back(low)
     token_grads = ScatterSum(
         weight_grads(
             [
@@ -1008,9 +1008,6 @@
         if turn == CHAIN - 3:
             slabs = states_between(tied(last_slab, grad_mid))
             across = tied(across, slabs)
-        if turn == CHAIN - 4:
-            state_rows_out = states_whole(tied(slabs, grad_mid))
-            across = tied(across, state_rows_out)
         grad_state_qkv, low = chain_back_inputs(
             query_total, [here, beside, across], cross_pieces, position ^ turn, qkv_state_flat
         )
@@ -1026,16 +1023,21 @@
 
     token_pair_grads[CHAIN - 1] = jnp.zeros_like(token_pair_grads[0])
     pair_stack = jnp.stack(token_pair_grads)
-    pair_grad = pair_grad + pos_scatter([choose(pair_stack, position ^ k) for k in range(CHAIN)])
+    shares = [choose(pair_stack, position ^ k) for k in range(CHAIN)]
+    pair_grad = pair_grad + shares[0]
+    here, there = split_rows(swap(jnp.concatenate([shares[1], shares[3]]).astype(LOW), 1), 2)
+    far_share = (shares[2] + there.astype(HIGH)).astype(LOW)
+    pair_grad = pair_grad + here.astype(HIGH) + swap(far_share, 2).astype(HIGH)
+    state_rows_out = states_whole(tied(slabs, far_share))
     layer_output = mixed_one + tp_scatter(
-        [plain_dot(part, down_tok) for part in tied(tuple(active), pair_stack)]
+        [plain_dot(part, down_tok) for part in tied(tuple(active), far_share)]
     )
     qkv_parts = list(zip(*kept_qkv))
     rest_parts = list(zip(*kept_rest))
     state_grads = ScatterSum(
         weight_grads(
             [
-                (qkv_parts[0], qkv_parts[1]),
+                (tied(qkv_parts[0], far_share), qkv_parts[1]),
                 (rest_parts[1], rest_parts[0]),
                 (rest_parts[2], rest_parts[3]),
                 (rest_parts[5], rest_parts[4]),
@@ -1043,7 +1045,7 @@
             False,
         )
     )
-    pair_grad = tied(pair_grad, layer_output, state_grads.grads)
+    pair_grad = tied(pair_grad, layer_output, state_grads.grads, state_rows_out)
     grad_qkv = jnp.concatenate([query_grad, pair_grad], axis=1).astype(LOW)
     grad_normed = tp_scatter(
         [dot_second(part, qkv_tok_flat) for part in split_rows(grad_qkv, n_tp)]

time: 837 us -> 859 us (1.026)
  local copies, waits for them, and re-layouts: 118 us -> 147 us
  waiting for transfers between devices: 297 us -> 279 us
    unnamed x638 -> x664, local copies, waits for them, and re-layouts: 80.6 us -> 102 us
    ppermute x30, waiting for transfers between devices: 64.3 us -> 55 us  [tp_from(): return lax.ppermute(array, 'tp', [((i + k) % n, i) for i in range(n)])]
  transfers between devices with their start and end apart: 144 -> 144, of which waited for: 77 -> 71; matrix products, arithmetic and copies ran while one was open for 15% -> 18% of each run, Pallas kernels for 6% -> 6%
where the time goes in v11:
time: 859 us; the launch traced here: 848 us
  waiting for transfers between devices  279 us (32%)
  starting transfers between devices  189 us (22%)
  local copies, waits for them, and re-layouts  147 us (17%)
  Pallas kernels  90.9 us (11%)
  other arithmetic  63.2 us (7%)
  matrix products  57.9 us (7%)
  between operations  21.4 us (2%)
    ppermute x66, waiting for transfers between devices, tp_to(): return lax.ppermute(array, 'tp', [(i, (i + k) % n) for i in range(n)])  160 us
    ppermute x66, starting transfers between devices, tp_to(): return lax.ppermute(array, 'tp', [(i, (i + k) % n) for i in range(n)])  104 us
    unnamed x664, local copies, waits for them, and re-layouts  102 us
    pallas_call x27, Pallas kernels, fused(): pl.pallas_call(whole, out_shape=[jax.ShapeDtypeStruct(shape, kind) for sh...  73 us
    ppermute x30, waiting for transfers between devices, tp_from(): return lax.ppermute(array, 'tp', [((i + k) % n, i) for i in range(n)])  55 us
    ppermute x31, waiting for transfers between devices, swap(): return lax.ppermute(array, 'seq', [(s, s ^ k) for s in range(n)])  47.3 us
    dot_general x27, matrix products, plain_dot(): return jnp.dot(former, latter, preferred_element_type=HIGH)  35.9 us
    ppermute x30, starting transfers between devices, tp_from(): return lax.ppermute(array, 'tp', [((i + k) % n, i) for i in range(n)])  32.2 us
  transfers between devices with their start and end apart: 144, of which 71 were waited for; matrix products, arithmetic and copies ran while one was open for 18% of the time, Pallas kernels for 6%

profile of v11, /device:TPU:0, one launch (start us, length us, event | category | flops | bytes accessed | tf_op | source)
XLA Modules:
  0.0 848.1 jit_solution(17085652586822750604)
XLA Ops:
  39.6 6.2 collective-permute-done.2
  61.0 7.6 collective-permute-start.11
  100.3 6.0 collective-permute-done.13.refs_1_
  115.7 10.7 %collective-permute-done.17 = bf16[512,512]{1,0:T(8,128)(2,1)S(1)} collective-permute-done((bf16[512,512]{1,0:T(8,128)(2,1)S(1)}, bf16[512,512]{1,0:T(8,128)(2,1)S(1)}, u32[]{:S(2)}, u32[]{:S(2)}) %collective-permute-start.17) | collective-permute-done | bytes 524320 | tf_op jit(solution)/shard_map/ppermute | solution.py:120
  140.2 5.2 collective-permute-done.19.refs_1_
  179.8 5.4 collective-permute-done.26.refs_4_
  205.3 4.8 collective-permute-done.29.refs_2_
  217.0 5.6 collective-permute-done.31.refs_2_
  232.8 5.4 collective-permute-done.35.refs_4_
  252.3 6.2 collective-permute-done.37.refs_1_
  258.5 4.8 collective-permute-done.38.refs_2_
  272.0 5.4 collective-permute-done.40.refs_2_
  287.7 5.4 collective-permute-done.44.refs_4_
  307.8 5.3 collective-permute-done.46
  313.2 4.8 collective-permute-done.47
  324.7 9.3 %collective-permute-done.51.refs_3_ = bf16[128,1024]{1,0:T(8,128)(2,1)S(1)} collective-permute-done((bf16[128,1024]{1,0:T(8,128)(2,1)S(1)}, bf16[128,1024]{1,0:T(8,128)(2,1)S(1)}, u32[]{:S(2)}, u32[]{:S(2)}) %collective-permute-start.51) | collective-permute-done | bytes 262176 | tf_op jit(solution)/shard_map/ppermute | solution.py:79
  349.4 4.8 collective-permute-done.53
  358.5 7.0 collective-permute-done.55.refs_14_
  401.8 7.4 collective-permute-done.61.refs_2_
  458.3 6.0 collective-permute-done.72
  464.3 5.0 collective-permute-done.73
  476.6 7.1 collective-permute-done.75.refs_2_
  539.9 5.7 collective-permute-done.86.refs_2_
  560.9 5.6 collective-permute-done.89.refs_2_
  612.0 5.2 shard_map.425
  669.9 7.4 collective-permute-done.106.refs_15_
  687.6 6.0 shard_map.426
  704.6 6.8 collective-permute-done.112
  717.4 4.9 shard_map.427
  751.7 4.8 collective-permute-start.124
  763.6 6.5 collective-permute-done.124
  772.7 7.7 collective-permute-done.125
  (1184 shorter events, 630.5 us)
Async XLA Ops:
  7.2 565.3 %reduce-scatter.3.cloned.1.call-start = ((), (), s32[]{:S(2)}) async-start(), calls=%async_computation.2 | async-start | bytes 5406720 | tf_op jit(solution)/shard_map/reduce_scatter | solution.py:212
  58.4 20.0 %collective-permute-start.8 = (bf16[128,1024]{1,0:T(8,128)(2,1)S(1)}, bf16[128,1024]{1,0:T(8,128)(2,1)S(1)}, u32[]{:S(2)}, u32[]{:S(2)}) collective-permute-start(bf16[128,1024]{1,0:T(8,128)(2,1)S(1)} %multiply_convert_fusion.11.refs_5_), channel_id=1, source_target_pairs={{3,0},{0,1},{1,2},{2,3},{7,4},{4,5},{5,6},{6,7},{11,8},{8,9},{9,10... | collective-permute-start | bytes 786440 | tf_op jit(solution)/shard_map/ppermute | solution.py:79
  61.0 24.8 %collective-permute-start.11 = (bf16[128,512]{1,0:T(8,128)(2,1)S(1)}, bf16[128,512]{1,0:T(8,128)(2,1)S(1)}, u32[]{:S(2)}, u32[]{:S(2)}) collective-permute-start(bf16[128,512]{1,0:T(8,128)(2,1)S(1)} %slice.335.refs_2_), channel_id=1, source_target_pairs={{0,8},{4,12},{8,0},{12,4},{16,24},{20,28},{24,16},{28,20},{32,40},... | collective-permute-start | bytes 393224 | tf_op jit(solution)/shard_map/ppermute | solution.py:120
  318.9 15.1 %collective-permute-start.51 = (bf16[128,1024]{1,0:T(8,128)(2,1)S(1)}, bf16[128,1024]{1,0:T(8,128)(2,1)S(1)}, u32[]{:S(2)}, u32[]{:S(2)}) collective-permute-start(bf16[128,1024]{1,0:T(8,128)(2,1)S(1)} %multiply_convert_fusion.5.refs_0_), channel_id=1, source_target_pairs={{3,0},{0,1},{1,2},{2,3},{7,4},{4,5},{5,6},{6,7},{11,8},{8,9},{9,10... | collective-permute-start | bytes 786440 | tf_op jit(solution)/shard_map/ppermute | solution.py:79
  318.9 18.0 %collective-permute-start.50 = (bf16[128,1024]{1,0:T(8,128)(2,1)S(1)}, bf16[128,1024]{1,0:T(8,128)(2,1)S(1)}, u32[]{:S(2)}, u32[]{:S(2)}) collective-permute-start(bf16[128,1024]{1,0:T(8,128)(2,1)S(1)} %multiply_convert_fusion.5.refs_0_), channel_id=1, source_target_pairs={{2,0},{3,1},{0,2},{1,3},{6,4},{7,5},{4,6},{5,7},{10,8},{11,9},{8,1... | collective-permute-start | bytes 786440 | tf_op jit(solution)/shard_map/ppermute | solution.py:79
  321.0 18.7 %collective-permute-start.49 = (bf16[128,1024]{1,0:T(8,128)(2,1)S(1)}, bf16[128,1024]{1,0:T(8,128)(2,1)S(1)}, u32[]{:S(2)}, u32[]{:S(2)}) collective-permute-start(bf16[128,1024]{1,0:T(8,128)(2,1)S(1)} %multiply_convert_fusion.5.refs_0_), channel_id=1, source_target_pairs={{1,0},{2,1},{3,2},{0,3},{5,4},{6,5},{7,6},{4,7},{9,8},{10,9},{11,1... | collective-permute-start | bytes 786440 | tf_op jit(solution)/shard_map/ppermute | solution.py:79
  398.2 333.2 %reduce-scatter.5.cloned.1.call-start = ((), (), s32[]{:S(2)}) async-start(), calls=%async_computation.3 | async-start | bytes 7028736 | tf_op jit(solution)/shard_map/reduce_scatter | solution.py:212
  398.6 15.0 %collective-permute-start.62 = (bf16[128,1024]{1,0:T(8,128)(2,1)}, bf16[128,1024]{1,0:T(8,128)(2,1)S(1)}, u32[]{:S(2)}, u32[]{:S(2)}) collective-permute-start(bf16[128,1024]{1,0:T(8,128)(2,1)} %copy-done.157), channel_id=1, source_target_pairs={{0,1},{1,2},{2,3},{3,0},{4,5},{5,6},{6,7},{7,4},{8,9},{9,10},{10,1... | collective-permute-start | bytes 786440 | tf_op jit(solution)/shard_map/ppermute | solution.py:84
  398.6 15.0 %collective-permute-start.63 = (bf16[128,1024]{1,0:T(8,128)(2,1)}, bf16[128,1024]{1,0:T(8,128)(2,1)S(1)}, u32[]{:S(2)}, u32[]{:S(2)}) collective-permute-start(bf16[128,1024]{1,0:T(8,128)(2,1)} %copy-done.157), channel_id=1, source_target_pairs={{0,3},{1,0},{2,1},{3,2},{4,7},{5,4},{6,5},{7,6},{8,11},{9,8},{10,9... | collective-permute-start | bytes 786440 | tf_op jit(solution)/shard_map/ppermute | solution.py:84
  425.3 15.9 %collective-permute-start.65 = (bf16[128,1024]{1,0:T(8,128)(2,1)S(1)}, bf16[128,1024]{1,0:T(8,128)(2,1)S(1)}, u32[]{:S(2)}, u32[]{:S(2)}) collective-permute-start(bf16[128,1024]{1,0:T(8,128)(2,1)S(1)} %get-tuple-element.250.refs_1_), channel_id=1, source_target_pairs={{0,1},{1,2},{2,3},{3,0},{4,5},{5,6},{6,7},{7,4},{8,9},{9,10},{10,1... | collective-permute-start | bytes 786440 | tf_op jit(solution)/shard_map/ppermute | solution.py:84
  434.7 16.4 %collective-permute-start.70 = (bf16[128,1024]{1,0:T(8,128)(2,1)S(1)}, bf16[128,1024]{1,0:T(8,128)(2,1)S(1)}, u32[]{:S(2)}, u32[]{:S(2)}) collective-permute-start(bf16[128,1024]{1,0:T(8,128)(2,1)S(1)} %get-tuple-element.262.refs_0_), channel_id=1, source_target_pairs={{0,1},{1,2},{2,3},{3,0},{4,5},{5,6},{6,7},{7,4},{8,9},{9,10},{10,1... | collective-permute-start | bytes 786440 | tf_op jit(solution)/shard_map/ppermute | solution.py:84
  435.5 15.6 %collective-permute-start.71 = (bf16[128,1024]{1,0:T(8,128)(2,1)S(1)}, bf16[128,1024]{1,0:T(8,128)(2,1)S(1)}, u32[]{:S(2)}, u32[]{:S(2)}) collective-permute-start(bf16[128,1024]{1,0:T(8,128)(2,1)S(1)} %get-tuple-element.262.refs_0_), channel_id=1, source_target_pairs={{0,3},{1,0},{2,1},{3,2},{4,7},{5,4},{6,5},{7,6},{8,11},{9,8},{10,9... | collective-permute-start | bytes 786440 | tf_op jit(solution)/shard_map/ppermute | solution.py:84
  595.2 51.4 %collective-permute-start.96 = (bf16[512,512]{1,0:T(8,128)(2,1)}, bf16[512,512]{1,0:T(8,128)(2,1)}, u32[]{:S(2)}, u32[]{:S(2)}) collective-permute-start(bf16[512,512]{1,0:T(8,128)(2,1)} %copy-done.239), channel_id=1, source_target_pairs={{4,0},{8,4},{12,8},{20,16},{24,20},{28,24},{36,32},{40,36},{44,40}... | collective-permute-start | bytes 1572872 | tf_op jit(solution)/shard_map/ppermute | solution.py:897
  606.5 17.4 %collective-permute-start.100 = (bf16[4,32,1024]{2,1,0:T(8,128)(2,1)}, bf16[4,32,1024]{2,1,0:T(8,128)(2,1)}, u32[]{:S(2)}, u32[]{:S(2)}) collective-permute-start(bf16[4,32,1024]{2,1,0:T(8,128)(2,1)} %pad_maximum_fusion.10), channel_id=1, source_target_pairs={{1,0},{2,1},{3,2},{0,3},{5,4},{6,5},{7,6},{4,7},{9,8},{10,9},{11,1... | collective-permute-start | bytes 786440 | tf_op jit(solution)/shard_map/ppermute | solution.py:79
  607.1 22.5 %collective-permute-start.101 = (bf16[4,32,1024]{2,1,0:T(8,128)(2,1)}, bf16[4,32,1024]{2,1,0:T(8,128)(2,1)}, u32[]{:S(2)}, u32[]{:S(2)}) collective-permute-start(bf16[4,32,1024]{2,1,0:T(8,128)(2,1)} %pad_maximum_fusion.10), channel_id=1, source_target_pairs={{2,0},{3,1},{0,2},{1,3},{6,4},{7,5},{4,6},{5,7},{10,8},{11,9},{8,1... | collective-permute-start | bytes 786440 | tf_op jit(solution)/shard_map/ppermute | solution.py:79
  607.8 23.5 %collective-permute-start.102 = (bf16[4,32,1024]{2,1,0:T(8,128)(2,1)}, bf16[4,32,1024]{2,1,0:T(8,128)(2,1)}, u32[]{:S(2)}, u32[]{:S(2)}) collective-permute-start(bf16[4,32,1024]{2,1,0:T(8,128)(2,1)} %pad_maximum_fusion.10), channel_id=1, source_target_pairs={{3,0},{0,1},{1,2},{2,3},{7,4},{4,5},{5,6},{6,7},{11,8},{8,9},{9,10... | collective-permute-start | bytes 786440 | tf_op jit(solution)/shard_map/ppermute | solution.py:79
  608.6 38.0 %collective-permute-start.97 = (bf16[512,512]{1,0:T(8,128)(2,1)}, bf16[512,512]{1,0:T(8,128)(2,1)}, u32[]{:S(2)}, u32[]{:S(2)}) collective-permute-start(bf16[512,512]{1,0:T(8,128)(2,1)} %fusion.27), channel_id=1, source_target_pairs={{0,8},{4,12},{8,0},{12,4},{16,24},{20,28},{24,16},{28,20},{32,40},... | collective-permute-start | bytes 1572872 | tf_op jit(solution)/shard_map/ppermute | solution.py:120
  623.8 21.5 %collective-permute-start.93 = (bf16[128,1024]{1,0:T(8,128)(2,1)}, bf16[128,1024]{1,0:T(8,128)(2,1)S(1)}, u32[]{:S(2)}, u32[]{:S(2)}) collective-permute-start(bf16[128,1024]{1,0:T(8,128)(2,1)} %convolution_convert_fusion.12), channel_id=1, source_target_pairs={{0,2},{1,3},{2,0},{3,1},{4,6},{5,7},{6,4},{7,5},{8,10},{9,11},{10,... | collective-permute-start | bytes 786440 | tf_op jit(solution)/shard_map/ppermute | solution.py:84
  629.6 15.7 %collective-permute-start.94 = (bf16[128,1024]{1,0:T(8,128)(2,1)S(1)}, bf16[128,1024]{1,0:T(8,128)(2,1)S(1)}, u32[]{:S(2)}, u32[]{:S(2)}) collective-permute-start(bf16[128,1024]{1,0:T(8,128)(2,1)S(1)} %copy-done.291), channel_id=1, source_target_pairs={{0,1},{1,2},{2,3},{3,0},{4,5},{5,6},{6,7},{7,4},{8,9},{9,10},{10,1... | collective-permute-start | bytes 786440 | tf_op jit(solution)/shard_map/ppermute | solution.py:84
  696.4 42.2 %collective-permute-start.122 = (bf16[512,2816]{1,0:T(8,128)(2,1)}, bf16[512,2816]{1,0:T(8,128)(2,1)}, u32[]{:S(2)}, u32[]{:S(2)}) collective-permute-start(bf16[512,2816]{1,0:T(8,128)(2,1)} %get-tuple-element.350), channel_id=1, source_target_pairs={{0,4},{4,0},{8,12},{12,8},{16,20},{20,16},{24,28},{28,24},{32,36},... | collective-permute-start | bytes 8650760 | tf_op jit(solution)/shard_map/ppermute | solution.py:120
  699.6 15.2 %collective-permute-start.114 = (bf16[128,1024]{1,0:T(8,128)(2,1)S(1)}, bf16[128,1024]{1,0:T(8,128)(2,1)S(1)}, u32[]{:S(2)}, u32[]{:S(2)}) collective-permute-start(bf16[128,1024]{1,0:T(8,128)(2,1)S(1)} %get-tuple-element.441), channel_id=1, source_target_pairs={{3,0},{0,1},{1,2},{2,3},{7,4},{4,5},{5,6},{6,7},{11,8},{8,9},{9,10... | collective-permute-start | bytes 786440 | tf_op jit(solution)/shard_map/ppermute | solution.py:79
  751.7 18.4 %collective-permute-start.124 = (bf16[4,32,2176]{2,1,0:T(8,128)(2,1)S(1)}, bf16[4,32,2176]{2,1,0:T(8,128)(2,1)S(1)}, u32[]{:S(2)}, u32[]{:S(2)}) collective-permute-start(bf16[4,32,2176]{2,1,0:T(8,128)(2,1)S(1)} %get-tuple-element.475), channel_id=1, source_target_pairs={{0,16},{4,20},{8,24},{12,28},{16,0},{20,4},{24,8},{28,12},{32,48},... | collective-permute-start | bytes 1671176 | tf_op jit(solution)/shard_map/ppermute | solution.py:249
  756.5 23.9 %collective-permute-start.125 = (bf16[4,32,2176]{2,1,0:T(8,128)(2,1)S(1)}, bf16[4,32,2176]{2,1,0:T(8,128)(2,1)S(1)}, u32[]{:S(2)}, u32[]{:S(2)}) collective-permute-start(bf16[4,32,2176]{2,1,0:T(8,128)(2,1)S(1)} %get-tuple-element.477), channel_id=1, source_target_pairs={{0,8},{4,12},{8,16},{12,20},{16,24},{20,28},{24,0},{28,4},{32,40},... | collective-permute-start | bytes 1671176 | tf_op jit(solution)/shard_map/ppermute | solution.py:249
  756.5 23.9 %collective-permute-start.126 = (bf16[4,32,2176]{2,1,0:T(8,128)(2,1)S(1)}, bf16[4,32,2176]{2,1,0:T(8,128)(2,1)S(1)}, u32[]{:S(2)}, u32[]{:S(2)}) collective-permute-start(bf16[4,32,2176]{2,1,0:T(8,128)(2,1)S(1)} %get-tuple-element.476), channel_id=1, source_target_pairs={{0,24},{4,28},{8,0},{12,4},{16,8},{20,12},{24,16},{28,20},{32,56},... | collective-permute-start | bytes 1671176 | tf_op jit(solution)/shard_map/ppermute | solution.py:249
  760.0 25.0 %collective-permute-start.127 = (bf16[4,32,2304]{2,1,0:T(8,128)(2,1)S(1)}, bf16[4,32,2304]{2,1,0:T(8,128)(2,1)S(1)}, u32[]{:S(2)}, u32[]{:S(2)}) collective-permute-start(bf16[4,32,2304]{2,1,0:T(8,128)(2,1)S(1)} %get-tuple-element.472), channel_id=1, source_target_pairs={{0,64},{4,68},{8,72},{12,76},{16,80},{20,84},{24,88},{28,92},{32,9... | collective-permute-start | bytes 1769480 | tf_op jit(solution)/shard_map/ppermute | solution.py:249
  763.0 26.4 %collective-permute-start.128 = (bf16[4,32,2304]{2,1,0:T(8,128)(2,1)S(1)}, bf16[4,32,2304]{2,1,0:T(8,128)(2,1)S(1)}, u32[]{:S(2)}, u32[]{:S(2)}) collective-permute-start(bf16[4,32,2304]{2,1,0:T(8,128)(2,1)S(1)} %get-tuple-element.474), channel_id=1, source_target_pairs={{0,32},{4,36},{8,40},{12,44},{16,48},{20,52},{24,56},{28,60},{32,6... | collective-permute-start | bytes 1769480 | tf_op jit(solution)/shard_map/ppermute | solution.py:249
  770.1 19.7 %collective-permute-start.129 = (bf16[4,32,2304]{2,1,0:T(8,128)(2,1)S(1)}, bf16[4,32,2304]{2,1,0:T(8,128)(2,1)S(1)}, u32[]{:S(2)}, u32[]{:S(2)}) collective-permute-start(bf16[4,32,2304]{2,1,0:T(8,128)(2,1)S(1)} %get-tuple-element.473), channel_id=1, source_target_pairs={{0,96},{4,100},{8,104},{12,108},{16,112},{20,116},{24,120},{28,124... | collective-permute-start | bytes 1769480 | tf_op jit(solution)/shard_map/ppermute | solution.py:249
  781.5 25.8 %collective-permute-start.136 = (bf16[32,2176]{1,0:T(8,128)(2,1)}, bf16[32,2176]{1,0:T(8,128)(2,1)}, u32[]{:S(2)}, u32[]{:S(2)}) collective-permute-start(bf16[32,2176]{1,0:T(8,128)(2,1)} %get-tuple-element.483), channel_id=1, source_target_pairs={{0,64},{4,68},{8,72},{12,76},{16,80},{20,84},{24,88},{28,92},{32,9... | collective-permute-start | bytes 417800 | tf_op jit(solution)/shard_map/ppermute | solution.py:249
  784.4 27.5 %collective-permute-start.137 = (bf16[32,2176]{1,0:T(8,128)(2,1)}, bf16[32,2176]{1,0:T(8,128)(2,1)}, u32[]{:S(2)}, u32[]{:S(2)}) collective-permute-start(bf16[32,2176]{1,0:T(8,128)(2,1)} %get-tuple-element.485), channel_id=1, source_target_pairs={{0,32},{4,36},{8,40},{12,44},{16,48},{20,52},{24,56},{28,60},{32,6... | collective-permute-start | bytes 417800 | tf_op jit(solution)/shard_map/ppermute | solution.py:249
  785.0 26.9 %collective-permute-start.138 = (bf16[32,2176]{1,0:T(8,128)(2,1)}, bf16[32,2176]{1,0:T(8,128)(2,1)}, u32[]{:S(2)}, u32[]{:S(2)}) collective-permute-start(bf16[32,2176]{1,0:T(8,128)(2,1)} %get-tuple-element.484), channel_id=1, source_target_pairs={{0,96},{4,100},{8,104},{12,108},{16,112},{20,116},{24,120},{28,124... | collective-permute-start | bytes 417800 | tf_op jit(solution)/shard_map/ppermute | solution.py:249
  798.2 38.6 %collective-permute-start.130 = (bf16[128,1024]{1,0:T(8,128)(2,1)}, bf16[128,1024]{1,0:T(8,128)(2,1)}, u32[]{:S(2)}, u32[]{:S(2)}) collective-permute-start(bf16[128,1024]{1,0:T(8,128)(2,1)} %get-tuple-element.440), channel_id=1, source_target_pairs={{1,0},{2,1},{3,2},{0,3},{5,4},{6,5},{7,6},{4,7},{9,8},{10,9},{11,1... | collective-permute-start | bytes 786440 | tf_op jit(solution)/shard_map/ppermute | solution.py:79
  799.1 39.3 %collective-permute-start.131 = (bf16[128,1024]{1,0:T(8,128)(2,1)}, bf16[128,1024]{1,0:T(8,128)(2,1)}, u32[]{:S(2)}, u32[]{:S(2)}) collective-permute-start(bf16[128,1024]{1,0:T(8,128)(2,1)} %get-tuple-element.440), channel_id=1, source_target_pairs={{2,0},{3,1},{0,2},{1,3},{6,4},{7,5},{4,6},{5,7},{10,8},{11,9},{8,1... | collective-permute-start | bytes 786440 | tf_op jit(solution)/shard_map/ppermute | solution.py:79
  (438 other events, 3916.7 us)
Sparse Core Ops, SparseCore 0:
  398.3 85.6 reduce-scatter.2
  623.9 91.2 reduce-scatter.4

commit v12 on v10

--- a/solution.py
+++ b/solution.py
@@ -100,6 +100,11 @@
     for k in far_first(n):
         total = total + tp_to(parts[k].astype(LOW), k).astype(HIGH)
     return total
+
+
+def tp_parts(parts):
+    n = lax.axis_size("tp")
+    return [parts[0]] + [tp_to(parts[k].astype(LOW), k) for k in far_first(n)]
 
 
 def tp_total(part):
@@ -514,6 +519,34 @@
     for ref in refs[1:]:
         total = total + ref[...].astype(HIGH)
     return total
+
+
+def rows_norm(parts, residual, gain):
+    n = len(parts)
+
+    def kernel(*refs):
+        residual_ref, gain_ref, total_ref, normed_ref = refs[n:]
+        total = residual_ref[...].astype(HIGH) + added(refs[:n])
+        total_ref[...] = total
+        normed_ref[...] = layer_norm(total, gain_ref[...]).astype(LOW)
+
+    outs = [(residual.shape, HIGH), (residual.shape, LOW)]
+    return fused(kernel, outs, [*parts, residual, gain.reshape(1, -1)], residual.size)
+
+
+def rows_back(parts, matrix, gain, residual):
+    n = len(parts)
+
+    def kernel(*refs):
+        matrix_ref, gain_ref, residual_ref, total_ref, low_ref = refs[n:]
+        total = residual_ref[...].astype(HIGH) + norm_back(
+            matrix_ref[...], gain_ref[...], added(refs[:n])
+        )
+        total_ref[...], low_ref[...] = total, total.astype(LOW)
+
+    outs = [(matrix.shape, HIGH), (matrix.shape, LOW)]
+    operands = [*parts, matrix, gain.reshape(1, -1), residual]
+    return fused(kernel, outs, operands, matrix.size)
 
 
 def chain_attend(queries, pieces, stack, index, out_flat):
@@ -788,10 +821,9 @@
     keep_one, keep_two = jax.nn.sigmoid(gate_bias)
     cotangent_rows = turned(cotangent, tp_index * piece_rows)
     own_input = input_rows[:piece_rows]
-    win_mixed = own_input + tp_scatter(
-        [plain_dot(part, out_win) for part in split_rows(win_heads, n_tp)]
-    )
-    win_ffn_in = tp_gather(layer_norm(win_mixed, norm_wffn).astype(LOW))
+    parts = tp_parts([plain_dot(part, out_win) for part in split_rows(win_heads, n_tp)])
+    win_mixed, low = rows_norm(parts, own_input, norm_wffn)
+    win_ffn_in = tp_gather(low)
     win_hidden = [plain_dot(part, up_win) for part in win_ffn_in]
     win_active = [gelu_exact(part).astype(LOW) for part in win_hidden]
 
@@ -806,10 +838,10 @@
     state_qkv = plain_dot(state_normed, qkv_state_flat).astype(LOW)
     state_queries = state_qkv[:, :width]
     state_pieces = pos_gather(state_qkv[:, width:])
-    layer_one = win_mixed + tp_scatter([plain_dot(part, down_win) for part in win_active])
-    layer_one = tied(layer_one, state_pieces)
-
-    normed_pieces = tp_gather(layer_norm(layer_one, norm_tok).astype(LOW))
+    parts = tp_parts([plain_dot(part, down_win) for part in win_active])
+    layer_one, low = rows_norm(tied(parts, state_pieces), win_mixed, norm_tok)
+
+    normed_pieces = tp_gather(low)
     normed = jnp.concatenate(normed_pieces)
     token_qkv = plain_dot(normed, qkv_tok_flat).astype(LOW)
     queries, pair = token_qkv[:, :width], token_qkv[:, width:]
@@ -862,22 +894,22 @@
 
     cross_heads, cross_token_logs = attend(queries, my_state_pair)
     token_heads = jnp.concatenate([own_heads, cross_heads], axis=1)
-    proj_total = tp_scatter(
+    parts = tp_parts(
         [plain_dot(part, out_tok_flat) for part in split_rows(token_heads, n_tp)]
     )
     cotangents = split_rows(tied(cotangent_rows, token_heads), n_tp)
     grad_active = [dot_second(part, down_tok) for part in cotangents]
-    mixed_one = layer_one + tied(proj_total, *grad_active)
-    ffn_in = tp_gather(layer_norm(mixed_one, norm_ffn).astype(LOW))
+    mixed_one, low = rows_norm(tied(parts, *grad_active), layer_one, norm_ffn)
+    ffn_in = tp_gather(low)
     hidden = [plain_dot(part, up_tok) for part in ffn_in]
 
     grad_hidden = [
         gelu_slope(part, grad).astype(LOW) for part, grad in zip(hidden, grad_active)
     ]
     active = [gelu_exact(part).astype(LOW) for part in hidden]
-    grad_ffn_in = tp_scatter([dot_second(part, up_tok) for part in grad_hidden])
-    grad_mixed = cotangents[0].astype(HIGH) + norm_back(mixed_one, norm_ffn, grad_ffn_in)
-    grad_proj_pieces = tp_gather(grad_mixed.astype(LOW))
+    parts = tp_parts([dot_second(part, up_tok) for part in grad_hidden])
+    grad_mixed, low = rows_back(parts, mixed_one, norm_ffn, cotangents[0])
+    grad_proj_pieces = tp_gather(low)
     grad_proj = jnp.concatenate(grad_proj_pieces)
     grad_heads = dot_second(grad_proj, out_tok_flat).astype(LOW)
     cross_query_grad, cross_pair_grad = attend_back(
@@ -932,17 +964,7 @@
     )
     parts = [low] + sent_around(low)
     query_grad, pair_grad = own_back()
-    token_grads = ScatterSum(
-        weight_grads(
-            [
-                (tied(tuple(ffn_in), query_grad), grad_hidden),
-                ([cotangent_rows], active),
-                (grad_proj_pieces, [token_heads]),
-            ],
-            False,
-        )
-    )
-    parts = tied(parts, token_grads.grads)
+    parts = tied(parts, query_grad)
     kept_qkv, kept_rest = [(state_normed, grad_state_qkv)], []
     token_pair_grads = [None] * CHAIN
     init_grad = jnp.zeros((slab_rows, model_width), HIGH)
@@ -979,8 +1001,18 @@
         init_grad = init_grad + jnp.where(flags[turn + 1], grad_next, 0.0)
         bias_two = bias_two + sums
         parts = [low] + sent_around(low)
-        if turn == 0:
-            parts = tied(parts, token_grads.total)
+        if turn == CHAIN - 3:
+            token_grads = ScatterSum(
+                weight_grads(
+                    [
+                        (tied(tuple(ffn_in), low), grad_hidden),
+                        ([cotangent_rows], active),
+                        (grad_proj_pieces, [token_heads]),
+                    ],
+                    False,
+                )
+            )
+            parts = tied(parts, token_grads.grads)
         grad_mid, grad_update, sums, query_total, here, across, sent, token_grad = chain_back_heads(
             parts,
             mid_state,
@@ -1043,19 +1075,17 @@
             False,
         )
     )
-    pair_grad = tied(pair_grad, layer_output, state_grads.grads)
+    pair_grad = tied(pair_grad, layer_output, state_grads.grads, token_grads.total)
     grad_qkv = jnp.concatenate([query_grad, pair_grad], axis=1).astype(LOW)
-    grad_normed = tp_scatter(
-        [dot_second(part, qkv_tok_flat) for part in split_rows(grad_qkv, n_tp)]
-    )
-    grad_layer_one = grad_mixed + norm_back(layer_one, norm_tok, grad_normed)
-
-    grad_win_out = tp_gather(grad_layer_one.astype(LOW))
+    parts = tp_parts([dot_second(part, qkv_tok_flat) for part in split_rows(grad_qkv, n_tp)])
+    grad_layer_one, low = rows_back(parts, layer_one, norm_tok, grad_mixed)
+
+    grad_win_out = tp_gather(low)
     grad_win_hidden = [
         gelu_slope(part, dot_second(grad, down_win)).astype(LOW)
         for part, grad in zip(win_hidden, grad_win_out)
     ]
-    grad_win_ffn_in = tp_scatter([dot_second(part, up_win) for part in grad_win_hidden])
+    parts = tp_parts([dot_second(part, up_win) for part in grad_win_hidden])
 
     middle_grads = SeqSum(
         weight_grads(
@@ -1066,9 +1096,9 @@
             ]
         )
     )
-    grad_win_ffn_in = tied(grad_win_ffn_in, middle_grads.other)
-    grad_win_mixed = grad_layer_one + norm_back(win_mixed, norm_wffn, grad_win_ffn_in)
-    grad_win_pieces = tp_gather(grad_win_mixed.astype(LOW))
+    parts = tied(parts, middle_grads.other)
+    grad_win_mixed, low = rows_back(parts, win_mixed, norm_wffn, grad_layer_one)
+    grad_win_pieces = tp_gather(low)
     middle_halves = middle_grads.cores(grad_win_mixed)
     grad_win_proj = jnp.concatenate(grad_win_pieces)
     grad_win_heads = dot_second(grad_win_proj, out_win).astype(LOW)
@@ -1104,13 +1134,13 @@
     split_at = [half.shape[-1] for half in middle_halves]
     halves = [jnp.concatenate(both, axis=-1) for both in zip(middle_halves, last_halves)]
     parts = [dot_second(part, qkv_win_flat) for part in split_rows(grad_win_qkv, n_tp)]
-    grad_win_normed = tp_scatter(parts)
-    firsts = last_grads.across(*tied(halves, parts))
+    parts = tp_parts(parts)
+    firsts = last_grads.across(*tied(halves, parts[0]))
     one, two = last_grads.last(*firsts)
     middle_halves = one[:, : split_at[0]], two[:, : split_at[1]]
     last_halves = one[:, split_at[0] :], two[:, split_at[1] :]
-    back_input = norm_back(own_input, norm_win, tied(grad_win_normed, firsts))
-    grad_token_rows = natural(tp_gather((grad_win_mixed + back_input).astype(LOW)))
+    _, low = rows_back(tied(parts, firsts), own_input, norm_win, grad_win_mixed)
+    grad_token_rows = natural(tp_gather(low))
     output_rows = natural(tp_gather(tied(layer_output.astype(LOW), grad_win_heads)))
 
     own_columns = model_width // lax.axis_size("seq")

time: 837 us -> 850 us (1.016)
  other arithmetic: 55.3 us -> 41.8 us
  local copies, waits for them, and re-layouts: 118 us -> 129 us
    ppermute x30, waiting for transfers between devices: 64.3 us -> 77.1 us  [tp_from(): return lax.ppermute(array, 'tp', [((i + k) % n, i) for i in range(n)])]
    ppermute x66, waiting for transfers between devices: 168 us -> 157 us  [tp_to(): return lax.ppermute(array, 'tp', [(i, (i + k) % n) for i in range(n)])]
    ppermute x12, waiting for transfers between devices: 17.3 us -> 27.1 us  [stage(): total = total + lax.ppermute(sent, 'seq', self.pairs(*step(k))).astype(HIGH)]
    pallas_call x27 -> x34, Pallas kernels: 72.2 us -> 79.2 us  [fused(): pl.pallas_call(whole, out_shape=[jax.ShapeDtypeStruct(shape, kind) for sh...]
    unnamed x638 -> x711, local copies, waits for them, and re-layouts: 80.6 us -> 83.5 us
  transfers between devices with their start and end apart: 144 -> 144, of which waited for: 77 -> 70; matrix products, arithmetic and copies ran while one was open for 15% -> 16% of each run, Pallas kernels for 6% -> 6%
where the time goes in v12:
time: 850 us; the launch traced here: 839 us
  waiting for transfers between devices  305 us (36%)
  starting transfers between devices  185 us (22%)
  local copies, waits for them, and re-layouts  129 us (15%)
  Pallas kernels  97.3 us (11%)
  matrix products  58.6 us (7%)
  other arithmetic  41.8 us (5%)
  between operations  21.8 us (3%)
    ppermute x66, waiting for transfers between devices, tp_to(): return lax.ppermute(array, 'tp', [(i, (i + k) % n) for i in range(n)])  157 us
    ppermute x66, starting transfers between devices, tp_to(): return lax.ppermute(array, 'tp', [(i, (i + k) % n) for i in range(n)])  96.4 us
    unnamed x711, local copies, waits for them, and re-layouts  83.5 us
    pallas_call x34, Pallas kernels, fused(): pl.pallas_call(whole, out_shape=[jax.ShapeDtypeStruct(shape, kind) for sh...  79.2 us
    ppermute x30, waiting for transfers between devices, tp_from(): return lax.ppermute(array, 'tp', [((i + k) % n, i) for i in range(n)])  77.1 us
    ppermute x31, waiting for transfers between devices, swap(): return lax.ppermute(array, 'seq', [(s, s ^ k) for s in range(n)])  44.3 us
    dot_general x27, matrix products, plain_dot(): return jnp.dot(former, latter, preferred_element_type=HIGH)  37.5 us
    ppermute x30, starting transfers between devices, tp_from(): return lax.ppermute(array, 'tp', [((i + k) % n, i) for i in range(n)])  35.5 us
  transfers between devices with their start and end apart: 144, of which 70 were waited for; matrix products, arithmetic and copies ran while one was open for 16% of the time, Pallas kernels for 6%

profile of v12, /device:TPU:0, one launch (start us, length us, event | category | flops | bytes accessed | tf_op | source)
XLA Modules:
  0.0 839.3 jit_solution(710138245702420557)
XLA Ops:
  52.9 8.7 %collective-permute-done.6.refs_6_ = bf16[128,1024]{1,0:T(8,128)(2,1)S(1)} collective-permute-done((bf16[128,1024]{1,0:T(8,128)(2,1)S(1)}, bf16[128,1024]{1,0:T(8,128)(2,1)S(1)}, u32[]{:S(2)}, u32[]{:S(2)}) %collective-permute-start.6) | collective-permute-done | bytes 262176 | tf_op jit(solution)/shard_map/ppermute | solution.py:79
  91.7 7.2 collective-permute-done.13.refs_1_
  108.1 11.3 %collective-permute-done.17 = bf16[512,512]{1,0:T(8,128)(2,1)S(1)} collective-permute-done((bf16[512,512]{1,0:T(8,128)(2,1)S(1)}, bf16[512,512]{1,0:T(8,128)(2,1)S(1)}, u32[]{:S(2)}, u32[]{:S(2)}) %collective-permute-start.17) | collective-permute-done | bytes 524320 | tf_op jit(solution)/shard_map/ppermute | solution.py:125
  132.2 6.6 collective-permute-done.19.refs_1_
  138.8 4.8 collective-permute-done.20.refs_2_
  198.7 4.8 collective-permute-done.29.refs_2_
  210.1 5.9 collective-permute-done.31.refs_2_
  245.4 6.6 collective-permute-done.37.refs_1_
  252.0 4.8 collective-permute-done.38.refs_2_
  265.1 5.8 collective-permute-done.40.refs_2_
  303.3 6.2 collective-permute-done.46.refs_1_
  309.5 5.2 collective-permute-done.47.refs_2_
  321.2 9.0 %collective-permute-done.51.refs_3_ = bf16[128,1024]{1,0:T(8,128)(2,1)S(1)} collective-permute-done((bf16[128,1024]{1,0:T(8,128)(2,1)S(1)}, bf16[128,1024]{1,0:T(8,128)(2,1)S(1)}, u32[]{:S(2)}, u32[]{:S(2)}) %collective-permute-start.51) | collective-permute-done | bytes 262176 | tf_op jit(solution)/shard_map/ppermute | solution.py:79
  346.0 5.4 collective-permute-done.53.refs_2_
  355.8 7.1 collective-permute-done.55.refs_14_
  446.1 5.2 collective-permute-done.73
  458.5 5.5 collective-permute-done.75.refs_2_
  476.2 4.8 shard_map.423
  532.1 6.0 collective-permute-done.86.refs_2_
  550.1 5.9 collective-permute-done.89.refs_2_
  582.2 4.8 collective-permute-done.102
  590.7 5.1 shard_map.429
  636.9 5.1 collective-permute-done.105.refs_3_
  642.0 5.2 collective-permute-done.104.refs_2_
  653.5 7.0 collective-permute-done.110.refs_16_
  670.1 5.5 shard_map.431
  681.7 5.6 collective-permute-done.112
  690.4 4.8 collective-permute-done.114
  696.2 5.0 shard_map.433
  741.4 9.8 %collective-permute-done.124 = bf16[4,32,2176]{2,1,0:T(8,128)(2,1)S(1)} collective-permute-done((bf16[4,32,2176]{2,1,0:T(8,128)(2,1)S(1)}, bf16[4,32,2176]{2,1,0:T(8,128)(2,1)S(1)}, u32[]{:S(2)}, u32[]{:S(2)}) %collective-permute-start.124) | collective-permute-done | bytes 557088 | tf_op jit(solution)/shard_map/ppermute | solution.py:254
  754.2 7.7 collective-permute-done.125
  768.7 9.6 %collective-permute-done.128 = bf16[4,32,2304]{2,1,0:T(8,128)(2,1)S(1)} collective-permute-done((bf16[4,32,2304]{2,1,0:T(8,128)(2,1)S(1)}, bf16[4,32,2304]{2,1,0:T(8,128)(2,1)S(1)}, u32[]{:S(2)}, u32[]{:S(2)}) %collective-permute-start.128) | collective-permute-done | bytes 589856 | tf_op jit(solution)/shard_map/ppermute | solution.py:254
  (1207 shorter events, 615.5 us)
Async XLA Ops:
  7.2 623.5 %reduce-scatter.3.cloned.1.call-start = ((), (), s32[]{:S(2)}) async-start(), calls=%async_computation.2 | async-start | bytes 5406720 | tf_op jit(solution)/shard_map/reduce_scatter | solution.py:217
  45.9 15.7 %collective-permute-start.6 = (bf16[128,1024]{1,0:T(8,128)(2,1)S(1)}, bf16[128,1024]{1,0:T(8,128)(2,1)S(1)}, u32[]{:S(2)}, u32[]{:S(2)}) collective-permute-start(bf16[128,1024]{1,0:T(8,128)(2,1)S(1)} %get-tuple-element.219.refs_5_), channel_id=1, source_target_pairs={{1,0},{2,1},{3,2},{0,3},{5,4},{6,5},{7,6},{4,7},{9,8},{10,9},{11,1... | collective-permute-start | bytes 786440 | tf_op jit(solution)/shard_map/ppermute | solution.py:79
  49.6 15.1 %collective-permute-start.4 = (bf16[128,1024]{1,0:T(8,128)(2,1)S(1)}, bf16[128,1024]{1,0:T(8,128)(2,1)S(1)}, u32[]{:S(2)}, u32[]{:S(2)}) collective-permute-start(bf16[128,1024]{1,0:T(8,128)(2,1)S(1)} %get-tuple-element.219.refs_5_), channel_id=1, source_target_pairs={{2,0},{3,1},{0,2},{1,3},{6,4},{7,5},{4,6},{5,7},{10,8},{11,9},{8,1... | collective-permute-start | bytes 786440 | tf_op jit(solution)/shard_map/ppermute | solution.py:79
  50.6 24.2 %collective-permute-start.8 = (bf16[128,1024]{1,0:T(8,128)(2,1)S(1)}, bf16[128,1024]{1,0:T(8,128)(2,1)S(1)}, u32[]{:S(2)}, u32[]{:S(2)}) collective-permute-start(bf16[128,1024]{1,0:T(8,128)(2,1)S(1)} %get-tuple-element.219.refs_5_), channel_id=1, source_target_pairs={{3,0},{0,1},{1,2},{2,3},{7,4},{4,5},{5,6},{6,7},{11,8},{8,9},{9,10... | collective-permute-start | bytes 786440 | tf_op jit(solution)/shard_map/ppermute | solution.py:79
  315.1 15.2 %collective-permute-start.51 = (bf16[128,1024]{1,0:T(8,128)(2,1)S(1)}, bf16[128,1024]{1,0:T(8,128)(2,1)S(1)}, u32[]{:S(2)}, u32[]{:S(2)}) collective-permute-start(bf16[128,1024]{1,0:T(8,128)(2,1)S(1)} %get-tuple-element.304.refs_0_), channel_id=1, source_target_pairs={{3,0},{0,1},{1,2},{2,3},{7,4},{4,5},{5,6},{6,7},{11,8},{8,9},{9,10... | collective-permute-start | bytes 786440 | tf_op jit(solution)/shard_map/ppermute | solution.py:79
  315.1 18.4 %collective-permute-start.50 = (bf16[128,1024]{1,0:T(8,128)(2,1)S(1)}, bf16[128,1024]{1,0:T(8,128)(2,1)S(1)}, u32[]{:S(2)}, u32[]{:S(2)}) collective-permute-start(bf16[128,1024]{1,0:T(8,128)(2,1)S(1)} %get-tuple-element.304.refs_0_), channel_id=1, source_target_pairs={{2,0},{3,1},{0,2},{1,3},{6,4},{7,5},{4,6},{5,7},{10,8},{11,9},{8,1... | collective-permute-start | bytes 786440 | tf_op jit(solution)/shard_map/ppermute | solution.py:79
  317.2 19.7 %collective-permute-start.49 = (bf16[128,1024]{1,0:T(8,128)(2,1)S(1)}, bf16[128,1024]{1,0:T(8,128)(2,1)S(1)}, u32[]{:S(2)}, u32[]{:S(2)}) collective-permute-start(bf16[128,1024]{1,0:T(8,128)(2,1)S(1)} %get-tuple-element.304.refs_0_), channel_id=1, source_target_pairs={{1,0},{2,1},{3,2},{0,3},{5,4},{6,5},{7,6},{4,7},{9,8},{10,9},{11,1... | collective-permute-start | bytes 786440 | tf_op jit(solution)/shard_map/ppermute | solution.py:79
  406.4 17.2 %collective-permute-start.65 = (bf16[128,1024]{1,0:T(8,128)(2,1)}, bf16[128,1024]{1,0:T(8,128)(2,1)S(1)}, u32[]{:S(2)}, u32[]{:S(2)}) collective-permute-start(bf16[128,1024]{1,0:T(8,128)(2,1)} %get-tuple-element.281.refs_1_), channel_id=1, source_target_pairs={{0,1},{1,2},{2,3},{3,0},{4,5},{5,6},{6,7},{7,4},{8,9},{9,10},{10,1... | collective-permute-start | bytes 786440 | tf_op jit(solution)/shard_map/ppermute | solution.py:84
  408.1 15.5 %collective-permute-start.66 = (bf16[128,1024]{1,0:T(8,128)(2,1)}, bf16[128,1024]{1,0:T(8,128)(2,1)S(1)}, u32[]{:S(2)}, u32[]{:S(2)}) collective-permute-start(bf16[128,1024]{1,0:T(8,128)(2,1)} %get-tuple-element.281.refs_1_), channel_id=1, source_target_pairs={{0,3},{1,0},{2,1},{3,2},{4,7},{5,4},{6,5},{7,6},{8,11},{9,8},{10,9... | collective-permute-start | bytes 786440 | tf_op jit(solution)/shard_map/ppermute | solution.py:84
  483.3 232.3 %reduce-scatter.5.cloned.1.call-start = ((), (), s32[]{:S(2)}) async-start(), calls=%async_computation.3 | async-start | bytes 7028736 | tf_op jit(solution)/shard_map/reduce_scatter | solution.py:217
  602.6 23.8 %collective-permute-start.95 = (bf16[512,512]{1,0:T(8,128)(2,1)}, bf16[512,512]{1,0:T(8,128)(2,1)}, u32[]{:S(2)}, u32[]{:S(2)}) collective-permute-start(bf16[512,512]{1,0:T(8,128)(2,1)} %get-tuple-element.340), channel_id=1, source_target_pairs={{4,0},{8,4},{12,8},{20,16},{24,20},{28,24},{36,32},{40,36},{44,40}... | collective-permute-start | bytes 1572872 | tf_op jit(solution)/shard_map/ppermute | solution.py:929
  605.2 18.6 %collective-permute-start.92 = (bf16[128,1024]{1,0:T(8,128)(2,1)}, bf16[128,1024]{1,0:T(8,128)(2,1)}, u32[]{:S(2)}, u32[]{:S(2)}) collective-permute-start(bf16[128,1024]{1,0:T(8,128)(2,1)} %convolution_convert_fusion.15), channel_id=1, source_target_pairs={{0,2},{1,3},{2,0},{3,1},{4,6},{5,7},{6,4},{7,5},{8,10},{9,11},{10,... | collective-permute-start | bytes 786440 | tf_op jit(solution)/shard_map/ppermute | solution.py:84
  608.0 15.8 %collective-permute-start.93 = (bf16[128,1024]{1,0:T(8,128)(2,1)}, bf16[128,1024]{1,0:T(8,128)(2,1)}, u32[]{:S(2)}, u32[]{:S(2)}) collective-permute-start(bf16[128,1024]{1,0:T(8,128)(2,1)} %convolution_convert_fusion.14), channel_id=1, source_target_pairs={{0,1},{1,2},{2,3},{3,0},{4,5},{5,6},{6,7},{7,4},{8,9},{9,10},{10,1... | collective-permute-start | bytes 786440 | tf_op jit(solution)/shard_map/ppermute | solution.py:84
  613.6 15.0 %collective-permute-start.97 = (bf16[512,512]{1,0:T(8,128)(2,1)}, bf16[512,512]{1,0:T(8,128)(2,1)}, u32[]{:S(2)}, u32[]{:S(2)}) collective-permute-start(bf16[512,512]{1,0:T(8,128)(2,1)} %fusion.22), channel_id=1, source_target_pairs={{0,8},{4,12},{8,0},{12,4},{16,24},{20,28},{24,16},{28,20},{32,40},... | collective-permute-start | bytes 1572872 | tf_op jit(solution)/shard_map/ppermute | solution.py:125
  651.0 15.2 %collective-permute-start.106 = (bf16[128,1024]{1,0:T(8,128)(2,1)S(1)}, bf16[128,1024]{1,0:T(8,128)(2,1)S(1)}, u32[]{:S(2)}, u32[]{:S(2)}) collective-permute-start(bf16[128,1024]{1,0:T(8,128)(2,1)S(1)} %get-tuple-element.375.refs_13_), channel_id=1, source_target_pairs={{2,0},{3,1},{0,2},{1,3},{6,4},{7,5},{4,6},{5,7},{10,8},{11,9},{8,1... | collective-permute-start | bytes 786440 | tf_op jit(solution)/shard_map/ppermute | solution.py:79
  677.7 48.3 %collective-permute-start.122 = (bf16[512,2816]{1,0:T(8,128)(2,1)}, bf16[512,2816]{1,0:T(8,128)(2,1)}, u32[]{:S(2)}, u32[]{:S(2)}) collective-permute-start(bf16[512,2816]{1,0:T(8,128)(2,1)} %get-tuple-element.391), channel_id=1, source_target_pairs={{0,4},{4,0},{8,12},{12,8},{16,20},{20,16},{24,28},{28,24},{32,36},... | collective-permute-start | bytes 8650760 | tf_op jit(solution)/shard_map/ppermute | solution.py:125
  707.2 15.5 %collective-permute-start.116 = (bf16[128,1024]{1,0:T(8,128)(2,1)}, bf16[128,1024]{1,0:T(8,128)(2,1)}, u32[]{:S(2)}, u32[]{:S(2)}) collective-permute-start(bf16[128,1024]{1,0:T(8,128)(2,1)} %add_add_fusion), channel_id=1, source_target_pairs={{2,0},{3,1},{0,2},{1,3},{6,4},{7,5},{4,6},{5,7},{10,8},{11,9},{8,1... | collective-permute-start | bytes 786440 | tf_op jit(solution)/shard_map/ppermute | solution.py:79
  708.7 15.6 %collective-permute-start.117 = (bf16[128,1024]{1,0:T(8,128)(2,1)}, bf16[128,1024]{1,0:T(8,128)(2,1)}, u32[]{:S(2)}, u32[]{:S(2)}) collective-permute-start(bf16[128,1024]{1,0:T(8,128)(2,1)} %add_add_fusion), channel_id=1, source_target_pairs={{3,0},{0,1},{1,2},{2,3},{7,4},{4,5},{5,6},{6,7},{11,8},{8,9},{9,10... | collective-permute-start | bytes 786440 | tf_op jit(solution)/shard_map/ppermute | solution.py:79
  729.1 59.0 %collective-permute-start.121 = (bf16[128,1024]{1,0:T(8,128)(2,1)S(1)}, bf16[128,1024]{1,0:T(8,128)(2,1)S(1)}, u32[]{:S(2)}, u32[]{:S(2)}) collective-permute-start(bf16[128,1024]{1,0:T(8,128)(2,1)S(1)} %convolution_convert_fusion.3), channel_id=1, source_target_pairs={{0,3},{1,0},{2,1},{3,2},{4,7},{5,4},{6,5},{7,6},{8,11},{9,8},{10,9... | collective-permute-start | bytes 786440 | tf_op jit(solution)/shard_map/ppermute | solution.py:84
  731.2 60.1 %collective-permute-start.120 = (bf16[128,1024]{1,0:T(8,128)(2,1)S(1)}, bf16[128,1024]{1,0:T(8,128)(2,1)S(1)}, u32[]{:S(2)}, u32[]{:S(2)}) collective-permute-start(bf16[128,1024]{1,0:T(8,128)(2,1)S(1)} %convolution_convert_fusion.4), channel_id=1, source_target_pairs={{0,1},{1,2},{2,3},{3,0},{4,5},{5,6},{6,7},{7,4},{8,9},{9,10},{10,1... | collective-permute-start | bytes 786440 | tf_op jit(solution)/shard_map/ppermute | solution.py:84
  733.6 17.6 %collective-permute-start.124 = (bf16[4,32,2176]{2,1,0:T(8,128)(2,1)S(1)}, bf16[4,32,2176]{2,1,0:T(8,128)(2,1)S(1)}, u32[]{:S(2)}, u32[]{:S(2)}) collective-permute-start(bf16[4,32,2176]{2,1,0:T(8,128)(2,1)S(1)} %get-tuple-element.500), channel_id=1, source_target_pairs={{0,16},{4,20},{8,24},{12,28},{16,0},{20,4},{24,8},{28,12},{32,48},... | collective-permute-start | bytes 1671176 | tf_op jit(solution)/shard_map/ppermute | solution.py:254
  737.6 24.2 %collective-permute-start.125 = (bf16[4,32,2176]{2,1,0:T(8,128)(2,1)S(1)}, bf16[4,32,2176]{2,1,0:T(8,128)(2,1)S(1)}, u32[]{:S(2)}, u32[]{:S(2)}) collective-permute-start(bf16[4,32,2176]{2,1,0:T(8,128)(2,1)S(1)} %get-tuple-element.502), channel_id=1, source_target_pairs={{0,8},{4,12},{8,16},{12,20},{16,24},{20,28},{24,0},{28,4},{32,40},... | collective-permute-start | bytes 1671176 | tf_op jit(solution)/shard_map/ppermute | solution.py:254
  738.8 24.5 %collective-permute-start.126 = (bf16[4,32,2176]{2,1,0:T(8,128)(2,1)S(1)}, bf16[4,32,2176]{2,1,0:T(8,128)(2,1)S(1)}, u32[]{:S(2)}, u32[]{:S(2)}) collective-permute-start(bf16[4,32,2176]{2,1,0:T(8,128)(2,1)S(1)} %get-tuple-element.501), channel_id=1, source_target_pairs={{0,24},{4,28},{8,0},{12,4},{16,8},{20,12},{24,16},{28,20},{32,56},... | collective-permute-start | bytes 1671176 | tf_op jit(solution)/shard_map/ppermute | solution.py:254
  751.2 16.0 %collective-permute-start.127 = (bf16[4,32,2304]{2,1,0:T(8,128)(2,1)S(1)}, bf16[4,32,2304]{2,1,0:T(8,128)(2,1)S(1)}, u32[]{:S(2)}, u32[]{:S(2)}) collective-permute-start(bf16[4,32,2304]{2,1,0:T(8,128)(2,1)S(1)} %get-tuple-element.497), channel_id=1, source_target_pairs={{0,64},{4,68},{8,72},{12,76},{16,80},{20,84},{24,88},{28,92},{32,9... | collective-permute-start | bytes 1769480 | tf_op jit(solution)/shard_map/ppermute | solution.py:254
  761.9 16.5 %collective-permute-start.128 = (bf16[4,32,2304]{2,1,0:T(8,128)(2,1)S(1)}, bf16[4,32,2304]{2,1,0:T(8,128)(2,1)S(1)}, u32[]{:S(2)}, u32[]{:S(2)}) collective-permute-start(bf16[4,32,2304]{2,1,0:T(8,128)(2,1)S(1)} %get-tuple-element.499), channel_id=1, source_target_pairs={{0,32},{4,36},{8,40},{12,44},{16,48},{20,52},{24,56},{28,60},{32,6... | collective-permute-start | bytes 1769480 | tf_op jit(solution)/shard_map/ppermute | solution.py:254
  763.3 18.0 %collective-permute-start.129 = (bf16[4,32,2304]{2,1,0:T(8,128)(2,1)S(1)}, bf16[4,32,2304]{2,1,0:T(8,128)(2,1)S(1)}, u32[]{:S(2)}, u32[]{:S(2)}) collective-permute-start(bf16[4,32,2304]{2,1,0:T(8,128)(2,1)S(1)} %get-tuple-element.498), channel_id=1, source_target_pairs={{0,96},{4,100},{8,104},{12,108},{16,112},{20,116},{24,120},{28,124... | collective-permute-start | bytes 1769480 | tf_op jit(solution)/shard_map/ppermute | solution.py:254
  767.1 24.1 %collective-permute-start.119 = (bf16[128,1024]{1,0:T(8,128)(2,1)S(1)}, bf16[128,1024]{1,0:T(8,128)(2,1)S(1)}, u32[]{:S(2)}, u32[]{:S(2)}) collective-permute-start(bf16[128,1024]{1,0:T(8,128)(2,1)S(1)} %convolution_convert_fusion.5), channel_id=1, source_target_pairs={{0,2},{1,3},{2,0},{3,1},{4,6},{5,7},{6,4},{7,5},{8,10},{9,11},{10,... | collective-permute-start | bytes 786440 | tf_op jit(solution)/shard_map/ppermute | solution.py:84
  778.3 22.6 %collective-permute-start.136 = (bf16[32,2176]{1,0:T(8,128)(2,1)}, bf16[32,2176]{1,0:T(8,128)(2,1)}, u32[]{:S(2)}, u32[]{:S(2)}) collective-permute-start(bf16[32,2176]{1,0:T(8,128)(2,1)} %get-tuple-element.508), channel_id=1, source_target_pairs={{0,64},{4,68},{8,72},{12,76},{16,80},{20,84},{24,88},{28,92},{32,9... | collective-permute-start | bytes 417800 | tf_op jit(solution)/shard_map/ppermute | solution.py:254
  781.3 22.7 %collective-permute-start.137 = (bf16[32,2176]{1,0:T(8,128)(2,1)}, bf16[32,2176]{1,0:T(8,128)(2,1)}, u32[]{:S(2)}, u32[]{:S(2)}) collective-permute-start(bf16[32,2176]{1,0:T(8,128)(2,1)} %get-tuple-element.510), channel_id=1, source_target_pairs={{0,32},{4,36},{8,40},{12,44},{16,48},{20,52},{24,56},{28,60},{32,6... | collective-permute-start | bytes 417800 | tf_op jit(solution)/shard_map/ppermute | solution.py:254
  788.1 17.5 %collective-permute-start.138 = (bf16[32,2176]{1,0:T(8,128)(2,1)}, bf16[32,2176]{1,0:T(8,128)(2,1)}, u32[]{:S(2)}, u32[]{:S(2)}) collective-permute-start(bf16[32,2176]{1,0:T(8,128)(2,1)} %get-tuple-element.509), channel_id=1, source_target_pairs={{0,96},{4,100},{8,104},{12,108},{16,112},{20,116},{24,120},{28,124... | collective-permute-start | bytes 417800 | tf_op jit(solution)/shard_map/ppermute | solution.py:254
  792.6 35.3 %collective-permute-start.130 = (bf16[128,1024]{1,0:T(8,128)(2,1)S(1)}, bf16[128,1024]{1,0:T(8,128)(2,1)}, u32[]{:S(2)}, u32[]{:S(2)}) collective-permute-start(bf16[128,1024]{1,0:T(8,128)(2,1)S(1)} %get-tuple-element.410), channel_id=1, source_target_pairs={{1,0},{2,1},{3,2},{0,3},{5,4},{6,5},{7,6},{4,7},{9,8},{10,9},{11,1... | collective-permute-start | bytes 786440 | tf_op jit(solution)/shard_map/ppermute | solution.py:79
  795.8 33.7 %collective-permute-start.131 = (bf16[128,1024]{1,0:T(8,128)(2,1)S(1)}, bf16[128,1024]{1,0:T(8,128)(2,1)}, u32[]{:S(2)}, u32[]{:S(2)}) collective-permute-start(bf16[128,1024]{1,0:T(8,128)(2,1)S(1)} %get-tuple-element.410), channel_id=1, source_target_pairs={{2,0},{3,1},{0,2},{1,3},{6,4},{7,5},{4,6},{5,7},{10,8},{11,9},{8,1... | collective-permute-start | bytes 786440 | tf_op jit(solution)/shard_map/ppermute | solution.py:79
  (460 other events, 4170.9 us)
Sparse Core Ops, SparseCore 0:
  483.5 85.9 reduce-scatter.2
  598.9 88.0 reduce-scatter.4
